TPU v7x, 32 devices: a whole 2x2x4 slice. The times are simulated.
32 devices in a mesh: cell: 16 (over z, y, x), qgrp: 2 (over core).
Axes of the slice: x: 2, y: 2, z: 4, core: 2. Of those that a mesh axis runs over, the one named last changes fastest.
Arguments:
- supernode_embeddings: bfloat16 [8192, 768], P('cell'), may hold values from -6 to 6
- filled_supernode_tally: int32 [16], P('cell'), may hold values from 1 to 512, 6144 in all
- hidden_probe_states: bfloat16 [1024, 768], replicated, may hold values from -6 to 6
- softness_per_channel: float32 [2, 12], replicated, may hold values from 1 to 12, as said below
- gather_probe_projector: bfloat16 [768, 768], P(None, 'qgrp'), may hold values from -0.4375 to 0.4375
- gather_lookup_projector: bfloat16 [768, 768], P(None, 'qgrp'), may hold values from -0.4375 to 0.4375
- gather_content_projector: bfloat16 [768, 768], P(None, 'qgrp'), may hold values from -0.21875 to 0.21875
- gather_final_projector: bfloat16 [768, 768], P('qgrp'), may hold values from -0.21875 to 0.21875
- unpack_probe_projector: bfloat16 [768, 768], P(None, 'qgrp'), may hold values from -0.21875 to 0.21875
- unpack_lookup_projector: bfloat16 [768, 768], P(None, 'qgrp'), may hold values from -0.21875 to 0.21875
- unpack_content_projector: bfloat16 [768, 768], P(None, 'qgrp'), may hold values from -0.21875 to 0.21875
- unpack_final_projector: bfloat16 [768, 768], P('qgrp'), may hold values from -0.21875 to 0.21875
- hidden_state_gain: float32 [768], replicated, may hold values from 0.1 to 1.9
Outputs:
- latent_out: float32 [1024, 768], replicated
- tokens_out: float32 [8192, 768], P(('cell', 'qgrp'))
Inputs may be any that keep to these rules, and one draw needn't show every extreme that they name: Slots 0 to filled_supernode_tally[c] - 1 of cell block c hold its valid supernodes; its other slots are padding. `softness_per_channel`: A positive temperature for each head.
All inputs are finite; a program needn't handle non-finite values.
Results may differ from a plain program's by a relative error of at most 0.009.
The roundings to bfloat16 on the way count: a program that leaves them out, or rounds other values in their place, can miss the bound.
Values may be sent and summed in bfloat16 or wider, within the bound.
No kernel may reach another device: no remote copies, remote signals or barrier semaphores. Data moves between devices by JAX's collectives and lax.ppermute only.
A program may use at most 448 MiB of HBM per device.

v0:
```python
import math

import jax
import jax.numpy as jnp
from jax import lax
from jax.sharding import PartitionSpec as P

D = 768
HEADS = 12


MASKED_SCORE = -1e30
NORM_EPSILON = 1e-06


def rms_norm(values, gain):
    mean_square = jnp.mean(values * values, axis=-1, keepdims=True)
    return values * lax.rsqrt(mean_square + NORM_EPSILON) * gain


def masked_scores(queries, key_rows, score_scale, is_valid):
    scores = (
        jnp.einsum("lhd,khd->lhk", queries, key_rows, preferred_element_type=jnp.float32)
        * score_scale[None, :, None]
    )
    return jnp.where(is_valid[None, None, :], scores, jnp.float32(MASKED_SCORE))


def decode_rows(
    row_data, q_weight, k_weight, v_weight, score_scale, latent_half, per_channel_dimension
):
    row_total = row_data.shape[0]
    latent_rows = latent_half.shape[0]
    heads_here = q_weight.shape[1] // per_channel_dimension
    dec_queries = (
        jnp.dot(row_data, q_weight, preferred_element_type=jnp.float32)
        .astype(jnp.bfloat16)
        .reshape(row_total, heads_here, per_channel_dimension)
    )
    dec_keys = (
        jnp.dot(latent_half, k_weight, preferred_element_type=jnp.float32)
        .astype(jnp.bfloat16)
        .reshape(latent_rows, heads_here, per_channel_dimension)
    )
    dec_values = (
        jnp.dot(latent_half, v_weight, preferred_element_type=jnp.float32)
        .astype(jnp.bfloat16)
        .reshape(latent_rows, heads_here, per_channel_dimension)
    )
    row_block = math.gcd(row_total, 512)

    def visit(block_index, buffer):
        scores = (
            jnp.einsum("khd,lhd->khl", dec_queries, dec_keys, preferred_element_type=jnp.float32)
            * score_scale[None, :, None]
        )
        weights = jnp.exp(scores - jnp.max(scores, axis=-1, keepdims=True))
        denominator = jnp.sum(weights, axis=-1)
        mixed_heads = (
            jnp.einsum(
                "khl,lhd->khd",
                weights.astype(jnp.bfloat16),
                dec_values,
                preferred_element_type=jnp.float32,
            )
            / denominator[:, :, None]
        )
        mixed_heads = mixed_heads.astype(jnp.bfloat16).reshape(
            row_block, heads_here * per_channel_dimension
        )
        return mixed_heads

    buffer = jnp.zeros((row_total, heads_here * per_channel_dimension), jnp.bfloat16)
    block_count = row_total // row_block
    return lax.fori_loop(0, block_count, visit, buffer)


def body(
    supernode_embeddings,
    filled_supernode_tally,
    hidden_probe_states,
    softness_per_channel,
    gather_probe_projector,
    gather_lookup_projector,
    gather_content_projector,
    gather_final_projector,
    unpack_probe_projector,
    unpack_lookup_projector,
    unpack_content_projector,
    unpack_final_projector,
    hidden_state_gain,
):
    per_channel_dimension = D // HEADS
    local_channel_total = gather_probe_projector.shape[1] // per_channel_dimension
    slot_count = supernode_embeddings.shape[0]
    latent_rows = hidden_probe_states.shape[0]
    device_ordinal = lax.axis_index("qgrp")
    live_count = filled_supernode_tally[0]
    gather_multiplier = lax.dynamic_slice_in_dim(
        softness_per_channel[0], device_ordinal * local_channel_total, local_channel_total, 0
    ) * per_channel_dimension ** (-0.5)
    queries = (
        jnp.dot(hidden_probe_states, gather_probe_projector, preferred_element_type=jnp.float32)
        .astype(jnp.bfloat16)
        .reshape(latent_rows, local_channel_total, per_channel_dimension)
    )
    key_rows = (
        jnp.dot(supernode_embeddings, gather_lookup_projector, preferred_element_type=jnp.float32)
        .astype(jnp.bfloat16)
        .reshape(slot_count, local_channel_total, per_channel_dimension)
    )
    value_rows = (
        jnp.dot(supernode_embeddings, gather_content_projector, preferred_element_type=jnp.float32)
        .astype(jnp.bfloat16)
        .reshape(slot_count, local_channel_total, per_channel_dimension)
    )
    key_block = math.gcd(slot_count, 512)
    block_count = slot_count // key_block

    def block_scores(block_index):
        offset = block_index * key_block
        is_valid = offset + lax.iota(jnp.int32, key_block) < live_count
        return (masked_scores(queries, key_rows, gather_multiplier, is_valid), is_valid, offset)

    def find_max(block_index, running_max):
        scores, is_valid, offset = block_scores(block_index)
        return jnp.maximum(running_max, jnp.max(scores, axis=-1))

    run_max = lax.fori_loop(
        0,
        block_count,
        find_max,
        jnp.full((latent_rows, local_channel_total), MASKED_SCORE, jnp.float32),
    )

    def accumulate(block_index, running):
        run_sum, run_acc = running
        scores, is_valid, offset = block_scores(block_index)
        weights = jnp.exp(scores - run_max[:, :, None]) * is_valid[None, None, :].astype(
            jnp.float32
        )
        new_sum = run_sum + jnp.sum(weights, axis=-1)
        new_acc = run_acc + jnp.einsum(
            "lhk,khd->lhd",
            weights.astype(jnp.bfloat16),
            value_rows,
            preferred_element_type=jnp.float32,
        )
        return (new_sum, new_acc)

    initial = (
        jnp.zeros((latent_rows, local_channel_total), jnp.float32),
        jnp.zeros((latent_rows, local_channel_total, per_channel_dimension), jnp.float32),
    )
    run_sum, run_acc = lax.fori_loop(0, block_count, accumulate, initial)
    flat_acc = run_acc.reshape(latent_rows, local_channel_total * per_channel_dimension)
    global_max = lax.pmax(run_max, "cell")
    factor = jnp.exp(run_max - global_max)
    total_sum, total_acc = lax.psum(
        (run_sum * factor, flat_acc * jnp.repeat(factor, per_channel_dimension, axis=1)), "cell"
    )
    attended = (total_acc / jnp.repeat(total_sum, per_channel_dimension, axis=1)).astype(
        jnp.bfloat16
    )
    partial_value = jnp.dot(attended, gather_final_projector, preferred_element_type=jnp.float32)
    summed = lax.psum(partial_value, "qgrp")
    latent_out = rms_norm(hidden_probe_states.astype(jnp.float32) + summed, hidden_state_gain)
    latent_half = latent_out.astype(jnp.bfloat16)
    unpack_multiplier_uniform = softness_per_channel[1] * per_channel_dimension ** (-0.5)
    half_rows = slot_count // lax.axis_size("qgrp")
    own_begin = device_ordinal * half_rows
    own_tokens = lax.dynamic_slice_in_dim(supernode_embeddings, own_begin, half_rows, 0)
    own_valid = own_begin + lax.iota(jnp.int32, half_rows) < live_count
    local_scale = lax.dynamic_slice_in_dim(
        unpack_multiplier_uniform, device_ordinal * local_channel_total, local_channel_total, 0
    )
    attended_rows = decode_rows(
        supernode_embeddings,
        unpack_probe_projector,
        unpack_lookup_projector,
        unpack_content_projector,
        local_scale,
        latent_half,
        per_channel_dimension,
    )
    update = lax.psum_scatter(
        jnp.dot(attended_rows, unpack_final_projector, preferred_element_type=jnp.float32),
        "qgrp",
        scatter_dimension=0,
        tiled=True,
    )
    tokens_out = jnp.where(
        own_valid[:, None], own_tokens.astype(jnp.float32) + update, jnp.float32(0.0)
    )
    return (latent_out, tokens_out)


def solution(mesh):
    placed = (
        P("cell", None),
        P("cell"),
        P(),
        P(),
        P(None, "qgrp"),
        P(None, "qgrp"),
        P(None, "qgrp"),
        P("qgrp", None),
        P(None, "qgrp"),
        P(None, "qgrp"),
        P(None, "qgrp"),
        P("qgrp", None),
        P(),
    )
    return jax.shard_map(
        body,
        mesh=mesh,
        in_specs=placed,
        out_specs=(P(), P(("cell", "qgrp"), None)),
        check_vma=False,
    )
```

profile of v0, /device:TPU:0, one launch (start us, length us, event | category | flops | bytes accessed | tf_op | source)
XLA Modules:
  0.0 284.2 jit_solution(17296626207132756466)
XLA Ops:
  7.2 0.0 copy-start
  7.2 0.0 all-reduce.3.cloned.1.call-start
  7.2 0.8 slice_multiply_fusion
  8.7 2.4 convolution_convert_fusion.2
  11.0 1.8 convolution_convert_fusion.4
  12.8 0.1 fusion.26
  12.9 0.0 copy-start.8
  12.9 0.0 copy-start.11
  12.9 5.8 %bitcast_reduce_fusion.1 = (f32[1024,6]{0,1:T(8,128)S(1)}, f32[6,512,1024]{2,1,0:T(8,128)}) fusion(f32[6]{0:T(128)S(1)} %get-tuple-element.56, pred[512]{0:T(512)(128)(4,1)S(1)} %iota_compare_fusion, bf16[512,6,64]{0,2,1:T(8,128)(2,1)S(1)} %bitcast.83, bf16[1024,6,64]{0,2,1:T(8,128)(2,1)S(1)} %bitcast.81), kind=kOutput, calls=%fused_computation.4 | convolution fusion | flops 412084224 | bytes 13787672 | tf_op jit(solution)/shard_map/while/body/eval_jaxpr/lhd,khd->lhk/dot_general | solution.py:23
  18.7 78.6 %pmax.7 = f32[1024,6]{0,1:T(8,128)S(1)} all-reduce(f32[1024,6]{0,1:T(8,128)S(1)} %broadcast_maximum_fusion), channel_id=1, replica_groups=mesh['cell'=16,'qgrp'=2] {'cell'}, use_global_device_ids=true, to_apply=%region_1.0 | all-reduce | flops 6144 | bytes 49152 | tf_op jit(solution)/shard_map/pmax | solution.py:157
  97.3 0.0 copy-done.8
  97.3 0.0 copy-done.11
  97.3 0.5 convolution_convert_fusion.5
  97.8 0.0 copy-start.1
  97.8 7.8 %fusion.5 = f32[1024,6]{0,1:T(8,128)S(1)} fusion(f32[6,512,1024]{2,1,0:T(8,128)} %get-tuple-element.53, f32[512]{0:T(512)S(1)} %fusion.29, f32[1024,6]{0,1:T(8,128)S(1)} %broadcast_maximum_fusion, f32[6]{0:T(128)S(1)} %get-tuple-element.56, pred[512]{0:T(512)(128)(4,1)S(1)} %iota_compare_fusion), kind=kLoop, calls=%fused_computation.10 | loop fusion | flops 15722496 | bytes 12634648 | tf_op jit(solution)/shard_map/while/body/eval_jaxpr/reduce_sum | solution.py:142
  105.6 0.5 copy-done.1
  106.1 4.5 %bitcast_multiply_fusion = f32[1024,6,64]{0,2,1:T(8,128)} fusion(bf16[512,6,64]{0,2,1:T(8,128)(2,1)S(1)} %bitcast.85, f32[6,512,1024]{2,1,0:T(8,128)S(1)} %copy-done.1, f32[512]{0:T(512)S(1)} %fusion.29, f32[1024,6]{0,1:T(8,128)S(1)} %broadcast_maximum_fusion, f32[6]{0:T(128)S(1)} %get-tuple-element.56, pred[512]{0:T(512)(128)(4,1)S(1)} %iota_compare_fusion, ...), kind=kOutput, calls=%fused_computation.19 | convolution fusion | flops 418775040 | bytes 14600728 | tf_op jit(solution)/shard_map/while/body/eval_jaxpr/lhk,khd->lhd/dot_general | solution.py:143
  110.6 0.0 all-reduce.3.cloned.1.call-update
  110.6 0.0 copy-start.4
  110.6 0.0 all-reduce.5.cloned.1.call-start
  110.7 72.5 %psum.22 = f32[1024,6]{0,1:T(8,128)S(1)} all-reduce(f32[1024,6]{0,1:T(8,128)S(1)} %get-tuple-element.48), channel_id=1, replica_groups=mesh['cell'=16,'qgrp'=2] {'cell'}, use_global_device_ids=true, to_apply=%region_4.0 | all-reduce | flops 6144 | bytes 49152 | tf_op jit(solution)/shard_map/psum | solution.py:159
  183.1 41.4 %all-reduce.3.cloned.1.call-done = f32[1024,384]{0,1:T(8,128)} async-done(((f32[1024,384]{0,1:T(8,128)}), f32[1024,384]{0,1:T(8,128)}) %all-reduce.3.cloned.1.call-update) | async-done | bytes 1572880 | tf_op jit(solution)/shard_map/psum | solution.py:159
  224.5 1.6 fusion.11
  226.1 0.0 copy-done
  226.1 0.0 copy-start.10
  226.1 2.7 fusion.31
  228.8 0.0 all-reduce.5.cloned.1.call-update
  228.8 0.2 reduce-scatter.2.cloned.1.call-start
  229.1 1.8 convolution_convert_fusion.3
  230.9 0.0 copy-start.5
  230.9 20.6 %all-reduce.5.cloned.1.call-done = f32[1024,768]{1,0:T(8,128)} async-done(((f32[1024,768]{1,0:T(8,128)}), f32[1024,768]{1,0:T(8,128)}) %all-reduce.5.cloned.1.call-update) | async-done | bytes 3145744 | tf_op jit(solution)/shard_map/psum | solution.py:166
  251.5 0.0 copy-done.4
  251.5 0.0 copy-start.3
  251.5 2.5 multiply_reduce_fusion
  254.1 0.0 copy-start.6
  254.1 0.0 copy-done.10
  254.1 0.3 copy-done.3
  254.4 0.5 multiply_multiply_fusion
  254.8 0.0 copy-done.5
  254.9 0.0 copy-start.2
  254.9 0.8 convolution_convert_fusion
  255.7 0.0 copy-done.6
  255.7 0.8 convolution_convert_fusion.1
  256.5 2.2 bitcast_reduce_fusion
  258.8 0.0 copy-done.2
  258.8 2.1 fusion.3
  260.9 0.0 copy-start.7
  260.9 0.0 copy-start.9
  260.9 2.4 fusion.20
  263.3 0.0 copy-done.7
  263.3 1.8 fusion.32
  265.1 0.0 reduce-scatter.2.cloned.1.call-update
  265.1 10.4 %reduce-scatter.2.cloned.1.call-done = f32[256,768]{1,0:T(8,128)} async-done(((f32[512,768]{1,0:T(8,128)}), f32[256,768]{1,0:T(8,128)}) %reduce-scatter.2.cloned.1.call-update) | async-done | bytes 786448 | tf_op jit(solution)/shard_map/reduce_scatter | solution.py:186
  275.5 0.0 copy-done.9
  275.5 2.1 add_select_fusion
  (6 shorter events, 0.0 us)
Async XLA Ops:
  7.2 218.9 %copy-start = (bf16[384,768]{1,0:T(8,128)(2,1)S(1)}, bf16[384,768]{1,0:T(8,128)(2,1)}, u32[]{:S(2)}) copy-start(bf16[384,768]{1,0:T(8,128)(2,1)} %param.20) | copy-start | bytes 1769476
  7.2 217.3 %all-reduce.3.cloned.1.call-start = ((), (), s32[]{:S(2)}) async-start(), calls=%async_computation.1 | async-start | bytes 3145728 | tf_op jit(solution)/shard_map/psum | solution.py:159
  12.9 84.4 %copy-start.8 = (bf16[512,768]{1,0:T(8,128)(2,1)S(1)}, bf16[512,768]{1,0:T(8,128)(2,1)}, u32[]{:S(2)}) copy-start(bf16[512,768]{1,0:T(8,128)(2,1)} %param.13) | copy-start | bytes 2359300
  12.9 84.4 %copy-start.11 = (bf16[768,384]{1,0:T(8,128)(2,1)S(1)}, bf16[768,384]{1,0:T(8,128)(2,1)}, u32[]{:S(2)}) copy-start(bf16[768,384]{1,0:T(8,128)(2,1)} %param.19) | copy-start | bytes 1769476
  97.8 8.3 %copy-start.1 = (f32[6,512,1024]{2,1,0:T(8,128)S(1)}, f32[6,512,1024]{2,1,0:T(8,128)}, u32[]{:S(2)}) copy-start(f32[6,512,1024]{2,1,0:T(8,128)} %get-tuple-element.53) | copy-start | bytes 37748740
  110.6 140.9 %copy-start.4 = (bf16[1024,768]{1,0:T(8,128)(2,1)S(1)}, bf16[1024,768]{1,0:T(8,128)(2,1)}, u32[]{:S(2)}) copy-start(bf16[1024,768]{1,0:T(8,128)(2,1)} %param.15) | copy-start | bytes 4718596
  110.6 140.9 %all-reduce.5.cloned.1.call-start = ((), (), s32[]{:S(2)}) async-start(), calls=%async_computation.2 | async-start | bytes 6291456 | tf_op jit(solution)/shard_map/psum | solution.py:166
  226.1 28.0 %copy-start.10 = (f32[768]{0:T(1024)S(1)}, f32[768]{0:T(1024)}, u32[]{:S(2)}) copy-start(f32[768]{0:T(1024)} %param.25) | copy-start | bytes 9220
  228.8 46.6 %reduce-scatter.2.cloned.1.call-start = ((), (), s32[]{:S(2)}) async-start(), calls=%async_computation.3 | async-start | bytes 2359296 | tf_op jit(solution)/shard_map/reduce_scatter | solution.py:186
  230.9 24.0 %copy-start.5 = (bf16[768,384]{1,0:T(8,128)(2,1)S(1)}, bf16[768,384]{1,0:T(8,128)(2,1)}, u32[]{:S(2)}) copy-start(bf16[768,384]{1,0:T(8,128)(2,1)} %param.22) | copy-start | bytes 1769476
  251.5 2.8 copy-start.3
  254.1 1.6 copy-start.6
  254.9 3.9 %copy-start.2 = (f32[1024,768]{1,0:T(8,128)}, f32[1024,768]{1,0:T(8,128)S(1)}, u32[]{:S(2)}) copy-start(f32[1024,768]{1,0:T(8,128)S(1)} %multiply_multiply_fusion) | copy-start | bytes 9437188
  260.9 2.4 copy-start.7
  260.9 14.6 %copy-start.9 = (bf16[512,768]{1,0:T(8,128)(2,1)S(1)}, bf16[512,768]{1,0:T(8,128)(2,1)}, u32[]{:S(2)}) copy-start(bf16[512,768]{1,0:T(8,128)(2,1)} %param.13) | copy-start | bytes 2359300
Sparse Core Ops, SparseCore 0:
  110.7 113.7 all-reduce.2
  229.0 22.5 all-reduce.4
  265.2 10.2 reduce-scatter.1
where the time goes:
time: 284 us
  blocking collectives  151 us (53%)
  waiting for transfers between devices  72.5 us (26%)
  matrix products  27.4 us (10%)
  other arithmetic  17.5 us (6%)
  between operations  14.6 us (5%)
    pmax x1, blocking collectives, body(): global_max = lax.pmax(run_max, 'cell')  78.6 us
    psum x1, blocking collectives, body(): lax.psum((run_sum * factor, flat_acc * jnp.repeat(factor, per_channel_dim...  72.5 us
    psum x1, waiting for transfers between devices, body(): lax.psum((run_sum * factor, flat_acc * jnp.repeat(factor, per_channel_dim...  41.4 us
    psum x1, waiting for transfers between devices, body(): summed = lax.psum(partial_value, 'qgrp')  20.6 us
    reduce_scatter x1, waiting for transfers between devices, body(): lax.psum_scatter(jnp.dot(attended_rows, unpack_final_projector, preferred...  10.4 us
    reduce_sum x1, other arithmetic, accumulate(): new_sum = run_sum + jnp.sum(weights, axis=-1)  7.77 us
    dot_general x1, matrix products, masked_scores(): jnp.einsum('lhd,khd->lhk', queries, key_rows, preferred_element_type=jnp....  5.77 us
  transfers between devices with their start and end apart: 3, of which 3 were waited for; matrix products, arithmetic and copies ran while one was open for 1% of the time, Pallas kernels for 0%

commit v1 on v0

v1 whole, which is shorter than its diff:
```python
import functools
import math

import jax
import jax.numpy as jnp
from jax import lax
from jax.experimental import pallas as pl
from jax.experimental.pallas import tpu as pltpu
from jax.sharding import PartitionSpec as P

HEAD_DIM = 64
PAIR = 2 * HEAD_DIM
NORM_EPSILON = 1e-06
LOG2E = math.log2(math.e)
F32 = jnp.float32
BF16 = jnp.bfloat16
MIB = 1 << 20

TERMS = 3


def nn(a, b):
    return lax.dot_general(a, b, (((1,), (0,)), ((), ())), preferred_element_type=F32)


def nt(a, b):
    return lax.dot_general(a, b, (((1,), (1,)), ((), ())), preferred_element_type=F32)


def tn(a, b):
    return lax.dot_general(a, b, (((0,), (0,)), ((), ())), preferred_element_type=F32)


def log_rows(width):
    return -(-TERMS * (width // HEAD_DIM) // 16) * 16


def pack_logs(logs):
    width = logs.shape[1]
    heads = width // HEAD_DIM
    shape = (log_rows(width), width)
    row = lax.broadcasted_iota(jnp.int32, shape, 0)
    lane = lax.broadcasted_iota(jnp.int32, shape, 1)
    total, rest = None, logs
    for term in range(TERMS):
        part = rest.astype(BF16)
        rest = rest - part.astype(F32)
        at = row - term * heads
        pick = (at >= 0) & (at < heads) & (lane == at * HEAD_DIM)
        found = nt(jnp.where(pick, 1.0, 0.0).astype(BF16), part)
        total = found if total is None else total + found
    return total.astype(BF16)


def unpack_logs(packed, width):
    heads = width // HEAD_DIM
    shape = (packed.shape[0], width)
    row = lax.broadcasted_iota(jnp.int32, shape, 0)
    lane_head = lax.shift_right_logical(lax.broadcasted_iota(jnp.int32, shape, 1), 6)
    spread = functools.reduce(
        jnp.logical_or, [row == lane_head + term * heads for term in range(TERMS)]
    )
    return tn(packed, jnp.where(spread, 1.0, 0.0).astype(BF16))


def merge(values_a, logs_a, values_b, logs_b):
    top = jnp.maximum(logs_a, logs_b)
    part_a, part_b = jnp.exp2(logs_a - top), jnp.exp2(logs_b - top)
    whole = part_a + part_b
    return (part_a * values_a + part_b * values_b) / whole, top + jnp.log2(whole)


def scale_row(softness_ref, which, heads):
    first = lax.axis_index("qgrp") * heads
    lane_head = lax.shift_right_logical(
        lax.broadcasted_iota(jnp.int32, (1, heads * HEAD_DIM), 1), 6
    )
    row = jnp.zeros((1, heads * HEAD_DIM), F32)
    for head in range(heads):
        row = jnp.where(lane_head == head, softness_ref[which, first + head], row)
    return row * (HEAD_DIM**-0.5 * LOG2E)


def split_scaled(queries, row):
    scaled = queries.astype(BF16).astype(F32) * row
    high = scaled.astype(BF16)
    return high, (scaled - high.astype(F32)).astype(BF16)


def pair_keys(keys):
    lane = lax.broadcasted_iota(jnp.int32, keys.shape, 1)
    zero = jnp.zeros_like(keys)
    first, second = jnp.where(lane < HEAD_DIM, keys, zero), jnp.where(lane < HEAD_DIM, zero, keys)
    return jnp.concatenate(
        [jnp.concatenate([first, first], axis=1), jnp.concatenate([second, second], axis=1)], axis=0
    )


def pair_values(values, counted):
    lane = lax.broadcasted_iota(jnp.int32, values.shape, 1)
    zero = jnp.zeros_like(values)
    low = lane < HEAD_DIM
    top = jnp.concatenate([jnp.where(low, values, zero), jnp.where(low, counted, zero)], axis=1)
    end = jnp.concatenate([jnp.where(low, zero, values), jnp.where(low, zero, counted)], axis=1)
    return jnp.concatenate([top, end], axis=0)


def attend_pair(high, low, keys, values):
    count = keys.shape[0] // 2
    scores = nt(jnp.concatenate([high, low], axis=1), keys)
    top_a = jnp.max(scores[:, :count], axis=1, keepdims=True)
    top_b = jnp.max(scores[:, count:], axis=1, keepdims=True)
    weights = jnp.concatenate(
        [
            jnp.exp2(scores[:, :count] - top_a).astype(BF16),
            jnp.exp2(scores[:, count:] - top_b).astype(BF16),
        ],
        axis=1,
    )
    sums = nn(weights, values)
    lane = lax.broadcasted_iota(jnp.int32, (high.shape[0], PAIR), 1)
    top = jnp.where(lane < HEAD_DIM, top_a, top_b)
    return sums[:, :PAIR], sums[:, PAIR:], top


def encode_quads(quads, latents, query_weight, keys, values, count, softness, put):
    width = query_weight.shape[1]
    rows = latents.shape[0] // 4
    slots = keys.shape[0]
    row = scale_row(softness, 0, width // HEAD_DIM)
    counted = jnp.where(
        lax.broadcasted_iota(jnp.int32, (slots, PAIR), 0) < count, 1.0, 0.0
    ).astype(BF16)
    queries = []
    for quad in quads:
        part = latents[pl.ds(pl.multiple_of(quad * rows, rows), rows), :]
        queries.append(split_scaled(nn(part, query_weight[...]), row))
    for pair in range(width // PAIR):
        lanes = slice(pair * PAIR, (pair + 1) * PAIR)
        key_block = pair_keys(keys[:, lanes])
        value_block = pair_values(values[:, lanes], counted)
        for index in range(len(quads)):
            high, low = queries[index]
            sums, total, top = attend_pair(high[:, lanes], low[:, lanes], key_block, value_block)
            put(index, lanes, sums / total, top + jnp.log2(total))


def bits_of():
    cell, core = lax.axis_index("cell"), lax.axis_index("qgrp")
    quad = jnp.bitwise_and(cell, 3)
    return quad, core


def encode_send_kernel(
    count, softness, latents, tokens, wq, wk, wv, message, keys_out, values_out, logs
):
    quad, core = bits_of()
    slots, rows = tokens.shape[0], latents.shape[0] // 4
    is_valid = lax.broadcasted_iota(jnp.int32, keys_out.shape, 0) < count[0]
    keys = nn(tokens[...], wk[...])
    keys_out[...] = jnp.where(is_valid, keys, keys[0:1, :]).astype(BF16)
    values_out[...] = jnp.where(is_valid, nn(tokens[...], wv[...]), 0.0).astype(BF16)

    def put(index, lanes, values, log):
        message[index, :rows, lanes] = values.astype(BF16)
        logs[index, :, lanes] = log

    quads = [jnp.bitwise_xor(quad, 3), jnp.bitwise_xor(quad, 1 + core)]
    encode_quads(quads, latents, wq, keys_out, values_out, count[0], softness, put)
    for index in range(2):
        message[index, rows:, :] = jnp.zeros_like(message[index, rows:, :])
        message[index, rows:, :rows] = pack_logs(logs[index])


def encode_keep_kernel(count, softness, latents, wq, keys, values, kept, logs):
    quad, core = bits_of()

    def put(index, lanes, part, log):
        kept[index, :, lanes] = part
        logs[index, :, lanes] = log

    quads = [jnp.bitwise_xor(quad, 2 - core), quad]
    encode_quads(quads, latents, wq, keys, values, count[0], softness, put)


def write_message(message, values, logs):
    rows = values.shape[0]
    message[:rows, :] = values.astype(BF16)
    message[rows:, :] = jnp.zeros_like(message[rows:, :])
    message[rows:, :rows] = pack_logs(logs)


def read_message(message, rows):
    width = message.shape[1]
    return message[:rows, :].astype(F32), unpack_logs(message[rows:, :rows], width)


def merge_two_kernel(values, logs, came, message, kept, kept_logs):
    rows = values.shape[1]
    for index in range(2):
        part, log = merge(values[index], logs[index], *read_message(came.at[index], rows))
        if index == 0:
            write_message(message, part, log)
        else:
            kept[...] = part
            kept_logs[...] = log


def merge_one_kernel(values, logs, came, message):
    rows = values.shape[0]
    part, log = merge(values[...], logs[...], *read_message(came, rows))
    write_message(message, part, log)


def merge_even_kernel(own_bit, other_bit, last, rows, mine, came, out):
    core = lax.axis_index("qgrp")
    bit = jnp.where(core == 0, own_bit, other_bit)
    is_low = jnp.bitwise_and(lax.axis_index("cell"), bit) == 0

    def both(first, second):
        part, log = merge(*read_message(first, rows), *read_message(second, rows))
        if last:
            out[...] = part.astype(BF16)
        else:
            write_message(out, part, log)

    @pl.when(is_low)
    def _():
        both(mine, came)

    @pl.when(jnp.logical_not(is_low))
    def _():
        both(came, mine)


def latent_kernel(attended, other, weight, other_weight, latents, gain, out):
    quad, core = bits_of()
    rows = attended.shape[0]
    start = pl.ds(pl.multiple_of(quad * rows, rows), rows)

    def finish(first, second, first_weight, second_weight):
        update = nn(first[...], first_weight[...]) + nn(second[...], second_weight[...])
        pre = latents[start, :].astype(F32) + update
        mean_square = jnp.mean(pre * pre, axis=-1, keepdims=True)
        out[...] = (pre * lax.rsqrt(mean_square + NORM_EPSILON) * gain[...]).astype(BF16)

    @pl.when(core == 0)
    def _():
        finish(attended, other, weight, other_weight)

    @pl.when(core != 0)
    def _():
        finish(other, attended, other_weight, weight)


def decode_kernel(softness, tokens, wq, wk, wv, own, x_side, y_side, diag_low, diag_high,
                  latent_out, send, keep, gathered):
    quad, core = bits_of()
    rows = own.shape[0]
    width = wq.shape[1]
    pieces = [(own, quad), (x_side, quad ^ 1), (y_side, quad ^ 2)]
    for index, (piece, at) in enumerate(pieces):
        gathered[index * rows:(index + 1) * rows, :] = piece[...]
        latent_out[pl.ds(pl.multiple_of(at * rows, rows), rows), :] = piece[...].astype(F32)
    half = diag_low.shape[0]
    for index, piece in enumerate([diag_low, diag_high]):
        start = 3 * rows + index * half
        gathered[start:start + half, :] = piece[...]
        at = (quad ^ 3) * rows + index * half
        latent_out[pl.ds(pl.multiple_of(at, half), half), :] = piece[...].astype(F32)
    keys = nn(gathered[...], wk[...]).astype(BF16)
    values = nn(gathered[...], wv[...]).astype(BF16)
    row = scale_row(softness, 1, width // HEAD_DIM)
    block = tokens.shape[0] // 2
    outs = [send, keep]
    queries = []
    for index in range(2):
        at = core if index else 1 - core
        part = tokens[pl.ds(pl.multiple_of(at * block, block), block), :]
        queries.append(split_scaled(nn(part, wq[...]), row))
    one = jnp.ones((keys.shape[0], PAIR), BF16)
    for pair in range(width // PAIR):
        lanes = slice(pair * PAIR, (pair + 1) * PAIR)
        key_block = pair_keys(keys[:, lanes])
        value_block = pair_values(values[:, lanes], one)
        for index in range(2):
            high, low = queries[index]
            sums, total, _ = attend_pair(high[:, lanes], low[:, lanes], key_block, value_block)
            outs[index][:, lanes] = (sums / total).astype(BF16)


def tokens_kernel(count, attended, other, weight, other_weight, tokens, out):
    core = lax.axis_index("qgrp")
    rows = attended.shape[0]
    update = nn(attended[...], weight[...]) + nn(other[...], other_weight[...])
    start = core * rows
    own = tokens[pl.ds(pl.multiple_of(start, rows), rows), :].astype(F32)
    is_valid = start + lax.broadcasted_iota(jnp.int32, out.shape, 0) < count[0]
    out[...] = jnp.where(is_valid, own + update, 0.0)


VMEM = pl.BlockSpec(memory_space=pltpu.VMEM)
SMEM = pl.BlockSpec(memory_space=pltpu.SMEM)


def call(kernel, ins, outs, *args, scratch=(), vmem=24, flops=0, name=None):
    shapes = [jax.ShapeDtypeStruct(*out) for out in outs]
    moved = sum(a.size * a.dtype.itemsize for a in [*args, *shapes])
    return pl.pallas_call(
        kernel,
        out_shape=shapes,
        in_specs=[SMEM if kind == "s" else VMEM for kind in ins],
        out_specs=[VMEM] * len(outs),
        scratch_shapes=list(scratch),
        compiler_params=pltpu.CompilerParams(vmem_limit_bytes=vmem * MIB),
        cost_estimate=pl.CostEstimate(flops=flops, bytes_accessed=moved, transcendentals=0),
        name=name,
    )(*args)


def body(tokens, tally, latents, softness, wq, wk, wv, wo, dq, dk, dv, do, gain):
    cells = lax.axis_size("cell")
    total_rows, model = latents.shape
    rows, width = total_rows // 4, wq.shape[1]
    slots = tokens.shape[0]
    half_slots = slots // 2
    deep = rows + log_rows(width)

    def swap(array):
        return lax.ppermute(array, "qgrp", [(0, 1), (1, 0)])

    def trade(array, bit_0, bit_1):
        pairs = []
        for cell in range(cells):
            pairs.append((2 * cell, 2 * (cell ^ bit_0)))
            pairs.append((2 * cell + 1, 2 * (cell ^ bit_1) + 1))
        return lax.ppermute(array, ("cell", "qgrp"), pairs)

    attention = 4 * 512 * slots * width * 4
    message, keys, values = call(
        encode_send_kernel, "ssvvvvv",
        [((2, deep, width), BF16), ((slots, width), BF16), ((slots, width), BF16)],
        tally, softness, latents, tokens, wq, wk, wv,
        scratch=[pltpu.VMEM((2, rows, width), F32)], flops=attention, name="encode_send",
    )
    came = trade(message, 1, 2)
    kept, kept_logs = call(
        encode_keep_kernel, "ssvvvv",
        [((2, rows, width), F32), ((2, rows, width), F32)],
        tally, softness, latents, wq, keys, values, flops=attention, name="encode_keep",
    )
    other_wo, other_do = swap(wo), swap(do)
    message, kept, kept_logs = call(
        merge_two_kernel, "vvv",
        [((deep, width), BF16), ((rows, width), F32), ((rows, width), F32)],
        kept, kept_logs, came, name="merge_two",
    )
    came = trade(message, 2, 1)
    (message,) = call(
        merge_one_kernel, "vvv", [((deep, width), BF16)], kept, kept_logs, came, name="merge_one"
    )
    bits = [4 << i for i in range(max(cells.bit_length() - 3, 0))]
    for index, (bit_0, bit_1) in enumerate(zip(bits, bits[::-1])):
        last = index == len(bits) - 1
        came = trade(message, bit_0, bit_1)
        (message,) = call(
            functools.partial(merge_even_kernel, bit_0, bit_1, last, rows), "vv",
            [((rows if last else deep, width), BF16)], message, came, name="merge_even",
        )
    attended = message[:rows]
    (own,) = call(
        latent_kernel, "vvvvvv", [((rows, model), BF16)],
        attended, swap(attended), wo, other_wo, latents, gain.reshape(1, model), name="latent",
    )
    came = trade(own, 1, 2)
    back = swap(came)
    core = lax.axis_index("qgrp")
    x_side = jnp.where(core == 0, came, back)
    y_side = jnp.where(core == 0, back, came)
    half = rows // 2
    piece = trade(jnp.where(core == 0, y_side[:half], x_side[half:]), 1, 2)
    piece_back = swap(piece)
    diag_low = jnp.where(core == 0, piece, piece_back)
    diag_high = jnp.where(core == 0, piece_back, piece)
    latent_out, send, keep = call(
        decode_kernel, "svvvvvvvvv",
        [((total_rows, model), F32), ((half_slots, width), BF16), ((half_slots, width), BF16)],
        softness, tokens, dq, dk, dv, own, x_side, y_side, diag_low, diag_high,
        scratch=[pltpu.VMEM((total_rows, model), BF16)], vmem=40, name="decode",
    )
    (tokens_out,) = call(
        tokens_kernel, "svvvvv", [((half_slots, model), F32)],
        tally, keep, swap(send), do, other_do, tokens, name="tokens",
    )
    return latent_out, tokens_out


def solution(mesh):
    placed = (
        P("cell", None), P("cell"), P(), P(),
        P(None, "qgrp"), P(None, "qgrp"), P(None, "qgrp"), P("qgrp", None),
        P(None, "qgrp"), P(None, "qgrp"), P(None, "qgrp"), P("qgrp", None), P(),
    )
    return jax.shard_map(
        body, mesh=mesh, in_specs=placed, out_specs=(P(), P(("cell", "qgrp"), None)),
        check_vma=False,
    )
```

time: 284 us -> 79.6 us (0.28)
  blocking collectives: 151 us -> 0 us
  waiting for transfers between devices: 72.5 us -> 34.2 us
  matrix products: 27.4 us -> 0 us
  Pallas kernels: 0 us -> 21.2 us
  other arithmetic: 17.5 us -> 1.22 us
  starting transfers between devices: 0.3 us -> 14.8 us
  between operations: 14.6 us -> 1.48 us
  local copies, waits for them, and re-layouts: 0.82 us -> 6.46 us
    pmax x1 -> x0, blocking collectives: 78.6 us -> none  [body(): global_max = lax.pmax(run_max, 'cell')]
    psum x1 -> x0, blocking collectives: 72.5 us -> none  [body(): lax.psum((run_sum * factor, flat_acc * jnp.repeat(factor, per_channel_dim...]
    psum x2 -> x0, waiting for transfers between devices: 62 us -> none  [the longest x1 41.4 us: body(): lax.psum((run_sum * factor, flat_acc * jnp.repeat(factor, per_channel_dim...]
    ppermute x0 -> x12, waiting for transfers between devices: none -> 34.2 us  [the longest x6 28.5 us: trade(): return lax.ppermute(array, ('cell', 'qgrp'), pairs)]
    dot_general x12 -> x0, matrix products: 27.4 us -> none  [the longest x1 5.77 us: masked_scores(): jnp.einsum('lhd,khd->lhk', queries, key_rows, preferred_element_type=jnp....]
    pallas_call x0 -> x9, Pallas kernels: none -> 21.2 us  [call(): pl.pallas_call(kernel, out_shape=shapes, in_specs=[SMEM if kind == 's' el...]
    ppermute x0 -> x12, starting transfers between devices: none -> 14.8 us  [the longest x6 14 us: trade(): return lax.ppermute(array, ('cell', 'qgrp'), pairs)]
    reduce_sum x3 -> x0, other arithmetic: 12.4 us -> none  [the longest x1 7.77 us: accumulate(): new_sum = run_sum + jnp.sum(weights, axis=-1)]
  transfers between devices with their start and end apart: 3 -> 12, of which waited for: 3 -> 10; matrix products, arithmetic and copies ran while one was open for 1% -> 0% of each run, Pallas kernels for 0% -> 16%
where the time goes in v1:
time: 79.6 us; the launch traced here: 79.3 us
  waiting for transfers between devices  34.2 us (43%)
  Pallas kernels  21.2 us (27%)
  starting transfers between devices  14.8 us (19%)
  local copies, waits for them, and re-layouts  6.46 us (8%)
  between operations  1.48 us (2%)
  other arithmetic  1.22 us (2%)
    ppermute x6, waiting for transfers between devices, trade(): return lax.ppermute(array, ('cell', 'qgrp'), pairs)  28.5 us
    pallas_call x9, Pallas kernels, call(): pl.pallas_call(kernel, out_shape=shapes, in_specs=[SMEM if kind == 's' el...  21.2 us
    ppermute x6, starting transfers between devices, trade(): return lax.ppermute(array, ('cell', 'qgrp'), pairs)  14 us
    unnamed x32, local copies, waits for them, and re-layouts  6.46 us
    ppermute x6, waiting for transfers between devices, swap(): return lax.ppermute(array, 'qgrp', [(0, 1), (1, 0)])  5.63 us
  transfers between devices with their start and end apart: 12, of which 10 were waited for; matrix products, arithmetic and copies ran while one was open for 0% of the time, Pallas kernels for 16%

profile of v1, /device:TPU:0, one launch (start us, length us, event | category | flops | bytes accessed | tf_op | source)
XLA Modules:
  0.0 79.3 jit_solution(3358171779348499675)
XLA Ops:
  1.3 0.0 copy-start
  1.3 1.1 %copy-done = bf16[512,768]{1,0:T(8,128)(2,1)S(1)} copy-done((bf16[512,768]{1,0:T(8,128)(2,1)S(1)}, bf16[512,768]{1,0:T(8,128)(2,1)}, u32[]{:S(2)}) %copy-start) | copy-done | bytes 786456
  2.4 0.0 copy-start.2
  2.4 1.4 %copy-done.2 = bf16[1024,768]{1,0:T(8,128)(2,1)S(1)} copy-done((bf16[1024,768]{1,0:T(8,128)(2,1)S(1)}, bf16[1024,768]{1,0:T(8,128)(2,1)}, u32[]{:S(2)}) %copy-start.2) | copy-done | bytes 1572888
  3.8 0.0 copy-start.9
  3.8 0.7 copy-done.9
  4.5 0.0 copy-start.11
  4.5 1.1 %copy-done.11 = bf16[768,384]{1,0:T(8,128)(2,1)S(1)} copy-done((bf16[768,384]{1,0:T(8,128)(2,1)S(1)}, bf16[768,384]{1,0:T(8,128)(2,1)}, u32[]{:S(2)}) %copy-start.11) | copy-done | bytes 589848
  5.6 0.0 copy-start.12
  5.6 1.1 %copy-done.12 = bf16[768,384]{1,0:T(8,128)(2,1)S(1)} copy-done((bf16[768,384]{1,0:T(8,128)(2,1)S(1)}, bf16[768,384]{1,0:T(8,128)(2,1)}, u32[]{:S(2)}) %copy-start.12) | copy-done | bytes 589848
  6.6 0.0 copy-start.13
  6.6 1.1 %copy-done.13 = bf16[768,384]{1,0:T(8,128)(2,1)S(1)} copy-done((bf16[768,384]{1,0:T(8,128)(2,1)S(1)}, bf16[768,384]{1,0:T(8,128)(2,1)}, u32[]{:S(2)}) %copy-start.13) | copy-done | bytes 589848
  7.7 0.0 copy-start.14
  7.7 4.6 %encode_send.1 = (bf16[2,288,384]{2,1,0:T(8,128)(2,1)S(1)}, bf16[512,384]{1,0:T(8,128)(2,1)S(1)}, bf16[512,384]{1,0:T(8,128)(2,1)S(1)}) custom-call(s32[1]{0:T(128)S(6)} %copy.15.count, f32[2,12]{1,0:T(2,128)S(1)} %copy-done.9, bf16[1024,768]{1,0:T(8,128)(2,1)S(1)} %copy-done.2, bf16[512,768]{1,0:T(8,128)(2,1)S(1)} %copy-done, ...), custom_call_target="tpu_custom_call" | custom-call | flops 1610612736 | bytes 5357668 | tf_op jit(solution)/shard_map/encode_send/pallas_call | solution.py:309
  12.3 3.0 %collective-permute-start = (bf16[2,288,384]{2,1,0:T(8,128)(2,1)S(1)}, bf16[2,288,384]{2,1,0:T(8,128)(2,1)S(1)}, u32[]{:S(2)}, u32[]{:S(2)}) collective-permute-start(bf16[2,288,384]{2,1,0:T(8,128)(2,1)S(1)} %get-tuple-element.17), channel_id=1, source_target_pairs={{0,2},{1,5},{2,0},{3,7},{4,6},{5,1},{6,4},{7,3},{8,10},{9,13},{10,... | collective-permute-start | bytes 1327112 | tf_op jit(solution)/shard_map/ppermute | solution.py:337
  15.3 0.0 copy-done.14
  15.3 3.1 %encode_keep.1 = (f32[2,256,384]{2,1,0:T(8,128)S(1)}, f32[2,256,384]{2,1,0:T(8,128)S(1)}) custom-call(s32[1]{0:T(128)S(6)} %copy.15.count, f32[2,12]{1,0:T(2,128)S(1)} %copy-done.9, bf16[1024,768]{1,0:T(8,128)(2,1)S(1)} %copy-done.2, bf16[768,384]{1,0:T(8,128)(2,1)S(1)} %copy-done.14, bf16[512,384]{1,0:T(8,128)(2,1)S(1)} %get-tuple-element.13.keys, ...), custom_call_target="tpu_custom_call" | custom-call | flops 1610612736 | bytes 4522084 | tf_op jit(solution)/shard_map/encode_keep/pallas_call | solution.py:309
  18.4 0.0 copy-start.15
  18.5 0.0 copy-start.3
  18.5 3.1 %collective-permute-done.came = bf16[2,288,384]{2,1,0:T(8,128)(2,1)S(1)} collective-permute-done((bf16[2,288,384]{2,1,0:T(8,128)(2,1)S(1)}, bf16[2,288,384]{2,1,0:T(8,128)(2,1)S(1)}, u32[]{:S(2)}, u32[]{:S(2)}) %collective-permute-start) | collective-permute-done | bytes 442400 | tf_op jit(solution)/shard_map/ppermute | solution.py:337
  21.6 0.8 %merge_two.1 = (bf16[288,384]{1,0:T(8,128)(2,1)S(1)}, f32[256,384]{1,0:T(8,128)S(1)}, f32[256,384]{1,0:T(8,128)S(1)}) custom-call(f32[2,256,384]{2,1,0:T(8,128)S(1)} %get-tuple-element.15.values, f32[2,256,384]{2,1,0:T(8,128)S(1)} %get-tuple-element.16.logs, bf16[2,288,384]{2,1,0:T(8,128)(2,1)S(1)} %collective-permute-done.came), custom_call_target="tpu_custom_call" | custom-call | bytes 3022848 | tf_op jit(solution)/shard_map/merge_two/pallas_call | solution.py:309
  22.4 2.1 %collective-permute-start.1 = (bf16[288,384]{1,0:T(8,128)(2,1)S(1)}, bf16[288,384]{1,0:T(8,128)(2,1)S(1)}, u32[]{:S(2)}, u32[]{:S(2)}) collective-permute-start(bf16[288,384]{1,0:T(8,128)(2,1)S(1)} %get-tuple-element.20), channel_id=1, source_target_pairs={{0,4},{1,3},{2,6},{3,1},{4,0},{5,7},{6,2},{7,5},{8,12},{9,11},{10,... | collective-permute-start | bytes 663560 | tf_op jit(solution)/shard_map/ppermute | solution.py:337
  24.6 3.9 %collective-permute-done.1.came = bf16[288,384]{1,0:T(8,128)(2,1)S(1)} collective-permute-done((bf16[288,384]{1,0:T(8,128)(2,1)S(1)}, bf16[288,384]{1,0:T(8,128)(2,1)S(1)}, u32[]{:S(2)}, u32[]{:S(2)}) %collective-permute-start.1) | collective-permute-done | bytes 221216 | tf_op jit(solution)/shard_map/ppermute | solution.py:337
  28.5 0.6 merge_one.1.mine
  29.1 2.1 %collective-permute-start.2 = (bf16[288,384]{1,0:T(8,128)(2,1)S(1)}, bf16[288,384]{1,0:T(8,128)(2,1)S(1)}, u32[]{:S(2)}, u32[]{:S(2)}) collective-permute-start(bf16[288,384]{1,0:T(8,128)(2,1)S(1)} %merge_one.1.mine), channel_id=1, source_target_pairs={{0,8},{1,17},{2,10},{3,19},{4,12},{5,21},{6,14},{7,23},{8,0},{9,25... | collective-permute-start | bytes 663560 | tf_op jit(solution)/shard_map/ppermute | solution.py:337
  31.2 0.0 copy-done.7
  31.3 0.0 collective-permute-start.5
  31.3 5.1 %collective-permute-done.2.came = bf16[288,384]{1,0:T(8,128)(2,1)S(1)} collective-permute-done((bf16[288,384]{1,0:T(8,128)(2,1)S(1)}, bf16[288,384]{1,0:T(8,128)(2,1)S(1)}, u32[]{:S(2)}, u32[]{:S(2)}) %collective-permute-start.2) | collective-permute-done | bytes 221216 | tf_op jit(solution)/shard_map/ppermute | solution.py:337
  36.4 0.7 merge_even.2.mine
  37.1 3.2 %collective-permute-start.3 = (bf16[288,384]{1,0:T(8,128)(2,1)S(1)}, bf16[288,384]{1,0:T(8,128)(2,1)S(1)}, u32[]{:S(2)}, u32[]{:S(2)}) collective-permute-start(bf16[288,384]{1,0:T(8,128)(2,1)S(1)} %merge_even.2.mine), channel_id=1, source_target_pairs={{0,16},{1,9},{2,18},{3,11},{4,20},{5,13},{6,22},{7,15},{8,24},{9,1... | collective-permute-start | bytes 663560 | tf_op jit(solution)/shard_map/ppermute | solution.py:337
  40.3 6.3 %collective-permute-done.3.came = bf16[288,384]{1,0:T(8,128)(2,1)S(1)} collective-permute-done((bf16[288,384]{1,0:T(8,128)(2,1)S(1)}, bf16[288,384]{1,0:T(8,128)(2,1)S(1)}, u32[]{:S(2)}, u32[]{:S(2)}) %collective-permute-start.3) | collective-permute-done | bytes 221216 | tf_op jit(solution)/shard_map/ppermute | solution.py:337
  46.6 0.4 merge_even.3.attended
  47.0 0.1 collective-permute-start.4
  47.1 0.0 copy-done.15
  47.1 0.0 copy-start.1
  47.1 0.0 copy-start.4
  47.1 0.0 copy-start.5
  47.2 0.0 copy-start.6
  47.2 0.0 copy-start.10
  47.2 0.0 collective-permute-done.5.other_weight
  47.2 1.3 %collective-permute-done.4.other = bf16[256,384]{1,0:T(8,128)(2,1)S(1)} collective-permute-done((bf16[256,384]{1,0:T(8,128)(2,1)S(1)}, bf16[256,384]{1,0:T(8,128)(2,1)S(1)}, u32[]{:S(2)}, u32[]{:S(2)}) %collective-permute-start.4) | collective-permute-done | bytes 196640 | tf_op jit(solution)/shard_map/ppermute | solution.py:330
  48.5 0.0 copy-done.3
  48.5 0.9 %latent.1.own = bf16[256,768]{1,0:T(8,128)(2,1)S(1)} custom-call(bf16[256,384]{1,0:T(8,128)(2,1)S(1)} %merge_even.3.attended, bf16[256,384]{1,0:T(8,128)(2,1)S(1)} %collective-permute-done.4.other, bf16[384,768]{1,0:T(8,128)(2,1)S(1)} %copy-done.7, bf16[384,768]{1,0:T(8,128)(2,1)S(1)} %collective-permute-done.5.other_weight, ...), custom_call_target="tpu_custom_call" | custom-call | bytes 3542016 | tf_op jit(solution)/shard_map/latent/pallas_call | solution.py:309
  49.4 1.8 %collective-permute-start.6 = (bf16[256,768]{1,0:T(8,128)(2,1)S(1)}, bf16[256,768]{1,0:T(8,128)(2,1)}, u32[]{:S(2)}, u32[]{:S(2)}) collective-permute-start(bf16[256,768]{1,0:T(8,128)(2,1)S(1)} %latent.1.own), channel_id=1, source_target_pairs={{0,2},{1,5},{2,0},{3,7},{4,6},{5,1},{6,4},{7,3},{8,10},{9,13},{10,... | collective-permute-start | bytes 1179656 | tf_op jit(solution)/shard_map/ppermute | solution.py:337
  51.2 6.2 %collective-permute-done.6 = bf16[256,768]{1,0:T(8,128)(2,1)} collective-permute-done((bf16[256,768]{1,0:T(8,128)(2,1)S(1)}, bf16[256,768]{1,0:T(8,128)(2,1)}, u32[]{:S(2)}, u32[]{:S(2)}) %collective-permute-start.6) | collective-permute-done | bytes 393248 | tf_op jit(solution)/shard_map/ppermute | solution.py:337
  57.4 0.0 collective-permute-start.7
  57.4 2.1 %collective-permute-done.7 = bf16[256,768]{1,0:T(8,128)(2,1)} collective-permute-done((bf16[256,768]{1,0:T(8,128)(2,1)}, bf16[256,768]{1,0:T(8,128)(2,1)}, u32[]{:S(2)}, u32[]{:S(2)}) %collective-permute-start.7) | collective-permute-done | bytes 393248 | tf_op jit(solution)/shard_map/ppermute | solution.py:330
  59.4 1.2 %broadcast_select_fusion = (bf16[256,768]{1,0:T(8,128)(2,1)S(1)}, bf16[256,768]{1,0:T(8,128)(2,1)S(1)}) fusion(bf16[256,768]{1,0:T(8,128)(2,1)} %collective-permute-done.7, bf16[256,768]{1,0:T(8,128)(2,1)} %collective-permute-done.6, pred[]{:T(512)S(6)} %eq.2), kind=kLoop, calls=%fused_computation | loop fusion | flops 393216 | bytes 1572865 | tf_op jit(solution)/shard_map/jit(_where)/select_n | solution.py:379
  60.6 1.8 %collective-permute-start.8 = (bf16[128,768]{1,0:T(8,128)(2,1)S(1)}, bf16[128,768]{1,0:T(8,128)(2,1)S(1)}, u32[]{:S(2)}, u32[]{:S(2)}) collective-permute-start(bf16[128,768]{1,0:T(8,128)(2,1)S(1)} %slice_select_fusion), channel_id=1, source_target_pairs={{0,2},{1,5},{2,0},{3,7},{4,6},{5,1},{6,4},{7,3},{8,10},{9,13},{10,... | collective-permute-start | bytes 589832 | tf_op jit(solution)/shard_map/ppermute | solution.py:337
  62.4 3.9 %collective-permute-done.8 = bf16[128,768]{1,0:T(8,128)(2,1)S(1)} collective-permute-done((bf16[128,768]{1,0:T(8,128)(2,1)S(1)}, bf16[128,768]{1,0:T(8,128)(2,1)S(1)}, u32[]{:S(2)}, u32[]{:S(2)}) %collective-permute-start.8) | collective-permute-done | bytes 196640 | tf_op jit(solution)/shard_map/ppermute | solution.py:337
  66.4 0.0 collective-permute-start.9
  66.4 0.0 copy-done.8
  66.4 0.5 collective-permute-start.11
  66.9 0.9 %collective-permute-done.9 = bf16[128,768]{1,0:T(8,128)(2,1)S(1)} collective-permute-done((bf16[128,768]{1,0:T(8,128)(2,1)S(1)}, bf16[128,768]{1,0:T(8,128)(2,1)S(1)}, u32[]{:S(2)}, u32[]{:S(2)}) %collective-permute-start.9) | collective-permute-done | bytes 196640 | tf_op jit(solution)/shard_map/ppermute | solution.py:330
  67.9 0.0 copy-done.1
  67.9 0.0 copy-done.4
  67.9 0.0 copy-done.5
  67.9 0.0 copy-done.6
  67.9 0.0 copy-done.10
  67.9 8.5 %decode.1 = (f32[1024,768]{1,0:T(8,128)}, bf16[256,384]{1,0:T(8,128)(2,1)S(1)}, bf16[256,384]{1,0:T(8,128)(2,1)S(1)}) custom-call(f32[2,12]{1,0:T(2,128)S(1)} %copy-done.10, bf16[512,768]{1,0:T(8,128)(2,1)S(1)} %copy-done.1, bf16[768,384]{1,0:T(8,128)(2,1)S(1)} %copy-done.4, bf16[768,384]{1,0:T(8,128)(2,1)S(1)} %copy-done.5, bf16[768,384]{1,0:T(8,128)(2,1)S(1)} %copy-done.6, ...), custom_call_target="tpu_custom_call" | custom-call | bytes 7667808 | tf_op jit(solution)/shard_map/decode/pallas_call | solution.py:309
  76.4 0.1 collective-permute-start.10
  76.5 0.0 collective-permute-done.11.other_weight
  76.5 1.3 %collective-permute-done.10.other = bf16[256,384]{1,0:T(8,128)(2,1)S(1)} collective-permute-done((bf16[256,384]{1,0:T(8,128)(2,1)S(1)}, bf16[256,384]{1,0:T(8,128)(2,1)S(1)}, u32[]{:S(2)}, u32[]{:S(2)}) %collective-permute-start.10) | collective-permute-done | bytes 196640 | tf_op jit(solution)/shard_map/ppermute | solution.py:330
  77.8 1.4 %tokens.6 = f32[256,768]{1,0:T(8,128)} custom-call(s32[1]{0:T(128)S(6)} %copy.15.count, bf16[256,384]{1,0:T(8,128)(2,1)S(1)} %get-tuple-element.22.attended, bf16[256,384]{1,0:T(8,128)(2,1)S(1)} %collective-permute-done.10.other, bf16[384,768]{1,0:T(8,128)(2,1)S(1)} %copy-done.8, bf16[384,768]{1,0:T(8,128)(2,1)S(1)} %collective-permute-done.11.other_weight, ...), custom_call_target="tpu_custom_call" | custom-call | bytes 3145732 | tf_op jit(solution)/shard_map/tokens/pallas_call | solution.py:309
  (5 shorter events, 0.1 us)
Async XLA Ops:
  1.3 1.1 %copy-start = (bf16[512,768]{1,0:T(8,128)(2,1)S(1)}, bf16[512,768]{1,0:T(8,128)(2,1)}, u32[]{:S(2)}) copy-start(bf16[512,768]{1,0:T(8,128)(2,1)} %tokens.7) | copy-start | bytes 2359300
  2.4 1.4 %copy-start.2 = (bf16[1024,768]{1,0:T(8,128)(2,1)S(1)}, bf16[1024,768]{1,0:T(8,128)(2,1)}, u32[]{:S(2)}) copy-start(bf16[1024,768]{1,0:T(8,128)(2,1)} %latents.5) | copy-start | bytes 4718596
  3.8 0.7 copy-start.9
  4.5 1.1 %copy-start.11 = (bf16[768,384]{1,0:T(8,128)(2,1)S(1)}, bf16[768,384]{1,0:T(8,128)(2,1)}, u32[]{:S(2)}) copy-start(bf16[768,384]{1,0:T(8,128)(2,1)} %wk.2) | copy-start | bytes 1769476
  5.6 1.1 %copy-start.12 = (bf16[768,384]{1,0:T(8,128)(2,1)S(1)}, bf16[768,384]{1,0:T(8,128)(2,1)}, u32[]{:S(2)}) copy-start(bf16[768,384]{1,0:T(8,128)(2,1)} %wv.2) | copy-start | bytes 1769476
  6.6 1.1 %copy-start.13 = (bf16[768,384]{1,0:T(8,128)(2,1)S(1)}, bf16[768,384]{1,0:T(8,128)(2,1)}, u32[]{:S(2)}) copy-start(bf16[768,384]{1,0:T(8,128)(2,1)} %wq.4) | copy-start | bytes 1769476
  7.7 7.6 %copy-start.14 = (bf16[768,384]{1,0:T(8,128)(2,1)S(1)}, bf16[768,384]{1,0:T(8,128)(2,1)}, u32[]{:S(2)}) copy-start(bf16[768,384]{1,0:T(8,128)(2,1)} %wq.4) | copy-start | bytes 1769476
  12.3 9.3 %collective-permute-start = (bf16[2,288,384]{2,1,0:T(8,128)(2,1)S(1)}, bf16[2,288,384]{2,1,0:T(8,128)(2,1)S(1)}, u32[]{:S(2)}, u32[]{:S(2)}) collective-permute-start(bf16[2,288,384]{2,1,0:T(8,128)(2,1)S(1)} %get-tuple-element.17), channel_id=1, source_target_pairs={{0,2},{1,5},{2,0},{3,7},{4,6},{5,1},{6,4},{7,3},{8,10},{9,13},{10,... | collective-permute-start | bytes 1327112 | tf_op jit(solution)/shard_map/ppermute | solution.py:337
  15.3 15.9 %copy-start.7 = (bf16[384,768]{1,0:T(8,128)(2,1)S(1)}, bf16[384,768]{1,0:T(8,128)(2,1)}, u32[]{:S(2)}) copy-start(bf16[384,768]{1,0:T(8,128)(2,1)} %weight.2) | copy-start | bytes 1769476
  18.4 28.7 %copy-start.15 = (f32[768]{0:T(1024)S(1)}, f32[768]{0:T(1024)}, u32[]{:S(2)}) copy-start(f32[768]{0:T(1024)} %param.25) | copy-start | bytes 9220
  18.5 30.1 %copy-start.3 = (bf16[1024,768]{1,0:T(8,128)(2,1)S(1)}, bf16[1024,768]{1,0:T(8,128)(2,1)}, u32[]{:S(2)}) copy-start(bf16[1024,768]{1,0:T(8,128)(2,1)} %latents.5) | copy-start | bytes 4718596
  22.4 6.0 %collective-permute-start.1 = (bf16[288,384]{1,0:T(8,128)(2,1)S(1)}, bf16[288,384]{1,0:T(8,128)(2,1)S(1)}, u32[]{:S(2)}, u32[]{:S(2)}) collective-permute-start(bf16[288,384]{1,0:T(8,128)(2,1)S(1)} %get-tuple-element.20), channel_id=1, source_target_pairs={{0,4},{1,3},{2,6},{3,1},{4,0},{5,7},{6,2},{7,5},{8,12},{9,11},{10,... | collective-permute-start | bytes 663560 | tf_op jit(solution)/shard_map/ppermute | solution.py:337
  29.1 7.3 %collective-permute-start.2 = (bf16[288,384]{1,0:T(8,128)(2,1)S(1)}, bf16[288,384]{1,0:T(8,128)(2,1)S(1)}, u32[]{:S(2)}, u32[]{:S(2)}) collective-permute-start(bf16[288,384]{1,0:T(8,128)(2,1)S(1)} %merge_one.1.mine), channel_id=1, source_target_pairs={{0,8},{1,17},{2,10},{3,19},{4,12},{5,21},{6,14},{7,23},{8,0},{9,25... | collective-permute-start | bytes 663560 | tf_op jit(solution)/shard_map/ppermute | solution.py:337
  31.3 15.9 %collective-permute-start.5 = (bf16[384,768]{1,0:T(8,128)(2,1)S(1)}, bf16[384,768]{1,0:T(8,128)(2,1)S(1)}, u32[]{:S(2)}, u32[]{:S(2)}) collective-permute-start(bf16[384,768]{1,0:T(8,128)(2,1)S(1)} %copy-done.7), channel_id=1, source_target_pairs={{0,1},{1,0},{2,3},{3,2},{4,5},{5,4},{6,7},{7,6},{8,9},{9,8},{10,11... | collective-permute-start | bytes 1769480 | tf_op jit(solution)/shard_map/ppermute | solution.py:330
  37.1 29.3 %copy-start.8 = (bf16[384,768]{1,0:T(8,128)(2,1)S(1)}, bf16[384,768]{1,0:T(8,128)(2,1)}, u32[]{:S(2)}) copy-start(bf16[384,768]{1,0:T(8,128)(2,1)} %weight.3) | copy-start | bytes 1769476
  37.1 9.5 %collective-permute-start.3 = (bf16[288,384]{1,0:T(8,128)(2,1)S(1)}, bf16[288,384]{1,0:T(8,128)(2,1)S(1)}, u32[]{:S(2)}, u32[]{:S(2)}) collective-permute-start(bf16[288,384]{1,0:T(8,128)(2,1)S(1)} %merge_even.2.mine), channel_id=1, source_target_pairs={{0,16},{1,9},{2,18},{3,11},{4,20},{5,13},{6,22},{7,15},{8,24},{9,1... | collective-permute-start | bytes 663560 | tf_op jit(solution)/shard_map/ppermute | solution.py:337
  47.0 1.5 %collective-permute-start.4 = (bf16[256,384]{1,0:T(8,128)(2,1)S(1)}, bf16[256,384]{1,0:T(8,128)(2,1)S(1)}, u32[]{:S(2)}, u32[]{:S(2)}) collective-permute-start(bf16[256,384]{1,0:T(8,128)(2,1)S(1)} %merge_even.3.attended), channel_id=1, source_target_pairs={{0,1},{1,0},{2,3},{3,2},{4,5},{5,4},{6,7},{7,6},{8,9},{9,8},{10,11... | collective-permute-start | bytes 589832 | tf_op jit(solution)/shard_map/ppermute | solution.py:330
  47.1 20.7 %copy-start.1 = (bf16[512,768]{1,0:T(8,128)(2,1)S(1)}, bf16[512,768]{1,0:T(8,128)(2,1)}, u32[]{:S(2)}) copy-start(bf16[512,768]{1,0:T(8,128)(2,1)} %tokens.7) | copy-start | bytes 2359300
  47.1 20.7 %copy-start.4 = (bf16[768,384]{1,0:T(8,128)(2,1)S(1)}, bf16[768,384]{1,0:T(8,128)(2,1)}, u32[]{:S(2)}) copy-start(bf16[768,384]{1,0:T(8,128)(2,1)} %wq.5) | copy-start | bytes 1769476
  47.1 20.7 %copy-start.5 = (bf16[768,384]{1,0:T(8,128)(2,1)S(1)}, bf16[768,384]{1,0:T(8,128)(2,1)}, u32[]{:S(2)}) copy-start(bf16[768,384]{1,0:T(8,128)(2,1)} %wk.3) | copy-start | bytes 1769476
  47.2 20.7 %copy-start.6 = (bf16[768,384]{1,0:T(8,128)(2,1)S(1)}, bf16[768,384]{1,0:T(8,128)(2,1)}, u32[]{:S(2)}) copy-start(bf16[768,384]{1,0:T(8,128)(2,1)} %wv.3) | copy-start | bytes 1769476
  47.2 20.7 %copy-start.10 = (f32[2,12]{1,0:T(2,128)S(1)}, f32[2,12]{1,0:T(2,128)}, u32[]{:S(2)}) copy-start(f32[2,12]{1,0:T(2,128)} %softness.5) | copy-start | bytes 292
  49.4 7.9 %collective-permute-start.6 = (bf16[256,768]{1,0:T(8,128)(2,1)S(1)}, bf16[256,768]{1,0:T(8,128)(2,1)}, u32[]{:S(2)}, u32[]{:S(2)}) collective-permute-start(bf16[256,768]{1,0:T(8,128)(2,1)S(1)} %latent.1.own), channel_id=1, source_target_pairs={{0,2},{1,5},{2,0},{3,7},{4,6},{5,1},{6,4},{7,3},{8,10},{9,13},{10,... | collective-permute-start | bytes 1179656 | tf_op jit(solution)/shard_map/ppermute | solution.py:337
  57.4 2.1 %collective-permute-start.7 = (bf16[256,768]{1,0:T(8,128)(2,1)}, bf16[256,768]{1,0:T(8,128)(2,1)}, u32[]{:S(2)}, u32[]{:S(2)}) collective-permute-start(bf16[256,768]{1,0:T(8,128)(2,1)} %collective-permute-done.6), channel_id=1, source_target_pairs={{0,1},{1,0},{2,3},{3,2},{4,5},{5,4},{6,7},{7,6},{8,9},{9,8},{10,11... | collective-permute-start | bytes 1179656 | tf_op jit(solution)/shard_map/ppermute | solution.py:330
  60.6 5.7 %collective-permute-start.8 = (bf16[128,768]{1,0:T(8,128)(2,1)S(1)}, bf16[128,768]{1,0:T(8,128)(2,1)S(1)}, u32[]{:S(2)}, u32[]{:S(2)}) collective-permute-start(bf16[128,768]{1,0:T(8,128)(2,1)S(1)} %slice_select_fusion), channel_id=1, source_target_pairs={{0,2},{1,5},{2,0},{3,7},{4,6},{5,1},{6,4},{7,3},{8,10},{9,13},{10,... | collective-permute-start | bytes 589832 | tf_op jit(solution)/shard_map/ppermute | solution.py:337
  66.4 1.4 %collective-permute-start.9 = (bf16[128,768]{1,0:T(8,128)(2,1)S(1)}, bf16[128,768]{1,0:T(8,128)(2,1)S(1)}, u32[]{:S(2)}, u32[]{:S(2)}) collective-permute-start(bf16[128,768]{1,0:T(8,128)(2,1)S(1)} %collective-permute-done.8), channel_id=1, source_target_pairs={{0,1},{1,0},{2,3},{3,2},{4,5},{5,4},{6,7},{7,6},{8,9},{9,8},{10,11... | collective-permute-start | bytes 589832 | tf_op jit(solution)/shard_map/ppermute | solution.py:330
  66.4 10.1 %collective-permute-start.11 = (bf16[384,768]{1,0:T(8,128)(2,1)S(1)}, bf16[384,768]{1,0:T(8,128)(2,1)S(1)}, u32[]{:S(2)}, u32[]{:S(2)}) collective-permute-start(bf16[384,768]{1,0:T(8,128)(2,1)S(1)} %copy-done.8), channel_id=1, source_target_pairs={{0,1},{1,0},{2,3},{3,2},{4,5},{5,4},{6,7},{7,6},{8,9},{9,8},{10,11... | collective-permute-start | bytes 1769480 | tf_op jit(solution)/shard_map/ppermute | solution.py:330
  76.4 1.4 %collective-permute-start.10 = (bf16[256,384]{1,0:T(8,128)(2,1)S(1)}, bf16[256,384]{1,0:T(8,128)(2,1)S(1)}, u32[]{:S(2)}, u32[]{:S(2)}) collective-permute-start(bf16[256,384]{1,0:T(8,128)(2,1)S(1)} %get-tuple-element.23), channel_id=1, source_target_pairs={{0,1},{1,0},{2,3},{3,2},{4,5},{5,4},{6,7},{7,6},{8,9},{9,8},{10,11... | collective-permute-start | bytes 589832 | tf_op jit(solution)/shard_map/ppermute | solution.py:330

commit v2 on v1

v2 whole, which is shorter than its diff:
```python
import functools
import math

import jax
import jax.numpy as jnp
from jax import lax
from jax.experimental import pallas as pl
from jax.experimental.pallas import tpu as pltpu
from jax.sharding import PartitionSpec as P

HEAD_DIM = 64
PAIR = 2 * HEAD_DIM
NORM_EPSILON = 1e-06
LOG2E = math.log2(math.e)
F32 = jnp.float32
BF16 = jnp.bfloat16
MIB = 1 << 20


def nn(a, b):
    return lax.dot_general(a, b, (((1,), (0,)), ((), ())), preferred_element_type=F32)


def nt(a, b):
    return lax.dot_general(a, b, (((1,), (1,)), ((), ())), preferred_element_type=F32)


def tn(a, b):
    return lax.dot_general(a, b, (((0,), (0,)), ((), ())), preferred_element_type=F32)


def log_rows(width):
    return -(-2 * (width // HEAD_DIM) // 16) * 16


def spread_of(shape, first, heads):
    row = lax.broadcasted_iota(jnp.int32, shape, 0) - first
    lane = lax.broadcasted_iota(jnp.int32, shape, 1)
    return row, lane, (row >= 0) & (row < heads)


def pack_logs(logs):
    rows, width = logs.shape
    heads, half = width // HEAD_DIM, rows // 2

    def found(part, first):
        row, lane, inside = spread_of((log_rows(width), width), first, heads)
        pick = inside & (lane == row * HEAD_DIM)
        return nt(jnp.where(pick, 1.0, 0.0).astype(BF16), part)

    high = logs.astype(BF16)
    rest = logs - high.astype(F32)
    middle = rest.astype(BF16)
    low = (rest - middle.astype(F32)).astype(BF16)
    below = found(high, 0) + found(middle, heads)
    beside = found(low[:half], 0) + found(low[half:], heads)
    return jnp.concatenate([below, beside], axis=1).astype(BF16)


def unpack_logs(packed, width):
    heads = width // HEAD_DIM
    rows = packed.shape[1] * 2 // 3

    def spread(first):
        row, lane, inside = spread_of((packed.shape[0], width), first, heads)
        return inside & (lax.shift_right_logical(lane, 6) == row)

    def as_matrix(mask):
        return jnp.where(mask, 1.0, 0.0).astype(BF16)

    top, end = spread(0), spread(heads)
    beside = packed[:, rows:]
    low = jnp.concatenate([tn(beside, as_matrix(top)), tn(beside, as_matrix(end))], axis=0)
    return tn(packed[:, :rows], as_matrix(top | end)) + low


def merge(values_a, logs_a, values_b, logs_b):
    top = jnp.maximum(logs_a, logs_b)
    part_a, part_b = jnp.exp2(logs_a - top), jnp.exp2(logs_b - top)
    whole = part_a + part_b
    return (part_a * values_a + part_b * values_b) / whole, top + jnp.log2(whole)


def scale_row(softness_ref, which, heads):
    first = lax.axis_index("qgrp") * heads
    lane_head = lax.shift_right_logical(
        lax.broadcasted_iota(jnp.int32, (1, heads * HEAD_DIM), 1), 6
    )
    row = jnp.zeros((1, heads * HEAD_DIM), F32)
    for head in range(heads):
        row = jnp.where(lane_head == head, softness_ref[which, first + head], row)
    return row * (HEAD_DIM**-0.5 * LOG2E)


def split_scaled(queries, row):
    scaled = queries.astype(BF16).astype(F32) * row
    high = scaled.astype(BF16)
    return high, (scaled - high.astype(F32)).astype(BF16)


def pair_keys(keys):
    lane = lax.broadcasted_iota(jnp.int32, keys.shape, 1)
    zero = jnp.zeros_like(keys)
    first, second = jnp.where(lane < HEAD_DIM, keys, zero), jnp.where(lane < HEAD_DIM, zero, keys)
    return jnp.concatenate(
        [jnp.concatenate([first, first], axis=1), jnp.concatenate([second, second], axis=1)], axis=0
    )


def pair_values(values, counted):
    lane = lax.broadcasted_iota(jnp.int32, values.shape, 1)
    zero = jnp.zeros_like(values)
    low = lane < HEAD_DIM
    top = jnp.concatenate([jnp.where(low, values, zero), jnp.where(low, counted, zero)], axis=1)
    end = jnp.concatenate([jnp.where(low, zero, values), jnp.where(low, zero, counted)], axis=1)
    return jnp.concatenate([top, end], axis=0)


def attend_pair(high, low, keys, values):
    count = keys.shape[0] // 2
    scores = nt(jnp.concatenate([high, low], axis=1), keys)
    top_a = jnp.max(scores[:, :count], axis=1, keepdims=True)
    top_b = jnp.max(scores[:, count:], axis=1, keepdims=True)
    weights = jnp.concatenate(
        [
            jnp.exp2(scores[:, :count] - top_a).astype(BF16),
            jnp.exp2(scores[:, count:] - top_b).astype(BF16),
        ],
        axis=1,
    )
    sums = nn(weights, values)
    lane = lax.broadcasted_iota(jnp.int32, (high.shape[0], PAIR), 1)
    top = jnp.where(lane < HEAD_DIM, top_a, top_b)
    return sums[:, :PAIR], sums[:, PAIR:], top


def encode_rows(part, query_weight, keys, values, count, scale, put):
    width = query_weight.shape[1]
    slots = keys.shape[0]
    slot = lax.broadcasted_iota(jnp.int32, (slots, PAIR), 0)
    counted = jnp.where(slot < count, 1.0, 0.0).astype(BF16)
    high, low = split_scaled(nn(part, query_weight[...]), scale)
    for pair in range(width // PAIR):
        lanes = slice(pair * PAIR, (pair + 1) * PAIR)
        key_block = pair_keys(keys[:, lanes])
        value_block = pair_values(values[:, lanes], counted)
        sums, total, top = attend_pair(high[:, lanes], low[:, lanes], key_block, value_block)
        put(lanes, sums / total, top + jnp.log2(total))


def bits_of():
    cell, core = lax.axis_index("cell"), lax.axis_index("qgrp")
    quad = jnp.bitwise_and(cell, 3)
    return quad, core


def start_all(pairs, arrived):
    moves = [
        pltpu.make_async_copy(source, goal, arrived.at[index])
        for index, (source, goal) in enumerate(pairs)
    ]
    for move in moves:
        move.start()
    return moves


def wait_all(moves):
    for move in moves:
        move.wait()


def quarter(latents, quad, rows):
    return latents.at[pl.ds(pl.multiple_of(quad * rows, rows), rows), :]


def encode_first_kernel(
    tally, softness_far, latents_far, tokens_far, wq_far, wk_far, wv_far,
    message, keys, values, scales, count_out,
    count, softness, latents, tokens, wq, wk, wv, logs, arrived,
):
    quad, core = bits_of()
    rows = latents.shape[0]
    moves = start_all(
        [
            (tally, count), (tokens_far, tokens), (wk_far, wk), (wv_far, wv), (wq_far, wq),
            (softness_far, softness), (quarter(latents_far, quad ^ 3, rows), latents),
        ],
        arrived,
    )
    wait_all(moves[:3])
    is_valid = lax.broadcasted_iota(jnp.int32, keys.shape, 0) < count[0]
    made = nn(tokens[...], wk[...])
    keys[...] = jnp.where(is_valid, made, made[0:1, :]).astype(BF16)
    moves[3].wait()
    values[...] = jnp.where(is_valid, nn(tokens[...], wv[...]), 0.0).astype(BF16)
    wait_all(moves[4:])
    count_out[...] = jnp.full(count_out.shape, count[0], jnp.int32)
    for which in range(2):
        row = scale_row(softness, which, wq.shape[1] // HEAD_DIM)
        scales[which] = jnp.broadcast_to(row, scales.shape[1:])
    encode_into(message, latents[...], wq, keys, values, count_out, scales, logs)


def encode_into(message, part, wq, keys, values, count, scales, logs):
    rows = part.shape[0]

    def put(lanes, sums, log):
        message[:rows, lanes] = sums.astype(BF16)
        logs[:, lanes] = log

    encode_rows(part, wq, keys, values, count[0:1, :], scales[0, 0:1, :], put)
    message[rows:, :] = pack_logs(logs[...])


def encode_side_kernel(
    bit_0, bit_1, count, scales, latents, wq, keys, values, message, logs
):
    quad, core = bits_of()
    rows = logs.shape[0]
    side = quad ^ jnp.where(core == 0, bit_0, bit_1)
    part = quarter(latents, side, rows)[...]
    encode_into(message, part, wq, keys, values, count, scales, logs)


def encode_own_kernel(count, scales, latents, wq, keys, values, came, kept, logs):
    quad, core = bits_of()
    rows = kept.shape[0]

    def put(lanes, part, log):
        kept[:, lanes] = part
        logs[:, lanes] = log

    part = quarter(latents, quad, rows)[...]
    encode_rows(part, wq, keys, values, count[0:1, :], scales[0, 0:1, :], put)
    kept[...], logs[...] = merge(kept[...], logs[...], *read_message(came, rows))


def write_message(message, values, logs):
    rows = values.shape[0]
    message[:rows, :] = values.astype(BF16)
    message[rows:, :] = pack_logs(logs)


def read_message(message, rows):
    width = message.shape[1]
    return message[:rows, :].astype(F32), unpack_logs(message[rows:, :], width)


def merge_sides_kernel(values, logs, first, second, message):
    rows = values.shape[0]
    part, log = merge(values[...], logs[...], *read_message(first, rows))
    part, log = merge(part, log, *read_message(second, rows))
    write_message(message, part, log)


def merge_even_kernel(own_bit, other_bit, last, rows, mine, came, out):
    core = lax.axis_index("qgrp")
    bit = jnp.where(core == 0, own_bit, other_bit)
    is_low = jnp.bitwise_and(lax.axis_index("cell"), bit) == 0

    def both(first, second):
        part, log = merge(*read_message(first, rows), *read_message(second, rows))
        if last:
            out[...] = part.astype(BF16)
        else:
            write_message(out, part, log)

    @pl.when(is_low)
    def _():
        both(mine, came)

    @pl.when(jnp.logical_not(is_low))
    def _():
        both(came, mine)


def latent_kernel(attended, other, weight, other_weight, latents, gain, out, half):
    quad, core = bits_of()
    rows = attended.shape[0]
    start = pl.ds(pl.multiple_of(quad * rows, rows), rows)

    def finish(first, second, first_weight, second_weight):
        update = nn(first[...], first_weight[...]) + nn(second[...], second_weight[...])
        pre = latents[start, :].astype(F32) + update
        mean_square = jnp.mean(pre * pre, axis=-1, keepdims=True)
        out[...] = (pre * lax.rsqrt(mean_square + NORM_EPSILON) * gain[...]).astype(BF16)

    @pl.when(core == 0)
    def _():
        finish(attended, other, weight, other_weight)
        half[...] = out[:rows // 2, :]

    @pl.when(core != 0)
    def _():
        finish(other, attended, other_weight, weight)
        half[...] = out[rows // 2:, :]


def decode_queries_kernel(scales, tokens, wq, out):
    width = wq.shape[1]
    high, low = split_scaled(nn(tokens[...], wq[...]), scales[1, 0:1, :])
    for pair in range(width // PAIR):
        lanes = slice(pair * PAIR, (pair + 1) * PAIR)
        out[pair, :, :PAIR] = high[:, lanes]
        out[pair, :, PAIR:] = low[:, lanes]


def place_rows(pieces, spots, latent_out, staged, sent):
    moves, start = [], 0
    for index, (piece, spot) in enumerate(zip(pieces, spots)):
        count = piece.shape[0]
        staged[start:start + count, :] = piece[...].astype(F32)
        moves.append(
            pltpu.make_async_copy(
                staged.at[pl.ds(start, count), :],
                latent_out.at[pl.ds(pl.multiple_of(spot, count), count), :],
                sent.at[index],
            )
        )
        moves[-1].start()
        start += count
    return moves


def decode_part(queries, keys, values, state, lanes):
    high, low = queries[:, :PAIR], queries[:, PAIR:]
    one = jnp.ones((keys.shape[0], PAIR), BF16)
    sums, total, top = attend_pair(high, low, pair_keys(keys), pair_values(values, one))
    if state is None:
        return sums, total, top
    old_sums, old_total, old_top = state
    new_top = jnp.maximum(top, old_top)
    old, new = jnp.exp2(old_top - new_top), jnp.exp2(top - new_top)
    return old * old_sums + new * sums, old * old_total + new * total, new_top


def decode_step_kernel(is_first, where, *refs):
    queries, wk, wv, *refs = refs
    quad, core = bits_of()
    count = len(where(quad, core, 0))
    pieces, refs = refs[:count], refs[count:]
    state = None
    if not is_first:
        _, *state = refs[:4]
        refs = refs[4:]
    latent_out, sums, total, top, gathered, staged, sent = refs
    model = gathered.shape[1]
    rows = latent_out.shape[0] // 4
    moves = place_rows(pieces, where(quad, core, rows), latent_out, staged, sent)
    start = 0
    for piece in pieces:
        gathered[start:start + piece.shape[0], :] = piece[...]
        start += piece.shape[0]
    keys = nn(gathered[...], wk[...]).astype(BF16)
    values = nn(gathered[...], wv[...]).astype(BF16)
    block = queries.shape[1] // 2
    for pair in range(queries.shape[0]):
        lanes = slice(pair * PAIR, (pair + 1) * PAIR)
        for index in range(2):
            at = slice(index * block, (index + 1) * block)
            old = None if is_first else [part[at, lanes] for part in state]
            new = decode_part(queries[pair, at, :], keys[:, lanes], values[:, lanes], old, lanes)
            for out, part in zip((sums, total, top), new):
                out[at, lanes] = part
    for move in moves:
        move.wait()


def decode_send_kernel(
    queries, wk, wv, mine, came, latent_in, sums, total, top,
    latent_out, send, keys, values, gathered, staged, sent,
):
    quad, core = bits_of()
    rows, half = latent_out.shape[0] // 4, mine.shape[0]
    diagonal = (quad ^ 3) * rows
    spots = [diagonal + core * half, diagonal + (1 - core) * half]
    moves = place_rows([mine, came], spots, latent_out, staged, sent)
    gathered[:half, :] = mine[...]
    gathered[half:, :] = came[...]
    keys[...] = nn(gathered[...], wk[...]).astype(BF16)
    values[...] = nn(gathered[...], wv[...]).astype(BF16)
    decode_last(1 - core, queries, keys, values, sums, total, top, send)
    for move in moves:
        move.wait()


def decode_last(which, queries, keys, values, sums, total, top, out):
    block = out.shape[0]
    at = pl.ds(pl.multiple_of(which * block, block), block)
    for pair in range(queries.shape[0]):
        lanes = slice(pair * PAIR, (pair + 1) * PAIR)
        old = [part[at, lanes] for part in (sums, total, top)]
        new = decode_part(queries[pair, at, :], keys[:, lanes], values[:, lanes], old, lanes)
        out[:, lanes] = (new[0] / new[1]).astype(BF16)


def decode_keep_kernel(queries, keys, values, sums, total, top, keep):
    core = lax.axis_index("qgrp")
    decode_last(core, queries, keys, values, sums, total, top, keep)


def tokens_kernel(count, attended, other, weight, other_weight, tokens, out):
    core = lax.axis_index("qgrp")
    rows = attended.shape[0]
    update = nn(attended[...], weight[...]) + nn(other[...], other_weight[...])
    start = core * rows
    own = tokens[pl.ds(pl.multiple_of(start, rows), rows), :].astype(F32)
    is_valid = start + lax.broadcasted_iota(jnp.int32, out.shape, 0) < count[0:1, 0:1]
    out[...] = jnp.where(is_valid, own + update, 0.0)


SPACES = {
    "v": pl.BlockSpec(memory_space=pltpu.VMEM),
    "h": pl.BlockSpec(memory_space=pltpu.HBM),
    "a": pl.BlockSpec(memory_space=pl.ANY),
}


def call(kernel, ins, outs, *args, far=(), alias=None, scratch=(), vmem=24, flops=0, after=(),
         name=None):
    given, more = len(args), len(after)
    args = [
        pltpu.with_memory_space_constraint(arg, pltpu.HBM) if kind == "h" else arg
        for kind, arg in zip(ins, args)
    ]
    if more:
        alone = kernel

        def kernel(*refs):
            alone(*refs[:given], *refs[given + more:])

    shapes = [jax.ShapeDtypeStruct(*out) for out in outs]
    moved = sum(a.size * a.dtype.itemsize for a in [*args, *shapes])
    return pl.pallas_call(
        kernel,
        out_shape=shapes,
        in_specs=[SPACES[kind] for kind in ins + "h" * more],
        out_specs=[SPACES["h" if index in far else "v"] for index in range(len(outs))],
        input_output_aliases=alias or {},
        scratch_shapes=list(scratch),
        compiler_params=pltpu.CompilerParams(vmem_limit_bytes=vmem * MIB),
        cost_estimate=pl.CostEstimate(flops=flops, bytes_accessed=moved, transcendentals=0),
        name=name,
    )(*args, *after)


def body(tokens, tally, latents, softness, wq, wk, wv, wo, dq, dk, dv, do, gain):
    cells = lax.axis_size("cell")
    total_rows, model = latents.shape
    rows, width = total_rows // 4, wq.shape[1]
    slots = tokens.shape[0]
    half_slots = slots // 2
    deep = rows + log_rows(width)

    def swap(array):
        return lax.ppermute(array, "qgrp", [(0, 1), (1, 0)])

    def trade(array, bit_0, bit_1):
        pairs = []
        for cell in range(cells):
            pairs.append((2 * cell, 2 * (cell ^ bit_0)))
            pairs.append((2 * cell + 1, 2 * (cell ^ bit_1) + 1))
        return lax.ppermute(array, ("cell", "qgrp"), pairs)

    attention = 4 * 256 * slots * width * 4
    sent = ((deep, width), BF16)
    message, keys, values, scales, count = call(
        encode_first_kernel, "ahhhhhh",
        [
            sent, *[((slots, width), BF16)] * 2,
            ((2, 8, width), F32), ((8, PAIR), jnp.int32),
        ],
        tally, softness, latents, tokens, wq, wk, wv,
        scratch=[
            pltpu.SMEM(tally.shape, tally.dtype), pltpu.SMEM(softness.shape, F32),
            pltpu.VMEM((rows, model), BF16), pltpu.VMEM(tokens.shape, BF16),
            *[pltpu.VMEM((model, width), BF16)] * 3, pltpu.VMEM((rows, width), F32),
            pltpu.SemaphoreType.DMA((7,)),
        ],
        flops=attention, name="encode_corner",
    )
    corner = trade(message, 3, 3)

    def encode_side(bit_0, bit_1, after):
        (message,) = call(
            functools.partial(encode_side_kernel, bit_0, bit_1), "vvvvvv", [sent],
            count, scales, latents, wq, keys, values,
            scratch=[pltpu.VMEM((rows, width), F32)],
            flops=attention, after=after, name="encode_side",
        )
        return message

    message = encode_side(1, 2, [])
    first = trade(message, 1, 2)
    message = encode_side(2, 1, [message])
    second = trade(message, 2, 1)
    kept, kept_logs = call(
        encode_own_kernel, "vvvvvvv", [((rows, width), F32)] * 2,
        count, scales, latents, wq, keys, values, corner,
        flops=attention, after=[message], name="encode_own",
    )
    other_wo, other_do = swap(wo), swap(do)
    (message,) = call(
        merge_sides_kernel, "vvvv", [sent], kept, kept_logs, first, second, name="merge_sides"
    )
    (queries,) = call(
        decode_queries_kernel, "vvv", [((width // PAIR, slots, 2 * PAIR), BF16)],
        scales, tokens, dq, after=[message], name="decode_queries",
    )
    bits = [4 << i for i in range(max(cells.bit_length() - 3, 0))]
    for index, (bit_0, bit_1) in enumerate(zip(bits, bits[::-1])):
        last = index == len(bits) - 1
        came = trade(message, bit_0, bit_1)
        (message,) = call(
            functools.partial(merge_even_kernel, bit_0, bit_1, last, rows), "vv",
            [((rows, width), BF16) if last else sent], message, came,
            after=[queries] if last else [], name="merge_even",
        )
    attended = message[:rows]
    half = rows // 2
    own, own_half = call(
        latent_kernel, "vvvvvv", [((rows, model), BF16), ((half, model), BF16)],
        attended, swap(attended), wo, other_wo, latents, gain.reshape(1, model), name="latent",
    )
    first = trade(own_half, 1, 2)
    second = trade(own_half, 2, 1)
    whole = ((total_rows, model), F32)
    state_out = [((slots, width), F32)] * 3

    def scratch(count, pieces):
        return [
            pltpu.VMEM((count, model), BF16), pltpu.VMEM((count, model), F32),
            pltpu.SemaphoreType.DMA((pieces,)),
        ]

    def own_spot(quad, core, rows):
        return [quad * rows]

    def side_spots(quad, core, rows):
        half = rows // 2
        return [
            (quad ^ (1 + core)) * rows + core * half,
            (quad ^ (2 - core)) * rows + (1 - core) * half,
            (quad ^ (2 - core)) * rows + core * half,
            (quad ^ (1 + core)) * rows + (1 - core) * half,
        ]

    latent_out, *state = call(
        functools.partial(decode_step_kernel, True, own_spot), "vvvv",
        [whole, *state_out], queries, dk, dv, own,
        far=(0,), scratch=scratch(rows, 1), flops=attention, name="decode_own",
    )
    first, own = lax.optimization_barrier((first, state[0]))
    state[0] = own
    third = trade(first, 2, 1)
    latent_out, *state = call(
        functools.partial(decode_step_kernel, False, side_spots), "vvvvvvvhvvv",
        [whole, *state_out], queries, dk, dv, first, swap(first), second, swap(second),
        latent_out, *state, far=(0,), alias={7: 0},
        scratch=scratch(2 * rows, 4), vmem=32, flops=2 * attention, name="decode_sides",
    )
    third, late = lax.optimization_barrier((third, state[0]))
    state[0] = late
    latent_out, send, keys, values = call(
        decode_send_kernel, "vvvvvhvvv",
        [whole, ((half_slots, width), BF16), *[((rows, width), BF16)] * 2],
        queries, dk, dv, third, swap(third), latent_out, *state, far=(0,), alias={5: 0},
        scratch=scratch(rows, 2), flops=attention // 2, name="decode_send",
    )
    (keep,) = call(
        decode_keep_kernel, "vvvvvv", [((half_slots, width), BF16)],
        queries, keys, values, *state, flops=attention // 2, name="decode_keep",
    )
    (tokens_out,) = call(
        tokens_kernel, "vvvvvv", [((half_slots, model), F32)],
        count, keep, swap(send), do, other_do, tokens, name="tokens",
    )
    return latent_out, tokens_out


def solution(mesh):
    placed = (
        P("cell", None), P("cell"), P(), P(),
        P(None, "qgrp"), P(None, "qgrp"), P(None, "qgrp"), P("qgrp", None),
        P(None, "qgrp"), P(None, "qgrp"), P(None, "qgrp"), P("qgrp", None), P(),
    )
    return jax.shard_map(
        body, mesh=mesh, in_specs=placed, out_specs=(P(), P(("cell", "qgrp"), None)),
        check_vma=False,
    )
```

time: 79.6 us -> 61.2 us (0.77)
  waiting for transfers between devices: 34.2 us -> 17.7 us
  local copies, waits for them, and re-layouts: 6.46 us -> 0.04 us
  Pallas kernels: 21.2 us -> 24.9 us
  starting transfers between devices: 14.8 us -> 16.8 us
  other arithmetic: 1.22 us -> 0 us
    ppermute x6 -> x8, waiting for transfers between devices: 28.5 us -> 15.1 us  [trade(): return lax.ppermute(array, ('cell', 'qgrp'), pairs)]
    unnamed x32 -> x18, local copies, waits for them, and re-layouts: 6.46 us -> 0.04 us
    pallas_call x9 -> x14, Pallas kernels: 21.2 us -> 24.9 us  [call(): pl.pallas_call(kernel, out_shape=shapes, in_specs=[SPACES[kind] for kind...]
    ppermute x6 -> x7, waiting for transfers between devices: 5.63 us -> 2.62 us  [swap(): return lax.ppermute(array, 'qgrp', [(0, 1), (1, 0)])]
    ppermute x6 -> x8, starting transfers between devices: 14 us -> 15.5 us  [trade(): return lax.ppermute(array, ('cell', 'qgrp'), pairs)]
    select_n x3 -> x0, other arithmetic: 1.22 us -> none  [the longest x1 1.17 us: body(): y_side = jnp.where(core == 0, back, came)]
  transfers between devices with their start and end apart: 12 -> 15, of which waited for: 10 -> 9; matrix products, arithmetic and copies ran while one was open for 0% -> 0% of each run, Pallas kernels for 16% -> 28%
where the time goes in v2:
time: 61.2 us; the launch traced here: 61.1 us
  Pallas kernels  24.9 us (41%)
  waiting for transfers between devices  17.7 us (29%)
  starting transfers between devices  16.8 us (27%)
  between operations  1.58 us (3%)
    pallas_call x14, Pallas kernels, call(): pl.pallas_call(kernel, out_shape=shapes, in_specs=[SPACES[kind] for kind...  24.9 us
    ppermute x8, starting transfers between devices, trade(): return lax.ppermute(array, ('cell', 'qgrp'), pairs)  15.5 us
    ppermute x8, waiting for transfers between devices, trade(): return lax.ppermute(array, ('cell', 'qgrp'), pairs)  15.1 us
    ppermute x7, waiting for transfers between devices, swap(): return lax.ppermute(array, 'qgrp', [(0, 1), (1, 0)])  2.62 us
    ppermute x7, starting transfers between devices, swap(): return lax.ppermute(array, 'qgrp', [(0, 1), (1, 0)])  1.31 us
  transfers between devices with their start and end apart: 15, of which 9 were waited for; matrix products, arithmetic and copies ran while one was open for 0% of the time, Pallas kernels for 28%

profile of v2, /device:TPU:0, one launch (start us, length us, event | category | flops | bytes accessed | tf_op | source)
XLA Modules:
  0.0 61.1 jit_solution(13814046874689337047)
XLA Ops:
  0.6 0.0 copy-start
  0.6 0.0 copy-start.1
  1.4 4.5 %encode_corner.1 = (bf16[272,384]{1,0:T(8,128)(2,1)S(1)}, bf16[512,384]{1,0:T(8,128)(2,1)S(1)}, bf16[512,384]{1,0:T(8,128)(2,1)S(1)}, f32[2,8,384]{2,1,0:T(8,128)S(1)}, s32[8,128]{1,0:T(8,128)S(1)}) custom-call(s32[1]{0:T(128)S(6)} %copy.19.tally, f32[2,12]{1,0:T(2,128)} %softness_far.1, bf16[1024,768]{1,0:T(8,128)(2,1)} %latents.3, ...), custom_call_target="tpu_custom_call" | custom-call | flops 805306368 | bytes 5152868 | tf_op jit(solution)/shard_map/encode_corner/pallas_call | solution.py:434
  5.9 4.0 %collective-permute-start = (bf16[272,384]{1,0:T(8,128)(2,1)S(1)}, bf16[272,384]{1,0:T(8,128)(2,1)S(1)}, u32[]{:S(2)}, u32[]{:S(2)}) collective-permute-start(bf16[272,384]{1,0:T(8,128)(2,1)S(1)} %get-tuple-element.31), channel_id=1, source_target_pairs={{0,6},{1,7},{2,4},{3,5},{4,2},{5,3},{6,0},{7,1},{8,14},{9,15},{10,... | collective-permute-start | bytes 626696 | tf_op jit(solution)/shard_map/ppermute | solution.py:463
  9.9 0.0 copy-done
  9.9 0.0 copy-done.1
  9.9 1.9 %encode_side.2.refs_6_ = bf16[272,384]{1,0:T(8,128)(2,1)S(1)} custom-call(s32[8,128]{1,0:T(8,128)S(1)} %get-tuple-element.28.count.refs_0_, f32[2,8,384]{2,1,0:T(8,128)S(1)} %get-tuple-element.27.scales.refs_1_.refs_0_, bf16[1024,768]{1,0:T(8,128)(2,1)S(1)} %copy-done, bf16[768,384]{1,0:T(8,128)(2,1)S(1)} %copy-done.1, ...), custom_call_target="tpu_custom_call" | custom-call | flops 805306368 | bytes 3186688 | tf_op jit(solution)/shard_map/encode_side/pallas_call | solution.py:434
  11.8 1.9 %encode_side.3.refs_7_ = bf16[272,384]{1,0:T(8,128)(2,1)S(1)} custom-call(s32[8,128]{1,0:T(8,128)S(1)} %get-tuple-element.28.count.refs_0_, f32[2,8,384]{2,1,0:T(8,128)S(1)} %get-tuple-element.27.scales.refs_1_.refs_0_, bf16[1024,768]{1,0:T(8,128)(2,1)S(1)} %copy-done, bf16[768,384]{1,0:T(8,128)(2,1)S(1)} %copy-done.1, ...), custom_call_target="tpu_custom_call" | custom-call | flops 805306368 | bytes 3186688 | tf_op jit(solution)/shard_map/encode_side/pallas_call | solution.py:434
  13.8 0.0 copy-start.5
  13.8 0.0 copy-start.2
  13.8 0.0 copy-start.6
  13.8 0.6 collective-permute-start.2
  14.3 0.1 collective-permute-start.1
  14.4 0.6 %collective-permute-done.refs_6_ = bf16[272,384]{1,0:T(8,128)(2,1)S(1)} collective-permute-done((bf16[272,384]{1,0:T(8,128)(2,1)S(1)}, bf16[272,384]{1,0:T(8,128)(2,1)S(1)}, u32[]{:S(2)}, u32[]{:S(2)}) %collective-permute-start) | collective-permute-done | bytes 208928 | tf_op jit(solution)/shard_map/ppermute | solution.py:463
  15.1 1.7 %encode_own.1 = (f32[256,384]{1,0:T(8,128)S(1)}, f32[256,384]{1,0:T(8,128)S(1)}) custom-call(s32[8,128]{1,0:T(8,128)S(1)} %get-tuple-element.28.count.refs_0_, f32[2,8,384]{2,1,0:T(8,128)S(1)} %get-tuple-element.27.scales.refs_1_.refs_0_, bf16[1024,768]{1,0:T(8,128)(2,1)S(1)} %copy-done, bf16[768,384]{1,0:T(8,128)(2,1)S(1)} %copy-done.1, ...), custom_call_target="tpu_custom_call" | custom-call | flops 805306368 | bytes 3973120 | tf_op jit(solution)/shard_map/encode_own/pallas_call | solution.py:434
  16.8 0.0 copy-start.8
  16.8 3.9 %collective-permute-done.2.second = bf16[272,384]{1,0:T(8,128)(2,1)S(1)} collective-permute-done((bf16[272,384]{1,0:T(8,128)(2,1)S(1)}, bf16[272,384]{1,0:T(8,128)(2,1)S(1)}, u32[]{:S(2)}, u32[]{:S(2)}) %collective-permute-start.2) | collective-permute-done | bytes 208928 | tf_op jit(solution)/shard_map/ppermute | solution.py:463
  20.7 0.0 collective-permute-done.1.first
  20.7 0.9 %merge_sides.1.refs_3_.mine = bf16[272,384]{1,0:T(8,128)(2,1)S(1)} custom-call(f32[256,384]{1,0:T(8,128)S(1)} %get-tuple-element.32.values, f32[256,384]{1,0:T(8,128)S(1)} %get-tuple-element.33.logs, bf16[272,384]{1,0:T(8,128)(2,1)S(1)} %collective-permute-done.1.first, bf16[272,384]{1,0:T(8,128)(2,1)S(1)} %collective-permute-done.2.second), custom_call_target="tpu_custom_call" | custom-call | bytes 1413120 | tf_op jit(solution)/shard_map/merge_sides/pallas_call | solution.py:434
  21.7 1.6 %collective-permute-start.3 = (bf16[272,384]{1,0:T(8,128)(2,1)S(1)}, bf16[272,384]{1,0:T(8,128)(2,1)S(1)}, u32[]{:S(2)}, u32[]{:S(2)}) collective-permute-start(bf16[272,384]{1,0:T(8,128)(2,1)S(1)} %merge_sides.1.refs_3_.mine), channel_id=1, source_target_pairs={{0,8},{1,17},{2,10},{3,19},{4,12},{5,21},{6,14},{7,23},{8,0},{9,25... | collective-permute-start | bytes 626696 | tf_op jit(solution)/shard_map/ppermute | solution.py:463
  23.3 0.0 copy-done.5
  23.3 0.0 collective-permute-start.6
  23.3 4.5 %collective-permute-done.3.came = bf16[272,384]{1,0:T(8,128)(2,1)S(1)} collective-permute-done((bf16[272,384]{1,0:T(8,128)(2,1)S(1)}, bf16[272,384]{1,0:T(8,128)(2,1)S(1)}, u32[]{:S(2)}, u32[]{:S(2)}) %collective-permute-start.3) | collective-permute-done | bytes 208928 | tf_op jit(solution)/shard_map/ppermute | solution.py:463
  27.8 0.8 %merge_even.2.refs_0_ = bf16[272,384]{1,0:T(8,128)(2,1)S(1)} custom-call(bf16[272,384]{1,0:T(8,128)(2,1)S(1)} %merge_sides.1.refs_3_.mine, bf16[272,384]{1,0:T(8,128)(2,1)S(1)} %collective-permute-done.3.came), custom_call_target="tpu_custom_call" | custom-call | bytes 626688 | tf_op jit(solution)/shard_map/merge_even/pallas_call | solution.py:434
  28.6 0.0 copy-start.3
  28.6 0.0 copy-start.4
  28.6 3.6 %collective-permute-start.4 = (bf16[272,384]{1,0:T(8,128)(2,1)S(1)}, bf16[272,384]{1,0:T(8,128)(2,1)S(1)}, u32[]{:S(2)}, u32[]{:S(2)}) collective-permute-start(bf16[272,384]{1,0:T(8,128)(2,1)S(1)} %merge_even.2.refs_0_), channel_id=1, source_target_pairs={{0,16},{1,9},{2,18},{3,11},{4,20},{5,13},{6,22},{7,15},{8,24},{9,1... | collective-permute-start | bytes 626696 | tf_op jit(solution)/shard_map/ppermute | solution.py:463
  32.2 0.0 copy-done.2
  32.2 0.0 copy-done.6
  32.2 0.6 %decode_queries.1.refs_2_.refs_0_.queries = bf16[3,512,256]{2,1,0:T(8,128)(2,1)S(1)} custom-call(f32[2,8,384]{2,1,0:T(8,128)S(1)} %get-tuple-element.27.scales.refs_1_.refs_0_, bf16[512,768]{1,0:T(8,128)(2,1)S(1)} %copy-done.2, bf16[768,384]{1,0:T(8,128)(2,1)S(1)} %copy-done.6, bf16[272,384]{1,0:T(8,128)(2,1)S(1)} %merge_sides.1.refs_3_.mine), custom_call_target="tpu_custom_call" | custom-call | bytes 2187264 | tf_op jit(solution)/shard_map/decode_queries/pallas_call | solution.py:434
  32.8 3.5 %collective-permute-done.4.refs_1_ = bf16[272,384]{1,0:T(8,128)(2,1)S(1)} collective-permute-done((bf16[272,384]{1,0:T(8,128)(2,1)S(1)}, bf16[272,384]{1,0:T(8,128)(2,1)S(1)}, u32[]{:S(2)}, u32[]{:S(2)}) %collective-permute-start.4) | collective-permute-done | bytes 208928 | tf_op jit(solution)/shard_map/ppermute | solution.py:463
  36.3 0.5 merge_even.3.attended
  36.8 0.0 copy-start.7
  36.8 0.2 collective-permute-start.5
  37.0 0.0 copy-done.8
  37.0 0.0 collective-permute-done.6.other_weight
  37.0 1.3 %collective-permute-done.5.other = bf16[256,384]{1,0:T(8,128)(2,1)S(1)} collective-permute-done((bf16[256,384]{1,0:T(8,128)(2,1)S(1)}, bf16[256,384]{1,0:T(8,128)(2,1)S(1)}, u32[]{:S(2)}, u32[]{:S(2)}) %collective-permute-start.5) | collective-permute-done | bytes 196640 | tf_op jit(solution)/shard_map/ppermute | solution.py:456
  38.3 0.9 %latent.1 = (bf16[256,768]{1,0:T(8,128)(2,1)S(1)}, bf16[128,768]{1,0:T(8,128)(2,1)S(1)}) custom-call(bf16[256,384]{1,0:T(8,128)(2,1)S(1)} %merge_even.3.attended, bf16[256,384]{1,0:T(8,128)(2,1)S(1)} %collective-permute-done.5.other, bf16[384,768]{1,0:T(8,128)(2,1)S(1)} %copy-done.5, bf16[384,768]{1,0:T(8,128)(2,1)S(1)} %collective-permute-done.6.other_weight, ...), custom_call_target="tpu_custom_call" | custom-call | bytes 3738624 | tf_op jit(solution)/shard_map/latent/pallas_call | solution.py:434
  39.2 3.3 %collective-permute-start.7 = (bf16[128,768]{1,0:T(8,128)(2,1)S(1)}, bf16[128,768]{1,0:T(8,128)(2,1)S(1)}, u32[]{:S(2)}, u32[]{:S(2)}) collective-permute-start(bf16[128,768]{1,0:T(8,128)(2,1)S(1)} %get-tuple-element.34), channel_id=1, source_target_pairs={{0,2},{1,5},{2,0},{3,7},{4,6},{5,1},{6,4},{7,3},{8,10},{9,13},{10,... | collective-permute-start | bytes 589832 | tf_op jit(solution)/shard_map/ppermute | solution.py:463
  42.6 0.7 %collective-permute-start.10 = (bf16[128,768]{1,0:T(8,128)(2,1)S(1)}, bf16[128,768]{1,0:T(8,128)(2,1)S(1)}, u32[]{:S(2)}, u32[]{:S(2)}) collective-permute-start(bf16[128,768]{1,0:T(8,128)(2,1)S(1)} %get-tuple-element.34), channel_id=1, source_target_pairs={{0,4},{1,3},{2,6},{3,1},{4,0},{5,7},{6,2},{7,5},{8,12},{9,11},{10,... | collective-permute-start | bytes 589832 | tf_op jit(solution)/shard_map/ppermute | solution.py:463
  43.2 0.0 copy-done.3
  43.2 0.0 copy-done.4
  43.2 2.4 %decode_own.1 = (f32[1024,768]{1,0:T(8,128)}, f32[512,384]{1,0:T(8,128)S(1)}, f32[512,384]{1,0:T(8,128)S(1)}, f32[512,384]{1,0:T(8,128)S(1)}) custom-call(bf16[3,512,256]{2,1,0:T(8,128)(2,1)S(1)} %decode_queries.1.refs_2_.refs_0_.queries, bf16[768,384]{1,0:T(8,128)(2,1)S(1)} %copy-done.3, bf16[768,384]{1,0:T(8,128)(2,1)S(1)} %copy-done.4, ...), custom_call_target="tpu_custom_call" | custom-call | flops 805306368 | bytes 7864320 | tf_op jit(solution)/shard_map/decode_own/pallas_call | solution.py:434
  45.7 2.0 %collective-permute-done.7.refs_3_ = bf16[128,768]{1,0:T(8,128)(2,1)S(1)} collective-permute-done((bf16[128,768]{1,0:T(8,128)(2,1)S(1)}, bf16[128,768]{1,0:T(8,128)(2,1)S(1)}, u32[]{:S(2)}, u32[]{:S(2)}) %collective-permute-start.7) | collective-permute-done | bytes 196640 | tf_op jit(solution)/shard_map/ppermute | solution.py:463
  47.6 0.0 collective-permute-start.9
  47.6 0.6 collective-permute-done.10.refs_5_
  48.2 0.1 collective-permute-start.11
  48.4 1.7 %collective-permute-start.8 = (bf16[128,768]{1,0:T(8,128)(2,1)S(1)}, bf16[128,768]{1,0:T(8,128)(2,1)S(1)}, u32[]{:S(2)}, u32[]{:S(2)}) collective-permute-start(bf16[128,768]{1,0:T(8,128)(2,1)S(1)} %collective-permute-done.7.refs_3_), channel_id=1, source_target_pairs={{0,4},{1,3},{2,6},{3,1},{4,0},{5,7},{6,2},{7,5},{8,12},{9,11},{10,... | collective-permute-start | bytes 589832 | tf_op jit(solution)/shard_map/ppermute | solution.py:463
  50.0 0.0 copy-done.7
  50.0 0.1 collective-permute-start.14
  50.2 0.0 collective-permute-done.9.refs_4_
  50.2 0.0 collective-permute-done.11.refs_6_
  50.2 4.3 %decode_sides.1 = (f32[1024,768]{1,0:T(8,128)}, f32[512,384]{1,0:T(8,128)S(1)}, f32[512,384]{1,0:T(8,128)S(1)}, f32[512,384]{1,0:T(8,128)S(1)}) custom-call(bf16[3,512,256]{2,1,0:T(8,128)(2,1)S(1)} %decode_queries.1.refs_2_.refs_0_.queries, bf16[768,384]{1,0:T(8,128)(2,1)S(1)} %copy-done.3, ...), custom_call_target="tpu_custom_call", output_to_operand_aliasing={{0}: (7, {})} | custom-call | flops 1610612736 | bytes 13762560 | tf_op jit(solution)/shard_map/decode_sides/pallas_call | solution.py:434
  54.5 0.0 collective-permute-done.8.mine
  54.5 0.5 collective-permute-start.12
  55.0 1.1 %collective-permute-done.12.came = bf16[128,768]{1,0:T(8,128)(2,1)S(1)} collective-permute-done((bf16[128,768]{1,0:T(8,128)(2,1)S(1)}, bf16[128,768]{1,0:T(8,128)(2,1)S(1)}, u32[]{:S(2)}, u32[]{:S(2)}) %collective-permute-start.12) | collective-permute-done | bytes 196640 | tf_op jit(solution)/shard_map/ppermute | solution.py:456
  56.0 2.1 %decode_send.1 = (f32[1024,768]{1,0:T(8,128)}, bf16[256,384]{1,0:T(8,128)(2,1)S(1)}, bf16[256,384]{1,0:T(8,128)(2,1)S(1)}, bf16[256,384]{1,0:T(8,128)(2,1)S(1)}) custom-call(bf16[3,512,256]{2,1,0:T(8,128)(2,1)S(1)} %decode_queries.1.refs_2_.refs_0_.queries, bf16[768,384]{1,0:T(8,128)(2,1)S(1)} %copy-done.3, ...), custom_call_target="tpu_custom_call", output_to_operand_aliasing={{0}: (5, {})} | custom-call | flops 402653184 | bytes 11599872 | tf_op jit(solution)/shard_map/decode_send/pallas_call | solution.py:434
  58.1 0.4 collective-permute-start.13
  58.6 0.8 %decode_keep.1.attended = bf16[256,384]{1,0:T(8,128)(2,1)S(1)} custom-call(bf16[3,512,256]{2,1,0:T(8,128)(2,1)S(1)} %decode_queries.1.refs_2_.refs_0_.queries, bf16[256,384]{1,0:T(8,128)(2,1)S(1)} %get-tuple-element.49.keys, bf16[256,384]{1,0:T(8,128)(2,1)S(1)} %get-tuple-element.50.values, f32[512,384]{1,0:T(8,128)S(1)} %get-tuple-element.45.sums, ...), custom_call_target="tpu_custom_call" | custom-call | flops 402653184 | bytes 3735552 | tf_op jit(solution)/shard_map/decode_keep/pallas_call | solution.py:434
  59.4 0.0 collective-permute-done.14.other_weight
  59.4 0.2 collective-permute-done.13.other
  59.6 1.4 %tokens.2 = f32[256,768]{1,0:T(8,128)} custom-call(s32[8,128]{1,0:T(8,128)S(1)} %get-tuple-element.28.count.refs_0_, bf16[256,384]{1,0:T(8,128)(2,1)S(1)} %decode_keep.1.attended, bf16[256,384]{1,0:T(8,128)(2,1)S(1)} %collective-permute-done.13.other, bf16[384,768]{1,0:T(8,128)(2,1)S(1)} %copy-done.7, ...), custom_call_target="tpu_custom_call" | custom-call | bytes 3149824 | tf_op jit(solution)/shard_map/tokens/pallas_call | solution.py:434
  (1 shorter events, 0.0 us)
Async XLA Ops:
  0.6 9.3 %copy-start = (bf16[1024,768]{1,0:T(8,128)(2,1)S(1)}, bf16[1024,768]{1,0:T(8,128)(2,1)}, u32[]{:S(2)}) copy-start(bf16[1024,768]{1,0:T(8,128)(2,1)} %latents.3) | copy-start | bytes 4718596
  0.6 9.3 %copy-start.1 = (bf16[768,384]{1,0:T(8,128)(2,1)S(1)}, bf16[768,384]{1,0:T(8,128)(2,1)}, u32[]{:S(2)}) copy-start(bf16[768,384]{1,0:T(8,128)(2,1)} %refs_3_.3) | copy-start | bytes 1769476
  5.9 9.1 %collective-permute-start = (bf16[272,384]{1,0:T(8,128)(2,1)S(1)}, bf16[272,384]{1,0:T(8,128)(2,1)S(1)}, u32[]{:S(2)}, u32[]{:S(2)}) collective-permute-start(bf16[272,384]{1,0:T(8,128)(2,1)S(1)} %get-tuple-element.31), channel_id=1, source_target_pairs={{0,6},{1,7},{2,4},{3,5},{4,2},{5,3},{6,0},{7,1},{8,14},{9,15},{10,... | collective-permute-start | bytes 626696 | tf_op jit(solution)/shard_map/ppermute | solution.py:463
  13.8 9.5 %copy-start.5 = (bf16[384,768]{1,0:T(8,128)(2,1)S(1)}, bf16[384,768]{1,0:T(8,128)(2,1)}, u32[]{:S(2)}) copy-start(bf16[384,768]{1,0:T(8,128)(2,1)} %weight.2) | copy-start | bytes 1769476
  13.8 18.4 %copy-start.2 = (bf16[512,768]{1,0:T(8,128)(2,1)S(1)}, bf16[512,768]{1,0:T(8,128)(2,1)}, u32[]{:S(2)}) copy-start(bf16[512,768]{1,0:T(8,128)(2,1)} %tokens.3) | copy-start | bytes 2359300
  13.8 18.4 %copy-start.6 = (bf16[768,384]{1,0:T(8,128)(2,1)S(1)}, bf16[768,384]{1,0:T(8,128)(2,1)}, u32[]{:S(2)}) copy-start(bf16[768,384]{1,0:T(8,128)(2,1)} %refs_2_.7) | copy-start | bytes 1769476
  13.8 6.9 %collective-permute-start.2 = (bf16[272,384]{1,0:T(8,128)(2,1)S(1)}, bf16[272,384]{1,0:T(8,128)(2,1)S(1)}, u32[]{:S(2)}, u32[]{:S(2)}) collective-permute-start(bf16[272,384]{1,0:T(8,128)(2,1)S(1)} %encode_side.3.refs_7_), channel_id=1, source_target_pairs={{0,4},{1,3},{2,6},{3,1},{4,0},{5,7},{6,2},{7,5},{8,12},{9,11},{10,... | collective-permute-start | bytes 626696 | tf_op jit(solution)/shard_map/ppermute | solution.py:463
  14.3 6.4 %collective-permute-start.1 = (bf16[272,384]{1,0:T(8,128)(2,1)S(1)}, bf16[272,384]{1,0:T(8,128)(2,1)S(1)}, u32[]{:S(2)}, u32[]{:S(2)}) collective-permute-start(bf16[272,384]{1,0:T(8,128)(2,1)S(1)} %encode_side.2.refs_6_), channel_id=1, source_target_pairs={{0,2},{1,5},{2,0},{3,7},{4,6},{5,1},{6,4},{7,3},{8,10},{9,13},{10,... | collective-permute-start | bytes 626696 | tf_op jit(solution)/shard_map/ppermute | solution.py:463
  16.8 20.2 %copy-start.8 = (f32[768]{0:T(1024)S(1)}, f32[768]{0:T(1024)}, u32[]{:S(2)}) copy-start(f32[768]{0:T(1024)} %param.25) | copy-start | bytes 9220
  21.7 6.1 %collective-permute-start.3 = (bf16[272,384]{1,0:T(8,128)(2,1)S(1)}, bf16[272,384]{1,0:T(8,128)(2,1)S(1)}, u32[]{:S(2)}, u32[]{:S(2)}) collective-permute-start(bf16[272,384]{1,0:T(8,128)(2,1)S(1)} %merge_sides.1.refs_3_.mine), channel_id=1, source_target_pairs={{0,8},{1,17},{2,10},{3,19},{4,12},{5,21},{6,14},{7,23},{8,0},{9,25... | collective-permute-start | bytes 626696 | tf_op jit(solution)/shard_map/ppermute | solution.py:463
  23.3 13.7 %collective-permute-start.6 = (bf16[384,768]{1,0:T(8,128)(2,1)S(1)}, bf16[384,768]{1,0:T(8,128)(2,1)S(1)}, u32[]{:S(2)}, u32[]{:S(2)}) collective-permute-start(bf16[384,768]{1,0:T(8,128)(2,1)S(1)} %copy-done.5), channel_id=1, source_target_pairs={{0,1},{1,0},{2,3},{3,2},{4,5},{5,4},{6,7},{7,6},{8,9},{9,8},{10,11... | collective-permute-start | bytes 1769480 | tf_op jit(solution)/shard_map/ppermute | solution.py:456
  28.6 14.6 %copy-start.3 = (bf16[768,384]{1,0:T(8,128)(2,1)S(1)}, bf16[768,384]{1,0:T(8,128)(2,1)}, u32[]{:S(2)}) copy-start(bf16[768,384]{1,0:T(8,128)(2,1)} %wk.1) | copy-start | bytes 1769476
  28.6 14.6 %copy-start.4 = (bf16[768,384]{1,0:T(8,128)(2,1)S(1)}, bf16[768,384]{1,0:T(8,128)(2,1)}, u32[]{:S(2)}) copy-start(bf16[768,384]{1,0:T(8,128)(2,1)} %wv.1) | copy-start | bytes 1769476
  28.6 7.7 %collective-permute-start.4 = (bf16[272,384]{1,0:T(8,128)(2,1)S(1)}, bf16[272,384]{1,0:T(8,128)(2,1)S(1)}, u32[]{:S(2)}, u32[]{:S(2)}) collective-permute-start(bf16[272,384]{1,0:T(8,128)(2,1)S(1)} %merge_even.2.refs_0_), channel_id=1, source_target_pairs={{0,16},{1,9},{2,18},{3,11},{4,20},{5,13},{6,22},{7,15},{8,24},{9,1... | collective-permute-start | bytes 626696 | tf_op jit(solution)/shard_map/ppermute | solution.py:463
  36.8 13.2 %copy-start.7 = (bf16[384,768]{1,0:T(8,128)(2,1)S(1)}, bf16[384,768]{1,0:T(8,128)(2,1)}, u32[]{:S(2)}) copy-start(bf16[384,768]{1,0:T(8,128)(2,1)} %weight.3) | copy-start | bytes 1769476
  36.8 1.5 %collective-permute-start.5 = (bf16[256,384]{1,0:T(8,128)(2,1)S(1)}, bf16[256,384]{1,0:T(8,128)(2,1)S(1)}, u32[]{:S(2)}, u32[]{:S(2)}) collective-permute-start(bf16[256,384]{1,0:T(8,128)(2,1)S(1)} %merge_even.3.attended), channel_id=1, source_target_pairs={{0,1},{1,0},{2,3},{3,2},{4,5},{5,4},{6,7},{7,6},{8,9},{9,8},{10,11... | collective-permute-start | bytes 589832 | tf_op jit(solution)/shard_map/ppermute | solution.py:456
  39.2 8.4 %collective-permute-start.7 = (bf16[128,768]{1,0:T(8,128)(2,1)S(1)}, bf16[128,768]{1,0:T(8,128)(2,1)S(1)}, u32[]{:S(2)}, u32[]{:S(2)}) collective-permute-start(bf16[128,768]{1,0:T(8,128)(2,1)S(1)} %get-tuple-element.34), channel_id=1, source_target_pairs={{0,2},{1,5},{2,0},{3,7},{4,6},{5,1},{6,4},{7,3},{8,10},{9,13},{10,... | collective-permute-start | bytes 589832 | tf_op jit(solution)/shard_map/ppermute | solution.py:463
  42.6 5.7 %collective-permute-start.10 = (bf16[128,768]{1,0:T(8,128)(2,1)S(1)}, bf16[128,768]{1,0:T(8,128)(2,1)S(1)}, u32[]{:S(2)}, u32[]{:S(2)}) collective-permute-start(bf16[128,768]{1,0:T(8,128)(2,1)S(1)} %get-tuple-element.34), channel_id=1, source_target_pairs={{0,4},{1,3},{2,6},{3,1},{4,0},{5,7},{6,2},{7,5},{8,12},{9,11},{10,... | collective-permute-start | bytes 589832 | tf_op jit(solution)/shard_map/ppermute | solution.py:463
  47.6 2.5 %collective-permute-start.9 = (bf16[128,768]{1,0:T(8,128)(2,1)S(1)}, bf16[128,768]{1,0:T(8,128)(2,1)S(1)}, u32[]{:S(2)}, u32[]{:S(2)}) collective-permute-start(bf16[128,768]{1,0:T(8,128)(2,1)S(1)} %collective-permute-done.7.refs_3_), channel_id=1, source_target_pairs={{0,1},{1,0},{2,3},{3,2},{4,5},{5,4},{6,7},{7,6},{8,9},{9,8},{10,11... | collective-permute-start | bytes 589832 | tf_op jit(solution)/shard_map/ppermute | solution.py:456
  48.2 1.9 %collective-permute-start.11 = (bf16[128,768]{1,0:T(8,128)(2,1)S(1)}, bf16[128,768]{1,0:T(8,128)(2,1)S(1)}, u32[]{:S(2)}, u32[]{:S(2)}) collective-permute-start(bf16[128,768]{1,0:T(8,128)(2,1)S(1)} %collective-permute-done.10.refs_5_), channel_id=1, source_target_pairs={{0,1},{1,0},{2,3},{3,2},{4,5},{5,4},{6,7},{7,6},{8,9},{9,8},{10,11... | collective-permute-start | bytes 589832 | tf_op jit(solution)/shard_map/ppermute | solution.py:456
  48.4 6.1 %collective-permute-start.8 = (bf16[128,768]{1,0:T(8,128)(2,1)S(1)}, bf16[128,768]{1,0:T(8,128)(2,1)S(1)}, u32[]{:S(2)}, u32[]{:S(2)}) collective-permute-start(bf16[128,768]{1,0:T(8,128)(2,1)S(1)} %collective-permute-done.7.refs_3_), channel_id=1, source_target_pairs={{0,4},{1,3},{2,6},{3,1},{4,0},{5,7},{6,2},{7,5},{8,12},{9,11},{10,... | collective-permute-start | bytes 589832 | tf_op jit(solution)/shard_map/ppermute | solution.py:463
  50.0 9.4 %collective-permute-start.14 = (bf16[384,768]{1,0:T(8,128)(2,1)S(1)}, bf16[384,768]{1,0:T(8,128)(2,1)S(1)}, u32[]{:S(2)}, u32[]{:S(2)}) collective-permute-start(bf16[384,768]{1,0:T(8,128)(2,1)S(1)} %copy-done.7), channel_id=1, source_target_pairs={{0,1},{1,0},{2,3},{3,2},{4,5},{5,4},{6,7},{7,6},{8,9},{9,8},{10,11... | collective-permute-start | bytes 1769480 | tf_op jit(solution)/shard_map/ppermute | solution.py:456
  54.5 1.5 %collective-permute-start.12 = (bf16[128,768]{1,0:T(8,128)(2,1)S(1)}, bf16[128,768]{1,0:T(8,128)(2,1)S(1)}, u32[]{:S(2)}, u32[]{:S(2)}) collective-permute-start(bf16[128,768]{1,0:T(8,128)(2,1)S(1)} %collective-permute-done.8.mine), channel_id=1, source_target_pairs={{0,1},{1,0},{2,3},{3,2},{4,5},{5,4},{6,7},{7,6},{8,9},{9,8},{10,11... | collective-permute-start | bytes 589832 | tf_op jit(solution)/shard_map/ppermute | solution.py:456
  58.1 1.5 %collective-permute-start.13 = (bf16[256,384]{1,0:T(8,128)(2,1)S(1)}, bf16[256,384]{1,0:T(8,128)(2,1)S(1)}, u32[]{:S(2)}, u32[]{:S(2)}) collective-permute-start(bf16[256,384]{1,0:T(8,128)(2,1)S(1)} %get-tuple-element.51), channel_id=1, source_target_pairs={{0,1},{1,0},{2,3},{3,2},{4,5},{5,4},{6,7},{7,6},{8,9},{9,8},{10,11... | collective-permute-start | bytes 589832 | tf_op jit(solution)/shard_map/ppermute | solution.py:456

commit v3 on v2

--- a/solution.py
+++ b/solution.py
@@ -52,14 +52,15 @@
     rest = logs - high.astype(F32)
     middle = rest.astype(BF16)
     low = (rest - middle.astype(F32)).astype(BF16)
+    if 3 * rows <= width:
+        return jnp.concatenate([found(part, 0) for part in (high, middle, low)], axis=1).astype(BF16)
     below = found(high, 0) + found(middle, heads)
     beside = found(low[:half], 0) + found(low[half:], heads)
     return jnp.concatenate([below, beside], axis=1).astype(BF16)
 
 
-def unpack_logs(packed, width):
+def unpack_logs(packed, rows, width):
     heads = width // HEAD_DIM
-    rows = packed.shape[1] * 2 // 3
 
     def spread(first):
         row, lane, inside = spread_of((packed.shape[0], width), first, heads)
@@ -69,6 +70,9 @@
         return jnp.where(mask, 1.0, 0.0).astype(BF16)
 
     top, end = spread(0), spread(heads)
+    if 3 * rows <= width:
+        terms = [packed[:, term * rows:(term + 1) * rows] for term in range(3)]
+        return sum(tn(term, as_matrix(top)) for term in terms)
     beside = packed[:, rows:]
     low = jnp.concatenate([tn(beside, as_matrix(top)), tn(beside, as_matrix(end))], axis=0)
     return tn(packed[:, :rows], as_matrix(top | end)) + low
@@ -212,17 +216,15 @@
     message[rows:, :] = pack_logs(logs[...])
 
 
-def encode_side_kernel(
-    bit_0, bit_1, count, scales, latents, wq, keys, values, message, logs
-):
+def encode_side_kernel(count, scales, latents, wq, keys, values, message, logs):
     quad, core = bits_of()
     rows = logs.shape[0]
-    side = quad ^ jnp.where(core == 0, bit_0, bit_1)
+    side = quad ^ jnp.where(core == 0, 1, 2)
     part = quarter(latents, side, rows)[...]
     encode_into(message, part, wq, keys, values, count, scales, logs)
 
 
-def encode_own_kernel(count, scales, latents, wq, keys, values, came, kept, logs):
+def encode_keep_kernel(is_own, count, scales, latents, wq, keys, values, kept, logs):
     quad, core = bits_of()
     rows = kept.shape[0]
 
@@ -230,10 +232,9 @@
         kept[:, lanes] = part
         logs[:, lanes] = log
 
-    part = quarter(latents, quad, rows)[...]
+    at = quad if is_own else quad ^ jnp.where(core == 0, 2, 1)
+    part = quarter(latents, at, rows)[...]
     encode_rows(part, wq, keys, values, count[0:1, :], scales[0, 0:1, :], put)
-    kept[...], logs[...] = merge(kept[...], logs[...], *read_message(came, rows))
-
 
 def write_message(message, values, logs):
     rows = values.shape[0]
@@ -243,13 +244,23 @@
 
 def read_message(message, rows):
     width = message.shape[1]
-    return message[:rows, :].astype(F32), unpack_logs(message[rows:, :], width)
-
-
-def merge_sides_kernel(values, logs, first, second, message):
+    return message[:rows, :].astype(F32), unpack_logs(message[rows:, :], rows, width)
+
+
+def merge_one_kernel(values, logs, came, message):
     rows = values.shape[0]
-    part, log = merge(values[...], logs[...], *read_message(first, rows))
-    part, log = merge(part, log, *read_message(second, rows))
+    part, log = merge(values[...], logs[...], *read_message(came, rows))
+    write_message(message, part, log)
+
+
+def merge_sides_kernel(which, values, logs, first, second, message):
+    rows = values.shape[0]
+    half = rows // 2
+    at = slice(which * half, (which + 1) * half)
+    part, log = values[at, :], logs[at, :]
+    for came in (first, second):
+        came_part, came_log = read_message(came, rows)
+        part, log = merge(part, log, came_part[at], came_log[at])
     write_message(message, part, log)
 
 
@@ -274,35 +285,50 @@
         both(came, mine)
 
 
-def latent_kernel(attended, other, weight, other_weight, latents, gain, out, half):
+def latent_kernel(which, attended, other, weight, other_weight, latents, gain, *refs):
     quad, core = bits_of()
-    rows = attended.shape[0]
-    start = pl.ds(pl.multiple_of(quad * rows, rows), rows)
+    half = attended.shape[0]
+    start = pl.ds(pl.multiple_of((2 * quad + which) * half, half), half)
 
     def finish(first, second, first_weight, second_weight):
         update = nn(first[...], first_weight[...]) + nn(second[...], second_weight[...])
         pre = latents[start, :].astype(F32) + update
         mean_square = jnp.mean(pre * pre, axis=-1, keepdims=True)
-        out[...] = (pre * lax.rsqrt(mean_square + NORM_EPSILON) * gain[...]).astype(BF16)
+        done = (pre * lax.rsqrt(mean_square + NORM_EPSILON) * gain[...]).astype(BF16)
+        if which == 0:
+            refs[0][...] = done
+        else:
+            low, out, own_half = refs
+            out[:half, :] = low[...]
+            out[half:, :] = done
+            own_half[...] = jnp.where(core == 0, low[...], done)
 
     @pl.when(core == 0)
     def _():
         finish(attended, other, weight, other_weight)
-        half[...] = out[:rows // 2, :]
 
     @pl.when(core != 0)
     def _():
         finish(other, attended, other_weight, weight)
-        half[...] = out[rows // 2:, :]
-
-
-def decode_queries_kernel(scales, tokens, wq, out):
+
+
+def groups_of(pairs):
+    first = -(-2 * pairs // 3)
+    return [range(first), range(first, pairs)]
+
+
+def decode_prepare_kernel(scales, tokens, wq, wk, wv, out, *weights):
     width = wq.shape[1]
     high, low = split_scaled(nn(tokens[...], wq[...]), scales[1, 0:1, :])
     for pair in range(width // PAIR):
         lanes = slice(pair * PAIR, (pair + 1) * PAIR)
         out[pair, :, :PAIR] = high[:, lanes]
         out[pair, :, PAIR:] = low[:, lanes]
+    for group, both in zip(groups_of(width // PAIR), weights):
+        lanes = slice(group[0] * PAIR, (group[-1] + 1) * PAIR)
+        size = len(group) * PAIR
+        both[:, :size] = wk[:, lanes]
+        both[:, size:] = wv[:, lanes]
 
 
 def place_rows(pieces, spots, latent_out, staged, sent):
@@ -322,7 +348,7 @@
     return moves
 
 
-def decode_part(queries, keys, values, state, lanes):
+def decode_part(queries, keys, values, state):
     high, low = queries[:, :PAIR], queries[:, PAIR:]
     one = jnp.ones((keys.shape[0], PAIR), BF16)
     sums, total, top = attend_pair(high, low, pair_keys(keys), pair_values(values, one))
@@ -334,42 +360,65 @@
     return old * old_sums + new * sums, old * old_total + new * total, new_top
 
 
-def decode_step_kernel(is_first, where, *refs):
-    queries, wk, wv, *refs = refs
+def decode_group(group, queries, both, at, state, put):
+    size = len(group) * PAIR
+    for place, pair in enumerate(group):
+        lanes = slice(place * PAIR, (place + 1) * PAIR)
+        value_lanes = slice(size + place * PAIR, size + (place + 1) * PAIR)
+        old = None if state is None else [part[at, lanes] for part in state]
+        put(lanes, pair, decode_part(queries[pair, at, :], both[:, lanes], both[:, value_lanes], old))
+
+
+def decode_tokens(group, queries, both, state, new_state):
+    block = queries.shape[1] // 2
+    for index in range(2):
+        at = slice(index * block, (index + 1) * block)
+
+        def put(lanes, pair, new):
+            for out, part in zip(new_state, new):
+                out[at, lanes] = part
+
+        decode_group(group, queries, both, at, state, put)
+
+
+def decode_own_kernel(queries, weights, more_weights, own, latent_out, *refs):
+    *states, staged, sent = refs
     quad, core = bits_of()
-    count = len(where(quad, core, 0))
-    pieces, refs = refs[:count], refs[count:]
-    state = None
-    if not is_first:
-        _, *state = refs[:4]
-        refs = refs[4:]
-    latent_out, sums, total, top, gathered, staged, sent = refs
-    model = gathered.shape[1]
-    rows = latent_out.shape[0] // 4
-    moves = place_rows(pieces, where(quad, core, rows), latent_out, staged, sent)
-    start = 0
-    for piece in pieces:
-        gathered[start:start + piece.shape[0], :] = piece[...]
-        start += piece.shape[0]
-    keys = nn(gathered[...], wk[...]).astype(BF16)
-    values = nn(gathered[...], wv[...]).astype(BF16)
-    block = queries.shape[1] // 2
-    for pair in range(queries.shape[0]):
-        lanes = slice(pair * PAIR, (pair + 1) * PAIR)
-        for index in range(2):
-            at = slice(index * block, (index + 1) * block)
-            old = None if is_first else [part[at, lanes] for part in state]
-            new = decode_part(queries[pair, at, :], keys[:, lanes], values[:, lanes], old, lanes)
-            for out, part in zip((sums, total, top), new):
-                out[at, lanes] = part
-    for move in moves:
-        move.wait()
-
-
-def decode_send_kernel(
-    queries, wk, wv, mine, came, latent_in, sums, total, top,
-    latent_out, send, keys, values, gathered, staged, sent,
-):
+    rows = own.shape[0]
+    moves = place_rows([own], [quad * rows], latent_out, staged, sent)
+    for group, weight, state in zip(
+        groups_of(queries.shape[0]), [weights, more_weights], [states[:3], states[3:]]
+    ):
+        both = nn(own[...], weight[...]).astype(BF16)
+        decode_tokens(group, queries, both, None, state)
+    wait_all(moves)
+
+
+def decode_sides_kernel(queries, weights, mine_a, came_a, mine_b, came_b, latent_in, *refs):
+    state, (latent_out, gathered, *new_state, staged, sent) = refs[:3], refs[3:]
+    quad, core = bits_of()
+    half = mine_a.shape[0]
+    rows = 2 * half
+    near, far = (quad ^ (1 + core)) * rows, (quad ^ (2 - core)) * rows
+    this, that = core * half, (1 - core) * half
+    pieces = [mine_a, came_a, mine_b, came_b]
+    moves = place_rows(
+        pieces, [near + this, far + that, far + this, near + that], latent_out, staged, sent
+    )
+    for index, piece in enumerate(pieces):
+        gathered[index * half:(index + 1) * half, :] = piece[...]
+    both = nn(gathered[...], weights[...]).astype(BF16)
+    decode_tokens(groups_of(queries.shape[0])[0], queries, both, state, new_state)
+    wait_all(moves)
+
+
+def decode_rest_kernel(queries, weights, gathered, *refs):
+    both = nn(gathered[...], weights[...]).astype(BF16)
+    decode_tokens(groups_of(queries.shape[0])[1], queries, both, refs[:3], refs[3:])
+
+
+def decode_send_kernel(queries, weights, more_weights, mine, came, latent_in, *refs):
+    states, (latent_out, send, *boths, gathered, staged, sent) = refs[:6], refs[6:]
     quad, core = bits_of()
     rows, half = latent_out.shape[0] // 4, mine.shape[0]
     diagonal = (quad ^ 3) * rows
@@ -377,36 +426,46 @@
     moves = place_rows([mine, came], spots, latent_out, staged, sent)
     gathered[:half, :] = mine[...]
     gathered[half:, :] = came[...]
-    keys[...] = nn(gathered[...], wk[...]).astype(BF16)
-    values[...] = nn(gathered[...], wv[...]).astype(BF16)
-    decode_last(1 - core, queries, keys, values, sums, total, top, send)
-    for move in moves:
-        move.wait()
-
-
-def decode_last(which, queries, keys, values, sums, total, top, out):
+    for both, weight in zip(boths, [weights, more_weights]):
+        both[...] = nn(gathered[...], weight[...]).astype(BF16)
+    decode_last(1 - core, queries, boths, states, send)
+    wait_all(moves)
+
+
+def decode_last(which, queries, boths, states, out):
     block = out.shape[0]
     at = pl.ds(pl.multiple_of(which * block, block), block)
-    for pair in range(queries.shape[0]):
-        lanes = slice(pair * PAIR, (pair + 1) * PAIR)
-        old = [part[at, lanes] for part in (sums, total, top)]
-        new = decode_part(queries[pair, at, :], keys[:, lanes], values[:, lanes], old, lanes)
-        out[:, lanes] = (new[0] / new[1]).astype(BF16)
-
-
-def decode_keep_kernel(queries, keys, values, sums, total, top, keep):
+
+    def put(lanes, pair, new):
+        out[:, pair * PAIR:(pair + 1) * PAIR] = (new[0] / new[1]).astype(BF16)
+
+    for group, both, state in zip(
+        groups_of(queries.shape[0]), boths, [states[:3], states[3:]]
+    ):
+        decode_group(group, queries, both, at, state, put)
+
+
+def decode_keep_kernel(queries, both, more_both, tokens, weight, *refs):
+    *states, base, attended = refs
     core = lax.axis_index("qgrp")
-    decode_last(core, queries, keys, values, sums, total, top, keep)
-
-
-def tokens_kernel(count, attended, other, weight, other_weight, tokens, out):
-    core = lax.axis_index("qgrp")
-    rows = attended.shape[0]
-    update = nn(attended[...], weight[...]) + nn(other[...], other_weight[...])
-    start = core * rows
-    own = tokens[pl.ds(pl.multiple_of(start, rows), rows), :].astype(F32)
-    is_valid = start + lax.broadcasted_iota(jnp.int32, out.shape, 0) < count[0:1, 0:1]
-    out[...] = jnp.where(is_valid, own + update, 0.0)
+    decode_last(core, queries, [both, more_both], states, attended)
+    rows = base.shape[0]
+    own = tokens[pl.ds(pl.multiple_of(core * rows, rows), rows), :].astype(F32)
+    base[...] = own + nn(attended[...], weight[...])
+
+
+def tokens_kernel(count, base, other, weight, out, staged, sent):
+    start = lax.axis_index("qgrp") * base.shape[0]
+    rows = base.shape[0] // 2
+    moves = []
+    for index in range(2):
+        at = pl.ds(index * rows, rows)
+        value = base[at, :] + nn(other[at, :], weight[...])
+        slot = start + index * rows + lax.broadcasted_iota(jnp.int32, value.shape, 0)
+        staged[at, :] = jnp.where(slot < count[0:1, 0:1], value, 0.0)
+        moves.append(pltpu.make_async_copy(staged.at[at, :], out.at[at, :], sent.at[index]))
+        moves[-1].start()
+    wait_all(moves)
 
 
 SPACES = {
@@ -416,7 +475,7 @@
 }
 
 
-def call(kernel, ins, outs, *args, far=(), alias=None, scratch=(), vmem=24, flops=0, after=(),
+def call(kernel, ins, outs, *args, far=(), alias=None, scratch=(), vmem=24, flops=0, moved=0, after=(),
          name=None):
     given, more = len(args), len(after)
     args = [
@@ -430,7 +489,7 @@
             alone(*refs[:given], *refs[given + more:])
 
     shapes = [jax.ShapeDtypeStruct(*out) for out in outs]
-    moved = sum(a.size * a.dtype.itemsize for a in [*args, *shapes])
+    moved = moved or sum(a.size * a.dtype.itemsize for a in [*args, *shapes])
     return pl.pallas_call(
         kernel,
         out_shape=shapes,
@@ -479,101 +538,113 @@
         ],
         flops=attention, name="encode_corner",
     )
-    corner = trade(message, 3, 3)
-
-    def encode_side(bit_0, bit_1, after):
-        (message,) = call(
-            functools.partial(encode_side_kernel, bit_0, bit_1), "vvvvvv", [sent],
-            count, scales, latents, wq, keys, values,
-            scratch=[pltpu.VMEM((rows, width), F32)],
-            flops=attention, after=after, name="encode_side",
-        )
-        return message
-
-    message = encode_side(1, 2, [])
+    came = trade(message, 1, 2)
+    state = [((rows, width), F32)] * 2
+    passed = call(
+        functools.partial(encode_keep_kernel, False), "vvvvvv", state,
+        count, scales, latents, wq, keys, values, flops=attention, name="encode_pass",
+    )
+    (message,) = call(
+        encode_side_kernel, "vvvvvv", [sent], count, scales, latents, wq, keys, values,
+        scratch=[pltpu.VMEM((rows, width), F32)], flops=attention, after=passed[1:],
+        name="encode_side",
+    )
     first = trade(message, 1, 2)
-    message = encode_side(2, 1, [message])
+    (message,) = call(
+        merge_one_kernel, "vvv", [sent], *passed, came, after=[message], name="merge_pass"
+    )
     second = trade(message, 2, 1)
     kept, kept_logs = call(
-        encode_own_kernel, "vvvvvvv", [((rows, width), F32)] * 2,
-        count, scales, latents, wq, keys, values, corner,
+        functools.partial(encode_keep_kernel, True), "vvvvvv", state,
+        count, scales, latents, wq, keys, values,
         flops=attention, after=[message], name="encode_own",
     )
     other_wo, other_do = swap(wo), swap(do)
-    (message,) = call(
-        merge_sides_kernel, "vvvv", [sent], kept, kept_logs, first, second, name="merge_sides"
-    )
-    (queries,) = call(
-        decode_queries_kernel, "vvv", [((width // PAIR, slots, 2 * PAIR), BF16)],
-        scales, tokens, dq, after=[message], name="decode_queries",
+    half = rows // 2
+    parts = []
+    for which in range(2):
+        parts += call(
+            functools.partial(merge_sides_kernel, which), "vvvv",
+            [((half + log_rows(width), width), BF16)], kept, kept_logs, first, second,
+            after=parts, name="merge_sides",
+        )
+    sizes = [len(group) * PAIR for group in groups_of(width // PAIR)]
+    queries, *weights = call(
+        decode_prepare_kernel, "vvvvv",
+        [
+            ((width // PAIR, slots, 2 * PAIR), BF16),
+            *[((model, 2 * size), BF16) for size in sizes],
+        ],
+        scales, tokens, dq, dk, dv, after=parts, name="decode_prepare",
     )
     bits = [4 << i for i in range(max(cells.bit_length() - 3, 0))]
     for index, (bit_0, bit_1) in enumerate(zip(bits, bits[::-1])):
         last = index == len(bits) - 1
-        came = trade(message, bit_0, bit_1)
-        (message,) = call(
-            functools.partial(merge_even_kernel, bit_0, bit_1, last, rows), "vv",
-            [((rows, width), BF16) if last else sent], message, came,
-            after=[queries] if last else [], name="merge_even",
-        )
-    attended = message[:rows]
-    half = rows // 2
+        merged = []
+        for part, came in [(part, trade(part, bit_0, bit_1)) for part in parts]:
+            merged += call(
+                functools.partial(merge_even_kernel, bit_0, bit_1, last, half), "vv",
+                [((half, width), BF16) if last else (part.shape, BF16)], part, came,
+                after=[*merged, queries] if last else merged, name="merge_even",
+            )
+        parts = merged
+    parts = [part[:half] for part in parts]
+    (own_low,) = call(
+        functools.partial(latent_kernel, 0), "vvvvvv", [((half, model), BF16)],
+        parts[0], swap(parts[0]), wo, other_wo, latents, gain.reshape(1, model),
+        after=parts[1:], name="latent_low",
+    )
     own, own_half = call(
-        latent_kernel, "vvvvvv", [((rows, model), BF16), ((half, model), BF16)],
-        attended, swap(attended), wo, other_wo, latents, gain.reshape(1, model), name="latent",
+        functools.partial(latent_kernel, 1), "vvvvvvv",
+        [((rows, model), BF16), ((half, model), BF16)],
+        parts[1], swap(parts[1]), wo, other_wo, latents, gain.reshape(1, model), own_low,
+        name="latent",
     )
     first = trade(own_half, 1, 2)
     second = trade(own_half, 2, 1)
     whole = ((total_rows, model), F32)
-    state_out = [((slots, width), F32)] * 3
+    states_out = [((slots, size), F32) for size in sizes for _ in range(3)]
 
     def scratch(count, pieces):
-        return [
-            pltpu.VMEM((count, model), BF16), pltpu.VMEM((count, model), F32),
-            pltpu.SemaphoreType.DMA((pieces,)),
-        ]
-
-    def own_spot(quad, core, rows):
-        return [quad * rows]
-
-    def side_spots(quad, core, rows):
-        half = rows // 2
-        return [
-            (quad ^ (1 + core)) * rows + core * half,
-            (quad ^ (2 - core)) * rows + (1 - core) * half,
-            (quad ^ (2 - core)) * rows + core * half,
-            (quad ^ (1 + core)) * rows + (1 - core) * half,
-        ]
-
-    latent_out, *state = call(
-        functools.partial(decode_step_kernel, True, own_spot), "vvvv",
-        [whole, *state_out], queries, dk, dv, own,
+        return [pltpu.VMEM((count, model), F32), pltpu.SemaphoreType.DMA((pieces,))]
+
+    latent_out, *states = call(
+        decode_own_kernel, "vvvv", [whole, *states_out], queries, *weights, own,
         far=(0,), scratch=scratch(rows, 1), flops=attention, name="decode_own",
     )
-    first, own = lax.optimization_barrier((first, state[0]))
-    state[0] = own
+    first, states[0] = lax.optimization_barrier((first, states[0]))
     third = trade(first, 2, 1)
-    latent_out, *state = call(
-        functools.partial(decode_step_kernel, False, side_spots), "vvvvvvvhvvv",
-        [whole, *state_out], queries, dk, dv, first, swap(first), second, swap(second),
-        latent_out, *state, far=(0,), alias={7: 0},
-        scratch=scratch(2 * rows, 4), vmem=32, flops=2 * attention, name="decode_sides",
-    )
-    third, late = lax.optimization_barrier((third, state[0]))
-    state[0] = late
-    latent_out, send, keys, values = call(
-        decode_send_kernel, "vvvvvhvvv",
-        [whole, ((half_slots, width), BF16), *[((rows, width), BF16)] * 2],
-        queries, dk, dv, third, swap(third), latent_out, *state, far=(0,), alias={5: 0},
-        scratch=scratch(rows, 2), flops=attention // 2, name="decode_send",
-    )
-    (keep,) = call(
-        decode_keep_kernel, "vvvvvv", [((half_slots, width), BF16)],
-        queries, keys, values, *state, flops=attention // 2, name="decode_keep",
+    latent_out, gathered, *side = call(
+        decode_sides_kernel, "vvvvvvhvvv", [whole, ((2 * rows, model), BF16), *states_out[:3]],
+        queries, weights[0], first, swap(first), second, swap(second), latent_out, *states[:3],
+        far=(0,), alias={6: 0}, scratch=scratch(2 * rows, 4), vmem=28, flops=attention,
+        name="decode_sides",
+    )
+    third, side[0] = lax.optimization_barrier((third, side[0]))
+    came = swap(third)
+    rest = call(
+        decode_rest_kernel, "vvvvvv", states_out[3:], queries, weights[1], gathered, *states[3:],
+        flops=attention, after=side[1:2], name="decode_rest",
+    )
+    states = [*side, *rest]
+    latent_out, send, *boths = call(
+        decode_send_kernel, "vvvvvhvvvvvv",
+        [
+            whole, ((half_slots, width), BF16),
+            *[((rows, 2 * size), BF16) for size in sizes],
+        ],
+        queries, *weights, third, came, latent_out, *states, far=(0,), alias={5: 0},
+        scratch=[pltpu.VMEM((rows, model), BF16), *scratch(rows, 2)],
+        flops=attention // 2, name="decode_send",
+    )
+    (base,) = call(
+        decode_keep_kernel, "vvvvvvvvvvv", [((half_slots, model), F32)],
+        queries, *boths, tokens, do, *states, scratch=[pltpu.VMEM((half_slots, width), BF16)],
+        flops=attention // 2, name="decode_keep",
     )
     (tokens_out,) = call(
-        tokens_kernel, "vvvvvv", [((half_slots, model), F32)],
-        count, keep, swap(send), do, other_do, tokens, name="tokens",
+        tokens_kernel, "vvvv", [((half_slots, model), F32)], count, base, swap(send), other_do,
+        far=(0,), scratch=scratch(half_slots, 2), name="tokens",
     )
     return latent_out, tokens_out
 

time: 61.2 us -> 58.3 us (0.953)
  waiting for transfers between devices: 17.7 us -> 11.8 us
  Pallas kernels: 24.9 us -> 27.2 us
    ppermute x8 -> x10, waiting for transfers between devices: 15.1 us -> 11.2 us  [trade(): return lax.ppermute(array, ('cell', 'qgrp'), pairs)]
    pallas_call x14 -> x20, Pallas kernels: 24.9 us -> 27.2 us  [call(): pl.pallas_call(kernel, out_shape=shapes, in_specs=[SPACES[kind] for kind...]
    ppermute x7 -> x8, waiting for transfers between devices: 2.62 us -> 0.58 us  [swap(): return lax.ppermute(array, 'qgrp', [(0, 1), (1, 0)])]
    ppermute x8 -> x10, starting transfers between devices: 15.5 us -> 16 us  [trade(): return lax.ppermute(array, ('cell', 'qgrp'), pairs)]
    ppermute x7 -> x8, starting transfers between devices: 1.31 us -> 1.23 us  [swap(): return lax.ppermute(array, 'qgrp', [(0, 1), (1, 0)])]
  transfers between devices with their start and end apart: 15 -> 18, of which waited for: 9 -> 8; matrix products, arithmetic and copies ran while one was open for 0% -> 0% of each run, Pallas kernels for 28% -> 36%
where the time goes in v3:
time: 58.3 us; the launch traced here: 58.1 us
  Pallas kernels  27.2 us (47%)
  starting transfers between devices  17.2 us (30%)
  waiting for transfers between devices  11.8 us (20%)
  between operations  1.88 us (3%)
    pallas_call x20, Pallas kernels, call(): pl.pallas_call(kernel, out_shape=shapes, in_specs=[SPACES[kind] for kind...  27.2 us
    ppermute x10, starting transfers between devices, trade(): return lax.ppermute(array, ('cell', 'qgrp'), pairs)  16 us
    ppermute x10, waiting for transfers between devices, trade(): return lax.ppermute(array, ('cell', 'qgrp'), pairs)  11.2 us
    ppermute x8, starting transfers between devices, swap(): return lax.ppermute(array, 'qgrp', [(0, 1), (1, 0)])  1.23 us
  transfers between devices with their start and end apart: 18, of which 8 were waited for; matrix products, arithmetic and copies ran while one was open for 0% of the time, Pallas kernels for 36%

profile of v3, /device:TPU:0, one launch (start us, length us, event | category | flops | bytes accessed | tf_op | source)
XLA Modules:
  0.0 58.1 jit_solution(5377832091301116980)
XLA Ops:
  0.6 0.0 copy-start
  0.6 0.0 copy-start.2
  1.5 4.5 %encode_corner.1 = (bf16[272,384]{1,0:T(8,128)(2,1)S(1)}, bf16[512,384]{1,0:T(8,128)(2,1)S(1)}, bf16[512,384]{1,0:T(8,128)(2,1)S(1)}, f32[2,8,384]{2,1,0:T(8,128)S(1)}, s32[8,128]{1,0:T(8,128)S(1)}) custom-call(s32[1]{0:T(128)S(6)} %copy.19.tally, f32[2,12]{1,0:T(2,128)} %softness_far.1, bf16[1024,768]{1,0:T(8,128)(2,1)} %latents.3, ...), custom_call_target="tpu_custom_call" | custom-call | flops 805306368 | bytes 5152868 | tf_op jit(solution)/shard_map/encode_corner/pallas_call | solution.py:493
  6.0 3.0 %collective-permute-start = (bf16[272,384]{1,0:T(8,128)(2,1)S(1)}, bf16[272,384]{1,0:T(8,128)(2,1)S(1)}, u32[]{:S(2)}, u32[]{:S(2)}) collective-permute-start(bf16[272,384]{1,0:T(8,128)(2,1)S(1)} %get-tuple-element.45), channel_id=1, source_target_pairs={{0,2},{1,5},{2,0},{3,7},{4,6},{5,1},{6,4},{7,3},{8,10},{9,13},{10,... | collective-permute-start | bytes 626696 | tf_op jit(solution)/shard_map/ppermute | solution.py:522
  9.0 0.0 copy-done.3
  9.0 0.0 collective-permute-start.8
  9.0 1.5 %encode_pass.1 = (f32[256,384]{1,0:T(8,128)S(1)}, f32[256,384]{1,0:T(8,128)S(1)}) custom-call(s32[8,128]{1,0:T(8,128)S(1)} %get-tuple-element.40.count.refs_0_, f32[2,8,384]{2,1,0:T(8,128)S(1)} %get-tuple-element.39.scales.refs_1_.refs_0_, bf16[1024,768]{1,0:T(8,128)(2,1)S(1)} %copy-done, bf16[768,384]{1,0:T(8,128)(2,1)S(1)} %copy-done.2, ...), custom_call_target="tpu_custom_call" | custom-call | flops 805306368 | bytes 3764224 | tf_op jit(solution)/shard_map/encode_pass/pallas_call | solution.py:493
  10.5 1.9 %encode_side.1.refs_3_ = bf16[272,384]{1,0:T(8,128)(2,1)S(1)} custom-call(s32[8,128]{1,0:T(8,128)S(1)} %get-tuple-element.40.count.refs_0_, f32[2,8,384]{2,1,0:T(8,128)S(1)} %get-tuple-element.39.scales.refs_1_.refs_0_, bf16[1024,768]{1,0:T(8,128)(2,1)S(1)} %copy-done, bf16[768,384]{1,0:T(8,128)(2,1)S(1)} %copy-done.2, ...), custom_call_target="tpu_custom_call" | custom-call | flops 805306368 | bytes 3186688 | tf_op jit(solution)/shard_map/encode_side/pallas_call | solution.py:493
  12.4 1.1 %collective-permute-start.1 = (bf16[272,384]{1,0:T(8,128)(2,1)S(1)}, bf16[272,384]{1,0:T(8,128)(2,1)S(1)}, u32[]{:S(2)}, u32[]{:S(2)}) collective-permute-start(bf16[272,384]{1,0:T(8,128)(2,1)S(1)} %encode_side.1.refs_3_), channel_id=1, source_target_pairs={{0,2},{1,5},{2,0},{3,7},{4,6},{5,1},{6,4},{7,3},{8,10},{9,13},{10,... | collective-permute-start | bytes 626696 | tf_op jit(solution)/shard_map/ppermute | solution.py:522
  13.5 0.0 collective-permute-done.refs_2_
  13.5 0.7 %merge_pass.1.refs_6_ = bf16[272,384]{1,0:T(8,128)(2,1)S(1)} custom-call(f32[256,384]{1,0:T(8,128)S(1)} %get-tuple-element.43.refs_0_, f32[256,384]{1,0:T(8,128)S(1)} %get-tuple-element.44.refs_6_.refs_1_, bf16[272,384]{1,0:T(8,128)(2,1)S(1)} %collective-permute-done.refs_2_, bf16[272,384]{1,0:T(8,128)(2,1)S(1)} %encode_side.1.refs_3_), custom_call_target="tpu_custom_call" | custom-call | bytes 1204224 | tf_op jit(solution)/shard_map/merge_pass/pallas_call | solution.py:493
  14.2 0.0 copy-start.4
  14.2 0.0 copy-start.5
  14.3 0.0 copy-start.6
  14.3 1.4 %collective-permute-start.2 = (bf16[272,384]{1,0:T(8,128)(2,1)S(1)}, bf16[272,384]{1,0:T(8,128)(2,1)S(1)}, u32[]{:S(2)}, u32[]{:S(2)}) collective-permute-start(bf16[272,384]{1,0:T(8,128)(2,1)S(1)} %merge_pass.1.refs_6_), channel_id=1, source_target_pairs={{0,4},{1,3},{2,6},{3,1},{4,0},{5,7},{6,2},{7,5},{8,12},{9,11},{10,... | collective-permute-start | bytes 626696 | tf_op jit(solution)/shard_map/ppermute | solution.py:522
  15.6 1.5 %encode_own.1 = (f32[256,384]{1,0:T(8,128)S(1)}, f32[256,384]{1,0:T(8,128)S(1)}) custom-call(s32[8,128]{1,0:T(8,128)S(1)} %get-tuple-element.40.count.refs_0_, f32[2,8,384]{2,1,0:T(8,128)S(1)} %get-tuple-element.39.scales.refs_1_.refs_0_, bf16[1024,768]{1,0:T(8,128)(2,1)S(1)} %copy-done, bf16[768,384]{1,0:T(8,128)(2,1)S(1)} %copy-done.2, ...), custom_call_target="tpu_custom_call" | custom-call | flops 805306368 | bytes 3764224 | tf_op jit(solution)/shard_map/encode_own/pallas_call | solution.py:493
  17.1 1.7 %collective-permute-done.1.first.refs_2_ = bf16[272,384]{1,0:T(8,128)(2,1)S(1)} collective-permute-done((bf16[272,384]{1,0:T(8,128)(2,1)S(1)}, bf16[272,384]{1,0:T(8,128)(2,1)S(1)}, u32[]{:S(2)}, u32[]{:S(2)}) %collective-permute-start.1) | collective-permute-done | bytes 208928 | tf_op jit(solution)/shard_map/ppermute | solution.py:522
  18.9 1.3 %collective-permute-done.2.second.refs_3_ = bf16[272,384]{1,0:T(8,128)(2,1)S(1)} collective-permute-done((bf16[272,384]{1,0:T(8,128)(2,1)S(1)}, bf16[272,384]{1,0:T(8,128)(2,1)S(1)}, u32[]{:S(2)}, u32[]{:S(2)}) %collective-permute-start.2) | collective-permute-done | bytes 208928 | tf_op jit(solution)/shard_map/ppermute | solution.py:522
  20.1 0.7 %merge_sides.2.refs_4_.refs_5_.mine = bf16[144,384]{1,0:T(8,128)(2,1)S(1)} custom-call(f32[256,384]{1,0:T(8,128)S(1)} %get-tuple-element.46.values.refs_0_, f32[256,384]{1,0:T(8,128)S(1)} %get-tuple-element.47.logs.refs_1_, bf16[272,384]{1,0:T(8,128)(2,1)S(1)} %collective-permute-done.1.first.refs_2_, bf16[272,384]{1,0:T(8,128)(2,1)S(1)} %collective-permute-done.2.second.refs_3_), custom_call_target="tpu_custom_call" | custom-call | bytes 1314816 | tf_op jit(solution)/shard_map/merge_sides/pallas_call | solution.py:493
  20.8 1.6 %collective-permute-start.4 = (bf16[144,384]{1,0:T(8,128)(2,1)S(1)}, bf16[144,384]{1,0:T(8,128)(2,1)S(1)}, u32[]{:S(2)}, u32[]{:S(2)}) collective-permute-start(bf16[144,384]{1,0:T(8,128)(2,1)S(1)} %merge_sides.2.refs_4_.refs_5_.mine), channel_id=1, source_target_pairs={{0,8},{1,17},{2,10},{3,19},{4,12},{5,21},{6,14},{7,23},{8,0},{9,25... | collective-permute-start | bytes 331784 | tf_op jit(solution)/shard_map/ppermute | solution.py:522
  22.4 0.7 %merge_sides.3.refs_6_.refs_0_ = bf16[144,384]{1,0:T(8,128)(2,1)S(1)} custom-call(f32[256,384]{1,0:T(8,128)S(1)} %get-tuple-element.46.values.refs_0_, f32[256,384]{1,0:T(8,128)S(1)} %get-tuple-element.47.logs.refs_1_, bf16[272,384]{1,0:T(8,128)(2,1)S(1)} %collective-permute-done.1.first.refs_2_, bf16[272,384]{1,0:T(8,128)(2,1)S(1)} %collective-permute-done.2.second.refs_3_, ...), custom_call_target="tpu_custom_call" | custom-call | bytes 1314816 | tf_op jit(solution)/shard_map/merge_sides/pallas_call | solution.py:493
  23.1 0.5 collective-permute-start.3
  23.6 3.1 %collective-permute-done.4.came = bf16[144,384]{1,0:T(8,128)(2,1)S(1)} collective-permute-done((bf16[144,384]{1,0:T(8,128)(2,1)S(1)}, bf16[144,384]{1,0:T(8,128)(2,1)S(1)}, u32[]{:S(2)}, u32[]{:S(2)}) %collective-permute-start.4) | collective-permute-done | bytes 110624 | tf_op jit(solution)/shard_map/ppermute | solution.py:522
  26.7 0.6 %merge_even.4.refs_2_.refs_0_ = bf16[144,384]{1,0:T(8,128)(2,1)S(1)} custom-call(bf16[144,384]{1,0:T(8,128)(2,1)S(1)} %merge_sides.2.refs_4_.refs_5_.mine, bf16[144,384]{1,0:T(8,128)(2,1)S(1)} %collective-permute-done.4.came), custom_call_target="tpu_custom_call" | custom-call | bytes 331776 | tf_op jit(solution)/shard_map/merge_even/pallas_call | solution.py:493
  27.3 1.8 %collective-permute-start.6 = (bf16[144,384]{1,0:T(8,128)(2,1)S(1)}, bf16[144,384]{1,0:T(8,128)(2,1)S(1)}, u32[]{:S(2)}, u32[]{:S(2)}) collective-permute-start(bf16[144,384]{1,0:T(8,128)(2,1)S(1)} %merge_even.4.refs_2_.refs_0_), channel_id=1, source_target_pairs={{0,16},{1,9},{2,18},{3,11},{4,20},{5,13},{6,22},{7,15},{8,24},{9,1... | collective-permute-start | bytes 331784 | tf_op jit(solution)/shard_map/ppermute | solution.py:522
  29.2 0.0 collective-permute-done.3.refs_1_
  29.2 0.6 %merge_even.5.refs_0_ = bf16[144,384]{1,0:T(8,128)(2,1)S(1)} custom-call(bf16[144,384]{1,0:T(8,128)(2,1)S(1)} %merge_sides.3.refs_6_.refs_0_, bf16[144,384]{1,0:T(8,128)(2,1)S(1)} %collective-permute-done.3.refs_1_, bf16[144,384]{1,0:T(8,128)(2,1)S(1)} %merge_even.4.refs_2_.refs_0_), custom_call_target="tpu_custom_call" | custom-call | bytes 331776 | tf_op jit(solution)/shard_map/merge_even/pallas_call | solution.py:493
  29.7 2.5 %collective-permute-start.5 = (bf16[144,384]{1,0:T(8,128)(2,1)S(1)}, bf16[144,384]{1,0:T(8,128)(2,1)S(1)}, u32[]{:S(2)}, u32[]{:S(2)}) collective-permute-start(bf16[144,384]{1,0:T(8,128)(2,1)S(1)} %merge_even.5.refs_0_), channel_id=1, source_target_pairs={{0,16},{1,9},{2,18},{3,11},{4,20},{5,13},{6,22},{7,15},{8,24},{9,1... | collective-permute-start | bytes 331784 | tf_op jit(solution)/shard_map/ppermute | solution.py:522
  32.2 0.7 %decode_prepare.1 = (bf16[3,512,256]{2,1,0:T(8,128)(2,1)S(1)}, bf16[768,512]{1,0:T(8,128)(2,1)S(1)}, bf16[768,256]{1,0:T(8,128)(2,1)S(1)}) custom-call(f32[2,8,384]{2,1,0:T(8,128)S(1)} %get-tuple-element.39.scales.refs_1_.refs_0_, bf16[512,768]{1,0:T(8,128)(2,1)S(1)} %copy-done.1, bf16[768,384]{1,0:T(8,128)(2,1)S(1)} %copy-done.4, ...), custom_call_target="tpu_custom_call" | custom-call | bytes 4546560 | tf_op jit(solution)/shard_map/decode_prepare/pallas_call | solution.py:493
  32.9 0.4 collective-permute-done.6.refs_1_
  33.4 0.4 merge_even.6.refs_2_.refs_0_
  33.8 0.1 collective-permute-start.9
  33.9 1.7 %collective-permute-done.5.refs_1_ = bf16[144,384]{1,0:T(8,128)(2,1)S(1)} collective-permute-done((bf16[144,384]{1,0:T(8,128)(2,1)S(1)}, bf16[144,384]{1,0:T(8,128)(2,1)S(1)}, u32[]{:S(2)}, u32[]{:S(2)}) %collective-permute-start.5) | collective-permute-done | bytes 110624 | tf_op jit(solution)/shard_map/ppermute | solution.py:522
  35.6 0.4 merge_even.7.refs_6_.attended
  36.0 0.1 collective-permute-start.7
  36.1 0.0 copy-done.8
  36.1 0.0 collective-permute-done.8.refs_3_.other_weight
  36.1 0.0 collective-permute-done.9.refs_1_
  36.1 0.7 %latent_low.1.refs_0_ = bf16[128,768]{1,0:T(8,128)(2,1)S(1)} custom-call(bf16[128,384]{1,0:T(8,128)(2,1)S(1)} %merge_even.6.refs_2_.refs_0_, bf16[128,384]{1,0:T(8,128)(2,1)S(1)} %collective-permute-done.9.refs_1_, bf16[384,768]{1,0:T(8,128)(2,1)S(1)} %copy-done.3, bf16[384,768]{1,0:T(8,128)(2,1)S(1)} %collective-permute-done.8.refs_3_.other_weight, ...), custom_call_target="tpu_custom_call" | custom-call | bytes 3148800 | tf_op jit(solution)/shard_map/latent_low/pallas_call | solution.py:493
  36.8 0.0 copy-start.7
  36.8 0.6 collective-permute-done.7.other
  37.3 0.5 latent.1
  37.8 1.2 %collective-permute-start.10 = (bf16[128,768]{1,0:T(8,128)(2,1)S(1)}, bf16[128,768]{1,0:T(8,128)(2,1)S(1)}, u32[]{:S(2)}, u32[]{:S(2)}) collective-permute-start(bf16[128,768]{1,0:T(8,128)(2,1)S(1)} %get-tuple-element.51), channel_id=1, source_target_pairs={{0,2},{1,5},{2,0},{3,7},{4,6},{5,1},{6,4},{7,3},{8,10},{9,13},{10,... | collective-permute-start | bytes 589832 | tf_op jit(solution)/shard_map/ppermute | solution.py:522
  39.1 1.6 %collective-permute-start.13 = (bf16[128,768]{1,0:T(8,128)(2,1)S(1)}, bf16[128,768]{1,0:T(8,128)(2,1)S(1)}, u32[]{:S(2)}, u32[]{:S(2)}) collective-permute-start(bf16[128,768]{1,0:T(8,128)(2,1)S(1)} %get-tuple-element.51), channel_id=1, source_target_pairs={{0,4},{1,3},{2,6},{3,1},{4,0},{5,7},{6,2},{7,5},{8,12},{9,11},{10,... | collective-permute-start | bytes 589832 | tf_op jit(solution)/shard_map/ppermute | solution.py:522
  40.6 2.7 %decode_own.1 = (f32[1024,768]{1,0:T(8,128)}, f32[512,256]{1,0:T(8,128)S(1)}, f32[512,256]{1,0:T(8,128)S(1)}, f32[512,256]{1,0:T(8,128)S(1)}, f32[512,128]{1,0:T...) custom-call(bf16[3,512,256]{2,1,0:T(8,128)(2,1)S(1)} %get-tuple-element.48.refs_2_.refs_3_.queries.refs_0_, ...), custom_call_target="tpu_custom_call" | custom-call | flops 805306368 | bytes 7864320 | tf_op jit(solution)/shard_map/decode_own/pallas_call | solution.py:493
  43.4 1.9 %collective-permute-done.10.mine_a = bf16[128,768]{1,0:T(8,128)(2,1)S(1)} collective-permute-done((bf16[128,768]{1,0:T(8,128)(2,1)S(1)}, bf16[128,768]{1,0:T(8,128)(2,1)S(1)}, u32[]{:S(2)}, u32[]{:S(2)}) %collective-permute-start.10) | collective-permute-done | bytes 196640 | tf_op jit(solution)/shard_map/ppermute | solution.py:522
  45.3 0.0 collective-permute-start.12
  45.3 0.0 collective-permute-done.13.mine_b
  45.3 0.5 collective-permute-start.14
  45.8 1.3 %collective-permute-start.11 = (bf16[128,768]{1,0:T(8,128)(2,1)S(1)}, bf16[128,768]{1,0:T(8,128)(2,1)S(1)}, u32[]{:S(2)}, u32[]{:S(2)}) collective-permute-start(bf16[128,768]{1,0:T(8,128)(2,1)S(1)} %collective-permute-done.10.mine_a), channel_id=1, source_target_pairs={{0,4},{1,3},{2,6},{3,1},{4,0},{5,7},{6,2},{7,5},{8,12},{9,11},{10,... | collective-permute-start | bytes 589832 | tf_op jit(solution)/shard_map/ppermute | solution.py:522
  47.1 0.0 collective-permute-start.17
  47.1 0.0 collective-permute-done.12.came_a
  47.1 0.0 collective-permute-done.14.came_b
  47.1 3.3 %decode_sides.1 = (f32[1024,768]{1,0:T(8,128)}, bf16[512,768]{1,0:T(8,128)(2,1)S(1)}, f32[512,256]{1,0:T(8,128)S(1)}, f32[512,256]{1,0:T(8,128)S(1)}, f32[512,256]{1,0:T(8,128)S(1)}) custom-call(bf16[3,512,256]{2,1,0:T(8,128)(2,1)S(1)} %get-tuple-element.48.refs_2_.refs_3_.queries.refs_0_, ...), custom_call_target="tpu_custom_call", output_to_operand_aliasing={{0}: (6, {})} | custom-call | flops 805306368 | bytes 12582912 | tf_op jit(solution)/shard_map/decode_sides/pallas_call | solution.py:493
  50.4 1.0 %collective-permute-done.11.mine = bf16[128,768]{1,0:T(8,128)(2,1)S(1)} collective-permute-done((bf16[128,768]{1,0:T(8,128)(2,1)S(1)}, bf16[128,768]{1,0:T(8,128)(2,1)S(1)}, u32[]{:S(2)}, u32[]{:S(2)}) %collective-permute-start.11) | collective-permute-done | bytes 196640 | tf_op jit(solution)/shard_map/ppermute | solution.py:522
  51.5 0.0 collective-permute-start.15
  51.5 1.4 %decode_rest.1 = (f32[512,128]{1,0:T(8,128)S(1)}, f32[512,128]{1,0:T(8,128)S(1)}, f32[512,128]{1,0:T(8,128)S(1)}) custom-call(bf16[3,512,256]{2,1,0:T(8,128)(2,1)S(1)} %get-tuple-element.48.refs_2_.refs_3_.queries.refs_0_, bf16[768,256]{1,0:T(8,128)(2,1)S(1)} %get-tuple-element.50.more_weights.refs_1_, bf16[512,768]{1,0:T(8,128)(2,1)S(1)} %get-tuple-element.65.refs_2_, ...), custom_call_target="tpu_custom_call" | custom-call | flops 805306368 | bytes 3538944 | tf_op jit(solution)/shard_map/decode_rest/pallas_call | solution.py:493
  52.9 0.0 collective-permute-done.15.came
  52.9 2.1 %decode_send.1 = (f32[1024,768]{1,0:T(8,128)}, bf16[256,384]{1,0:T(8,128)(2,1)S(1)}, bf16[256,512]{1,0:T(8,128)(2,1)S(1)}, bf16[256,256]{1,0:T(8,128)(2,1)S(1)}) custom-call(bf16[3,512,256]{2,1,0:T(8,128)(2,1)S(1)} %get-tuple-element.48.refs_2_.refs_3_.queries.refs_0_, ...), custom_call_target="tpu_custom_call", output_to_operand_aliasing={{0}: (5, {})} | custom-call | flops 402653184 | bytes 11599872 | tf_op jit(solution)/shard_map/decode_send/pallas_call | solution.py:493
  55.0 0.6 collective-permute-start.16
  55.6 1.2 %decode_keep.1.base = f32[256,768]{1,0:T(8,128)S(1)} custom-call(bf16[3,512,256]{2,1,0:T(8,128)(2,1)S(1)} %get-tuple-element.48.refs_2_.refs_3_.queries.refs_0_, bf16[256,512]{1,0:T(8,128)(2,1)S(1)} %get-tuple-element.73.both, bf16[256,256]{1,0:T(8,128)(2,1)S(1)} %get-tuple-element.74.more_both, bf16[512,768]{1,0:T(8,128)(2,1)S(1)} %copy-done.1, ...), custom_call_target="tpu_custom_call" | custom-call | flops 402653184 | bytes 5701632 | tf_op jit(solution)/shard_map/decode_keep/pallas_call | solution.py:493
  56.7 0.0 collective-permute-done.17.weight
  56.7 0.0 collective-permute-done.16.other
  56.8 1.2 %tokens.3 = f32[256,768]{1,0:T(8,128)} custom-call(s32[8,128]{1,0:T(8,128)S(1)} %get-tuple-element.40.count.refs_0_, f32[256,768]{1,0:T(8,128)S(1)} %decode_keep.1.base, bf16[256,384]{1,0:T(8,128)(2,1)S(1)} %collective-permute-done.16.other, bf16[384,768]{1,0:T(8,128)(2,1)S(1)} %collective-permute-done.17.weight), custom_call_target="tpu_custom_call" | custom-call | bytes 2363392 | tf_op jit(solution)/shard_map/tokens/pallas_call | solution.py:493
  (11 shorter events, 0.0 us)
Async XLA Ops:
  0.6 8.4 %copy-start = (bf16[1024,768]{1,0:T(8,128)(2,1)S(1)}, bf16[1024,768]{1,0:T(8,128)(2,1)}, u32[]{:S(2)}) copy-start(bf16[1024,768]{1,0:T(8,128)(2,1)} %latents.3) | copy-start | bytes 4718596
  0.6 8.4 %copy-start.2 = (bf16[768,384]{1,0:T(8,128)(2,1)S(1)}, bf16[768,384]{1,0:T(8,128)(2,1)}, u32[]{:S(2)}) copy-start(bf16[768,384]{1,0:T(8,128)(2,1)} %refs_3_.4) | copy-start | bytes 1769476
  0.7 8.3 %copy-start.3 = (bf16[384,768]{1,0:T(8,128)(2,1)S(1)}, bf16[384,768]{1,0:T(8,128)(2,1)}, u32[]{:S(2)}) copy-start(bf16[384,768]{1,0:T(8,128)(2,1)} %weight.2) | copy-start | bytes 1769476
  6.0 7.5 %collective-permute-start = (bf16[272,384]{1,0:T(8,128)(2,1)S(1)}, bf16[272,384]{1,0:T(8,128)(2,1)S(1)}, u32[]{:S(2)}, u32[]{:S(2)}) collective-permute-start(bf16[272,384]{1,0:T(8,128)(2,1)S(1)} %get-tuple-element.45), channel_id=1, source_target_pairs={{0,2},{1,5},{2,0},{3,7},{4,6},{5,1},{6,4},{7,3},{8,10},{9,13},{10,... | collective-permute-start | bytes 626696 | tf_op jit(solution)/shard_map/ppermute | solution.py:522
  9.0 27.1 %collective-permute-start.8 = (bf16[384,768]{1,0:T(8,128)(2,1)S(1)}, bf16[384,768]{1,0:T(8,128)(2,1)S(1)}, u32[]{:S(2)}, u32[]{:S(2)}) collective-permute-start(bf16[384,768]{1,0:T(8,128)(2,1)S(1)} %copy-done.3), channel_id=1, source_target_pairs={{0,1},{1,0},{2,3},{3,2},{4,5},{5,4},{6,7},{7,6},{8,9},{9,8},{10,11... | collective-permute-start | bytes 1769480 | tf_op jit(solution)/shard_map/ppermute | solution.py:515
  12.4 6.4 %collective-permute-start.1 = (bf16[272,384]{1,0:T(8,128)(2,1)S(1)}, bf16[272,384]{1,0:T(8,128)(2,1)S(1)}, u32[]{:S(2)}, u32[]{:S(2)}) collective-permute-start(bf16[272,384]{1,0:T(8,128)(2,1)S(1)} %encode_side.1.refs_3_), channel_id=1, source_target_pairs={{0,2},{1,5},{2,0},{3,7},{4,6},{5,1},{6,4},{7,3},{8,10},{9,13},{10,... | collective-permute-start | bytes 626696 | tf_op jit(solution)/shard_map/ppermute | solution.py:522
  14.2 18.0 %copy-start.1 = (bf16[512,768]{1,0:T(8,128)(2,1)S(1)}, bf16[512,768]{1,0:T(8,128)(2,1)}, u32[]{:S(2)}) copy-start(bf16[512,768]{1,0:T(8,128)(2,1)} %tokens.2) | copy-start | bytes 2359300
  14.2 18.0 %copy-start.4 = (bf16[768,384]{1,0:T(8,128)(2,1)S(1)}, bf16[768,384]{1,0:T(8,128)(2,1)}, u32[]{:S(2)}) copy-start(bf16[768,384]{1,0:T(8,128)(2,1)} %refs_2_.6) | copy-start | bytes 1769476
  14.2 18.0 %copy-start.5 = (bf16[768,384]{1,0:T(8,128)(2,1)S(1)}, bf16[768,384]{1,0:T(8,128)(2,1)}, u32[]{:S(2)}) copy-start(bf16[768,384]{1,0:T(8,128)(2,1)} %refs_3_.5) | copy-start | bytes 1769476
  14.3 18.0 %copy-start.6 = (bf16[768,384]{1,0:T(8,128)(2,1)S(1)}, bf16[768,384]{1,0:T(8,128)(2,1)}, u32[]{:S(2)}) copy-start(bf16[768,384]{1,0:T(8,128)(2,1)} %refs_4_.2) | copy-start | bytes 1769476
  14.3 5.9 %collective-permute-start.2 = (bf16[272,384]{1,0:T(8,128)(2,1)S(1)}, bf16[272,384]{1,0:T(8,128)(2,1)S(1)}, u32[]{:S(2)}, u32[]{:S(2)}) collective-permute-start(bf16[272,384]{1,0:T(8,128)(2,1)S(1)} %merge_pass.1.refs_6_), channel_id=1, source_target_pairs={{0,4},{1,3},{2,6},{3,1},{4,0},{5,7},{6,2},{7,5},{8,12},{9,11},{10,... | collective-permute-start | bytes 626696 | tf_op jit(solution)/shard_map/ppermute | solution.py:522
  20.8 5.9 %collective-permute-start.4 = (bf16[144,384]{1,0:T(8,128)(2,1)S(1)}, bf16[144,384]{1,0:T(8,128)(2,1)S(1)}, u32[]{:S(2)}, u32[]{:S(2)}) collective-permute-start(bf16[144,384]{1,0:T(8,128)(2,1)S(1)} %merge_sides.2.refs_4_.refs_5_.mine), channel_id=1, source_target_pairs={{0,8},{1,17},{2,10},{3,19},{4,12},{5,21},{6,14},{7,23},{8,0},{9,25... | collective-permute-start | bytes 331784 | tf_op jit(solution)/shard_map/ppermute | solution.py:522
  23.1 12.9 %copy-start.8 = (f32[768]{0:T(1024)S(1)}, f32[768]{0:T(1024)}, u32[]{:S(2)}) copy-start(f32[768]{0:T(1024)} %param.25) | copy-start | bytes 9220
  23.1 6.0 %collective-permute-start.3 = (bf16[144,384]{1,0:T(8,128)(2,1)S(1)}, bf16[144,384]{1,0:T(8,128)(2,1)S(1)}, u32[]{:S(2)}, u32[]{:S(2)}) collective-permute-start(bf16[144,384]{1,0:T(8,128)(2,1)S(1)} %merge_sides.3.refs_6_.refs_0_), channel_id=1, source_target_pairs={{0,8},{1,17},{2,10},{3,19},{4,12},{5,21},{6,14},{7,23},{8,0},{9,25... | collective-permute-start | bytes 331784 | tf_op jit(solution)/shard_map/ppermute | solution.py:522
  27.3 6.1 %collective-permute-start.6 = (bf16[144,384]{1,0:T(8,128)(2,1)S(1)}, bf16[144,384]{1,0:T(8,128)(2,1)S(1)}, u32[]{:S(2)}, u32[]{:S(2)}) collective-permute-start(bf16[144,384]{1,0:T(8,128)(2,1)S(1)} %merge_even.4.refs_2_.refs_0_), channel_id=1, source_target_pairs={{0,16},{1,9},{2,18},{3,11},{4,20},{5,13},{6,22},{7,15},{8,24},{9,1... | collective-permute-start | bytes 331784 | tf_op jit(solution)/shard_map/ppermute | solution.py:522
  29.7 5.8 %collective-permute-start.5 = (bf16[144,384]{1,0:T(8,128)(2,1)S(1)}, bf16[144,384]{1,0:T(8,128)(2,1)S(1)}, u32[]{:S(2)}, u32[]{:S(2)}) collective-permute-start(bf16[144,384]{1,0:T(8,128)(2,1)S(1)} %merge_even.5.refs_0_), channel_id=1, source_target_pairs={{0,16},{1,9},{2,18},{3,11},{4,20},{5,13},{6,22},{7,15},{8,24},{9,1... | collective-permute-start | bytes 331784 | tf_op jit(solution)/shard_map/ppermute | solution.py:522
  33.8 2.3 %collective-permute-start.9 = (bf16[128,384]{1,0:T(8,128)(2,1)S(1)}, bf16[128,384]{1,0:T(8,128)(2,1)S(1)}, u32[]{:S(2)}, u32[]{:S(2)}) collective-permute-start(bf16[128,384]{1,0:T(8,128)(2,1)S(1)} %merge_even.6.refs_2_.refs_0_), channel_id=1, source_target_pairs={{0,1},{1,0},{2,3},{3,2},{4,5},{5,4},{6,7},{7,6},{8,9},{9,8},{10,11... | collective-permute-start | bytes 294920 | tf_op jit(solution)/shard_map/ppermute | solution.py:515
  36.0 1.4 %collective-permute-start.7 = (bf16[128,384]{1,0:T(8,128)(2,1)S(1)}, bf16[128,384]{1,0:T(8,128)(2,1)S(1)}, u32[]{:S(2)}, u32[]{:S(2)}) collective-permute-start(bf16[128,384]{1,0:T(8,128)(2,1)S(1)} %merge_even.7.refs_6_.attended), channel_id=1, source_target_pairs={{0,1},{1,0},{2,3},{3,2},{4,5},{5,4},{6,7},{7,6},{8,9},{9,8},{10,11... | collective-permute-start | bytes 294920 | tf_op jit(solution)/shard_map/ppermute | solution.py:515
  36.8 10.3 %copy-start.7 = (bf16[384,768]{1,0:T(8,128)(2,1)S(1)}, bf16[384,768]{1,0:T(8,128)(2,1)}, u32[]{:S(2)}) copy-start(bf16[384,768]{1,0:T(8,128)(2,1)} %weight.3) | copy-start | bytes 1769476
  37.8 7.5 %collective-permute-start.10 = (bf16[128,768]{1,0:T(8,128)(2,1)S(1)}, bf16[128,768]{1,0:T(8,128)(2,1)S(1)}, u32[]{:S(2)}, u32[]{:S(2)}) collective-permute-start(bf16[128,768]{1,0:T(8,128)(2,1)S(1)} %get-tuple-element.51), channel_id=1, source_target_pairs={{0,2},{1,5},{2,0},{3,7},{4,6},{5,1},{6,4},{7,3},{8,10},{9,13},{10,... | collective-permute-start | bytes 589832 | tf_op jit(solution)/shard_map/ppermute | solution.py:522
  39.1 6.2 %collective-permute-start.13 = (bf16[128,768]{1,0:T(8,128)(2,1)S(1)}, bf16[128,768]{1,0:T(8,128)(2,1)S(1)}, u32[]{:S(2)}, u32[]{:S(2)}) collective-permute-start(bf16[128,768]{1,0:T(8,128)(2,1)S(1)} %get-tuple-element.51), channel_id=1, source_target_pairs={{0,4},{1,3},{2,6},{3,1},{4,0},{5,7},{6,2},{7,5},{8,12},{9,11},{10,... | collective-permute-start | bytes 589832 | tf_op jit(solution)/shard_map/ppermute | solution.py:522
  45.3 1.8 %collective-permute-start.12 = (bf16[128,768]{1,0:T(8,128)(2,1)S(1)}, bf16[128,768]{1,0:T(8,128)(2,1)S(1)}, u32[]{:S(2)}, u32[]{:S(2)}) collective-permute-start(bf16[128,768]{1,0:T(8,128)(2,1)S(1)} %collective-permute-done.10.mine_a), channel_id=1, source_target_pairs={{0,1},{1,0},{2,3},{3,2},{4,5},{5,4},{6,7},{7,6},{8,9},{9,8},{10,11... | collective-permute-start | bytes 589832 | tf_op jit(solution)/shard_map/ppermute | solution.py:515
  45.3 1.8 %collective-permute-start.14 = (bf16[128,768]{1,0:T(8,128)(2,1)S(1)}, bf16[128,768]{1,0:T(8,128)(2,1)S(1)}, u32[]{:S(2)}, u32[]{:S(2)}) collective-permute-start(bf16[128,768]{1,0:T(8,128)(2,1)S(1)} %collective-permute-done.13.mine_b), channel_id=1, source_target_pairs={{0,1},{1,0},{2,3},{3,2},{4,5},{5,4},{6,7},{7,6},{8,9},{9,8},{10,11... | collective-permute-start | bytes 589832 | tf_op jit(solution)/shard_map/ppermute | solution.py:515
  45.8 5.7 %collective-permute-start.11 = (bf16[128,768]{1,0:T(8,128)(2,1)S(1)}, bf16[128,768]{1,0:T(8,128)(2,1)S(1)}, u32[]{:S(2)}, u32[]{:S(2)}) collective-permute-start(bf16[128,768]{1,0:T(8,128)(2,1)S(1)} %collective-permute-done.10.mine_a), channel_id=1, source_target_pairs={{0,4},{1,3},{2,6},{3,1},{4,0},{5,7},{6,2},{7,5},{8,12},{9,11},{10,... | collective-permute-start | bytes 589832 | tf_op jit(solution)/shard_map/ppermute | solution.py:522
  47.1 9.6 %collective-permute-start.17 = (bf16[384,768]{1,0:T(8,128)(2,1)S(1)}, bf16[384,768]{1,0:T(8,128)(2,1)S(1)}, u32[]{:S(2)}, u32[]{:S(2)}) collective-permute-start(bf16[384,768]{1,0:T(8,128)(2,1)S(1)} %copy-done.7), channel_id=1, source_target_pairs={{0,1},{1,0},{2,3},{3,2},{4,5},{5,4},{6,7},{7,6},{8,9},{9,8},{10,11... | collective-permute-start | bytes 1769480 | tf_op jit(solution)/shard_map/ppermute | solution.py:515
  51.5 1.5 %collective-permute-start.15 = (bf16[128,768]{1,0:T(8,128)(2,1)S(1)}, bf16[128,768]{1,0:T(8,128)(2,1)S(1)}, u32[]{:S(2)}, u32[]{:S(2)}) collective-permute-start(bf16[128,768]{1,0:T(8,128)(2,1)S(1)} %collective-permute-done.11.mine), channel_id=1, source_target_pairs={{0,1},{1,0},{2,3},{3,2},{4,5},{5,4},{6,7},{7,6},{8,9},{9,8},{10,11... | collective-permute-start | bytes 589832 | tf_op jit(solution)/shard_map/ppermute | solution.py:515
  55.0 1.7 %collective-permute-start.16 = (bf16[256,384]{1,0:T(8,128)(2,1)S(1)}, bf16[256,384]{1,0:T(8,128)(2,1)S(1)}, u32[]{:S(2)}, u32[]{:S(2)}) collective-permute-start(bf16[256,384]{1,0:T(8,128)(2,1)S(1)} %get-tuple-element.75), channel_id=1, source_target_pairs={{0,1},{1,0},{2,3},{3,2},{4,5},{5,4},{6,7},{7,6},{8,9},{9,8},{10,11... | collective-permute-start | bytes 589832 | tf_op jit(solution)/shard_map/ppermute | solution.py:515

commit v4 on v3

--- a/solution.py
+++ b/solution.py
@@ -30,59 +30,63 @@
 
 
 def log_rows(width):
-    return -(-2 * (width // HEAD_DIM) // 16) * 16
-
-
-def spread_of(shape, first, heads):
-    row = lax.broadcasted_iota(jnp.int32, shape, 0) - first
-    lane = lax.broadcasted_iota(jnp.int32, shape, 1)
-    return row, lane, (row >= 0) & (row < heads)
-
-
-def pack_logs(logs):
-    rows, width = logs.shape
-    heads, half = width // HEAD_DIM, rows // 2
-
-    def found(part, first):
-        row, lane, inside = spread_of((log_rows(width), width), first, heads)
-        pick = inside & (lane == row * HEAD_DIM)
-        return nt(jnp.where(pick, 1.0, 0.0).astype(BF16), part)
-
-    high = logs.astype(BF16)
-    rest = logs - high.astype(F32)
-    middle = rest.astype(BF16)
-    low = (rest - middle.astype(F32)).astype(BF16)
+    return 16
+
+
+def head_of(row):
+    return 2 * jnp.bitwise_and(row, 3) + jnp.bitwise_and(lax.shift_right_logical(row, 2), 1)
+
+
+def compact_logs(totals, tops):
+    lane = lax.broadcasted_iota(jnp.int32, tops[0].shape, 1)
+
+    def chosen(parts):
+        out = parts[-1]
+        for pair in range(len(parts) - 1):
+            out = jnp.where(jnp.bitwise_and(lane, 3) == pair, parts[pair], out)
+        return out
+
+    turned = (chosen(tops) + jnp.log2(chosen(totals))).T
+    row = lax.broadcasted_iota(jnp.int32, (8, turned.shape[1]), 0)
+    return jnp.where(row < 4, turned[:8], turned[HEAD_DIM:HEAD_DIM + 8])
+
+
+def pack_logs(logs, width):
+    rows = logs.shape[1]
+    high = logs.astype(BF16).astype(F32)
+    middle = (logs - high).astype(BF16).astype(F32)
+    low = (logs - high - middle).astype(BF16).astype(F32)
     if 3 * rows <= width:
-        return jnp.concatenate([found(part, 0) for part in (high, middle, low)], axis=1).astype(BF16)
-    below = found(high, 0) + found(middle, heads)
-    beside = found(low[:half], 0) + found(low[half:], heads)
+        terms = jnp.concatenate([high, middle, low], axis=1)
+        return jnp.concatenate([terms, jnp.zeros_like(terms)], axis=0).astype(BF16)
+    half = rows // 2
+    below = jnp.concatenate([high, middle], axis=0)
+    beside = jnp.concatenate([low[:, :half], low[:, half:]], axis=0)
     return jnp.concatenate([below, beside], axis=1).astype(BF16)
 
 
-def unpack_logs(packed, rows, width):
-    heads = width // HEAD_DIM
-
-    def spread(first):
-        row, lane, inside = spread_of((packed.shape[0], width), first, heads)
-        return inside & (lax.shift_right_logical(lane, 6) == row)
-
-    def as_matrix(mask):
-        return jnp.where(mask, 1.0, 0.0).astype(BF16)
-
-    top, end = spread(0), spread(heads)
-    if 3 * rows <= width:
-        terms = [packed[:, term * rows:(term + 1) * rows] for term in range(3)]
-        return sum(tn(term, as_matrix(top)) for term in terms)
-    beside = packed[:, rows:]
-    low = jnp.concatenate([tn(beside, as_matrix(top)), tn(beside, as_matrix(end))], axis=0)
-    return tn(packed[:, :rows], as_matrix(top | end)) + low
+def unpack_logs(packed, rows):
+    packed = packed.astype(F32)
+    if 3 * rows <= packed.shape[1]:
+        return packed[:8, :rows] + packed[:8, rows:2 * rows] + packed[:8, 2 * rows:3 * rows]
+    low = jnp.concatenate([packed[:8, rows:], packed[8:, rows:]], axis=1)
+    return packed[:8, :rows] + packed[8:, :rows] + low
 
 
 def merge(values_a, logs_a, values_b, logs_b):
+    width = values_a.shape[1]
     top = jnp.maximum(logs_a, logs_b)
     part_a, part_b = jnp.exp2(logs_a - top), jnp.exp2(logs_b - top)
     whole = part_a + part_b
-    return (part_a * values_a + part_b * values_b) / whole, top + jnp.log2(whole)
+    share = part_a / whole
+    high = share.astype(BF16).astype(F32)
+    terms = jnp.concatenate([high, share - high], axis=0).astype(BF16)
+    row = lax.broadcasted_iota(jnp.int32, (16, width), 0)
+    lane = lax.broadcasted_iota(jnp.int32, (16, width), 1)
+    inside = jnp.bitwise_and(row, 3) < width // PAIR
+    spread = inside & (lax.shift_right_logical(lane, 6) == head_of(row))
+    share = tn(terms, jnp.where(spread, 1.0, 0.0).astype(BF16))
+    return share * values_a + (1.0 - share) * values_b, top + jnp.log2(whole)
 
 
 def scale_row(softness_ref, which, heads):
@@ -144,12 +148,16 @@
     slot = lax.broadcasted_iota(jnp.int32, (slots, PAIR), 0)
     counted = jnp.where(slot < count, 1.0, 0.0).astype(BF16)
     high, low = split_scaled(nn(part, query_weight[...]), scale)
+    totals, tops = [], []
     for pair in range(width // PAIR):
         lanes = slice(pair * PAIR, (pair + 1) * PAIR)
         key_block = pair_keys(keys[:, lanes])
         value_block = pair_values(values[:, lanes], counted)
         sums, total, top = attend_pair(high[:, lanes], low[:, lanes], key_block, value_block)
-        put(lanes, sums / total, top + jnp.log2(total))
+        put(lanes, sums / total)
+        totals.append(total)
+        tops.append(top)
+    return compact_logs(totals, tops)
 
 
 def bits_of():
@@ -180,7 +188,7 @@
 def encode_first_kernel(
     tally, softness_far, latents_far, tokens_far, wq_far, wk_far, wv_far,
     message, keys, values, scales, count_out,
-    count, softness, latents, tokens, wq, wk, wv, logs, arrived,
+    count, softness, latents, tokens, wq, wk, wv, arrived,
 ):
     quad, core = bits_of()
     rows = latents.shape[0]
@@ -195,72 +203,71 @@
     is_valid = lax.broadcasted_iota(jnp.int32, keys.shape, 0) < count[0]
     made = nn(tokens[...], wk[...])
     keys[...] = jnp.where(is_valid, made, made[0:1, :]).astype(BF16)
-    moves[3].wait()
+    wait_all(moves[3:])
     values[...] = jnp.where(is_valid, nn(tokens[...], wv[...]), 0.0).astype(BF16)
-    wait_all(moves[4:])
     count_out[...] = jnp.full(count_out.shape, count[0], jnp.int32)
     for which in range(2):
         row = scale_row(softness, which, wq.shape[1] // HEAD_DIM)
         scales[which] = jnp.broadcast_to(row, scales.shape[1:])
-    encode_into(message, latents[...], wq, keys, values, count_out, scales, logs)
-
-
-def encode_into(message, part, wq, keys, values, count, scales, logs):
+    encode_into(message, latents[...], wq, keys, values, count_out, scales)
+
+
+def encode_into(message, part, wq, keys, values, count, scales):
     rows = part.shape[0]
 
-    def put(lanes, sums, log):
+    def put(lanes, sums):
         message[:rows, lanes] = sums.astype(BF16)
-        logs[:, lanes] = log
-
-    encode_rows(part, wq, keys, values, count[0:1, :], scales[0, 0:1, :], put)
-    message[rows:, :] = pack_logs(logs[...])
-
-
-def encode_side_kernel(count, scales, latents, wq, keys, values, message, logs):
+
+    logs = encode_rows(part, wq, keys, values, count[0:1, :], scales[0, 0:1, :], put)
+    message[rows:, :] = pack_logs(logs, message.shape[1])
+
+
+def encode_side_kernel(count, scales, latents, wq, keys, values, message):
     quad, core = bits_of()
-    rows = logs.shape[0]
+    rows = latents.shape[0] // 4
     side = quad ^ jnp.where(core == 0, 1, 2)
     part = quarter(latents, side, rows)[...]
-    encode_into(message, part, wq, keys, values, count, scales, logs)
+    encode_into(message, part, wq, keys, values, count, scales)
 
 
 def encode_keep_kernel(is_own, count, scales, latents, wq, keys, values, kept, logs):
     quad, core = bits_of()
     rows = kept.shape[0]
 
-    def put(lanes, part, log):
+    def put(lanes, part):
         kept[:, lanes] = part
-        logs[:, lanes] = log
 
     at = quad if is_own else quad ^ jnp.where(core == 0, 2, 1)
     part = quarter(latents, at, rows)[...]
-    encode_rows(part, wq, keys, values, count[0:1, :], scales[0, 0:1, :], put)
+    logs[...] = encode_rows(part, wq, keys, values, count[0:1, :], scales[0, 0:1, :], put)
 
 def write_message(message, values, logs):
     rows = values.shape[0]
     message[:rows, :] = values.astype(BF16)
-    message[rows:, :] = pack_logs(logs)
+    message[rows:, :] = pack_logs(logs, message.shape[1])
 
 
 def read_message(message, rows):
-    width = message.shape[1]
-    return message[:rows, :].astype(F32), unpack_logs(message[rows:, :], rows, width)
-
-
-def merge_one_kernel(values, logs, came, message):
+    return message[:rows, :].astype(F32), unpack_logs(message[rows:, :], rows)
+
+
+def merge_pass_kernel(values, logs, came, *messages):
     rows = values.shape[0]
+    half = rows // 2
     part, log = merge(values[...], logs[...], *read_message(came, rows))
-    write_message(message, part, log)
+    for which, message in enumerate(messages):
+        at = slice(which * half, (which + 1) * half)
+        write_message(message, part[at], log[:, at])
 
 
 def merge_sides_kernel(which, values, logs, first, second, message):
     rows = values.shape[0]
     half = rows // 2
     at = slice(which * half, (which + 1) * half)
-    part, log = values[at, :], logs[at, :]
-    for came in (first, second):
-        came_part, came_log = read_message(came, rows)
-        part, log = merge(part, log, came_part[at], came_log[at])
+    part, log = values[at, :], logs[:, at]
+    came_part, came_log = read_message(first, rows)
+    part, log = merge(part, log, came_part[at], came_log[:, at])
+    part, log = merge(part, log, *read_message(second, half))
     write_message(message, part, log)
 
 
@@ -329,6 +336,10 @@
         size = len(group) * PAIR
         both[:, :size] = wk[:, lanes]
         both[:, size:] = wv[:, lanes]
+
+
+def apart(work):
+    pl.when(lax.axis_index("qgrp") >= 0)(work)
 
 
 def place_rows(pieces, spots, latent_out, staged, sent):
@@ -386,50 +397,52 @@
     quad, core = bits_of()
     rows = own.shape[0]
     moves = place_rows([own], [quad * rows], latent_out, staged, sent)
-    for group, weight, state in zip(
-        groups_of(queries.shape[0]), [weights, more_weights], [states[:3], states[3:]]
-    ):
-        both = nn(own[...], weight[...]).astype(BF16)
-        decode_tokens(group, queries, both, None, state)
+
+    @apart
+    def _():
+        for group, weight, state in zip(
+            groups_of(queries.shape[0]), [weights, more_weights], [states[:3], states[3:]]
+        ):
+            both = nn(own[...], weight[...]).astype(BF16)
+            decode_tokens(group, queries, both, None, state)
+
     wait_all(moves)
 
 
-def decode_sides_kernel(queries, weights, mine_a, came_a, mine_b, came_b, latent_in, *refs):
-    state, (latent_out, gathered, *new_state, staged, sent) = refs[:3], refs[3:]
+def decode_sides_kernel(came, queries, weights, more_weights, near, far, latent_in, *refs):
+    states, (latent_out, *refs) = refs[:6], refs[6:]
+    new_states, (gathered, staged, sent) = refs[:6], refs[6:]
     quad, core = bits_of()
-    half = mine_a.shape[0]
-    rows = 2 * half
-    near, far = (quad ^ (1 + core)) * rows, (quad ^ (2 - core)) * rows
-    this, that = core * half, (1 - core) * half
-    pieces = [mine_a, came_a, mine_b, came_b]
-    moves = place_rows(
-        pieces, [near + this, far + that, far + this, near + that], latent_out, staged, sent
-    )
-    for index, piece in enumerate(pieces):
-        gathered[index * half:(index + 1) * half, :] = piece[...]
-    both = nn(gathered[...], weights[...]).astype(BF16)
-    decode_tokens(groups_of(queries.shape[0])[0], queries, both, state, new_state)
+    half = near.shape[0]
+    across = [quad ^ (1 + core), quad ^ (2 - core)]
+    which = 1 - core if came else core
+    pieces = [near, far]
+    spots = [(at * 2 + which) * half for at in (across[::-1] if came else across)]
+    moves = place_rows(pieces, spots, latent_out, staged, sent)
+
+    @apart
+    def _():
+        for index, piece in enumerate(pieces):
+            gathered[index * half:(index + 1) * half, :] = piece[...]
+        for group, weight, state, new_state in zip(
+            groups_of(queries.shape[0]), [weights, more_weights],
+            [states[:3], states[3:]], [new_states[:3], new_states[3:]],
+        ):
+            both = nn(gathered[...], weight[...]).astype(BF16)
+            decode_tokens(group, queries, both, state, new_state)
+
     wait_all(moves)
 
 
-def decode_rest_kernel(queries, weights, gathered, *refs):
-    both = nn(gathered[...], weights[...]).astype(BF16)
-    decode_tokens(groups_of(queries.shape[0])[1], queries, both, refs[:3], refs[3:])
-
-
-def decode_send_kernel(queries, weights, more_weights, mine, came, latent_in, *refs):
-    states, (latent_out, send, *boths, gathered, staged, sent) = refs[:6], refs[6:]
-    quad, core = bits_of()
-    rows, half = latent_out.shape[0] // 4, mine.shape[0]
-    diagonal = (quad ^ 3) * rows
-    spots = [diagonal + core * half, diagonal + (1 - core) * half]
-    moves = place_rows([mine, came], spots, latent_out, staged, sent)
+def decode_send_kernel(queries, weights, more_weights, mine, came, *refs):
+    states, (send, *boths, gathered) = refs[:6], refs[6:]
+    core = lax.axis_index("qgrp")
+    half = mine.shape[0]
     gathered[:half, :] = mine[...]
     gathered[half:, :] = came[...]
     for both, weight in zip(boths, [weights, more_weights]):
         both[...] = nn(gathered[...], weight[...]).astype(BF16)
     decode_last(1 - core, queries, boths, states, send)
-    wait_all(moves)
 
 
 def decode_last(which, queries, boths, states, out):
@@ -445,25 +458,35 @@
         decode_group(group, queries, both, at, state, put)
 
 
-def decode_keep_kernel(queries, both, more_both, tokens, weight, *refs):
-    *states, base, attended = refs
-    core = lax.axis_index("qgrp")
-    decode_last(core, queries, [both, more_both], states, attended)
-    rows = base.shape[0]
-    own = tokens[pl.ds(pl.multiple_of(core * rows, rows), rows), :].astype(F32)
-    base[...] = own + nn(attended[...], weight[...])
+def decode_keep_kernel(queries, both, more_both, tokens, weight, mine, came, latent_in, *refs):
+    *states, latent_out, base, attended, staged, sent = refs
+    quad, core = bits_of()
+    half = mine.shape[0]
+    corner = (quad ^ 3) * 2 * half
+    spots = [corner + core * half, corner + (1 - core) * half]
+    moves = place_rows([mine, came], spots, latent_out, staged, sent)
+
+    @apart
+    def _():
+        decode_last(core, queries, [both, more_both], states, attended)
+        rows = base.shape[0]
+        own = tokens[pl.ds(pl.multiple_of(core * rows, rows), rows), :].astype(F32)
+        base[...] = own + nn(attended[...], weight[...])
+
+    wait_all(moves)
 
 
 def tokens_kernel(count, base, other, weight, out, staged, sent):
     start = lax.axis_index("qgrp") * base.shape[0]
-    rows = base.shape[0] // 2
+    pieces = sent.shape[0]
+    columns = base.shape[1] // pieces
     moves = []
-    for index in range(2):
-        at = pl.ds(index * rows, rows)
-        value = base[at, :] + nn(other[at, :], weight[...])
-        slot = start + index * rows + lax.broadcasted_iota(jnp.int32, value.shape, 0)
-        staged[at, :] = jnp.where(slot < count[0:1, 0:1], value, 0.0)
-        moves.append(pltpu.make_async_copy(staged.at[at, :], out.at[at, :], sent.at[index]))
+    for index in range(pieces):
+        at = pl.ds(index * columns, columns)
+        value = base[:, at] + nn(other[...], weight[:, at])
+        slot = start + lax.broadcasted_iota(jnp.int32, value.shape, 0)
+        staged[:, at] = jnp.where(slot < count[0:1, 0:1], value, 0.0)
+        moves.append(pltpu.make_async_copy(staged.at[:, at], out.at[:, at], sent.at[index]))
         moves[-1].start()
     wait_all(moves)
 
@@ -533,39 +556,39 @@
         scratch=[
             pltpu.SMEM(tally.shape, tally.dtype), pltpu.SMEM(softness.shape, F32),
             pltpu.VMEM((rows, model), BF16), pltpu.VMEM(tokens.shape, BF16),
-            *[pltpu.VMEM((model, width), BF16)] * 3, pltpu.VMEM((rows, width), F32),
-            pltpu.SemaphoreType.DMA((7,)),
+            *[pltpu.VMEM((model, width), BF16)] * 3, pltpu.SemaphoreType.DMA((7,)),
         ],
         flops=attention, name="encode_corner",
     )
     came = trade(message, 1, 2)
-    state = [((rows, width), F32)] * 2
+    state = [((rows, width), F32), ((8, rows), F32)]
+    (message,) = call(
+        encode_side_kernel, "vvvvvv", [sent], count, scales, latents, wq, keys, values,
+        flops=attention, name="encode_side",
+    )
+    first = trade(message, 1, 2)
     passed = call(
         functools.partial(encode_keep_kernel, False), "vvvvvv", state,
-        count, scales, latents, wq, keys, values, flops=attention, name="encode_pass",
-    )
-    (message,) = call(
-        encode_side_kernel, "vvvvvv", [sent], count, scales, latents, wq, keys, values,
-        scratch=[pltpu.VMEM((rows, width), F32)], flops=attention, after=passed[1:],
-        name="encode_side",
-    )
-    first = trade(message, 1, 2)
-    (message,) = call(
-        merge_one_kernel, "vvv", [sent], *passed, came, after=[message], name="merge_pass"
-    )
-    second = trade(message, 2, 1)
+        count, scales, latents, wq, keys, values, flops=attention, after=[message],
+        name="encode_pass",
+    )
+    half = rows // 2
+    half_sent = ((half + log_rows(width), width), BF16)
+    messages = call(
+        merge_pass_kernel, "vvv", [half_sent] * 2, *passed, came, name="merge_pass"
+    )
+    seconds = [trade(message, 2, 1) for message in messages]
     kept, kept_logs = call(
         functools.partial(encode_keep_kernel, True), "vvvvvv", state,
         count, scales, latents, wq, keys, values,
-        flops=attention, after=[message], name="encode_own",
+        flops=attention, after=messages, name="encode_own",
     )
     other_wo, other_do = swap(wo), swap(do)
-    half = rows // 2
     parts = []
     for which in range(2):
         parts += call(
             functools.partial(merge_sides_kernel, which), "vvvv",
-            [((half + log_rows(width), width), BF16)], kept, kept_logs, first, second,
+            [half_sent], kept, kept_logs, first, seconds[which],
             after=parts, name="merge_sides",
         )
     sizes = [len(group) * PAIR for group in groups_of(width // PAIR)]
@@ -610,41 +633,40 @@
 
     latent_out, *states = call(
         decode_own_kernel, "vvvv", [whole, *states_out], queries, *weights, own,
-        far=(0,), scratch=scratch(rows, 1), flops=attention, name="decode_own",
+        after=[other_do], far=(0,), scratch=scratch(rows, 1), flops=attention, name="decode_own",
     )
     first, states[0] = lax.optimization_barrier((first, states[0]))
     third = trade(first, 2, 1)
-    latent_out, gathered, *side = call(
-        decode_sides_kernel, "vvvvvvhvvv", [whole, ((2 * rows, model), BF16), *states_out[:3]],
-        queries, weights[0], first, swap(first), second, swap(second), latent_out, *states[:3],
-        far=(0,), alias={6: 0}, scratch=scratch(2 * rows, 4), vmem=28, flops=attention,
-        name="decode_sides",
-    )
-    third, side[0] = lax.optimization_barrier((third, side[0]))
+
+    def decode_sides(came, near, far, latent_out, states):
+        latent_out, *states = call(
+            functools.partial(decode_sides_kernel, came), "vvvvvhvvvvvv", [whole, *states_out],
+            queries, *weights, near, far, latent_out, *states, far=(0,), alias={5: 0},
+            scratch=[pltpu.VMEM((rows, model), BF16), *scratch(rows, 2)], flops=attention,
+            name="decode_sides",
+        )
+        return latent_out, states
+
+    came_first, came_second = swap(first), swap(second)
+    latent_out, states = decode_sides(False, first, second, latent_out, states)
+    third, states[0] = lax.optimization_barrier((third, states[0]))
     came = swap(third)
-    rest = call(
-        decode_rest_kernel, "vvvvvv", states_out[3:], queries, weights[1], gathered, *states[3:],
-        flops=attention, after=side[1:2], name="decode_rest",
-    )
-    states = [*side, *rest]
-    latent_out, send, *boths = call(
-        decode_send_kernel, "vvvvvhvvvvvv",
-        [
-            whole, ((half_slots, width), BF16),
-            *[((rows, 2 * size), BF16) for size in sizes],
-        ],
-        queries, *weights, third, came, latent_out, *states, far=(0,), alias={5: 0},
-        scratch=[pltpu.VMEM((rows, model), BF16), *scratch(rows, 2)],
+    latent_out, states = decode_sides(True, came_first, came_second, latent_out, states)
+    send, *boths = call(
+        decode_send_kernel, "vvvvvvvvvvv",
+        [((half_slots, width), BF16), *[((rows, 2 * size), BF16) for size in sizes]],
+        queries, *weights, third, came, *states, scratch=[pltpu.VMEM((rows, model), BF16)],
         flops=attention // 2, name="decode_send",
     )
-    (base,) = call(
-        decode_keep_kernel, "vvvvvvvvvvv", [((half_slots, model), F32)],
-        queries, *boths, tokens, do, *states, scratch=[pltpu.VMEM((half_slots, width), BF16)],
+    latent_out, base = call(
+        decode_keep_kernel, "vvvvvvvhvvvvvv", [whole, ((half_slots, model), F32)],
+        queries, *boths, tokens, do, third, came, latent_out, *states, far=(0,), alias={7: 0},
+        scratch=[pltpu.VMEM((half_slots, width), BF16), *scratch(rows, 2)],
         flops=attention // 2, name="decode_keep",
     )
     (tokens_out,) = call(
         tokens_kernel, "vvvv", [((half_slots, model), F32)], count, base, swap(send), other_do,
-        far=(0,), scratch=scratch(half_slots, 2), name="tokens",
+        far=(0,), scratch=scratch(half_slots, 3 if model % 384 == 0 else 1), name="tokens",
     )
     return latent_out, tokens_out
 

time: 58.3 us -> 55.5 us (0.952)
  Pallas kernels: 27.2 us -> 22 us
  starting transfers between devices: 17.2 us -> 18.8 us
  waiting for transfers between devices: 11.8 us -> 12.6 us
    pallas_call x20, Pallas kernels: 27.2 us -> 22 us  [call(): pl.pallas_call(kernel, out_shape=shapes, in_specs=[SPACES[kind] for kind...]
    ppermute x10 -> x11, starting transfers between devices: 16 us -> 16.9 us  [trade(): return lax.ppermute(array, ('cell', 'qgrp'), pairs)]
    ppermute x8, starting transfers between devices: 1.23 us -> 1.9 us  [swap(): return lax.ppermute(array, 'qgrp', [(0, 1), (1, 0)])]
    ppermute x10 -> x11, waiting for transfers between devices: 11.2 us -> 11.8 us  [trade(): return lax.ppermute(array, ('cell', 'qgrp'), pairs)]
  transfers between devices with their start and end apart: 18 -> 19, of which waited for: 8 -> 7; matrix products, arithmetic and copies ran while one was open for 0% -> 0% of each run, Pallas kernels for 36% -> 28%
where the time goes in v4:
time: 55.5 us; the launch traced here: 55.4 us
  Pallas kernels  22 us (40%)
  starting transfers between devices  18.8 us (34%)
  waiting for transfers between devices  12.6 us (23%)
  between operations  1.9 us (3%)
    pallas_call x20, Pallas kernels, call(): pl.pallas_call(kernel, out_shape=shapes, in_specs=[SPACES[kind] for kind...  22 us
    ppermute x11, starting transfers between devices, trade(): return lax.ppermute(array, ('cell', 'qgrp'), pairs)  16.9 us
    ppermute x11, waiting for transfers between devices, trade(): return lax.ppermute(array, ('cell', 'qgrp'), pairs)  11.8 us
    ppermute x8, starting transfers between devices, swap(): return lax.ppermute(array, 'qgrp', [(0, 1), (1, 0)])  1.9 us
  transfers between devices with their start and end apart: 19, of which 7 were waited for; matrix products, arithmetic and copies ran while one was open for 0% of the time, Pallas kernels for 28%

profile of v4, /device:TPU:0, one launch (start us, length us, event | category | flops | bytes accessed | tf_op | source)
XLA Modules:
  0.0 55.4 jit_solution(4172318916309332286)
XLA Ops:
  1.5 0.0 copy-start.4
  1.5 4.2 %encode_corner.1 = (bf16[272,384]{1,0:T(8,128)(2,1)S(1)}, bf16[512,384]{1,0:T(8,128)(2,1)S(1)}, bf16[512,384]{1,0:T(8,128)(2,1)S(1)}, f32[2,8,384]{2,1,0:T(8,128)S(1)}, s32[8,128]{1,0:T(8,128)S(1)}) custom-call(s32[1]{0:T(128)S(6)} %copy.21.tally, f32[2,12]{1,0:T(2,128)} %softness_far.1, bf16[1024,768]{1,0:T(8,128)(2,1)} %latents.3, ...), custom_call_target="tpu_custom_call" | custom-call | flops 805306368 | bytes 5152868 | tf_op jit(solution)/shard_map/encode_corner/pallas_call | solution.py:516
  5.7 3.0 %collective-permute-start = (bf16[272,384]{1,0:T(8,128)(2,1)S(1)}, bf16[272,384]{1,0:T(8,128)(2,1)S(1)}, u32[]{:S(2)}, u32[]{:S(2)}) collective-permute-start(bf16[272,384]{1,0:T(8,128)(2,1)S(1)} %get-tuple-element.54), channel_id=1, source_target_pairs={{0,2},{1,5},{2,0},{3,7},{4,6},{5,1},{6,4},{7,3},{8,10},{9,13},{10,... | collective-permute-start | bytes 626696 | tf_op jit(solution)/shard_map/ppermute | solution.py:545
  8.7 0.0 collective-permute-start.9
  8.7 1.5 %encode_side.1.refs_6_ = bf16[272,384]{1,0:T(8,128)(2,1)S(1)} custom-call(s32[8,128]{1,0:T(8,128)S(1)} %get-tuple-element.49.count.refs_0_, f32[2,8,384]{2,1,0:T(8,128)S(1)} %get-tuple-element.48.scales.refs_1_.refs_0_, bf16[1024,768]{1,0:T(8,128)(2,1)S(1)} %copy-done, bf16[768,384]{1,0:T(8,128)(2,1)S(1)} %copy-done.1, ...), custom_call_target="tpu_custom_call" | custom-call | flops 805306368 | bytes 3186688 | tf_op jit(solution)/shard_map/encode_side/pallas_call | solution.py:516
  10.3 1.1 %collective-permute-start.1 = (bf16[272,384]{1,0:T(8,128)(2,1)S(1)}, bf16[272,384]{1,0:T(8,128)(2,1)S(1)}, u32[]{:S(2)}, u32[]{:S(2)}) collective-permute-start(bf16[272,384]{1,0:T(8,128)(2,1)S(1)} %encode_side.1.refs_6_), channel_id=1, source_target_pairs={{0,2},{1,5},{2,0},{3,7},{4,6},{5,1},{6,4},{7,3},{8,10},{9,13},{10,... | collective-permute-start | bytes 626696 | tf_op jit(solution)/shard_map/ppermute | solution.py:545
  11.4 0.7 %collective-permute-start.12 = (bf16[384,768]{1,0:T(8,128)(2,1)S(1)}, bf16[384,768]{1,0:T(8,128)(2,1)S(1)}, u32[]{:S(2)}, u32[]{:S(2)}) collective-permute-start(bf16[384,768]{1,0:T(8,128)(2,1)S(1)} %copy-done.4), channel_id=1, source_target_pairs={{0,1},{1,0},{2,3},{3,2},{4,5},{5,4},{6,7},{7,6},{8,9},{9,8},{10,11... | collective-permute-start | bytes 1769480 | tf_op jit(solution)/shard_map/ppermute | solution.py:538
  12.1 1.5 %encode_pass.1 = (f32[256,384]{1,0:T(8,128)S(1)}, f32[8,256]{1,0:T(8,128)S(1)}) custom-call(s32[8,128]{1,0:T(8,128)S(1)} %get-tuple-element.49.count.refs_0_, f32[2,8,384]{2,1,0:T(8,128)S(1)} %get-tuple-element.48.scales.refs_1_.refs_0_, bf16[1024,768]{1,0:T(8,128)(2,1)S(1)} %copy-done, bf16[768,384]{1,0:T(8,128)(2,1)S(1)} %copy-done.1, ...), custom_call_target="tpu_custom_call" | custom-call | flops 805306368 | bytes 3379200 | tf_op jit(solution)/shard_map/encode_pass/pallas_call | solution.py:516
  13.6 0.0 collective-permute-done.came
  13.6 0.0 copy-start.2
  13.6 0.0 copy-start.5
  13.6 0.0 copy-start.6
  13.6 0.0 copy-start.7
  13.7 0.3 merge_pass.1
  14.0 1.0 %collective-permute-start.2 = (bf16[144,384]{1,0:T(8,128)(2,1)S(1)}, bf16[144,384]{1,0:T(8,128)(2,1)S(1)}, u32[]{:S(2)}, u32[]{:S(2)}) collective-permute-start(bf16[144,384]{1,0:T(8,128)(2,1)S(1)} %get-tuple-element.55.refs_6_), channel_id=1, source_target_pairs={{0,4},{1,3},{2,6},{3,1},{4,0},{5,7},{6,2},{7,5},{8,12},{9,11},{10,... | collective-permute-start | bytes 331784 | tf_op jit(solution)/shard_map/ppermute | solution.py:545
  14.9 1.1 %collective-permute-start.3 = (bf16[144,384]{1,0:T(8,128)(2,1)S(1)}, bf16[144,384]{1,0:T(8,128)(2,1)S(1)}, u32[]{:S(2)}, u32[]{:S(2)}) collective-permute-start(bf16[144,384]{1,0:T(8,128)(2,1)S(1)} %get-tuple-element.56.refs_7_), channel_id=1, source_target_pairs={{0,4},{1,3},{2,6},{3,1},{4,0},{5,7},{6,2},{7,5},{8,12},{9,11},{10,... | collective-permute-start | bytes 331784 | tf_op jit(solution)/shard_map/ppermute | solution.py:545
  16.0 1.5 %encode_own.1 = (f32[256,384]{1,0:T(8,128)S(1)}, f32[8,256]{1,0:T(8,128)S(1)}) custom-call(s32[8,128]{1,0:T(8,128)S(1)} %get-tuple-element.49.count.refs_0_, f32[2,8,384]{2,1,0:T(8,128)S(1)} %get-tuple-element.48.scales.refs_1_.refs_0_, bf16[1024,768]{1,0:T(8,128)(2,1)S(1)} %copy-done, bf16[768,384]{1,0:T(8,128)(2,1)S(1)} %copy-done.1, ...), custom_call_target="tpu_custom_call" | custom-call | flops 805306368 | bytes 3379200 | tf_op jit(solution)/shard_map/encode_own/pallas_call | solution.py:516
  17.6 0.0 collective-permute-done.1.first.refs_2_
  17.6 1.2 %collective-permute-done.2.second = bf16[144,384]{1,0:T(8,128)(2,1)S(1)} collective-permute-done((bf16[144,384]{1,0:T(8,128)(2,1)S(1)}, bf16[144,384]{1,0:T(8,128)(2,1)S(1)}, u32[]{:S(2)}, u32[]{:S(2)}) %collective-permute-start.2) | collective-permute-done | bytes 110624 | tf_op jit(solution)/shard_map/ppermute | solution.py:545
  18.8 0.3 merge_sides.2.refs_4_.refs_5_.mine
  19.0 1.6 %collective-permute-start.5 = (bf16[144,384]{1,0:T(8,128)(2,1)S(1)}, bf16[144,384]{1,0:T(8,128)(2,1)S(1)}, u32[]{:S(2)}, u32[]{:S(2)}) collective-permute-start(bf16[144,384]{1,0:T(8,128)(2,1)S(1)} %merge_sides.2.refs_4_.refs_5_.mine), channel_id=1, source_target_pairs={{0,8},{1,17},{2,10},{3,19},{4,12},{5,21},{6,14},{7,23},{8,0},{9,25... | collective-permute-start | bytes 331784 | tf_op jit(solution)/shard_map/ppermute | solution.py:545
  20.7 0.0 collective-permute-done.3.refs_3_
  20.7 0.3 merge_sides.3.refs_6_.refs_0_
  21.0 0.0 copy-start.8
  21.0 0.9 %collective-permute-start.4 = (bf16[144,384]{1,0:T(8,128)(2,1)S(1)}, bf16[144,384]{1,0:T(8,128)(2,1)S(1)}, u32[]{:S(2)}, u32[]{:S(2)}) collective-permute-start(bf16[144,384]{1,0:T(8,128)(2,1)S(1)} %merge_sides.3.refs_6_.refs_0_), channel_id=1, source_target_pairs={{0,8},{1,17},{2,10},{3,19},{4,12},{5,21},{6,14},{7,23},{8,0},{9,25... | collective-permute-start | bytes 331784 | tf_op jit(solution)/shard_map/ppermute | solution.py:545
  21.9 2.2 %collective-permute-done.5.came = bf16[144,384]{1,0:T(8,128)(2,1)S(1)} collective-permute-done((bf16[144,384]{1,0:T(8,128)(2,1)S(1)}, bf16[144,384]{1,0:T(8,128)(2,1)S(1)}, u32[]{:S(2)}, u32[]{:S(2)}) %collective-permute-start.5) | collective-permute-done | bytes 110624 | tf_op jit(solution)/shard_map/ppermute | solution.py:545
  24.1 0.2 merge_even.4.refs_2_.refs_0_
  24.4 2.9 %collective-permute-start.7 = (bf16[144,384]{1,0:T(8,128)(2,1)S(1)}, bf16[144,384]{1,0:T(8,128)(2,1)S(1)}, u32[]{:S(2)}, u32[]{:S(2)}) collective-permute-start(bf16[144,384]{1,0:T(8,128)(2,1)S(1)} %merge_even.4.refs_2_.refs_0_), channel_id=1, source_target_pairs={{0,16},{1,9},{2,18},{3,11},{4,20},{5,13},{6,22},{7,15},{8,24},{9,1... | collective-permute-start | bytes 331784 | tf_op jit(solution)/shard_map/ppermute | solution.py:545
  27.2 0.0 collective-permute-done.4.refs_1_
  27.2 0.2 merge_even.5.refs_0_
  27.5 1.8 %collective-permute-start.6 = (bf16[144,384]{1,0:T(8,128)(2,1)S(1)}, bf16[144,384]{1,0:T(8,128)(2,1)S(1)}, u32[]{:S(2)}, u32[]{:S(2)}) collective-permute-start(bf16[144,384]{1,0:T(8,128)(2,1)S(1)} %merge_even.5.refs_0_), channel_id=1, source_target_pairs={{0,16},{1,9},{2,18},{3,11},{4,20},{5,13},{6,22},{7,15},{8,24},{9,1... | collective-permute-start | bytes 331784 | tf_op jit(solution)/shard_map/ppermute | solution.py:545
  29.3 0.7 %decode_prepare.1 = (bf16[3,512,256]{2,1,0:T(8,128)(2,1)S(1)}, bf16[768,512]{1,0:T(8,128)(2,1)S(1)}, bf16[768,256]{1,0:T(8,128)(2,1)S(1)}) custom-call(f32[2,8,384]{2,1,0:T(8,128)S(1)} %get-tuple-element.48.scales.refs_1_.refs_0_, bf16[512,768]{1,0:T(8,128)(2,1)S(1)} %copy-done.2, bf16[768,384]{1,0:T(8,128)(2,1)S(1)} %copy-done.5, ...), custom_call_target="tpu_custom_call" | custom-call | bytes 4546560 | tf_op jit(solution)/shard_map/decode_prepare/pallas_call | solution.py:516
  30.0 0.7 %collective-permute-done.7.refs_1_ = bf16[144,384]{1,0:T(8,128)(2,1)S(1)} collective-permute-done((bf16[144,384]{1,0:T(8,128)(2,1)S(1)}, bf16[144,384]{1,0:T(8,128)(2,1)S(1)}, u32[]{:S(2)}, u32[]{:S(2)}) %collective-permute-start.7) | collective-permute-done | bytes 110624 | tf_op jit(solution)/shard_map/ppermute | solution.py:545
  30.7 0.2 merge_even.6.refs_2_.refs_0_
  30.9 0.1 collective-permute-start.10
  31.0 2.7 %collective-permute-done.6.refs_1_ = bf16[144,384]{1,0:T(8,128)(2,1)S(1)} collective-permute-done((bf16[144,384]{1,0:T(8,128)(2,1)S(1)}, bf16[144,384]{1,0:T(8,128)(2,1)S(1)}, u32[]{:S(2)}, u32[]{:S(2)}) %collective-permute-start.6) | collective-permute-done | bytes 110624 | tf_op jit(solution)/shard_map/ppermute | solution.py:545
  33.6 0.2 merge_even.7.refs_6_.attended
  33.9 0.1 collective-permute-start.8
  34.0 0.0 collective-permute-done.9.refs_3_.other_weight
  34.0 0.0 collective-permute-done.10.refs_1_
  34.0 0.5 latent_low.1.refs_0_
  34.5 0.8 %collective-permute-done.8.other = bf16[128,384]{1,0:T(8,128)(2,1)S(1)} collective-permute-done((bf16[128,384]{1,0:T(8,128)(2,1)S(1)}, bf16[128,384]{1,0:T(8,128)(2,1)S(1)}, u32[]{:S(2)}, u32[]{:S(2)}) %collective-permute-start.8) | collective-permute-done | bytes 98336 | tf_op jit(solution)/shard_map/ppermute | solution.py:538
  35.3 0.5 latent.1
  35.8 1.0 %collective-permute-start.11 = (bf16[128,768]{1,0:T(8,128)(2,1)S(1)}, bf16[128,768]{1,0:T(8,128)(2,1)S(1)}, u32[]{:S(2)}, u32[]{:S(2)}) collective-permute-start(bf16[128,768]{1,0:T(8,128)(2,1)S(1)} %get-tuple-element.62), channel_id=1, source_target_pairs={{0,2},{1,5},{2,0},{3,7},{4,6},{5,1},{6,4},{7,3},{8,10},{9,13},{10,... | collective-permute-start | bytes 589832 | tf_op jit(solution)/shard_map/ppermute | solution.py:545
  36.7 1.5 %collective-permute-start.14 = (bf16[128,768]{1,0:T(8,128)(2,1)S(1)}, bf16[128,768]{1,0:T(8,128)(2,1)S(1)}, u32[]{:S(2)}, u32[]{:S(2)}) collective-permute-start(bf16[128,768]{1,0:T(8,128)(2,1)S(1)} %get-tuple-element.62), channel_id=1, source_target_pairs={{0,4},{1,3},{2,6},{3,1},{4,0},{5,7},{6,2},{7,5},{8,12},{9,11},{10,... | collective-permute-start | bytes 589832 | tf_op jit(solution)/shard_map/ppermute | solution.py:545
  38.3 0.0 collective-permute-done.12.refs_4_.weight
  38.3 2.1 %decode_own.1 = (f32[1024,768]{1,0:T(8,128)}, f32[512,256]{1,0:T(8,128)S(1)}, f32[512,256]{1,0:T(8,128)S(1)}, f32[512,256]{1,0:T(8,128)S(1)}, f32[512,128]{1,0:T...) custom-call(bf16[3,512,256]{2,1,0:T(8,128)(2,1)S(1)} %get-tuple-element.59.refs_2_.refs_3_.refs_0_.queries, ...), custom_call_target="tpu_custom_call" | custom-call | flops 805306368 | bytes 7864320 | tf_op jit(solution)/shard_map/decode_own/pallas_call | solution.py:516
  40.4 2.8 %collective-permute-done.11.near = bf16[128,768]{1,0:T(8,128)(2,1)S(1)} collective-permute-done((bf16[128,768]{1,0:T(8,128)(2,1)S(1)}, bf16[128,768]{1,0:T(8,128)(2,1)S(1)}, u32[]{:S(2)}, u32[]{:S(2)}) %collective-permute-start.11) | collective-permute-done | bytes 196640 | tf_op jit(solution)/shard_map/ppermute | solution.py:545
  43.3 0.9 %collective-permute-start.13 = (bf16[128,768]{1,0:T(8,128)(2,1)S(1)}, bf16[128,768]{1,0:T(8,128)(2,1)S(1)}, u32[]{:S(2)}, u32[]{:S(2)}) collective-permute-start(bf16[128,768]{1,0:T(8,128)(2,1)S(1)} %collective-permute-done.11.near), channel_id=1, source_target_pairs={{0,4},{1,3},{2,6},{3,1},{4,0},{5,7},{6,2},{7,5},{8,12},{9,11},{10,... | collective-permute-start | bytes 589832 | tf_op jit(solution)/shard_map/ppermute | solution.py:545
  44.2 0.0 collective-permute-start.16
  44.2 0.0 collective-permute-done.14.far
  44.2 0.5 collective-permute-start.17
  44.7 2.0 %decode_sides.2 = (f32[1024,768]{1,0:T(8,128)}, f32[512,256]{1,0:T(8,128)S(1)}, f32[512,256]{1,0:T(8,128)S(1)}, f32[512,256]{1,0:T(8,128)S(1)}, f32[512,128]{1,0...) custom-call(bf16[3,512,256]{2,1,0:T(8,128)(2,1)S(1)} %get-tuple-element.59.refs_2_., ...), custom_call_target="tpu_custom_call", output_to_operand_aliasing={{0}: (5, {})} | custom-call | flops 805306368 | bytes 13369344 | tf_op jit(solution)/shard_map/decode_sides/pallas_call | solution.py:516
  46.7 2.2 %collective-permute-done.13.mine = bf16[128,768]{1,0:T(8,128)(2,1)S(1)} collective-permute-done((bf16[128,768]{1,0:T(8,128)(2,1)S(1)}, bf16[128,768]{1,0:T(8,128)(2,1)S(1)}, u32[]{:S(2)}, u32[]{:S(2)}) %collective-permute-start.13) | collective-permute-done | bytes 196640 | tf_op jit(solution)/shard_map/ppermute | solution.py:545
  48.9 0.0 collective-permute-start.15
  48.9 0.0 collective-permute-done.17.far
  48.9 0.0 collective-permute-done.16.near
  49.0 2.0 %decode_sides.3 = (f32[1024,768]{1,0:T(8,128)}, f32[512,256]{1,0:T(8,128)S(1)}, f32[512,256]{1,0:T(8,128)S(1)}, f32[512,256]{1,0:T(8,128)S(1)}, f32[512,128]{1,0...) custom-call(bf16[3,512,256]{2,1,0:T(8,128)(2,1)S(1)} %get-tuple-element.59.refs_2_., ...), custom_call_target="tpu_custom_call", output_to_operand_aliasing={{0}: (5, {})} | custom-call | flops 805306368 | bytes 13369344 | tf_op jit(solution)/shard_map/decode_sides/pallas_call | solution.py:516
  51.0 0.0 collective-permute-done.15.came
  51.0 1.2 %decode_send.1 = (bf16[256,384]{1,0:T(8,128)(2,1)S(1)}, bf16[256,512]{1,0:T(8,128)(2,1)S(1)}, bf16[256,256]{1,0:T(8,128)(2,1)S(1)}) custom-call(bf16[3,512,256]{2,1,0:T(8,128)(2,1)S(1)} %get-tuple-element.59.refs_2_.refs_3_.refs_0_.queries, bf16[768,512]{1,0:T(8,128)(2,1)S(1)} %get-tuple-element.60.refs_1_.weights, ...), custom_call_target="tpu_custom_call" | custom-call | flops 402653184 | bytes 5308416 | tf_op jit(solution)/shard_map/decode_send/pallas_call | solution.py:516
  52.2 0.6 %collective-permute-start.18 = (bf16[256,384]{1,0:T(8,128)(2,1)S(1)}, bf16[256,384]{1,0:T(8,128)(2,1)S(1)}, u32[]{:S(2)}, u32[]{:S(2)}) collective-permute-start(bf16[256,384]{1,0:T(8,128)(2,1)S(1)} %get-tuple-element.93), channel_id=1, source_target_pairs={{0,1},{1,0},{2,3},{3,2},{4,5},{5,4},{6,7},{7,6},{8,9},{9,8},{10,11... | collective-permute-start | bytes 589832 | tf_op jit(solution)/shard_map/ppermute | solution.py:538
  52.8 1.2 %decode_keep.1 = (f32[1024,768]{1,0:T(8,128)}, f32[256,768]{1,0:T(8,128)S(1)}) custom-call(bf16[3,512,256]{2,1,0:T(8,128)(2,1)S(1)} %get-tuple-element.59.refs_2_.refs_3_.refs_0_.queries, bf16[256,512]{1,0:T(8,128)(2,1)S(1)} %get-tuple-element.88.both, bf16[256,256]{1,0:T(8,128)(2,1)S(1)} %get-tuple-element.89.more_both, ...), custom_call_target="tpu_custom_call", output_to_operand_aliasing={{0}: (7, {})} | custom-call | flops 402653184 | bytes 12386304 | tf_op jit(solution)/shard_map/decode_keep/pallas_call | solution.py:516
  54.0 0.0 collective-permute-done.18.other
  54.0 1.2 %tokens.3 = f32[256,768]{1,0:T(8,128)} custom-call(s32[8,128]{1,0:T(8,128)S(1)} %get-tuple-element.49.count.refs_0_, f32[256,768]{1,0:T(8,128)S(1)} %get-tuple-element.92.base, bf16[256,384]{1,0:T(8,128)(2,1)S(1)} %collective-permute-done.18.other, bf16[384,768]{1,0:T(8,128)(2,1)S(1)} %collective-permute-done.12.refs_4_.weight), custom_call_target="tpu_custom_call" | custom-call | bytes 2363392 | tf_op jit(solution)/shard_map/tokens/pallas_call | solution.py:516
  (13 shorter events, 0.0 us)
Async XLA Ops:
  0.6 8.1 %copy-start = (bf16[1024,768]{1,0:T(8,128)(2,1)S(1)}, bf16[1024,768]{1,0:T(8,128)(2,1)}, u32[]{:S(2)}) copy-start(bf16[1024,768]{1,0:T(8,128)(2,1)} %latents.3) | copy-start | bytes 4718596
  0.6 8.1 %copy-start.1 = (bf16[768,384]{1,0:T(8,128)(2,1)S(1)}, bf16[768,384]{1,0:T(8,128)(2,1)}, u32[]{:S(2)}) copy-start(bf16[768,384]{1,0:T(8,128)(2,1)} %refs_3_.4) | copy-start | bytes 1769476
  0.7 8.1 %copy-start.3 = (bf16[384,768]{1,0:T(8,128)(2,1)S(1)}, bf16[384,768]{1,0:T(8,128)(2,1)}, u32[]{:S(2)}) copy-start(bf16[384,768]{1,0:T(8,128)(2,1)} %weight.2) | copy-start | bytes 1769476
  1.5 9.9 %copy-start.4 = (bf16[384,768]{1,0:T(8,128)(2,1)S(1)}, bf16[384,768]{1,0:T(8,128)(2,1)}, u32[]{:S(2)}) copy-start(bf16[384,768]{1,0:T(8,128)(2,1)} %weight.3) | copy-start | bytes 1769476
  5.7 7.9 %collective-permute-start = (bf16[272,384]{1,0:T(8,128)(2,1)S(1)}, bf16[272,384]{1,0:T(8,128)(2,1)S(1)}, u32[]{:S(2)}, u32[]{:S(2)}) collective-permute-start(bf16[272,384]{1,0:T(8,128)(2,1)S(1)} %get-tuple-element.54), channel_id=1, source_target_pairs={{0,2},{1,5},{2,0},{3,7},{4,6},{5,1},{6,4},{7,3},{8,10},{9,13},{10,... | collective-permute-start | bytes 626696 | tf_op jit(solution)/shard_map/ppermute | solution.py:545
  8.7 25.3 %collective-permute-start.9 = (bf16[384,768]{1,0:T(8,128)(2,1)S(1)}, bf16[384,768]{1,0:T(8,128)(2,1)S(1)}, u32[]{:S(2)}, u32[]{:S(2)}) collective-permute-start(bf16[384,768]{1,0:T(8,128)(2,1)S(1)} %copy-done.3), channel_id=1, source_target_pairs={{0,1},{1,0},{2,3},{3,2},{4,5},{5,4},{6,7},{7,6},{8,9},{9,8},{10,11... | collective-permute-start | bytes 1769480 | tf_op jit(solution)/shard_map/ppermute | solution.py:538
  10.3 7.3 %collective-permute-start.1 = (bf16[272,384]{1,0:T(8,128)(2,1)S(1)}, bf16[272,384]{1,0:T(8,128)(2,1)S(1)}, u32[]{:S(2)}, u32[]{:S(2)}) collective-permute-start(bf16[272,384]{1,0:T(8,128)(2,1)S(1)} %encode_side.1.refs_6_), channel_id=1, source_target_pairs={{0,2},{1,5},{2,0},{3,7},{4,6},{5,1},{6,4},{7,3},{8,10},{9,13},{10,... | collective-permute-start | bytes 626696 | tf_op jit(solution)/shard_map/ppermute | solution.py:545
  11.4 26.9 %collective-permute-start.12 = (bf16[384,768]{1,0:T(8,128)(2,1)S(1)}, bf16[384,768]{1,0:T(8,128)(2,1)S(1)}, u32[]{:S(2)}, u32[]{:S(2)}) collective-permute-start(bf16[384,768]{1,0:T(8,128)(2,1)S(1)} %copy-done.4), channel_id=1, source_target_pairs={{0,1},{1,0},{2,3},{3,2},{4,5},{5,4},{6,7},{7,6},{8,9},{9,8},{10,11... | collective-permute-start | bytes 1769480 | tf_op jit(solution)/shard_map/ppermute | solution.py:538
  13.6 15.7 %copy-start.2 = (bf16[512,768]{1,0:T(8,128)(2,1)S(1)}, bf16[512,768]{1,0:T(8,128)(2,1)}, u32[]{:S(2)}) copy-start(bf16[512,768]{1,0:T(8,128)(2,1)} %tokens.2) | copy-start | bytes 2359300
  13.6 15.7 %copy-start.5 = (bf16[768,384]{1,0:T(8,128)(2,1)S(1)}, bf16[768,384]{1,0:T(8,128)(2,1)}, u32[]{:S(2)}) copy-start(bf16[768,384]{1,0:T(8,128)(2,1)} %refs_2_.6) | copy-start | bytes 1769476
  13.6 15.7 %copy-start.6 = (bf16[768,384]{1,0:T(8,128)(2,1)S(1)}, bf16[768,384]{1,0:T(8,128)(2,1)}, u32[]{:S(2)}) copy-start(bf16[768,384]{1,0:T(8,128)(2,1)} %refs_3_.5) | copy-start | bytes 1769476
  13.6 15.6 %copy-start.7 = (bf16[768,384]{1,0:T(8,128)(2,1)S(1)}, bf16[768,384]{1,0:T(8,128)(2,1)}, u32[]{:S(2)}) copy-start(bf16[768,384]{1,0:T(8,128)(2,1)} %refs_4_.2) | copy-start | bytes 1769476
  14.0 4.8 %collective-permute-start.2 = (bf16[144,384]{1,0:T(8,128)(2,1)S(1)}, bf16[144,384]{1,0:T(8,128)(2,1)S(1)}, u32[]{:S(2)}, u32[]{:S(2)}) collective-permute-start(bf16[144,384]{1,0:T(8,128)(2,1)S(1)} %get-tuple-element.55.refs_6_), channel_id=1, source_target_pairs={{0,4},{1,3},{2,6},{3,1},{4,0},{5,7},{6,2},{7,5},{8,12},{9,11},{10,... | collective-permute-start | bytes 331784 | tf_op jit(solution)/shard_map/ppermute | solution.py:545
  14.9 5.8 %collective-permute-start.3 = (bf16[144,384]{1,0:T(8,128)(2,1)S(1)}, bf16[144,384]{1,0:T(8,128)(2,1)S(1)}, u32[]{:S(2)}, u32[]{:S(2)}) collective-permute-start(bf16[144,384]{1,0:T(8,128)(2,1)S(1)} %get-tuple-element.56.refs_7_), channel_id=1, source_target_pairs={{0,4},{1,3},{2,6},{3,1},{4,0},{5,7},{6,2},{7,5},{8,12},{9,11},{10,... | collective-permute-start | bytes 331784 | tf_op jit(solution)/shard_map/ppermute | solution.py:545
  19.0 5.1 %collective-permute-start.5 = (bf16[144,384]{1,0:T(8,128)(2,1)S(1)}, bf16[144,384]{1,0:T(8,128)(2,1)S(1)}, u32[]{:S(2)}, u32[]{:S(2)}) collective-permute-start(bf16[144,384]{1,0:T(8,128)(2,1)S(1)} %merge_sides.2.refs_4_.refs_5_.mine), channel_id=1, source_target_pairs={{0,8},{1,17},{2,10},{3,19},{4,12},{5,21},{6,14},{7,23},{8,0},{9,25... | collective-permute-start | bytes 331784 | tf_op jit(solution)/shard_map/ppermute | solution.py:545
  21.0 13.0 %copy-start.8 = (f32[768]{0:T(1024)S(1)}, f32[768]{0:T(1024)}, u32[]{:S(2)}) copy-start(f32[768]{0:T(1024)} %param.25) | copy-start | bytes 9220
  21.0 6.3 %collective-permute-start.4 = (bf16[144,384]{1,0:T(8,128)(2,1)S(1)}, bf16[144,384]{1,0:T(8,128)(2,1)S(1)}, u32[]{:S(2)}, u32[]{:S(2)}) collective-permute-start(bf16[144,384]{1,0:T(8,128)(2,1)S(1)} %merge_sides.3.refs_6_.refs_0_), channel_id=1, source_target_pairs={{0,8},{1,17},{2,10},{3,19},{4,12},{5,21},{6,14},{7,23},{8,0},{9,25... | collective-permute-start | bytes 331784 | tf_op jit(solution)/shard_map/ppermute | solution.py:545
  24.4 6.3 %collective-permute-start.7 = (bf16[144,384]{1,0:T(8,128)(2,1)S(1)}, bf16[144,384]{1,0:T(8,128)(2,1)S(1)}, u32[]{:S(2)}, u32[]{:S(2)}) collective-permute-start(bf16[144,384]{1,0:T(8,128)(2,1)S(1)} %merge_even.4.refs_2_.refs_0_), channel_id=1, source_target_pairs={{0,16},{1,9},{2,18},{3,11},{4,20},{5,13},{6,22},{7,15},{8,24},{9,1... | collective-permute-start | bytes 331784 | tf_op jit(solution)/shard_map/ppermute | solution.py:545
  27.5 6.2 %collective-permute-start.6 = (bf16[144,384]{1,0:T(8,128)(2,1)S(1)}, bf16[144,384]{1,0:T(8,128)(2,1)S(1)}, u32[]{:S(2)}, u32[]{:S(2)}) collective-permute-start(bf16[144,384]{1,0:T(8,128)(2,1)S(1)} %merge_even.5.refs_0_), channel_id=1, source_target_pairs={{0,16},{1,9},{2,18},{3,11},{4,20},{5,13},{6,22},{7,15},{8,24},{9,1... | collective-permute-start | bytes 331784 | tf_op jit(solution)/shard_map/ppermute | solution.py:545
  30.9 3.1 %collective-permute-start.10 = (bf16[128,384]{1,0:T(8,128)(2,1)S(1)}, bf16[128,384]{1,0:T(8,128)(2,1)S(1)}, u32[]{:S(2)}, u32[]{:S(2)}) collective-permute-start(bf16[128,384]{1,0:T(8,128)(2,1)S(1)} %merge_even.6.refs_2_.refs_0_), channel_id=1, source_target_pairs={{0,1},{1,0},{2,3},{3,2},{4,5},{5,4},{6,7},{7,6},{8,9},{9,8},{10,11... | collective-permute-start | bytes 294920 | tf_op jit(solution)/shard_map/ppermute | solution.py:538
  33.9 1.4 %collective-permute-start.8 = (bf16[128,384]{1,0:T(8,128)(2,1)S(1)}, bf16[128,384]{1,0:T(8,128)(2,1)S(1)}, u32[]{:S(2)}, u32[]{:S(2)}) collective-permute-start(bf16[128,384]{1,0:T(8,128)(2,1)S(1)} %merge_even.7.refs_6_.attended), channel_id=1, source_target_pairs={{0,1},{1,0},{2,3},{3,2},{4,5},{5,4},{6,7},{7,6},{8,9},{9,8},{10,11... | collective-permute-start | bytes 294920 | tf_op jit(solution)/shard_map/ppermute | solution.py:538
  35.8 7.5 %collective-permute-start.11 = (bf16[128,768]{1,0:T(8,128)(2,1)S(1)}, bf16[128,768]{1,0:T(8,128)(2,1)S(1)}, u32[]{:S(2)}, u32[]{:S(2)}) collective-permute-start(bf16[128,768]{1,0:T(8,128)(2,1)S(1)} %get-tuple-element.62), channel_id=1, source_target_pairs={{0,2},{1,5},{2,0},{3,7},{4,6},{5,1},{6,4},{7,3},{8,10},{9,13},{10,... | collective-permute-start | bytes 589832 | tf_op jit(solution)/shard_map/ppermute | solution.py:545
  36.7 7.4 %collective-permute-start.14 = (bf16[128,768]{1,0:T(8,128)(2,1)S(1)}, bf16[128,768]{1,0:T(8,128)(2,1)S(1)}, u32[]{:S(2)}, u32[]{:S(2)}) collective-permute-start(bf16[128,768]{1,0:T(8,128)(2,1)S(1)} %get-tuple-element.62), channel_id=1, source_target_pairs={{0,4},{1,3},{2,6},{3,1},{4,0},{5,7},{6,2},{7,5},{8,12},{9,11},{10,... | collective-permute-start | bytes 589832 | tf_op jit(solution)/shard_map/ppermute | solution.py:545
  43.3 5.7 %collective-permute-start.13 = (bf16[128,768]{1,0:T(8,128)(2,1)S(1)}, bf16[128,768]{1,0:T(8,128)(2,1)S(1)}, u32[]{:S(2)}, u32[]{:S(2)}) collective-permute-start(bf16[128,768]{1,0:T(8,128)(2,1)S(1)} %collective-permute-done.11.near), channel_id=1, source_target_pairs={{0,4},{1,3},{2,6},{3,1},{4,0},{5,7},{6,2},{7,5},{8,12},{9,11},{10,... | collective-permute-start | bytes 589832 | tf_op jit(solution)/shard_map/ppermute | solution.py:545
  44.2 4.8 %collective-permute-start.16 = (bf16[128,768]{1,0:T(8,128)(2,1)S(1)}, bf16[128,768]{1,0:T(8,128)(2,1)S(1)}, u32[]{:S(2)}, u32[]{:S(2)}) collective-permute-start(bf16[128,768]{1,0:T(8,128)(2,1)S(1)} %collective-permute-done.11.near), channel_id=1, source_target_pairs={{0,1},{1,0},{2,3},{3,2},{4,5},{5,4},{6,7},{7,6},{8,9},{9,8},{10,11... | collective-permute-start | bytes 589832 | tf_op jit(solution)/shard_map/ppermute | solution.py:538
  44.2 4.8 %collective-permute-start.17 = (bf16[128,768]{1,0:T(8,128)(2,1)S(1)}, bf16[128,768]{1,0:T(8,128)(2,1)S(1)}, u32[]{:S(2)}, u32[]{:S(2)}) collective-permute-start(bf16[128,768]{1,0:T(8,128)(2,1)S(1)} %collective-permute-done.14.far), channel_id=1, source_target_pairs={{0,1},{1,0},{2,3},{3,2},{4,5},{5,4},{6,7},{7,6},{8,9},{9,8},{10,11... | collective-permute-start | bytes 589832 | tf_op jit(solution)/shard_map/ppermute | solution.py:538
  48.9 2.1 %collective-permute-start.15 = (bf16[128,768]{1,0:T(8,128)(2,1)S(1)}, bf16[128,768]{1,0:T(8,128)(2,1)S(1)}, u32[]{:S(2)}, u32[]{:S(2)}) collective-permute-start(bf16[128,768]{1,0:T(8,128)(2,1)S(1)} %collective-permute-done.13.mine), channel_id=1, source_target_pairs={{0,1},{1,0},{2,3},{3,2},{4,5},{5,4},{6,7},{7,6},{8,9},{9,8},{10,11... | collective-permute-start | bytes 589832 | tf_op jit(solution)/shard_map/ppermute | solution.py:538
  52.2 1.8 %collective-permute-start.18 = (bf16[256,384]{1,0:T(8,128)(2,1)S(1)}, bf16[256,384]{1,0:T(8,128)(2,1)S(1)}, u32[]{:S(2)}, u32[]{:S(2)}) collective-permute-start(bf16[256,384]{1,0:T(8,128)(2,1)S(1)} %get-tuple-element.93), channel_id=1, source_target_pairs={{0,1},{1,0},{2,3},{3,2},{4,5},{5,4},{6,7},{7,6},{8,9},{9,8},{10,11... | collective-permute-start | bytes 589832 | tf_op jit(solution)/shard_map/ppermute | solution.py:538

commit v5 on v4

--- a/solution.py
+++ b/solution.py
@@ -29,8 +29,8 @@
     return lax.dot_general(a, b, (((0,), (0,)), ((), ())), preferred_element_type=F32)
 
 
-def log_rows(width):
-    return 16
+def log_rows(rows, width):
+    return 8 if 3 * rows <= width else 16
 
 
 def head_of(row):
@@ -57,8 +57,7 @@
     middle = (logs - high).astype(BF16).astype(F32)
     low = (logs - high - middle).astype(BF16).astype(F32)
     if 3 * rows <= width:
-        terms = jnp.concatenate([high, middle, low], axis=1)
-        return jnp.concatenate([terms, jnp.zeros_like(terms)], axis=0).astype(BF16)
+        return jnp.concatenate([high, middle, low], axis=1).astype(BF16)
     half = rows // 2
     below = jnp.concatenate([high, middle], axis=0)
     beside = jnp.concatenate([low[:, :half], low[:, half:]], axis=0)
@@ -186,16 +185,21 @@
 
 
 def encode_first_kernel(
-    tally, softness_far, latents_far, tokens_far, wq_far, wk_far, wv_far,
-    message, keys, values, scales, count_out,
-    count, softness, latents, tokens, wq, wk, wv, arrived,
+    tally, softness_far, latents_far, tokens_far, wq_far, wk_far, wv_far, wo_far, do_far,
+    message, keys, values, scales, count_out, wq, latents, outputs,
+    count, softness, tokens, wk, wv, arrived,
 ):
     quad, core = bits_of()
-    rows = latents.shape[0]
+    rows, model = latents.shape[0] // 4, wo_far.shape[1]
     moves = start_all(
         [
             (tally, count), (tokens_far, tokens), (wk_far, wk), (wv_far, wv), (wq_far, wq),
-            (softness_far, softness), (quarter(latents_far, quad ^ 3, rows), latents),
+            (softness_far, softness),
+            *[
+                (quarter(latents_far, quad ^ other, rows), quarter(latents, quad ^ other, rows))
+                for other in (3, 1, 2, 0)
+            ],
+            (wo_far, outputs.at[:, :model]), (do_far, outputs.at[:, model:]),
         ],
         arrived,
     )
@@ -203,13 +207,15 @@
     is_valid = lax.broadcasted_iota(jnp.int32, keys.shape, 0) < count[0]
     made = nn(tokens[...], wk[...])
     keys[...] = jnp.where(is_valid, made, made[0:1, :]).astype(BF16)
-    wait_all(moves[3:])
+    wait_all(moves[3:7])
     values[...] = jnp.where(is_valid, nn(tokens[...], wv[...]), 0.0).astype(BF16)
     count_out[...] = jnp.full(count_out.shape, count[0], jnp.int32)
     for which in range(2):
         row = scale_row(softness, which, wq.shape[1] // HEAD_DIM)
         scales[which] = jnp.broadcast_to(row, scales.shape[1:])
-    encode_into(message, latents[...], wq, keys, values, count_out, scales)
+    part = quarter(latents, quad ^ 3, rows)[...]
+    encode_into(message, part, wq, keys, values, count_out, scales)
+    wait_all(moves[7:])
 
 
 def encode_into(message, part, wq, keys, values, count, scales):
@@ -294,11 +300,11 @@
 
 def latent_kernel(which, attended, other, weight, other_weight, latents, gain, *refs):
     quad, core = bits_of()
-    half = attended.shape[0]
+    half, model = attended.shape[0], weight.shape[1]
     start = pl.ds(pl.multiple_of((2 * quad + which) * half, half), half)
 
     def finish(first, second, first_weight, second_weight):
-        update = nn(first[...], first_weight[...]) + nn(second[...], second_weight[...])
+        update = nn(first[...], first_weight) + nn(second[...], second_weight)
         pre = latents[start, :].astype(F32) + update
         mean_square = jnp.mean(pre * pre, axis=-1, keepdims=True)
         done = (pre * lax.rsqrt(mean_square + NORM_EPSILON) * gain[...]).astype(BF16)
@@ -312,11 +318,11 @@
 
     @pl.when(core == 0)
     def _():
-        finish(attended, other, weight, other_weight)
+        finish(attended, other, weight[...], other_weight[:, :model])
 
     @pl.when(core != 0)
     def _():
-        finish(other, attended, other_weight, weight)
+        finish(other, attended, other_weight[:, :model], weight[...])
 
 
 def groups_of(pairs):
@@ -410,8 +416,10 @@
 
 
 def decode_sides_kernel(came, queries, weights, more_weights, near, far, latent_in, *refs):
-    states, (latent_out, *refs) = refs[:6], refs[6:]
-    new_states, (gathered, staged, sent) = refs[:6], refs[6:]
+    groups = groups_of(queries.shape[0])[:1 if came else 2]
+    count = 3 * len(groups)
+    states, (latent_out, *refs) = refs[:count], refs[count:]
+    new_states, (gathered, staged, sent) = refs[:count], refs[count:]
     quad, core = bits_of()
     half = near.shape[0]
     across = [quad ^ (1 + core), quad ^ (2 - core)]
@@ -424,14 +432,21 @@
     def _():
         for index, piece in enumerate(pieces):
             gathered[index * half:(index + 1) * half, :] = piece[...]
-        for group, weight, state, new_state in zip(
-            groups_of(queries.shape[0]), [weights, more_weights],
-            [states[:3], states[3:]], [new_states[:3], new_states[3:]],
-        ):
+        for index, (group, weight) in enumerate(zip(groups, [weights, more_weights])):
             both = nn(gathered[...], weight[...]).astype(BF16)
-            decode_tokens(group, queries, both, state, new_state)
+            at = slice(3 * index, 3 * index + 3)
+            decode_tokens(group, queries, both, states[at], new_states[at])
 
     wait_all(moves)
+
+
+def decode_rest_kernel(queries, weights, near, far, *refs):
+    state, (*new_state, gathered) = refs[:3], refs[3:]
+    half = near.shape[0]
+    gathered[:half, :] = near[...]
+    gathered[half:, :] = far[...]
+    both = nn(gathered[...], weights[...]).astype(BF16)
+    decode_tokens(groups_of(queries.shape[0])[1], queries, both, state, new_state)
 
 
 def decode_send_kernel(queries, weights, more_weights, mine, came, *refs):
@@ -483,7 +498,7 @@
     moves = []
     for index in range(pieces):
         at = pl.ds(index * columns, columns)
-        value = base[:, at] + nn(other[...], weight[:, at])
+        value = base[:, at] + nn(other[...], weight[:, pl.ds(out.shape[1] + index * columns, columns)])
         slot = start + lax.broadcasted_iota(jnp.int32, value.shape, 0)
         staged[:, at] = jnp.where(slot < count[0:1, 0:1], value, 0.0)
         moves.append(pltpu.make_async_copy(staged.at[:, at], out.at[:, at], sent.at[index]))
@@ -532,7 +547,7 @@
     rows, width = total_rows // 4, wq.shape[1]
     slots = tokens.shape[0]
     half_slots = slots // 2
-    deep = rows + log_rows(width)
+    deep = rows + log_rows(rows, width)
 
     def swap(array):
         return lax.ppermute(array, "qgrp", [(0, 1), (1, 0)])
@@ -546,17 +561,18 @@
 
     attention = 4 * 256 * slots * width * 4
     sent = ((deep, width), BF16)
-    message, keys, values, scales, count = call(
-        encode_first_kernel, "ahhhhhh",
+    message, keys, values, scales, count, wq, latents, outputs = call(
+        encode_first_kernel, "ahhhhhhhh",
         [
             sent, *[((slots, width), BF16)] * 2,
-            ((2, 8, width), F32), ((8, PAIR), jnp.int32),
+            ((2, 8, width), F32), ((8, PAIR), jnp.int32), (wq.shape, BF16), (latents.shape, BF16),
+            ((width, 2 * model), BF16),
         ],
-        tally, softness, latents, tokens, wq, wk, wv,
+        tally, softness, latents, tokens, wq, wk, wv, wo, do,
         scratch=[
             pltpu.SMEM(tally.shape, tally.dtype), pltpu.SMEM(softness.shape, F32),
-            pltpu.VMEM((rows, model), BF16), pltpu.VMEM(tokens.shape, BF16),
-            *[pltpu.VMEM((model, width), BF16)] * 3, pltpu.SemaphoreType.DMA((7,)),
+            pltpu.VMEM(tokens.shape, BF16), *[pltpu.VMEM((model, width), BF16)] * 2,
+            pltpu.SemaphoreType.DMA((12,)),
         ],
         flops=attention, name="encode_corner",
     )
@@ -573,7 +589,7 @@
         name="encode_pass",
     )
     half = rows // 2
-    half_sent = ((half + log_rows(width), width), BF16)
+    half_sent = ((half + log_rows(half, width), width), BF16)
     messages = call(
         merge_pass_kernel, "vvv", [half_sent] * 2, *passed, came, name="merge_pass"
     )
@@ -583,7 +599,7 @@
         count, scales, latents, wq, keys, values,
         flops=attention, after=messages, name="encode_own",
     )
-    other_wo, other_do = swap(wo), swap(do)
+    other_outputs = swap(outputs)
     parts = []
     for which in range(2):
         parts += call(
@@ -614,13 +630,13 @@
     parts = [part[:half] for part in parts]
     (own_low,) = call(
         functools.partial(latent_kernel, 0), "vvvvvv", [((half, model), BF16)],
-        parts[0], swap(parts[0]), wo, other_wo, latents, gain.reshape(1, model),
+        parts[0], swap(parts[0]), wo, other_outputs, latents, gain.reshape(1, model),
         after=parts[1:], name="latent_low",
     )
     own, own_half = call(
         functools.partial(latent_kernel, 1), "vvvvvvv",
         [((rows, model), BF16), ((half, model), BF16)],
-        parts[1], swap(parts[1]), wo, other_wo, latents, gain.reshape(1, model), own_low,
+        parts[1], swap(parts[1]), wo, other_outputs, latents, gain.reshape(1, model), own_low,
         name="latent",
     )
     first = trade(own_half, 1, 2)
@@ -633,25 +649,33 @@
 
     latent_out, *states = call(
         decode_own_kernel, "vvvv", [whole, *states_out], queries, *weights, own,
-        after=[other_do], far=(0,), scratch=scratch(rows, 1), flops=attention, name="decode_own",
+        far=(0,), scratch=scratch(rows, 1), flops=attention, name="decode_own",
     )
     first, states[0] = lax.optimization_barrier((first, states[0]))
     third = trade(first, 2, 1)
 
     def decode_sides(came, near, far, latent_out, states):
-        latent_out, *states = call(
-            functools.partial(decode_sides_kernel, came), "vvvvvhvvvvvv", [whole, *states_out],
-            queries, *weights, near, far, latent_out, *states, far=(0,), alias={5: 0},
+        used = states[:3] if came else states
+        latent_out, *used = call(
+            functools.partial(decode_sides_kernel, came), "vvvvvh" + "v" * len(used),
+            [whole, *states_out[:len(used)]],
+            queries, *weights, near, far, latent_out, *used, far=(0,), alias={5: 0},
             scratch=[pltpu.VMEM((rows, model), BF16), *scratch(rows, 2)], flops=attention,
             name="decode_sides",
         )
-        return latent_out, states
+        return latent_out, [*used, *states[len(used):]]
 
     came_first, came_second = swap(first), swap(second)
     latent_out, states = decode_sides(False, first, second, latent_out, states)
+    latent_out, states = decode_sides(True, came_first, came_second, latent_out, states)
     third, states[0] = lax.optimization_barrier((third, states[0]))
     came = swap(third)
-    latent_out, states = decode_sides(True, came_first, came_second, latent_out, states)
+    states[3:] = call(
+        decode_rest_kernel, "vvvvvvv", states_out[3:],
+        queries, weights[1], came_first, came_second, *states[3:],
+        scratch=[pltpu.VMEM((rows, model), BF16)], flops=attention, after=states[1:2],
+        name="decode_rest",
+    )
     send, *boths = call(
         decode_send_kernel, "vvvvvvvvvvv",
         [((half_slots, width), BF16), *[((rows, 2 * size), BF16) for size in sizes]],
@@ -665,7 +689,7 @@
         flops=attention // 2, name="decode_keep",
     )
     (tokens_out,) = call(
-        tokens_kernel, "vvvv", [((half_slots, model), F32)], count, base, swap(send), other_do,
+        tokens_kernel, "vvvv", [((half_slots, model), F32)], count, base, swap(send), other_outputs,
         far=(0,), scratch=scratch(half_slots, 3 if model % 384 == 0 else 1), name="tokens",
     )
     return latent_out, tokens_out

time: 55.5 us -> 54.1 us (0.975)
  waiting for transfers between devices: 12.6 us -> 10.7 us
    ppermute x11, waiting for transfers between devices: 11.8 us -> 9.37 us  [trade(): return lax.ppermute(array, ('cell', 'qgrp'), pairs)]
    ppermute x11, starting transfers between devices: 16.9 us -> 17.9 us  [trade(): return lax.ppermute(array, ('cell', 'qgrp'), pairs)]
    ppermute x8 -> x7, starting transfers between devices: 1.9 us -> 0.99 us  [swap(): return lax.ppermute(array, 'qgrp', [(0, 1), (1, 0)])]
    ppermute x8 -> x7, waiting for transfers between devices: 0.77 us -> 1.3 us  [swap(): return lax.ppermute(array, 'qgrp', [(0, 1), (1, 0)])]
    pallas_call x20 -> x21, Pallas kernels: 22 us -> 22.4 us  [call(): pl.pallas_call(kernel, out_shape=shapes, in_specs=[SPACES[kind] for kind...]
  transfers between devices with their start and end apart: 19 -> 18, of which waited for: 7 -> 12; matrix products, arithmetic and copies ran while one was open for 0% -> 0% of each run, Pallas kernels for 28% -> 28%
where the time goes in v5:
time: 54.1 us; the launch traced here: 53.7 us
  Pallas kernels  22.4 us (41%)
  starting transfers between devices  18.9 us (35%)
  waiting for transfers between devices  10.7 us (20%)
  between operations  1.71 us (3%)
    pallas_call x21, Pallas kernels, call(): pl.pallas_call(kernel, out_shape=shapes, in_specs=[SPACES[kind] for kind...  22.4 us
    ppermute x11, starting transfers between devices, trade(): return lax.ppermute(array, ('cell', 'qgrp'), pairs)  17.9 us
    ppermute x11, waiting for transfers between devices, trade(): return lax.ppermute(array, ('cell', 'qgrp'), pairs)  9.37 us
    ppermute x7, waiting for transfers between devices, swap(): return lax.ppermute(array, 'qgrp', [(0, 1), (1, 0)])  1.3 us
  transfers between devices with their start and end apart: 18, of which 12 were waited for; matrix products, arithmetic and copies ran while one was open for 0% of the time, Pallas kernels for 28%

profile of v5, /device:TPU:0, one launch (start us, length us, event | category | flops | bytes accessed | tf_op | source)
XLA Modules:
  0.0 53.7 jit_solution(7335793473879026352)
XLA Ops:
  1.3 4.2 %encode_corner.1 = (bf16[272,384]{1,0:T(8,128)(2,1)S(1)}, bf16[512,384]{1,0:T(8,128)(2,1)S(1)}, bf16[512,384]{1,0:T(8,128)(2,1)S(1)}, f32[2,8,384]{2,1,0:T(8,128...) custom-call(s32[1]{0:T(128)S(6)} %copy.21.tally, ...), custom_call_target="tpu_custom_call" | custom-call | flops 805306368 | bytes 9674852 | tf_op jit(solution)/shard_map/encode_corner/pallas_call | solution.py:531
  5.5 0.5 collective-permute-start.9
  6.0 2.6 %collective-permute-start = (bf16[272,384]{1,0:T(8,128)(2,1)S(1)}, bf16[272,384]{1,0:T(8,128)(2,1)S(1)}, u32[]{:S(2)}, u32[]{:S(2)}) collective-permute-start(bf16[272,384]{1,0:T(8,128)(2,1)S(1)} %get-tuple-element.59), channel_id=1, source_target_pairs={{0,2},{1,5},{2,0},{3,7},{4,6},{5,1},{6,4},{7,3},{8,10},{9,13},{10,... | collective-permute-start | bytes 626696 | tf_op jit(solution)/shard_map/ppermute | solution.py:560
  8.6 1.5 %encode_side.1.refs_6_ = bf16[272,384]{1,0:T(8,128)(2,1)S(1)} custom-call(s32[8,128]{1,0:T(8,128)S(1)} %get-tuple-element.52.count.refs_0_, f32[2,8,384]{2,1,0:T(8,128)S(1)} %get-tuple-element.51.scales.refs_1_.refs_0_, bf16[1024,768]{1,0:T(8,128)(2,1)S(1)} %get-tuple-element.53.latents.refs_2_.refs_4_, bf16[768,384]{1,0:T(8,128)(2,1)S(1)} %get-tuple-element.54.wq.refs_3_, ...), custom_call_target="tpu_custom_call" | custom-call | flops 805306368 | bytes 3186688 | tf_op jit(solution)/shard_map/encode_side/pallas_call | solution.py:531
  10.2 0.1 collective-permute-start.1
  10.2 1.5 %encode_pass.1 = (f32[256,384]{1,0:T(8,128)S(1)}, f32[8,256]{1,0:T(8,128)S(1)}) custom-call(s32[8,128]{1,0:T(8,128)S(1)} %get-tuple-element.52.count.refs_0_, f32[2,8,384]{2,1,0:T(8,128)S(1)} %get-tuple-element.51.scales.refs_1_.refs_0_, bf16[1024,768]{1,0:T(8,128)(2,1)S(1)} %get-tuple-element.53.latents.refs_2_.refs_4_, ...), custom_call_target="tpu_custom_call" | custom-call | flops 805306368 | bytes 3379200 | tf_op jit(solution)/shard_map/encode_pass/pallas_call | solution.py:531
  11.8 0.0 copy-start.3
  11.8 0.0 copy-start.4
  11.8 0.0 copy-start.5
  11.8 0.6 %collective-permute-done.came = bf16[272,384]{1,0:T(8,128)(2,1)S(1)} collective-permute-done((bf16[272,384]{1,0:T(8,128)(2,1)S(1)}, bf16[272,384]{1,0:T(8,128)(2,1)S(1)}, u32[]{:S(2)}, u32[]{:S(2)}) %collective-permute-start) | collective-permute-done | bytes 208928 | tf_op jit(solution)/shard_map/ppermute | solution.py:560
  12.4 0.3 merge_pass.1
  12.7 2.1 %collective-permute-start.2 = (bf16[136,384]{1,0:T(8,128)(2,1)S(1)}, bf16[136,384]{1,0:T(8,128)(2,1)S(1)}, u32[]{:S(2)}, u32[]{:S(2)}) collective-permute-start(bf16[136,384]{1,0:T(8,128)(2,1)S(1)} %get-tuple-element.60.refs_6_), channel_id=1, source_target_pairs={{0,4},{1,3},{2,6},{3,1},{4,0},{5,7},{6,2},{7,5},{8,12},{9,11},{10,... | collective-permute-start | bytes 313352 | tf_op jit(solution)/shard_map/ppermute | solution.py:560
  14.8 0.1 collective-permute-start.3
  14.9 1.5 %encode_own.1 = (f32[256,384]{1,0:T(8,128)S(1)}, f32[8,256]{1,0:T(8,128)S(1)}) custom-call(s32[8,128]{1,0:T(8,128)S(1)} %get-tuple-element.52.count.refs_0_, f32[2,8,384]{2,1,0:T(8,128)S(1)} %get-tuple-element.51.scales.refs_1_.refs_0_, bf16[1024,768]{1,0:T(8,128)(2,1)S(1)} %get-tuple-element.53.latents.refs_2_.refs_4_, ...), custom_call_target="tpu_custom_call" | custom-call | flops 805306368 | bytes 3379200 | tf_op jit(solution)/shard_map/encode_own/pallas_call | solution.py:531
  16.4 0.3 collective-permute-done.1.first.refs_2_
  16.8 0.7 %collective-permute-done.2.second = bf16[136,384]{1,0:T(8,128)(2,1)S(1)} collective-permute-done((bf16[136,384]{1,0:T(8,128)(2,1)S(1)}, bf16[136,384]{1,0:T(8,128)(2,1)S(1)}, u32[]{:S(2)}, u32[]{:S(2)}) %collective-permute-start.2) | collective-permute-done | bytes 104480 | tf_op jit(solution)/shard_map/ppermute | solution.py:560
  17.5 0.3 merge_sides.2.refs_4_.refs_5_.mine
  17.7 0.0 copy-start.6
  17.8 0.0 copy-start.1
  17.8 2.1 %collective-permute-start.5 = (bf16[136,384]{1,0:T(8,128)(2,1)S(1)}, bf16[136,384]{1,0:T(8,128)(2,1)S(1)}, u32[]{:S(2)}, u32[]{:S(2)}) collective-permute-start(bf16[136,384]{1,0:T(8,128)(2,1)S(1)} %merge_sides.2.refs_4_.refs_5_.mine), channel_id=1, source_target_pairs={{0,8},{1,17},{2,10},{3,19},{4,12},{5,21},{6,14},{7,23},{8,0},{9,25... | collective-permute-start | bytes 313352 | tf_op jit(solution)/shard_map/ppermute | solution.py:560
  19.9 0.0 collective-permute-done.3.refs_3_
  19.9 0.3 merge_sides.3.refs_6_.refs_0_
  20.2 1.2 %collective-permute-start.4 = (bf16[136,384]{1,0:T(8,128)(2,1)S(1)}, bf16[136,384]{1,0:T(8,128)(2,1)S(1)}, u32[]{:S(2)}, u32[]{:S(2)}) collective-permute-start(bf16[136,384]{1,0:T(8,128)(2,1)S(1)} %merge_sides.3.refs_6_.refs_0_), channel_id=1, source_target_pairs={{0,8},{1,17},{2,10},{3,19},{4,12},{5,21},{6,14},{7,23},{8,0},{9,25... | collective-permute-start | bytes 313352 | tf_op jit(solution)/shard_map/ppermute | solution.py:560
  21.4 2.0 %collective-permute-done.5.came = bf16[136,384]{1,0:T(8,128)(2,1)S(1)} collective-permute-done((bf16[136,384]{1,0:T(8,128)(2,1)S(1)}, bf16[136,384]{1,0:T(8,128)(2,1)S(1)}, u32[]{:S(2)}, u32[]{:S(2)}) %collective-permute-start.5) | collective-permute-done | bytes 104480 | tf_op jit(solution)/shard_map/ppermute | solution.py:560
  23.4 0.2 merge_even.4.refs_2_.refs_0_
  23.6 2.6 %collective-permute-start.7 = (bf16[136,384]{1,0:T(8,128)(2,1)S(1)}, bf16[136,384]{1,0:T(8,128)(2,1)S(1)}, u32[]{:S(2)}, u32[]{:S(2)}) collective-permute-start(bf16[136,384]{1,0:T(8,128)(2,1)S(1)} %merge_even.4.refs_2_.refs_0_), channel_id=1, source_target_pairs={{0,16},{1,9},{2,18},{3,11},{4,20},{5,13},{6,22},{7,15},{8,24},{9,1... | collective-permute-start | bytes 313352 | tf_op jit(solution)/shard_map/ppermute | solution.py:560
  26.2 0.0 collective-permute-done.4.refs_1_
  26.2 0.2 merge_even.5.refs_0_
  26.4 1.8 %collective-permute-start.6 = (bf16[136,384]{1,0:T(8,128)(2,1)S(1)}, bf16[136,384]{1,0:T(8,128)(2,1)S(1)}, u32[]{:S(2)}, u32[]{:S(2)}) collective-permute-start(bf16[136,384]{1,0:T(8,128)(2,1)S(1)} %merge_even.5.refs_0_), channel_id=1, source_target_pairs={{0,16},{1,9},{2,18},{3,11},{4,20},{5,13},{6,22},{7,15},{8,24},{9,1... | collective-permute-start | bytes 313352 | tf_op jit(solution)/shard_map/ppermute | solution.py:560
  28.2 0.0 copy-done
  28.2 0.7 %decode_prepare.1 = (bf16[3,512,256]{2,1,0:T(8,128)(2,1)S(1)}, bf16[768,512]{1,0:T(8,128)(2,1)S(1)}, bf16[768,256]{1,0:T(8,128)(2,1)S(1)}) custom-call(f32[2,8,384]{2,1,0:T(8,128)S(1)} %get-tuple-element.51.scales.refs_1_.refs_0_, bf16[512,768]{1,0:T(8,128)(2,1)S(1)} %copy-done, bf16[768,384]{1,0:T(8,128)(2,1)S(1)} %copy-done.3, ...), custom_call_target="tpu_custom_call" | custom-call | bytes 4546560 | tf_op jit(solution)/shard_map/decode_prepare/pallas_call | solution.py:531
  29.0 0.5 collective-permute-done.7.refs_1_
  29.5 0.2 merge_even.6.refs_2_.refs_0_
  29.7 0.1 collective-permute-start.10
  29.8 2.7 %collective-permute-done.6.refs_1_ = bf16[136,384]{1,0:T(8,128)(2,1)S(1)} collective-permute-done((bf16[136,384]{1,0:T(8,128)(2,1)S(1)}, bf16[136,384]{1,0:T(8,128)(2,1)S(1)}, u32[]{:S(2)}, u32[]{:S(2)}) %collective-permute-start.6) | collective-permute-done | bytes 104480 | tf_op jit(solution)/shard_map/ppermute | solution.py:560
  32.5 0.2 merge_even.7.refs_6_.attended
  32.8 0.1 collective-permute-start.8
  32.9 0.0 collective-permute-done.10.refs_1_
  32.9 0.0 collective-permute-done.9.refs_3_.other_weight.weight
  32.9 0.0 copy-done.1
  32.9 0.5 latent_low.1.refs_0_
  33.4 0.7 %collective-permute-done.8.other = bf16[128,384]{1,0:T(8,128)(2,1)S(1)} collective-permute-done((bf16[128,384]{1,0:T(8,128)(2,1)S(1)}, bf16[128,384]{1,0:T(8,128)(2,1)S(1)}, u32[]{:S(2)}, u32[]{:S(2)}) %collective-permute-start.8) | collective-permute-done | bytes 98336 | tf_op jit(solution)/shard_map/ppermute | solution.py:553
  34.1 0.5 latent.1
  34.6 2.1 %collective-permute-start.11 = (bf16[128,768]{1,0:T(8,128)(2,1)S(1)}, bf16[128,768]{1,0:T(8,128)(2,1)S(1)}, u32[]{:S(2)}, u32[]{:S(2)}) collective-permute-start(bf16[128,768]{1,0:T(8,128)(2,1)S(1)} %get-tuple-element.68), channel_id=1, source_target_pairs={{0,2},{1,5},{2,0},{3,7},{4,6},{5,1},{6,4},{7,3},{8,10},{9,13},{10,... | collective-permute-start | bytes 589832 | tf_op jit(solution)/shard_map/ppermute | solution.py:560
  36.7 1.5 %collective-permute-start.14 = (bf16[128,768]{1,0:T(8,128)(2,1)S(1)}, bf16[128,768]{1,0:T(8,128)(2,1)S(1)}, u32[]{:S(2)}, u32[]{:S(2)}) collective-permute-start(bf16[128,768]{1,0:T(8,128)(2,1)S(1)} %get-tuple-element.68), channel_id=1, source_target_pairs={{0,4},{1,3},{2,6},{3,1},{4,0},{5,7},{6,2},{7,5},{8,12},{9,11},{10,... | collective-permute-start | bytes 589832 | tf_op jit(solution)/shard_map/ppermute | solution.py:560
  38.3 2.1 %decode_own.1 = (f32[1024,768]{1,0:T(8,128)}, f32[512,256]{1,0:T(8,128)S(1)}, f32[512,256]{1,0:T(8,128)S(1)}, f32[512,256]{1,0:T(8,128)S(1)}, f32[512,128]{1,0:T...) custom-call(bf16[3,512,256]{2,1,0:T(8,128)(2,1)S(1)} %get-tuple-element.64.refs_2_.refs_3_.queries.refs_0_, ...), custom_call_target="tpu_custom_call" | custom-call | flops 805306368 | bytes 7864320 | tf_op jit(solution)/shard_map/decode_own/pallas_call | solution.py:531
  40.4 1.4 %collective-permute-done.11.near = bf16[128,768]{1,0:T(8,128)(2,1)S(1)} collective-permute-done((bf16[128,768]{1,0:T(8,128)(2,1)S(1)}, bf16[128,768]{1,0:T(8,128)(2,1)S(1)}, u32[]{:S(2)}, u32[]{:S(2)}) %collective-permute-start.11) | collective-permute-done | bytes 196640 | tf_op jit(solution)/shard_map/ppermute | solution.py:560
  41.8 0.0 collective-permute-start.13
  41.8 0.6 %collective-permute-done.14.far = bf16[128,768]{1,0:T(8,128)(2,1)S(1)} collective-permute-done((bf16[128,768]{1,0:T(8,128)(2,1)S(1)}, bf16[128,768]{1,0:T(8,128)(2,1)S(1)}, u32[]{:S(2)}, u32[]{:S(2)}) %collective-permute-start.14) | collective-permute-done | bytes 196640 | tf_op jit(solution)/shard_map/ppermute | solution.py:560
  42.4 0.1 collective-permute-start.15
  42.5 1.7 %collective-permute-start.12 = (bf16[128,768]{1,0:T(8,128)(2,1)S(1)}, bf16[128,768]{1,0:T(8,128)(2,1)S(1)}, u32[]{:S(2)}, u32[]{:S(2)}) collective-permute-start(bf16[128,768]{1,0:T(8,128)(2,1)S(1)} %collective-permute-done.11.near), channel_id=1, source_target_pairs={{0,4},{1,3},{2,6},{3,1},{4,0},{5,7},{6,2},{7,5},{8,12},{9,11},{10,... | collective-permute-start | bytes 589832 | tf_op jit(solution)/shard_map/ppermute | solution.py:560
  44.2 2.0 %decode_sides.2 = (f32[1024,768]{1,0:T(8,128)}, f32[512,256]{1,0:T(8,128)S(1)}, f32[512,256]{1,0:T(8,128)S(1)}, f32[512,256]{1,0:T(8,128)S(1)}, f32[512,128]{1,0...) custom-call(bf16[3,512,256]{2,1,0:T(8,128)(2,1)S(1)} %get-tuple-element.64.refs_2_., ...), custom_call_target="tpu_custom_call", output_to_operand_aliasing={{0}: (5, {})} | custom-call | flops 805306368 | bytes 13369344 | tf_op jit(solution)/shard_map/decode_sides/pallas_call | solution.py:531
  46.3 0.0 collective-permute-done.13.near.refs_2_
  46.3 0.0 collective-permute-done.15.far.refs_3_
  46.3 1.3 %decode_sides.3 = (f32[1024,768]{1,0:T(8,128)}, f32[512,256]{1,0:T(8,128)S(1)}, f32[512,256]{1,0:T(8,128)S(1)}, f32[512,256]{1,0:T(8,128)S(1)}) custom-call(bf16[3,512,256]{2,1,0:T(8,128)(2,1)S(1)} %get-tuple-element.64.refs_2_.refs_3_.queries.refs_0_, bf16[768,512]{1,0:T(8,128)(2,1)S(1)} %get-tuple-element.65.weights, ...), custom_call_target="tpu_custom_call", output_to_operand_aliasing={{0}: (5, {})} | custom-call | flops 805306368 | bytes 11796480 | tf_op jit(solution)/shard_map/decode_sides/pallas_call | solution.py:531
  47.6 0.6 %collective-permute-done.12.mine = bf16[128,768]{1,0:T(8,128)(2,1)S(1)} collective-permute-done((bf16[128,768]{1,0:T(8,128)(2,1)S(1)}, bf16[128,768]{1,0:T(8,128)(2,1)S(1)}, u32[]{:S(2)}, u32[]{:S(2)}) %collective-permute-start.12) | collective-permute-done | bytes 196640 | tf_op jit(solution)/shard_map/ppermute | solution.py:560
  48.2 0.0 collective-permute-start.16
  48.2 0.9 %decode_rest.1 = (f32[512,128]{1,0:T(8,128)S(1)}, f32[512,128]{1,0:T(8,128)S(1)}, f32[512,128]{1,0:T(8,128)S(1)}) custom-call(bf16[3,512,256]{2,1,0:T(8,128)(2,1)S(1)} %get-tuple-element.64.refs_2_.refs_3_.queries.refs_0_, bf16[768,256]{1,0:T(8,128)(2,1)S(1)} %get-tuple-element.66.more_weights.refs_1_, ...), custom_call_target="tpu_custom_call" | custom-call | flops 805306368 | bytes 3145728 | tf_op jit(solution)/shard_map/decode_rest/pallas_call | solution.py:531
  49.2 0.5 collective-permute-done.16.came
  49.6 1.2 %decode_send.1 = (bf16[256,384]{1,0:T(8,128)(2,1)S(1)}, bf16[256,512]{1,0:T(8,128)(2,1)S(1)}, bf16[256,256]{1,0:T(8,128)(2,1)S(1)}) custom-call(bf16[3,512,256]{2,1,0:T(8,128)(2,1)S(1)} %get-tuple-element.64.refs_2_.refs_3_.queries.refs_0_, bf16[768,512]{1,0:T(8,128)(2,1)S(1)} %get-tuple-element.65.weights, ...), custom_call_target="tpu_custom_call" | custom-call | flops 402653184 | bytes 5308416 | tf_op jit(solution)/shard_map/decode_send/pallas_call | solution.py:531
  50.8 0.2 collective-permute-start.17
  51.0 1.2 %decode_keep.1 = (f32[1024,768]{1,0:T(8,128)}, f32[256,768]{1,0:T(8,128)S(1)}) custom-call(bf16[3,512,256]{2,1,0:T(8,128)(2,1)S(1)} %get-tuple-element.64.refs_2_.refs_3_.queries.refs_0_, bf16[256,512]{1,0:T(8,128)(2,1)S(1)} %get-tuple-element.94.both, bf16[256,256]{1,0:T(8,128)(2,1)S(1)} %get-tuple-element.95.more_both, ...), custom_call_target="tpu_custom_call", output_to_operand_aliasing={{0}: (7, {})} | custom-call | flops 402653184 | bytes 12386304 | tf_op jit(solution)/shard_map/decode_keep/pallas_call | solution.py:531
  52.3 0.1 collective-permute-done.17.other
  52.3 1.2 %tokens.3 = f32[256,768]{1,0:T(8,128)} custom-call(s32[8,128]{1,0:T(8,128)S(1)} %get-tuple-element.52.count.refs_0_, f32[256,768]{1,0:T(8,128)S(1)} %get-tuple-element.98.base, bf16[256,384]{1,0:T(8,128)(2,1)S(1)} %collective-permute-done.17.other, bf16[384,1536]{1,0:T(8,128)(2,1)S(1)} %collective-permute-done.9.refs_3_.other_weight.weight), custom_call_target="tpu_custom_call" | custom-call | bytes 2953216 | tf_op jit(solution)/shard_map/tokens/pallas_call | solution.py:531
  (8 shorter events, 0.0 us)
Async XLA Ops:
  5.5 27.4 %collective-permute-start.9 = (bf16[384,1536]{1,0:T(8,128)(2,1)S(1)}, bf16[384,1536]{1,0:T(8,128)(2,1)S(1)}, u32[]{:S(2)}, u32[]{:S(2)}) collective-permute-start(bf16[384,1536]{1,0:T(8,128)(2,1)S(1)} %get-tuple-element.67), channel_id=1, source_target_pairs={{0,1},{1,0},{2,3},{3,2},{4,5},{5,4},{6,7},{7,6},{8,9},{9,8},{10,11... | collective-permute-start | bytes 3538952 | tf_op jit(solution)/shard_map/ppermute | solution.py:553
  6.0 6.3 %collective-permute-start = (bf16[272,384]{1,0:T(8,128)(2,1)S(1)}, bf16[272,384]{1,0:T(8,128)(2,1)S(1)}, u32[]{:S(2)}, u32[]{:S(2)}) collective-permute-start(bf16[272,384]{1,0:T(8,128)(2,1)S(1)} %get-tuple-element.59), channel_id=1, source_target_pairs={{0,2},{1,5},{2,0},{3,7},{4,6},{5,1},{6,4},{7,3},{8,10},{9,13},{10,... | collective-permute-start | bytes 626696 | tf_op jit(solution)/shard_map/ppermute | solution.py:560
  10.2 6.6 %collective-permute-start.1 = (bf16[272,384]{1,0:T(8,128)(2,1)S(1)}, bf16[272,384]{1,0:T(8,128)(2,1)S(1)}, u32[]{:S(2)}, u32[]{:S(2)}) collective-permute-start(bf16[272,384]{1,0:T(8,128)(2,1)S(1)} %encode_side.1.refs_6_), channel_id=1, source_target_pairs={{0,2},{1,5},{2,0},{3,7},{4,6},{5,1},{6,4},{7,3},{8,10},{9,13},{10,... | collective-permute-start | bytes 626696 | tf_op jit(solution)/shard_map/ppermute | solution.py:560
  11.8 16.5 %copy-start = (bf16[512,768]{1,0:T(8,128)(2,1)S(1)}, bf16[512,768]{1,0:T(8,128)(2,1)}, u32[]{:S(2)}) copy-start(bf16[512,768]{1,0:T(8,128)(2,1)} %tokens.2) | copy-start | bytes 2359300
  11.8 16.5 %copy-start.3 = (bf16[768,384]{1,0:T(8,128)(2,1)S(1)}, bf16[768,384]{1,0:T(8,128)(2,1)}, u32[]{:S(2)}) copy-start(bf16[768,384]{1,0:T(8,128)(2,1)} %refs_2_.2) | copy-start | bytes 1769476
  11.8 16.4 %copy-start.4 = (bf16[768,384]{1,0:T(8,128)(2,1)S(1)}, bf16[768,384]{1,0:T(8,128)(2,1)}, u32[]{:S(2)}) copy-start(bf16[768,384]{1,0:T(8,128)(2,1)} %refs_3_.1) | copy-start | bytes 1769476
  11.8 16.4 %copy-start.5 = (bf16[768,384]{1,0:T(8,128)(2,1)S(1)}, bf16[768,384]{1,0:T(8,128)(2,1)}, u32[]{:S(2)}) copy-start(bf16[768,384]{1,0:T(8,128)(2,1)} %refs_4_.1) | copy-start | bytes 1769476
  12.7 4.8 %collective-permute-start.2 = (bf16[136,384]{1,0:T(8,128)(2,1)S(1)}, bf16[136,384]{1,0:T(8,128)(2,1)S(1)}, u32[]{:S(2)}, u32[]{:S(2)}) collective-permute-start(bf16[136,384]{1,0:T(8,128)(2,1)S(1)} %get-tuple-element.60.refs_6_), channel_id=1, source_target_pairs={{0,4},{1,3},{2,6},{3,1},{4,0},{5,7},{6,2},{7,5},{8,12},{9,11},{10,... | collective-permute-start | bytes 313352 | tf_op jit(solution)/shard_map/ppermute | solution.py:560
  14.8 5.1 %collective-permute-start.3 = (bf16[136,384]{1,0:T(8,128)(2,1)S(1)}, bf16[136,384]{1,0:T(8,128)(2,1)S(1)}, u32[]{:S(2)}, u32[]{:S(2)}) collective-permute-start(bf16[136,384]{1,0:T(8,128)(2,1)S(1)} %get-tuple-element.61.refs_7_), channel_id=1, source_target_pairs={{0,4},{1,3},{2,6},{3,1},{4,0},{5,7},{6,2},{7,5},{8,12},{9,11},{10,... | collective-permute-start | bytes 313352 | tf_op jit(solution)/shard_map/ppermute | solution.py:560
  17.7 15.1 %copy-start.6 = (f32[768]{0:T(1024)S(1)}, f32[768]{0:T(1024)}, u32[]{:S(2)}) copy-start(f32[768]{0:T(1024)} %param.25) | copy-start | bytes 9220
  17.8 15.1 %copy-start.1 = (bf16[384,768]{1,0:T(8,128)(2,1)S(1)}, bf16[384,768]{1,0:T(8,128)(2,1)}, u32[]{:S(2)}) copy-start(bf16[384,768]{1,0:T(8,128)(2,1)} %weight.2) | copy-start | bytes 1769476
  17.8 5.6 %collective-permute-start.5 = (bf16[136,384]{1,0:T(8,128)(2,1)S(1)}, bf16[136,384]{1,0:T(8,128)(2,1)S(1)}, u32[]{:S(2)}, u32[]{:S(2)}) collective-permute-start(bf16[136,384]{1,0:T(8,128)(2,1)S(1)} %merge_sides.2.refs_4_.refs_5_.mine), channel_id=1, source_target_pairs={{0,8},{1,17},{2,10},{3,19},{4,12},{5,21},{6,14},{7,23},{8,0},{9,25... | collective-permute-start | bytes 313352 | tf_op jit(solution)/shard_map/ppermute | solution.py:560
  20.2 6.0 %collective-permute-start.4 = (bf16[136,384]{1,0:T(8,128)(2,1)S(1)}, bf16[136,384]{1,0:T(8,128)(2,1)S(1)}, u32[]{:S(2)}, u32[]{:S(2)}) collective-permute-start(bf16[136,384]{1,0:T(8,128)(2,1)S(1)} %merge_sides.3.refs_6_.refs_0_), channel_id=1, source_target_pairs={{0,8},{1,17},{2,10},{3,19},{4,12},{5,21},{6,14},{7,23},{8,0},{9,25... | collective-permute-start | bytes 313352 | tf_op jit(solution)/shard_map/ppermute | solution.py:560
  23.6 5.9 %collective-permute-start.7 = (bf16[136,384]{1,0:T(8,128)(2,1)S(1)}, bf16[136,384]{1,0:T(8,128)(2,1)S(1)}, u32[]{:S(2)}, u32[]{:S(2)}) collective-permute-start(bf16[136,384]{1,0:T(8,128)(2,1)S(1)} %merge_even.4.refs_2_.refs_0_), channel_id=1, source_target_pairs={{0,16},{1,9},{2,18},{3,11},{4,20},{5,13},{6,22},{7,15},{8,24},{9,1... | collective-permute-start | bytes 313352 | tf_op jit(solution)/shard_map/ppermute | solution.py:560
  26.4 6.1 %collective-permute-start.6 = (bf16[136,384]{1,0:T(8,128)(2,1)S(1)}, bf16[136,384]{1,0:T(8,128)(2,1)S(1)}, u32[]{:S(2)}, u32[]{:S(2)}) collective-permute-start(bf16[136,384]{1,0:T(8,128)(2,1)S(1)} %merge_even.5.refs_0_), channel_id=1, source_target_pairs={{0,16},{1,9},{2,18},{3,11},{4,20},{5,13},{6,22},{7,15},{8,24},{9,1... | collective-permute-start | bytes 313352 | tf_op jit(solution)/shard_map/ppermute | solution.py:560
  29.7 3.1 %collective-permute-start.10 = (bf16[128,384]{1,0:T(8,128)(2,1)S(1)}, bf16[128,384]{1,0:T(8,128)(2,1)S(1)}, u32[]{:S(2)}, u32[]{:S(2)}) collective-permute-start(bf16[128,384]{1,0:T(8,128)(2,1)S(1)} %merge_even.6.refs_2_.refs_0_), channel_id=1, source_target_pairs={{0,1},{1,0},{2,3},{3,2},{4,5},{5,4},{6,7},{7,6},{8,9},{9,8},{10,11... | collective-permute-start | bytes 294920 | tf_op jit(solution)/shard_map/ppermute | solution.py:553
  32.8 1.4 %collective-permute-start.8 = (bf16[128,384]{1,0:T(8,128)(2,1)S(1)}, bf16[128,384]{1,0:T(8,128)(2,1)S(1)}, u32[]{:S(2)}, u32[]{:S(2)}) collective-permute-start(bf16[128,384]{1,0:T(8,128)(2,1)S(1)} %merge_even.7.refs_6_.attended), channel_id=1, source_target_pairs={{0,1},{1,0},{2,3},{3,2},{4,5},{5,4},{6,7},{7,6},{8,9},{9,8},{10,11... | collective-permute-start | bytes 294920 | tf_op jit(solution)/shard_map/ppermute | solution.py:553
  34.6 7.2 %collective-permute-start.11 = (bf16[128,768]{1,0:T(8,128)(2,1)S(1)}, bf16[128,768]{1,0:T(8,128)(2,1)S(1)}, u32[]{:S(2)}, u32[]{:S(2)}) collective-permute-start(bf16[128,768]{1,0:T(8,128)(2,1)S(1)} %get-tuple-element.68), channel_id=1, source_target_pairs={{0,2},{1,5},{2,0},{3,7},{4,6},{5,1},{6,4},{7,3},{8,10},{9,13},{10,... | collective-permute-start | bytes 589832 | tf_op jit(solution)/shard_map/ppermute | solution.py:560
  36.7 5.7 %collective-permute-start.14 = (bf16[128,768]{1,0:T(8,128)(2,1)S(1)}, bf16[128,768]{1,0:T(8,128)(2,1)S(1)}, u32[]{:S(2)}, u32[]{:S(2)}) collective-permute-start(bf16[128,768]{1,0:T(8,128)(2,1)S(1)} %get-tuple-element.68), channel_id=1, source_target_pairs={{0,4},{1,3},{2,6},{3,1},{4,0},{5,7},{6,2},{7,5},{8,12},{9,11},{10,... | collective-permute-start | bytes 589832 | tf_op jit(solution)/shard_map/ppermute | solution.py:560
  41.8 4.4 %collective-permute-start.13 = (bf16[128,768]{1,0:T(8,128)(2,1)S(1)}, bf16[128,768]{1,0:T(8,128)(2,1)S(1)}, u32[]{:S(2)}, u32[]{:S(2)}) collective-permute-start(bf16[128,768]{1,0:T(8,128)(2,1)S(1)} %collective-permute-done.11.near), channel_id=1, source_target_pairs={{0,1},{1,0},{2,3},{3,2},{4,5},{5,4},{6,7},{7,6},{8,9},{9,8},{10,11... | collective-permute-start | bytes 589832 | tf_op jit(solution)/shard_map/ppermute | solution.py:553
  42.4 3.9 %collective-permute-start.15 = (bf16[128,768]{1,0:T(8,128)(2,1)S(1)}, bf16[128,768]{1,0:T(8,128)(2,1)S(1)}, u32[]{:S(2)}, u32[]{:S(2)}) collective-permute-start(bf16[128,768]{1,0:T(8,128)(2,1)S(1)} %collective-permute-done.14.far), channel_id=1, source_target_pairs={{0,1},{1,0},{2,3},{3,2},{4,5},{5,4},{6,7},{7,6},{8,9},{9,8},{10,11... | collective-permute-start | bytes 589832 | tf_op jit(solution)/shard_map/ppermute | solution.py:553
  42.5 5.7 %collective-permute-start.12 = (bf16[128,768]{1,0:T(8,128)(2,1)S(1)}, bf16[128,768]{1,0:T(8,128)(2,1)S(1)}, u32[]{:S(2)}, u32[]{:S(2)}) collective-permute-start(bf16[128,768]{1,0:T(8,128)(2,1)S(1)} %collective-permute-done.11.near), channel_id=1, source_target_pairs={{0,4},{1,3},{2,6},{3,1},{4,0},{5,7},{6,2},{7,5},{8,12},{9,11},{10,... | collective-permute-start | bytes 589832 | tf_op jit(solution)/shard_map/ppermute | solution.py:560
  48.2 1.4 %collective-permute-start.16 = (bf16[128,768]{1,0:T(8,128)(2,1)S(1)}, bf16[128,768]{1,0:T(8,128)(2,1)S(1)}, u32[]{:S(2)}, u32[]{:S(2)}) collective-permute-start(bf16[128,768]{1,0:T(8,128)(2,1)S(1)} %collective-permute-done.12.mine), channel_id=1, source_target_pairs={{0,1},{1,0},{2,3},{3,2},{4,5},{5,4},{6,7},{7,6},{8,9},{9,8},{10,11... | collective-permute-start | bytes 589832 | tf_op jit(solution)/shard_map/ppermute | solution.py:553
  48.2 2.8 %copy-start.2 = (bf16[384,768]{1,0:T(8,128)(2,1)S(1)}, bf16[384,768]{1,0:T(8,128)(2,1)}, u32[]{:S(2)}) copy-start(bf16[384,768]{1,0:T(8,128)(2,1)} %weight.3) | copy-start | bytes 1769476
  50.8 1.5 %collective-permute-start.17 = (bf16[256,384]{1,0:T(8,128)(2,1)S(1)}, bf16[256,384]{1,0:T(8,128)(2,1)S(1)}, u32[]{:S(2)}, u32[]{:S(2)}) collective-permute-start(bf16[256,384]{1,0:T(8,128)(2,1)S(1)} %get-tuple-element.99), channel_id=1, source_target_pairs={{0,1},{1,0},{2,3},{3,2},{4,5},{5,4},{6,7},{7,6},{8,9},{9,8},{10,11... | collective-permute-start | bytes 589832 | tf_op jit(solution)/shard_map/ppermute | solution.py:553

commit v6 on v5

--- a/solution.py
+++ b/solution.py
@@ -187,7 +187,7 @@
 def encode_first_kernel(
     tally, softness_far, latents_far, tokens_far, wq_far, wk_far, wv_far, wo_far, do_far,
     message, keys, values, scales, count_out, wq, latents, outputs,
-    count, softness, tokens, wk, wv, arrived,
+    count, softness, tokens, wk, wv, arrived, arrived_later,
 ):
     quad, core = bits_of()
     rows, model = latents.shape[0] // 4, wo_far.shape[1]
@@ -195,11 +195,7 @@
         [
             (tally, count), (tokens_far, tokens), (wk_far, wk), (wv_far, wv), (wq_far, wq),
             (softness_far, softness),
-            *[
-                (quarter(latents_far, quad ^ other, rows), quarter(latents, quad ^ other, rows))
-                for other in (3, 1, 2, 0)
-            ],
-            (wo_far, outputs.at[:, :model]), (do_far, outputs.at[:, model:]),
+            (quarter(latents_far, quad ^ 3, rows), quarter(latents, quad ^ 3, rows)),
         ],
         arrived,
     )
@@ -207,15 +203,29 @@
     is_valid = lax.broadcasted_iota(jnp.int32, keys.shape, 0) < count[0]
     made = nn(tokens[...], wk[...])
     keys[...] = jnp.where(is_valid, made, made[0:1, :]).astype(BF16)
-    wait_all(moves[3:7])
+    wait_all(moves[3:])
+    later = start_all(
+        [
+            (wo_far, outputs.at[:, :model]), (do_far, outputs.at[:, model:]),
+            *[
+                (quarter(latents_far, quad ^ other, rows), quarter(latents, quad ^ other, rows))
+                for other in (1, 2, 0)
+            ],
+        ],
+        arrived_later,
+    )
     values[...] = jnp.where(is_valid, nn(tokens[...], wv[...]), 0.0).astype(BF16)
-    count_out[...] = jnp.full(count_out.shape, count[0], jnp.int32)
-    for which in range(2):
-        row = scale_row(softness, which, wq.shape[1] // HEAD_DIM)
-        scales[which] = jnp.broadcast_to(row, scales.shape[1:])
-    part = quarter(latents, quad ^ 3, rows)[...]
-    encode_into(message, part, wq, keys, values, count_out, scales)
-    wait_all(moves[7:])
+
+    @apart
+    def _():
+        count_out[...] = jnp.full(count_out.shape, count[0], jnp.int32)
+        for which in range(2):
+            row = scale_row(softness, which, wq.shape[1] // HEAD_DIM)
+            scales[which] = jnp.broadcast_to(row, scales.shape[1:])
+        part = quarter(latents, quad ^ 3, rows)[...]
+        encode_into(message, part, wq, keys, values, count_out, scales)
+
+    wait_all(later)
 
 
 def encode_into(message, part, wq, keys, values, count, scales):
@@ -572,7 +582,7 @@
         scratch=[
             pltpu.SMEM(tally.shape, tally.dtype), pltpu.SMEM(softness.shape, F32),
             pltpu.VMEM(tokens.shape, BF16), *[pltpu.VMEM((model, width), BF16)] * 2,
-            pltpu.SemaphoreType.DMA((12,)),
+            pltpu.SemaphoreType.DMA((7,)), pltpu.SemaphoreType.DMA((5,)),
         ],
         flops=attention, name="encode_corner",
     )

time: 54.1 us -> 54.1 us (level)
  no operation moved by 1% of the time
where the time goes in v6:
time: 54.1 us; the launch traced here: 53.6 us
  Pallas kernels  22.3 us (41%)
  starting transfers between devices  18.9 us (35%)
  waiting for transfers between devices  10.7 us (20%)
  between operations  1.71 us (3%)
    pallas_call x21, Pallas kernels, call(): pl.pallas_call(kernel, out_shape=shapes, in_specs=[SPACES[kind] for kind...  22.3 us
    ppermute x11, starting transfers between devices, trade(): return lax.ppermute(array, ('cell', 'qgrp'), pairs)  17.9 us
    ppermute x11, waiting for transfers between devices, trade(): return lax.ppermute(array, ('cell', 'qgrp'), pairs)  9.38 us
    ppermute x7, waiting for transfers between devices, swap(): return lax.ppermute(array, 'qgrp', [(0, 1), (1, 0)])  1.3 us
  transfers between devices with their start and end apart: 18, of which 12 were waited for; matrix products, arithmetic and copies ran while one was open for 0% of the time, Pallas kernels for 28%

profile of v6, /device:TPU:0, one launch (start us, length us, event | category | flops | bytes accessed | tf_op | source)
XLA Modules:
  0.0 53.6 jit_solution(918968957137891754)
XLA Ops:
  1.3 4.2 %encode_corner.1 = (bf16[272,384]{1,0:T(8,128)(2,1)S(1)}, bf16[512,384]{1,0:T(8,128)(2,1)S(1)}, bf16[512,384]{1,0:T(8,128)(2,1)S(1)}, f32[2,8,384]{2,1,0:T(8,128...) custom-call(s32[1]{0:T(128)S(6)} %copy.21.tally, ...), custom_call_target="tpu_custom_call" | custom-call | flops 805306368 | bytes 9674852 | tf_op jit(solution)/shard_map/encode_corner/pallas_call | solution.py:541
  5.5 0.5 collective-permute-start.9
  6.0 2.6 %collective-permute-start = (bf16[272,384]{1,0:T(8,128)(2,1)S(1)}, bf16[272,384]{1,0:T(8,128)(2,1)S(1)}, u32[]{:S(2)}, u32[]{:S(2)}) collective-permute-start(bf16[272,384]{1,0:T(8,128)(2,1)S(1)} %get-tuple-element.59), channel_id=1, source_target_pairs={{0,2},{1,5},{2,0},{3,7},{4,6},{5,1},{6,4},{7,3},{8,10},{9,13},{10,... | collective-permute-start | bytes 626696 | tf_op jit(solution)/shard_map/ppermute | solution.py:570
  8.5 1.5 %encode_side.1.refs_6_ = bf16[272,384]{1,0:T(8,128)(2,1)S(1)} custom-call(s32[8,128]{1,0:T(8,128)S(1)} %get-tuple-element.52.count.refs_0_, f32[2,8,384]{2,1,0:T(8,128)S(1)} %get-tuple-element.51.scales.refs_1_.refs_0_, bf16[1024,768]{1,0:T(8,128)(2,1)S(1)} %get-tuple-element.53.latents.refs_2_.refs_4_, bf16[768,384]{1,0:T(8,128)(2,1)S(1)} %get-tuple-element.54.wq.refs_3_, ...), custom_call_target="tpu_custom_call" | custom-call | flops 805306368 | bytes 3186688 | tf_op jit(solution)/shard_map/encode_side/pallas_call | solution.py:541
  10.1 0.1 collective-permute-start.1
  10.2 1.5 %encode_pass.1 = (f32[256,384]{1,0:T(8,128)S(1)}, f32[8,256]{1,0:T(8,128)S(1)}) custom-call(s32[8,128]{1,0:T(8,128)S(1)} %get-tuple-element.52.count.refs_0_, f32[2,8,384]{2,1,0:T(8,128)S(1)} %get-tuple-element.51.scales.refs_1_.refs_0_, bf16[1024,768]{1,0:T(8,128)(2,1)S(1)} %get-tuple-element.53.latents.refs_2_.refs_4_, ...), custom_call_target="tpu_custom_call" | custom-call | flops 805306368 | bytes 3379200 | tf_op jit(solution)/shard_map/encode_pass/pallas_call | solution.py:541
  11.7 0.0 copy-start.3
  11.7 0.0 copy-start.4
  11.7 0.0 copy-start.5
  11.8 0.6 %collective-permute-done.came = bf16[272,384]{1,0:T(8,128)(2,1)S(1)} collective-permute-done((bf16[272,384]{1,0:T(8,128)(2,1)S(1)}, bf16[272,384]{1,0:T(8,128)(2,1)S(1)}, u32[]{:S(2)}, u32[]{:S(2)}) %collective-permute-start) | collective-permute-done | bytes 208928 | tf_op jit(solution)/shard_map/ppermute | solution.py:570
  12.3 0.3 merge_pass.1
  12.6 2.1 %collective-permute-start.2 = (bf16[136,384]{1,0:T(8,128)(2,1)S(1)}, bf16[136,384]{1,0:T(8,128)(2,1)S(1)}, u32[]{:S(2)}, u32[]{:S(2)}) collective-permute-start(bf16[136,384]{1,0:T(8,128)(2,1)S(1)} %get-tuple-element.60.refs_6_), channel_id=1, source_target_pairs={{0,4},{1,3},{2,6},{3,1},{4,0},{5,7},{6,2},{7,5},{8,12},{9,11},{10,... | collective-permute-start | bytes 313352 | tf_op jit(solution)/shard_map/ppermute | solution.py:570
  14.7 0.1 collective-permute-start.3
  14.8 1.5 %encode_own.1 = (f32[256,384]{1,0:T(8,128)S(1)}, f32[8,256]{1,0:T(8,128)S(1)}) custom-call(s32[8,128]{1,0:T(8,128)S(1)} %get-tuple-element.52.count.refs_0_, f32[2,8,384]{2,1,0:T(8,128)S(1)} %get-tuple-element.51.scales.refs_1_.refs_0_, bf16[1024,768]{1,0:T(8,128)(2,1)S(1)} %get-tuple-element.53.latents.refs_2_.refs_4_, ...), custom_call_target="tpu_custom_call" | custom-call | flops 805306368 | bytes 3379200 | tf_op jit(solution)/shard_map/encode_own/pallas_call | solution.py:541
  16.4 0.4 collective-permute-done.1.first.refs_2_
  16.7 0.7 %collective-permute-done.2.second = bf16[136,384]{1,0:T(8,128)(2,1)S(1)} collective-permute-done((bf16[136,384]{1,0:T(8,128)(2,1)S(1)}, bf16[136,384]{1,0:T(8,128)(2,1)S(1)}, u32[]{:S(2)}, u32[]{:S(2)}) %collective-permute-start.2) | collective-permute-done | bytes 104480 | tf_op jit(solution)/shard_map/ppermute | solution.py:570
  17.4 0.3 merge_sides.2.refs_4_.refs_5_.mine
  17.7 0.0 copy-start.6
  17.7 0.0 copy-start.1
  17.7 2.1 %collective-permute-start.5 = (bf16[136,384]{1,0:T(8,128)(2,1)S(1)}, bf16[136,384]{1,0:T(8,128)(2,1)S(1)}, u32[]{:S(2)}, u32[]{:S(2)}) collective-permute-start(bf16[136,384]{1,0:T(8,128)(2,1)S(1)} %merge_sides.2.refs_4_.refs_5_.mine), channel_id=1, source_target_pairs={{0,8},{1,17},{2,10},{3,19},{4,12},{5,21},{6,14},{7,23},{8,0},{9,25... | collective-permute-start | bytes 313352 | tf_op jit(solution)/shard_map/ppermute | solution.py:570
  19.8 0.0 collective-permute-done.3.refs_3_
  19.9 0.3 merge_sides.3.refs_6_.refs_0_
  20.1 1.2 %collective-permute-start.4 = (bf16[136,384]{1,0:T(8,128)(2,1)S(1)}, bf16[136,384]{1,0:T(8,128)(2,1)S(1)}, u32[]{:S(2)}, u32[]{:S(2)}) collective-permute-start(bf16[136,384]{1,0:T(8,128)(2,1)S(1)} %merge_sides.3.refs_6_.refs_0_), channel_id=1, source_target_pairs={{0,8},{1,17},{2,10},{3,19},{4,12},{5,21},{6,14},{7,23},{8,0},{9,25... | collective-permute-start | bytes 313352 | tf_op jit(solution)/shard_map/ppermute | solution.py:570
  21.3 2.0 %collective-permute-done.5.came = bf16[136,384]{1,0:T(8,128)(2,1)S(1)} collective-permute-done((bf16[136,384]{1,0:T(8,128)(2,1)S(1)}, bf16[136,384]{1,0:T(8,128)(2,1)S(1)}, u32[]{:S(2)}, u32[]{:S(2)}) %collective-permute-start.5) | collective-permute-done | bytes 104480 | tf_op jit(solution)/shard_map/ppermute | solution.py:570
  23.3 0.2 merge_even.4.refs_2_.refs_0_
  23.5 2.6 %collective-permute-start.7 = (bf16[136,384]{1,0:T(8,128)(2,1)S(1)}, bf16[136,384]{1,0:T(8,128)(2,1)S(1)}, u32[]{:S(2)}, u32[]{:S(2)}) collective-permute-start(bf16[136,384]{1,0:T(8,128)(2,1)S(1)} %merge_even.4.refs_2_.refs_0_), channel_id=1, source_target_pairs={{0,16},{1,9},{2,18},{3,11},{4,20},{5,13},{6,22},{7,15},{8,24},{9,1... | collective-permute-start | bytes 313352 | tf_op jit(solution)/shard_map/ppermute | solution.py:570
  26.1 0.0 collective-permute-done.4.refs_1_
  26.1 0.2 merge_even.5.refs_0_
  26.4 1.8 %collective-permute-start.6 = (bf16[136,384]{1,0:T(8,128)(2,1)S(1)}, bf16[136,384]{1,0:T(8,128)(2,1)S(1)}, u32[]{:S(2)}, u32[]{:S(2)}) collective-permute-start(bf16[136,384]{1,0:T(8,128)(2,1)S(1)} %merge_even.5.refs_0_), channel_id=1, source_target_pairs={{0,16},{1,9},{2,18},{3,11},{4,20},{5,13},{6,22},{7,15},{8,24},{9,1... | collective-permute-start | bytes 313352 | tf_op jit(solution)/shard_map/ppermute | solution.py:570
  28.2 0.0 copy-done
  28.2 0.0 copy-done.3
  28.2 0.7 %decode_prepare.1 = (bf16[3,512,256]{2,1,0:T(8,128)(2,1)S(1)}, bf16[768,512]{1,0:T(8,128)(2,1)S(1)}, bf16[768,256]{1,0:T(8,128)(2,1)S(1)}) custom-call(f32[2,8,384]{2,1,0:T(8,128)S(1)} %get-tuple-element.51.scales.refs_1_.refs_0_, bf16[512,768]{1,0:T(8,128)(2,1)S(1)} %copy-done, bf16[768,384]{1,0:T(8,128)(2,1)S(1)} %copy-done.3, ...), custom_call_target="tpu_custom_call" | custom-call | bytes 4546560 | tf_op jit(solution)/shard_map/decode_prepare/pallas_call | solution.py:541
  28.9 0.5 collective-permute-done.7.refs_1_
  29.4 0.2 merge_even.6.refs_2_.refs_0_
  29.7 0.1 collective-permute-start.10
  29.8 2.7 %collective-permute-done.6.refs_1_ = bf16[136,384]{1,0:T(8,128)(2,1)S(1)} collective-permute-done((bf16[136,384]{1,0:T(8,128)(2,1)S(1)}, bf16[136,384]{1,0:T(8,128)(2,1)S(1)}, u32[]{:S(2)}, u32[]{:S(2)}) %collective-permute-start.6) | collective-permute-done | bytes 104480 | tf_op jit(solution)/shard_map/ppermute | solution.py:570
  32.5 0.2 merge_even.7.refs_6_.attended
  32.7 0.1 collective-permute-start.8
  32.8 0.0 collective-permute-done.10.refs_1_
  32.8 0.0 collective-permute-done.9.refs_3_.other_weight.weight
  32.9 0.5 latent_low.1.refs_0_
  33.4 0.7 %collective-permute-done.8.other = bf16[128,384]{1,0:T(8,128)(2,1)S(1)} collective-permute-done((bf16[128,384]{1,0:T(8,128)(2,1)S(1)}, bf16[128,384]{1,0:T(8,128)(2,1)S(1)}, u32[]{:S(2)}, u32[]{:S(2)}) %collective-permute-start.8) | collective-permute-done | bytes 98336 | tf_op jit(solution)/shard_map/ppermute | solution.py:563
  34.1 0.5 latent.1
  34.6 2.1 %collective-permute-start.11 = (bf16[128,768]{1,0:T(8,128)(2,1)S(1)}, bf16[128,768]{1,0:T(8,128)(2,1)S(1)}, u32[]{:S(2)}, u32[]{:S(2)}) collective-permute-start(bf16[128,768]{1,0:T(8,128)(2,1)S(1)} %get-tuple-element.68), channel_id=1, source_target_pairs={{0,2},{1,5},{2,0},{3,7},{4,6},{5,1},{6,4},{7,3},{8,10},{9,13},{10,... | collective-permute-start | bytes 589832 | tf_op jit(solution)/shard_map/ppermute | solution.py:570
  36.7 1.5 %collective-permute-start.14 = (bf16[128,768]{1,0:T(8,128)(2,1)S(1)}, bf16[128,768]{1,0:T(8,128)(2,1)S(1)}, u32[]{:S(2)}, u32[]{:S(2)}) collective-permute-start(bf16[128,768]{1,0:T(8,128)(2,1)S(1)} %get-tuple-element.68), channel_id=1, source_target_pairs={{0,4},{1,3},{2,6},{3,1},{4,0},{5,7},{6,2},{7,5},{8,12},{9,11},{10,... | collective-permute-start | bytes 589832 | tf_op jit(solution)/shard_map/ppermute | solution.py:570
  38.2 2.1 %decode_own.1 = (f32[1024,768]{1,0:T(8,128)}, f32[512,256]{1,0:T(8,128)S(1)}, f32[512,256]{1,0:T(8,128)S(1)}, f32[512,256]{1,0:T(8,128)S(1)}, f32[512,128]{1,0:T...) custom-call(bf16[3,512,256]{2,1,0:T(8,128)(2,1)S(1)} %get-tuple-element.64.refs_2_.refs_3_.queries.refs_0_, ...), custom_call_target="tpu_custom_call" | custom-call | flops 805306368 | bytes 7864320 | tf_op jit(solution)/shard_map/decode_own/pallas_call | solution.py:541
  40.4 1.4 %collective-permute-done.11.near = bf16[128,768]{1,0:T(8,128)(2,1)S(1)} collective-permute-done((bf16[128,768]{1,0:T(8,128)(2,1)S(1)}, bf16[128,768]{1,0:T(8,128)(2,1)S(1)}, u32[]{:S(2)}, u32[]{:S(2)}) %collective-permute-start.11) | collective-permute-done | bytes 196640 | tf_op jit(solution)/shard_map/ppermute | solution.py:570
  41.8 0.0 collective-permute-start.13
  41.8 0.6 %collective-permute-done.14.far = bf16[128,768]{1,0:T(8,128)(2,1)S(1)} collective-permute-done((bf16[128,768]{1,0:T(8,128)(2,1)S(1)}, bf16[128,768]{1,0:T(8,128)(2,1)S(1)}, u32[]{:S(2)}, u32[]{:S(2)}) %collective-permute-start.14) | collective-permute-done | bytes 196640 | tf_op jit(solution)/shard_map/ppermute | solution.py:570
  42.3 0.1 collective-permute-start.15
  42.5 1.7 %collective-permute-start.12 = (bf16[128,768]{1,0:T(8,128)(2,1)S(1)}, bf16[128,768]{1,0:T(8,128)(2,1)S(1)}, u32[]{:S(2)}, u32[]{:S(2)}) collective-permute-start(bf16[128,768]{1,0:T(8,128)(2,1)S(1)} %collective-permute-done.11.near), channel_id=1, source_target_pairs={{0,4},{1,3},{2,6},{3,1},{4,0},{5,7},{6,2},{7,5},{8,12},{9,11},{10,... | collective-permute-start | bytes 589832 | tf_op jit(solution)/shard_map/ppermute | solution.py:570
  44.2 2.0 %decode_sides.2 = (f32[1024,768]{1,0:T(8,128)}, f32[512,256]{1,0:T(8,128)S(1)}, f32[512,256]{1,0:T(8,128)S(1)}, f32[512,256]{1,0:T(8,128)S(1)}, f32[512,128]{1,0...) custom-call(bf16[3,512,256]{2,1,0:T(8,128)(2,1)S(1)} %get-tuple-element.64.refs_2_., ...), custom_call_target="tpu_custom_call", output_to_operand_aliasing={{0}: (5, {})} | custom-call | flops 805306368 | bytes 13369344 | tf_op jit(solution)/shard_map/decode_sides/pallas_call | solution.py:541
  46.2 0.0 collective-permute-done.13.near.refs_2_
  46.2 0.0 collective-permute-done.15.far.refs_3_
  46.2 1.3 %decode_sides.3 = (f32[1024,768]{1,0:T(8,128)}, f32[512,256]{1,0:T(8,128)S(1)}, f32[512,256]{1,0:T(8,128)S(1)}, f32[512,256]{1,0:T(8,128)S(1)}) custom-call(bf16[3,512,256]{2,1,0:T(8,128)(2,1)S(1)} %get-tuple-element.64.refs_2_.refs_3_.queries.refs_0_, bf16[768,512]{1,0:T(8,128)(2,1)S(1)} %get-tuple-element.65.weights, ...), custom_call_target="tpu_custom_call", output_to_operand_aliasing={{0}: (5, {})} | custom-call | flops 805306368 | bytes 11796480 | tf_op jit(solution)/shard_map/decode_sides/pallas_call | solution.py:541
  47.5 0.6 %collective-permute-done.12.mine = bf16[128,768]{1,0:T(8,128)(2,1)S(1)} collective-permute-done((bf16[128,768]{1,0:T(8,128)(2,1)S(1)}, bf16[128,768]{1,0:T(8,128)(2,1)S(1)}, u32[]{:S(2)}, u32[]{:S(2)}) %collective-permute-start.12) | collective-permute-done | bytes 196640 | tf_op jit(solution)/shard_map/ppermute | solution.py:570
  48.1 0.0 collective-permute-start.16
  48.1 0.9 %decode_rest.1 = (f32[512,128]{1,0:T(8,128)S(1)}, f32[512,128]{1,0:T(8,128)S(1)}, f32[512,128]{1,0:T(8,128)S(1)}) custom-call(bf16[3,512,256]{2,1,0:T(8,128)(2,1)S(1)} %get-tuple-element.64.refs_2_.refs_3_.queries.refs_0_, bf16[768,256]{1,0:T(8,128)(2,1)S(1)} %get-tuple-element.66.more_weights.refs_1_, ...), custom_call_target="tpu_custom_call" | custom-call | flops 805306368 | bytes 3145728 | tf_op jit(solution)/shard_map/decode_rest/pallas_call | solution.py:541
  49.1 0.5 collective-permute-done.16.came
  49.6 1.2 %decode_send.1 = (bf16[256,384]{1,0:T(8,128)(2,1)S(1)}, bf16[256,512]{1,0:T(8,128)(2,1)S(1)}, bf16[256,256]{1,0:T(8,128)(2,1)S(1)}) custom-call(bf16[3,512,256]{2,1,0:T(8,128)(2,1)S(1)} %get-tuple-element.64.refs_2_.refs_3_.queries.refs_0_, bf16[768,512]{1,0:T(8,128)(2,1)S(1)} %get-tuple-element.65.weights, ...), custom_call_target="tpu_custom_call" | custom-call | flops 402653184 | bytes 5308416 | tf_op jit(solution)/shard_map/decode_send/pallas_call | solution.py:541
  50.8 0.2 collective-permute-start.17
  51.0 1.2 %decode_keep.1 = (f32[1024,768]{1,0:T(8,128)}, f32[256,768]{1,0:T(8,128)S(1)}) custom-call(bf16[3,512,256]{2,1,0:T(8,128)(2,1)S(1)} %get-tuple-element.64.refs_2_.refs_3_.queries.refs_0_, bf16[256,512]{1,0:T(8,128)(2,1)S(1)} %get-tuple-element.94.both, bf16[256,256]{1,0:T(8,128)(2,1)S(1)} %get-tuple-element.95.more_both, ...), custom_call_target="tpu_custom_call", output_to_operand_aliasing={{0}: (7, {})} | custom-call | flops 402653184 | bytes 12386304 | tf_op jit(solution)/shard_map/decode_keep/pallas_call | solution.py:541
  52.2 0.1 collective-permute-done.17.other
  52.3 1.2 %tokens.3 = f32[256,768]{1,0:T(8,128)} custom-call(s32[8,128]{1,0:T(8,128)S(1)} %get-tuple-element.52.count.refs_0_, f32[256,768]{1,0:T(8,128)S(1)} %get-tuple-element.98.base, bf16[256,384]{1,0:T(8,128)(2,1)S(1)} %collective-permute-done.17.other, bf16[384,1536]{1,0:T(8,128)(2,1)S(1)} %collective-permute-done.9.refs_3_.other_weight.weight), custom_call_target="tpu_custom_call" | custom-call | bytes 2953216 | tf_op jit(solution)/shard_map/tokens/pallas_call | solution.py:541
  (8 shorter events, 0.0 us)
Async XLA Ops:
  5.5 27.4 %collective-permute-start.9 = (bf16[384,1536]{1,0:T(8,128)(2,1)S(1)}, bf16[384,1536]{1,0:T(8,128)(2,1)S(1)}, u32[]{:S(2)}, u32[]{:S(2)}) collective-permute-start(bf16[384,1536]{1,0:T(8,128)(2,1)S(1)} %get-tuple-element.67), channel_id=1, source_target_pairs={{0,1},{1,0},{2,3},{3,2},{4,5},{5,4},{6,7},{7,6},{8,9},{9,8},{10,11... | collective-permute-start | bytes 3538952 | tf_op jit(solution)/shard_map/ppermute | solution.py:563
  6.0 6.3 %collective-permute-start = (bf16[272,384]{1,0:T(8,128)(2,1)S(1)}, bf16[272,384]{1,0:T(8,128)(2,1)S(1)}, u32[]{:S(2)}, u32[]{:S(2)}) collective-permute-start(bf16[272,384]{1,0:T(8,128)(2,1)S(1)} %get-tuple-element.59), channel_id=1, source_target_pairs={{0,2},{1,5},{2,0},{3,7},{4,6},{5,1},{6,4},{7,3},{8,10},{9,13},{10,... | collective-permute-start | bytes 626696 | tf_op jit(solution)/shard_map/ppermute | solution.py:570
  10.1 6.6 %collective-permute-start.1 = (bf16[272,384]{1,0:T(8,128)(2,1)S(1)}, bf16[272,384]{1,0:T(8,128)(2,1)S(1)}, u32[]{:S(2)}, u32[]{:S(2)}) collective-permute-start(bf16[272,384]{1,0:T(8,128)(2,1)S(1)} %encode_side.1.refs_6_), channel_id=1, source_target_pairs={{0,2},{1,5},{2,0},{3,7},{4,6},{5,1},{6,4},{7,3},{8,10},{9,13},{10,... | collective-permute-start | bytes 626696 | tf_op jit(solution)/shard_map/ppermute | solution.py:570
  11.7 16.5 %copy-start = (bf16[512,768]{1,0:T(8,128)(2,1)S(1)}, bf16[512,768]{1,0:T(8,128)(2,1)}, u32[]{:S(2)}) copy-start(bf16[512,768]{1,0:T(8,128)(2,1)} %tokens.2) | copy-start | bytes 2359300
  11.7 16.5 %copy-start.3 = (bf16[768,384]{1,0:T(8,128)(2,1)S(1)}, bf16[768,384]{1,0:T(8,128)(2,1)}, u32[]{:S(2)}) copy-start(bf16[768,384]{1,0:T(8,128)(2,1)} %refs_2_.2) | copy-start | bytes 1769476
  11.7 16.4 %copy-start.4 = (bf16[768,384]{1,0:T(8,128)(2,1)S(1)}, bf16[768,384]{1,0:T(8,128)(2,1)}, u32[]{:S(2)}) copy-start(bf16[768,384]{1,0:T(8,128)(2,1)} %refs_3_.1) | copy-start | bytes 1769476
  11.7 16.4 %copy-start.5 = (bf16[768,384]{1,0:T(8,128)(2,1)S(1)}, bf16[768,384]{1,0:T(8,128)(2,1)}, u32[]{:S(2)}) copy-start(bf16[768,384]{1,0:T(8,128)(2,1)} %refs_4_.1) | copy-start | bytes 1769476
  12.6 4.8 %collective-permute-start.2 = (bf16[136,384]{1,0:T(8,128)(2,1)S(1)}, bf16[136,384]{1,0:T(8,128)(2,1)S(1)}, u32[]{:S(2)}, u32[]{:S(2)}) collective-permute-start(bf16[136,384]{1,0:T(8,128)(2,1)S(1)} %get-tuple-element.60.refs_6_), channel_id=1, source_target_pairs={{0,4},{1,3},{2,6},{3,1},{4,0},{5,7},{6,2},{7,5},{8,12},{9,11},{10,... | collective-permute-start | bytes 313352 | tf_op jit(solution)/shard_map/ppermute | solution.py:570
  14.7 5.1 %collective-permute-start.3 = (bf16[136,384]{1,0:T(8,128)(2,1)S(1)}, bf16[136,384]{1,0:T(8,128)(2,1)S(1)}, u32[]{:S(2)}, u32[]{:S(2)}) collective-permute-start(bf16[136,384]{1,0:T(8,128)(2,1)S(1)} %get-tuple-element.61.refs_7_), channel_id=1, source_target_pairs={{0,4},{1,3},{2,6},{3,1},{4,0},{5,7},{6,2},{7,5},{8,12},{9,11},{10,... | collective-permute-start | bytes 313352 | tf_op jit(solution)/shard_map/ppermute | solution.py:570
  17.7 15.1 %copy-start.6 = (f32[768]{0:T(1024)S(1)}, f32[768]{0:T(1024)}, u32[]{:S(2)}) copy-start(f32[768]{0:T(1024)} %param.25) | copy-start | bytes 9220
  17.7 15.2 %copy-start.1 = (bf16[384,768]{1,0:T(8,128)(2,1)S(1)}, bf16[384,768]{1,0:T(8,128)(2,1)}, u32[]{:S(2)}) copy-start(bf16[384,768]{1,0:T(8,128)(2,1)} %weight.2) | copy-start | bytes 1769476
  17.7 5.6 %collective-permute-start.5 = (bf16[136,384]{1,0:T(8,128)(2,1)S(1)}, bf16[136,384]{1,0:T(8,128)(2,1)S(1)}, u32[]{:S(2)}, u32[]{:S(2)}) collective-permute-start(bf16[136,384]{1,0:T(8,128)(2,1)S(1)} %merge_sides.2.refs_4_.refs_5_.mine), channel_id=1, source_target_pairs={{0,8},{1,17},{2,10},{3,19},{4,12},{5,21},{6,14},{7,23},{8,0},{9,25... | collective-permute-start | bytes 313352 | tf_op jit(solution)/shard_map/ppermute | solution.py:570
  20.1 6.0 %collective-permute-start.4 = (bf16[136,384]{1,0:T(8,128)(2,1)S(1)}, bf16[136,384]{1,0:T(8,128)(2,1)S(1)}, u32[]{:S(2)}, u32[]{:S(2)}) collective-permute-start(bf16[136,384]{1,0:T(8,128)(2,1)S(1)} %merge_sides.3.refs_6_.refs_0_), channel_id=1, source_target_pairs={{0,8},{1,17},{2,10},{3,19},{4,12},{5,21},{6,14},{7,23},{8,0},{9,25... | collective-permute-start | bytes 313352 | tf_op jit(solution)/shard_map/ppermute | solution.py:570
  23.5 5.9 %collective-permute-start.7 = (bf16[136,384]{1,0:T(8,128)(2,1)S(1)}, bf16[136,384]{1,0:T(8,128)(2,1)S(1)}, u32[]{:S(2)}, u32[]{:S(2)}) collective-permute-start(bf16[136,384]{1,0:T(8,128)(2,1)S(1)} %merge_even.4.refs_2_.refs_0_), channel_id=1, source_target_pairs={{0,16},{1,9},{2,18},{3,11},{4,20},{5,13},{6,22},{7,15},{8,24},{9,1... | collective-permute-start | bytes 313352 | tf_op jit(solution)/shard_map/ppermute | solution.py:570
  26.4 6.1 %collective-permute-start.6 = (bf16[136,384]{1,0:T(8,128)(2,1)S(1)}, bf16[136,384]{1,0:T(8,128)(2,1)S(1)}, u32[]{:S(2)}, u32[]{:S(2)}) collective-permute-start(bf16[136,384]{1,0:T(8,128)(2,1)S(1)} %merge_even.5.refs_0_), channel_id=1, source_target_pairs={{0,16},{1,9},{2,18},{3,11},{4,20},{5,13},{6,22},{7,15},{8,24},{9,1... | collective-permute-start | bytes 313352 | tf_op jit(solution)/shard_map/ppermute | solution.py:570
  29.7 3.1 %collective-permute-start.10 = (bf16[128,384]{1,0:T(8,128)(2,1)S(1)}, bf16[128,384]{1,0:T(8,128)(2,1)S(1)}, u32[]{:S(2)}, u32[]{:S(2)}) collective-permute-start(bf16[128,384]{1,0:T(8,128)(2,1)S(1)} %merge_even.6.refs_2_.refs_0_), channel_id=1, source_target_pairs={{0,1},{1,0},{2,3},{3,2},{4,5},{5,4},{6,7},{7,6},{8,9},{9,8},{10,11... | collective-permute-start | bytes 294920 | tf_op jit(solution)/shard_map/ppermute | solution.py:563
  32.7 1.4 %collective-permute-start.8 = (bf16[128,384]{1,0:T(8,128)(2,1)S(1)}, bf16[128,384]{1,0:T(8,128)(2,1)S(1)}, u32[]{:S(2)}, u32[]{:S(2)}) collective-permute-start(bf16[128,384]{1,0:T(8,128)(2,1)S(1)} %merge_even.7.refs_6_.attended), channel_id=1, source_target_pairs={{0,1},{1,0},{2,3},{3,2},{4,5},{5,4},{6,7},{7,6},{8,9},{9,8},{10,11... | collective-permute-start | bytes 294920 | tf_op jit(solution)/shard_map/ppermute | solution.py:563
  34.6 7.2 %collective-permute-start.11 = (bf16[128,768]{1,0:T(8,128)(2,1)S(1)}, bf16[128,768]{1,0:T(8,128)(2,1)S(1)}, u32[]{:S(2)}, u32[]{:S(2)}) collective-permute-start(bf16[128,768]{1,0:T(8,128)(2,1)S(1)} %get-tuple-element.68), channel_id=1, source_target_pairs={{0,2},{1,5},{2,0},{3,7},{4,6},{5,1},{6,4},{7,3},{8,10},{9,13},{10,... | collective-permute-start | bytes 589832 | tf_op jit(solution)/shard_map/ppermute | solution.py:570
  36.7 5.7 %collective-permute-start.14 = (bf16[128,768]{1,0:T(8,128)(2,1)S(1)}, bf16[128,768]{1,0:T(8,128)(2,1)S(1)}, u32[]{:S(2)}, u32[]{:S(2)}) collective-permute-start(bf16[128,768]{1,0:T(8,128)(2,1)S(1)} %get-tuple-element.68), channel_id=1, source_target_pairs={{0,4},{1,3},{2,6},{3,1},{4,0},{5,7},{6,2},{7,5},{8,12},{9,11},{10,... | collective-permute-start | bytes 589832 | tf_op jit(solution)/shard_map/ppermute | solution.py:570
  41.8 4.4 %collective-permute-start.13 = (bf16[128,768]{1,0:T(8,128)(2,1)S(1)}, bf16[128,768]{1,0:T(8,128)(2,1)S(1)}, u32[]{:S(2)}, u32[]{:S(2)}) collective-permute-start(bf16[128,768]{1,0:T(8,128)(2,1)S(1)} %collective-permute-done.11.near), channel_id=1, source_target_pairs={{0,1},{1,0},{2,3},{3,2},{4,5},{5,4},{6,7},{7,6},{8,9},{9,8},{10,11... | collective-permute-start | bytes 589832 | tf_op jit(solution)/shard_map/ppermute | solution.py:563
  42.3 3.9 %collective-permute-start.15 = (bf16[128,768]{1,0:T(8,128)(2,1)S(1)}, bf16[128,768]{1,0:T(8,128)(2,1)S(1)}, u32[]{:S(2)}, u32[]{:S(2)}) collective-permute-start(bf16[128,768]{1,0:T(8,128)(2,1)S(1)} %collective-permute-done.14.far), channel_id=1, source_target_pairs={{0,1},{1,0},{2,3},{3,2},{4,5},{5,4},{6,7},{7,6},{8,9},{9,8},{10,11... | collective-permute-start | bytes 589832 | tf_op jit(solution)/shard_map/ppermute | solution.py:563
  42.5 5.7 %collective-permute-start.12 = (bf16[128,768]{1,0:T(8,128)(2,1)S(1)}, bf16[128,768]{1,0:T(8,128)(2,1)S(1)}, u32[]{:S(2)}, u32[]{:S(2)}) collective-permute-start(bf16[128,768]{1,0:T(8,128)(2,1)S(1)} %collective-permute-done.11.near), channel_id=1, source_target_pairs={{0,4},{1,3},{2,6},{3,1},{4,0},{5,7},{6,2},{7,5},{8,12},{9,11},{10,... | collective-permute-start | bytes 589832 | tf_op jit(solution)/shard_map/ppermute | solution.py:570
  48.1 1.4 %collective-permute-start.16 = (bf16[128,768]{1,0:T(8,128)(2,1)S(1)}, bf16[128,768]{1,0:T(8,128)(2,1)S(1)}, u32[]{:S(2)}, u32[]{:S(2)}) collective-permute-start(bf16[128,768]{1,0:T(8,128)(2,1)S(1)} %collective-permute-done.12.mine), channel_id=1, source_target_pairs={{0,1},{1,0},{2,3},{3,2},{4,5},{5,4},{6,7},{7,6},{8,9},{9,8},{10,11... | collective-permute-start | bytes 589832 | tf_op jit(solution)/shard_map/ppermute | solution.py:563
  48.1 2.8 %copy-start.2 = (bf16[384,768]{1,0:T(8,128)(2,1)S(1)}, bf16[384,768]{1,0:T(8,128)(2,1)}, u32[]{:S(2)}) copy-start(bf16[384,768]{1,0:T(8,128)(2,1)} %weight.3) | copy-start | bytes 1769476
  50.8 1.5 %collective-permute-start.17 = (bf16[256,384]{1,0:T(8,128)(2,1)S(1)}, bf16[256,384]{1,0:T(8,128)(2,1)S(1)}, u32[]{:S(2)}, u32[]{:S(2)}) collective-permute-start(bf16[256,384]{1,0:T(8,128)(2,1)S(1)} %get-tuple-element.99), channel_id=1, source_target_pairs={{0,1},{1,0},{2,3},{3,2},{4,5},{5,4},{6,7},{7,6},{8,9},{9,8},{10,11... | collective-permute-start | bytes 589832 | tf_op jit(solution)/shard_map/ppermute | solution.py:563

commit v7 on v6

--- a/solution.py
+++ b/solution.py
@@ -650,7 +650,6 @@
         name="latent",
     )
     first = trade(own_half, 1, 2)
-    second = trade(own_half, 2, 1)
     whole = ((total_rows, model), F32)
     states_out = [((slots, size), F32) for size in sizes for _ in range(3)]
 
@@ -661,6 +660,8 @@
         decode_own_kernel, "vvvv", [whole, *states_out], queries, *weights, own,
         far=(0,), scratch=scratch(rows, 1), flops=attention, name="decode_own",
     )
+    own_half, states[0] = lax.optimization_barrier((own_half, states[0]))
+    second = trade(own_half, 2, 1)
     first, states[0] = lax.optimization_barrier((first, states[0]))
     third = trade(first, 2, 1)
 

time: 54.1 us -> 56.4 us (1.043)
  waiting for transfers between devices: 10.7 us -> 13 us
    ppermute x11, waiting for transfers between devices: 9.38 us -> 11.7 us  [trade(): return lax.ppermute(array, ('cell', 'qgrp'), pairs)]
  transfers between devices with their start and end apart: 18 -> 18, of which waited for: 12 -> 11; matrix products, arithmetic and copies ran while one was open for 0% -> 0% of each run, Pallas kernels for 28% -> 27%
where the time goes in v7:
time: 56.4 us; the launch traced here: 56.2 us
  Pallas kernels  22.3 us (40%)
  starting transfers between devices  19.1 us (34%)
  waiting for transfers between devices  13 us (23%)
  between operations  1.71 us (3%)
    pallas_call x21, Pallas kernels, call(): pl.pallas_call(kernel, out_shape=shapes, in_specs=[SPACES[kind] for kind...  22.3 us
    ppermute x11, starting transfers between devices, trade(): return lax.ppermute(array, ('cell', 'qgrp'), pairs)  17.8 us
    ppermute x11, waiting for transfers between devices, trade(): return lax.ppermute(array, ('cell', 'qgrp'), pairs)  11.7 us
    ppermute x7, starting transfers between devices, swap(): return lax.ppermute(array, 'qgrp', [(0, 1), (1, 0)])  1.38 us
    ppermute x7, waiting for transfers between devices, swap(): return lax.ppermute(array, 'qgrp', [(0, 1), (1, 0)])  1.3 us
  transfers between devices with their start and end apart: 18, of which 11 were waited for; matrix products, arithmetic and copies ran while one was open for 0% of the time, Pallas kernels for 27%

profile of v7, /device:TPU:0, one launch (start us, length us, event | category | flops | bytes accessed | tf_op | source)
XLA Modules:
  0.0 56.2 jit_solution(1479075176846247358)
XLA Ops:
  1.3 4.2 %encode_corner.1 = (bf16[272,384]{1,0:T(8,128)(2,1)S(1)}, bf16[512,384]{1,0:T(8,128)(2,1)S(1)}, bf16[512,384]{1,0:T(8,128)(2,1)S(1)}, f32[2,8,384]{2,1,0:T(8,128...) custom-call(s32[1]{0:T(128)S(6)} %copy.21.tally, ...), custom_call_target="tpu_custom_call" | custom-call | flops 805306368 | bytes 9674852 | tf_op jit(solution)/shard_map/encode_corner/pallas_call | solution.py:541
  5.5 0.5 collective-permute-start.9
  6.0 2.6 %collective-permute-start = (bf16[272,384]{1,0:T(8,128)(2,1)S(1)}, bf16[272,384]{1,0:T(8,128)(2,1)S(1)}, u32[]{:S(2)}, u32[]{:S(2)}) collective-permute-start(bf16[272,384]{1,0:T(8,128)(2,1)S(1)} %get-tuple-element.61), channel_id=1, source_target_pairs={{0,2},{1,5},{2,0},{3,7},{4,6},{5,1},{6,4},{7,3},{8,10},{9,13},{10,... | collective-permute-start | bytes 626696 | tf_op jit(solution)/shard_map/ppermute | solution.py:570
  8.5 1.5 %encode_side.1.refs_6_ = bf16[272,384]{1,0:T(8,128)(2,1)S(1)} custom-call(s32[8,128]{1,0:T(8,128)S(1)} %get-tuple-element.54.count.refs_0_, f32[2,8,384]{2,1,0:T(8,128)S(1)} %get-tuple-element.53.scales.refs_1_.refs_0_, bf16[1024,768]{1,0:T(8,128)(2,1)S(1)} %get-tuple-element.55.latents.refs_2_.refs_4_, bf16[768,384]{1,0:T(8,128)(2,1)S(1)} %get-tuple-element.56.wq.refs_3_, ...), custom_call_target="tpu_custom_call" | custom-call | flops 805306368 | bytes 3186688 | tf_op jit(solution)/shard_map/encode_side/pallas_call | solution.py:541
  10.1 0.1 collective-permute-start.1
  10.2 1.5 %encode_pass.1 = (f32[256,384]{1,0:T(8,128)S(1)}, f32[8,256]{1,0:T(8,128)S(1)}) custom-call(s32[8,128]{1,0:T(8,128)S(1)} %get-tuple-element.54.count.refs_0_, f32[2,8,384]{2,1,0:T(8,128)S(1)} %get-tuple-element.53.scales.refs_1_.refs_0_, bf16[1024,768]{1,0:T(8,128)(2,1)S(1)} %get-tuple-element.55.latents.refs_2_.refs_4_, ...), custom_call_target="tpu_custom_call" | custom-call | flops 805306368 | bytes 3379200 | tf_op jit(solution)/shard_map/encode_pass/pallas_call | solution.py:541
  11.7 0.0 copy-start.3
  11.7 0.0 copy-start.4
  11.7 0.0 copy-start.5
  11.8 0.6 %collective-permute-done.came = bf16[272,384]{1,0:T(8,128)(2,1)S(1)} collective-permute-done((bf16[272,384]{1,0:T(8,128)(2,1)S(1)}, bf16[272,384]{1,0:T(8,128)(2,1)S(1)}, u32[]{:S(2)}, u32[]{:S(2)}) %collective-permute-start) | collective-permute-done | bytes 208928 | tf_op jit(solution)/shard_map/ppermute | solution.py:570
  12.3 0.3 merge_pass.1
  12.6 2.1 %collective-permute-start.2 = (bf16[136,384]{1,0:T(8,128)(2,1)S(1)}, bf16[136,384]{1,0:T(8,128)(2,1)S(1)}, u32[]{:S(2)}, u32[]{:S(2)}) collective-permute-start(bf16[136,384]{1,0:T(8,128)(2,1)S(1)} %get-tuple-element.62.refs_6_), channel_id=1, source_target_pairs={{0,4},{1,3},{2,6},{3,1},{4,0},{5,7},{6,2},{7,5},{8,12},{9,11},{10,... | collective-permute-start | bytes 313352 | tf_op jit(solution)/shard_map/ppermute | solution.py:570
  14.7 0.1 collective-permute-start.3
  14.8 1.5 %encode_own.1 = (f32[256,384]{1,0:T(8,128)S(1)}, f32[8,256]{1,0:T(8,128)S(1)}) custom-call(s32[8,128]{1,0:T(8,128)S(1)} %get-tuple-element.54.count.refs_0_, f32[2,8,384]{2,1,0:T(8,128)S(1)} %get-tuple-element.53.scales.refs_1_.refs_0_, bf16[1024,768]{1,0:T(8,128)(2,1)S(1)} %get-tuple-element.55.latents.refs_2_.refs_4_, ...), custom_call_target="tpu_custom_call" | custom-call | flops 805306368 | bytes 3379200 | tf_op jit(solution)/shard_map/encode_own/pallas_call | solution.py:541
  16.4 0.4 collective-permute-done.1.first.refs_2_
  16.7 0.7 %collective-permute-done.2.second = bf16[136,384]{1,0:T(8,128)(2,1)S(1)} collective-permute-done((bf16[136,384]{1,0:T(8,128)(2,1)S(1)}, bf16[136,384]{1,0:T(8,128)(2,1)S(1)}, u32[]{:S(2)}, u32[]{:S(2)}) %collective-permute-start.2) | collective-permute-done | bytes 104480 | tf_op jit(solution)/shard_map/ppermute | solution.py:570
  17.4 0.3 merge_sides.2.refs_4_.refs_5_.mine
  17.7 0.0 copy-start.6
  17.7 0.0 copy-start.1
  17.7 2.1 %collective-permute-start.5 = (bf16[136,384]{1,0:T(8,128)(2,1)S(1)}, bf16[136,384]{1,0:T(8,128)(2,1)S(1)}, u32[]{:S(2)}, u32[]{:S(2)}) collective-permute-start(bf16[136,384]{1,0:T(8,128)(2,1)S(1)} %merge_sides.2.refs_4_.refs_5_.mine), channel_id=1, source_target_pairs={{0,8},{1,17},{2,10},{3,19},{4,12},{5,21},{6,14},{7,23},{8,0},{9,25... | collective-permute-start | bytes 313352 | tf_op jit(solution)/shard_map/ppermute | solution.py:570
  19.8 0.0 collective-permute-done.3.refs_3_
  19.9 0.3 merge_sides.3.refs_6_.refs_0_
  20.1 1.2 %collective-permute-start.4 = (bf16[136,384]{1,0:T(8,128)(2,1)S(1)}, bf16[136,384]{1,0:T(8,128)(2,1)S(1)}, u32[]{:S(2)}, u32[]{:S(2)}) collective-permute-start(bf16[136,384]{1,0:T(8,128)(2,1)S(1)} %merge_sides.3.refs_6_.refs_0_), channel_id=1, source_target_pairs={{0,8},{1,17},{2,10},{3,19},{4,12},{5,21},{6,14},{7,23},{8,0},{9,25... | collective-permute-start | bytes 313352 | tf_op jit(solution)/shard_map/ppermute | solution.py:570
  21.3 2.0 %collective-permute-done.5.came = bf16[136,384]{1,0:T(8,128)(2,1)S(1)} collective-permute-done((bf16[136,384]{1,0:T(8,128)(2,1)S(1)}, bf16[136,384]{1,0:T(8,128)(2,1)S(1)}, u32[]{:S(2)}, u32[]{:S(2)}) %collective-permute-start.5) | collective-permute-done | bytes 104480 | tf_op jit(solution)/shard_map/ppermute | solution.py:570
  23.3 0.2 merge_even.4.refs_2_.refs_0_
  23.5 2.6 %collective-permute-start.7 = (bf16[136,384]{1,0:T(8,128)(2,1)S(1)}, bf16[136,384]{1,0:T(8,128)(2,1)S(1)}, u32[]{:S(2)}, u32[]{:S(2)}) collective-permute-start(bf16[136,384]{1,0:T(8,128)(2,1)S(1)} %merge_even.4.refs_2_.refs_0_), channel_id=1, source_target_pairs={{0,16},{1,9},{2,18},{3,11},{4,20},{5,13},{6,22},{7,15},{8,24},{9,1... | collective-permute-start | bytes 313352 | tf_op jit(solution)/shard_map/ppermute | solution.py:570
  26.1 0.0 collective-permute-done.4.refs_1_
  26.1 0.2 merge_even.5.refs_0_
  26.4 1.8 %collective-permute-start.6 = (bf16[136,384]{1,0:T(8,128)(2,1)S(1)}, bf16[136,384]{1,0:T(8,128)(2,1)S(1)}, u32[]{:S(2)}, u32[]{:S(2)}) collective-permute-start(bf16[136,384]{1,0:T(8,128)(2,1)S(1)} %merge_even.5.refs_0_), channel_id=1, source_target_pairs={{0,16},{1,9},{2,18},{3,11},{4,20},{5,13},{6,22},{7,15},{8,24},{9,1... | collective-permute-start | bytes 313352 | tf_op jit(solution)/shard_map/ppermute | solution.py:570
  28.2 0.0 copy-done
  28.2 0.0 copy-done.3
  28.2 0.7 %decode_prepare.1 = (bf16[3,512,256]{2,1,0:T(8,128)(2,1)S(1)}, bf16[768,512]{1,0:T(8,128)(2,1)S(1)}, bf16[768,256]{1,0:T(8,128)(2,1)S(1)}) custom-call(f32[2,8,384]{2,1,0:T(8,128)S(1)} %get-tuple-element.53.scales.refs_1_.refs_0_, bf16[512,768]{1,0:T(8,128)(2,1)S(1)} %copy-done, bf16[768,384]{1,0:T(8,128)(2,1)S(1)} %copy-done.3, ...), custom_call_target="tpu_custom_call" | custom-call | bytes 4546560 | tf_op jit(solution)/shard_map/decode_prepare/pallas_call | solution.py:541
  28.9 0.5 collective-permute-done.7.refs_1_
  29.4 0.2 merge_even.6.refs_2_.refs_0_
  29.7 0.1 collective-permute-start.10
  29.8 2.7 %collective-permute-done.6.refs_1_ = bf16[136,384]{1,0:T(8,128)(2,1)S(1)} collective-permute-done((bf16[136,384]{1,0:T(8,128)(2,1)S(1)}, bf16[136,384]{1,0:T(8,128)(2,1)S(1)}, u32[]{:S(2)}, u32[]{:S(2)}) %collective-permute-start.6) | collective-permute-done | bytes 104480 | tf_op jit(solution)/shard_map/ppermute | solution.py:570
  32.5 0.2 merge_even.7.refs_6_.attended
  32.7 0.1 collective-permute-start.8
  32.8 0.0 collective-permute-done.10.refs_1_
  32.8 0.0 collective-permute-done.9.refs_3_.other_weight.weight
  32.9 0.5 latent_low.1.refs_0_
  33.4 0.7 %collective-permute-done.8.other = bf16[128,384]{1,0:T(8,128)(2,1)S(1)} collective-permute-done((bf16[128,384]{1,0:T(8,128)(2,1)S(1)}, bf16[128,384]{1,0:T(8,128)(2,1)S(1)}, u32[]{:S(2)}, u32[]{:S(2)}) %collective-permute-start.8) | collective-permute-done | bytes 98336 | tf_op jit(solution)/shard_map/ppermute | solution.py:563
  34.1 0.5 latent.1
  34.6 2.1 %collective-permute-start.11 = (bf16[128,768]{1,0:T(8,128)(2,1)S(1)}, bf16[128,768]{1,0:T(8,128)(2,1)S(1)}, u32[]{:S(2)}, u32[]{:S(2)}) collective-permute-start(bf16[128,768]{1,0:T(8,128)(2,1)S(1)} %get-tuple-element.75), channel_id=1, source_target_pairs={{0,2},{1,5},{2,0},{3,7},{4,6},{5,1},{6,4},{7,3},{8,10},{9,13},{10,... | collective-permute-start | bytes 589832 | tf_op jit(solution)/shard_map/ppermute | solution.py:570
  36.7 2.1 %decode_own.1 = (f32[1024,768]{1,0:T(8,128)}, f32[512,256]{1,0:T(8,128)S(1)}, f32[512,256]{1,0:T(8,128)S(1)}, f32[512,256]{1,0:T(8,128)S(1)}, f32[512,128]{1,0:T...) custom-call(bf16[3,512,256]{2,1,0:T(8,128)(2,1)S(1)} %get-tuple-element.66.refs_2_.refs_3_.queries.refs_0_, ...), custom_call_target="tpu_custom_call" | custom-call | flops 805306368 | bytes 7864320 | tf_op jit(solution)/shard_map/decode_own/pallas_call | solution.py:541
  38.8 1.6 %collective-permute-start.14 = (bf16[128,768]{1,0:T(8,128)(2,1)S(1)}, bf16[128,768]{1,0:T(8,128)(2,1)S(1)}, u32[]{:S(2)}, u32[]{:S(2)}) collective-permute-start(bf16[128,768]{1,0:T(8,128)(2,1)S(1)} %get-tuple-element.75), channel_id=1, source_target_pairs={{0,4},{1,3},{2,6},{3,1},{4,0},{5,7},{6,2},{7,5},{8,12},{9,11},{10,... | collective-permute-start | bytes 589832 | tf_op jit(solution)/shard_map/ppermute | solution.py:570
  40.4 0.0 collective-permute-done.11.near
  40.4 4.1 %collective-permute-done.14.far = bf16[128,768]{1,0:T(8,128)(2,1)S(1)} collective-permute-done((bf16[128,768]{1,0:T(8,128)(2,1)S(1)}, bf16[128,768]{1,0:T(8,128)(2,1)S(1)}, u32[]{:S(2)}, u32[]{:S(2)}) %collective-permute-start.14) | collective-permute-done | bytes 196640 | tf_op jit(solution)/shard_map/ppermute | solution.py:570
  44.5 0.0 collective-permute-start.15
  44.5 0.5 collective-permute-start.13
  45.0 1.5 %collective-permute-start.12 = (bf16[128,768]{1,0:T(8,128)(2,1)S(1)}, bf16[128,768]{1,0:T(8,128)(2,1)S(1)}, u32[]{:S(2)}, u32[]{:S(2)}) collective-permute-start(bf16[128,768]{1,0:T(8,128)(2,1)S(1)} %collective-permute-done.11.near), channel_id=1, source_target_pairs={{0,4},{1,3},{2,6},{3,1},{4,0},{5,7},{6,2},{7,5},{8,12},{9,11},{10,... | collective-permute-start | bytes 589832 | tf_op jit(solution)/shard_map/ppermute | solution.py:570
  46.6 2.0 %decode_sides.2 = (f32[1024,768]{1,0:T(8,128)}, f32[512,256]{1,0:T(8,128)S(1)}, f32[512,256]{1,0:T(8,128)S(1)}, f32[512,256]{1,0:T(8,128)S(1)}, f32[512,128]{1,0...) custom-call(bf16[3,512,256]{2,1,0:T(8,128)(2,1)S(1)} %get-tuple-element.66.refs_2_., ...), custom_call_target="tpu_custom_call", output_to_operand_aliasing={{0}: (5, {})} | custom-call | flops 805306368 | bytes 13369344 | tf_op jit(solution)/shard_map/decode_sides/pallas_call | solution.py:541
  48.6 0.0 collective-permute-done.15.far.refs_3_
  48.6 0.0 collective-permute-done.13.near.refs_2_
  48.6 1.3 %decode_sides.3 = (f32[1024,768]{1,0:T(8,128)}, f32[512,256]{1,0:T(8,128)S(1)}, f32[512,256]{1,0:T(8,128)S(1)}, f32[512,256]{1,0:T(8,128)S(1)}) custom-call(bf16[3,512,256]{2,1,0:T(8,128)(2,1)S(1)} %get-tuple-element.66.refs_2_.refs_3_.queries.refs_0_, bf16[768,512]{1,0:T(8,128)(2,1)S(1)} %get-tuple-element.67.weights, ...), custom_call_target="tpu_custom_call", output_to_operand_aliasing={{0}: (5, {})} | custom-call | flops 805306368 | bytes 11796480 | tf_op jit(solution)/shard_map/decode_sides/pallas_call | solution.py:541
  50.0 0.8 %collective-permute-done.12.mine = bf16[128,768]{1,0:T(8,128)(2,1)S(1)} collective-permute-done((bf16[128,768]{1,0:T(8,128)(2,1)S(1)}, bf16[128,768]{1,0:T(8,128)(2,1)S(1)}, u32[]{:S(2)}, u32[]{:S(2)}) %collective-permute-start.12) | collective-permute-done | bytes 196640 | tf_op jit(solution)/shard_map/ppermute | solution.py:570
  50.7 0.0 collective-permute-start.16
  50.7 0.9 %decode_rest.1 = (f32[512,128]{1,0:T(8,128)S(1)}, f32[512,128]{1,0:T(8,128)S(1)}, f32[512,128]{1,0:T(8,128)S(1)}) custom-call(bf16[3,512,256]{2,1,0:T(8,128)(2,1)S(1)} %get-tuple-element.66.refs_2_.refs_3_.queries.refs_0_, bf16[768,256]{1,0:T(8,128)(2,1)S(1)} %get-tuple-element.68.more_weights.refs_1_, ...), custom_call_target="tpu_custom_call" | custom-call | flops 805306368 | bytes 3145728 | tf_op jit(solution)/shard_map/decode_rest/pallas_call | solution.py:541
  51.7 0.5 collective-permute-done.16.came
  52.2 1.2 %decode_send.1 = (bf16[256,384]{1,0:T(8,128)(2,1)S(1)}, bf16[256,512]{1,0:T(8,128)(2,1)S(1)}, bf16[256,256]{1,0:T(8,128)(2,1)S(1)}) custom-call(bf16[3,512,256]{2,1,0:T(8,128)(2,1)S(1)} %get-tuple-element.66.refs_2_.refs_3_.queries.refs_0_, bf16[768,512]{1,0:T(8,128)(2,1)S(1)} %get-tuple-element.67.weights, ...), custom_call_target="tpu_custom_call" | custom-call | flops 402653184 | bytes 5308416 | tf_op jit(solution)/shard_map/decode_send/pallas_call | solution.py:541
  53.4 0.2 collective-permute-start.17
  53.6 1.2 %decode_keep.1 = (f32[1024,768]{1,0:T(8,128)}, f32[256,768]{1,0:T(8,128)S(1)}) custom-call(bf16[3,512,256]{2,1,0:T(8,128)(2,1)S(1)} %get-tuple-element.66.refs_2_.refs_3_.queries.refs_0_, bf16[256,512]{1,0:T(8,128)(2,1)S(1)} %get-tuple-element.98.both, bf16[256,256]{1,0:T(8,128)(2,1)S(1)} %get-tuple-element.99.more_both, ...), custom_call_target="tpu_custom_call", output_to_operand_aliasing={{0}: (7, {})} | custom-call | flops 402653184 | bytes 12386304 | tf_op jit(solution)/shard_map/decode_keep/pallas_call | solution.py:541
  54.8 0.1 collective-permute-done.17.other
  54.9 1.2 %tokens.3 = f32[256,768]{1,0:T(8,128)} custom-call(s32[8,128]{1,0:T(8,128)S(1)} %get-tuple-element.54.count.refs_0_, f32[256,768]{1,0:T(8,128)S(1)} %get-tuple-element.102.base, bf16[256,384]{1,0:T(8,128)(2,1)S(1)} %collective-permute-done.17.other, bf16[384,1536]{1,0:T(8,128)(2,1)S(1)} %collective-permute-done.9.refs_3_.other_weight.weight), custom_call_target="tpu_custom_call" | custom-call | bytes 2953216 | tf_op jit(solution)/shard_map/tokens/pallas_call | solution.py:541
  (8 shorter events, 0.0 us)
Async XLA Ops:
  5.5 27.4 %collective-permute-start.9 = (bf16[384,1536]{1,0:T(8,128)(2,1)S(1)}, bf16[384,1536]{1,0:T(8,128)(2,1)S(1)}, u32[]{:S(2)}, u32[]{:S(2)}) collective-permute-start(bf16[384,1536]{1,0:T(8,128)(2,1)S(1)} %get-tuple-element.69), channel_id=1, source_target_pairs={{0,1},{1,0},{2,3},{3,2},{4,5},{5,4},{6,7},{7,6},{8,9},{9,8},{10,11... | collective-permute-start | bytes 3538952 | tf_op jit(solution)/shard_map/ppermute | solution.py:563
  6.0 6.3 %collective-permute-start = (bf16[272,384]{1,0:T(8,128)(2,1)S(1)}, bf16[272,384]{1,0:T(8,128)(2,1)S(1)}, u32[]{:S(2)}, u32[]{:S(2)}) collective-permute-start(bf16[272,384]{1,0:T(8,128)(2,1)S(1)} %get-tuple-element.61), channel_id=1, source_target_pairs={{0,2},{1,5},{2,0},{3,7},{4,6},{5,1},{6,4},{7,3},{8,10},{9,13},{10,... | collective-permute-start | bytes 626696 | tf_op jit(solution)/shard_map/ppermute | solution.py:570
  10.1 6.6 %collective-permute-start.1 = (bf16[272,384]{1,0:T(8,128)(2,1)S(1)}, bf16[272,384]{1,0:T(8,128)(2,1)S(1)}, u32[]{:S(2)}, u32[]{:S(2)}) collective-permute-start(bf16[272,384]{1,0:T(8,128)(2,1)S(1)} %encode_side.1.refs_6_), channel_id=1, source_target_pairs={{0,2},{1,5},{2,0},{3,7},{4,6},{5,1},{6,4},{7,3},{8,10},{9,13},{10,... | collective-permute-start | bytes 626696 | tf_op jit(solution)/shard_map/ppermute | solution.py:570
  11.7 16.5 %copy-start = (bf16[512,768]{1,0:T(8,128)(2,1)S(1)}, bf16[512,768]{1,0:T(8,128)(2,1)}, u32[]{:S(2)}) copy-start(bf16[512,768]{1,0:T(8,128)(2,1)} %tokens.2) | copy-start | bytes 2359300
  11.7 16.5 %copy-start.3 = (bf16[768,384]{1,0:T(8,128)(2,1)S(1)}, bf16[768,384]{1,0:T(8,128)(2,1)}, u32[]{:S(2)}) copy-start(bf16[768,384]{1,0:T(8,128)(2,1)} %refs_2_.2) | copy-start | bytes 1769476
  11.7 16.4 %copy-start.4 = (bf16[768,384]{1,0:T(8,128)(2,1)S(1)}, bf16[768,384]{1,0:T(8,128)(2,1)}, u32[]{:S(2)}) copy-start(bf16[768,384]{1,0:T(8,128)(2,1)} %refs_3_.1) | copy-start | bytes 1769476
  11.7 16.4 %copy-start.5 = (bf16[768,384]{1,0:T(8,128)(2,1)S(1)}, bf16[768,384]{1,0:T(8,128)(2,1)}, u32[]{:S(2)}) copy-start(bf16[768,384]{1,0:T(8,128)(2,1)} %refs_4_.1) | copy-start | bytes 1769476
  12.6 4.8 %collective-permute-start.2 = (bf16[136,384]{1,0:T(8,128)(2,1)S(1)}, bf16[136,384]{1,0:T(8,128)(2,1)S(1)}, u32[]{:S(2)}, u32[]{:S(2)}) collective-permute-start(bf16[136,384]{1,0:T(8,128)(2,1)S(1)} %get-tuple-element.62.refs_6_), channel_id=1, source_target_pairs={{0,4},{1,3},{2,6},{3,1},{4,0},{5,7},{6,2},{7,5},{8,12},{9,11},{10,... | collective-permute-start | bytes 313352 | tf_op jit(solution)/shard_map/ppermute | solution.py:570
  14.7 5.1 %collective-permute-start.3 = (bf16[136,384]{1,0:T(8,128)(2,1)S(1)}, bf16[136,384]{1,0:T(8,128)(2,1)S(1)}, u32[]{:S(2)}, u32[]{:S(2)}) collective-permute-start(bf16[136,384]{1,0:T(8,128)(2,1)S(1)} %get-tuple-element.63.refs_7_), channel_id=1, source_target_pairs={{0,4},{1,3},{2,6},{3,1},{4,0},{5,7},{6,2},{7,5},{8,12},{9,11},{10,... | collective-permute-start | bytes 313352 | tf_op jit(solution)/shard_map/ppermute | solution.py:570
  17.7 15.1 %copy-start.6 = (f32[768]{0:T(1024)S(1)}, f32[768]{0:T(1024)}, u32[]{:S(2)}) copy-start(f32[768]{0:T(1024)} %param.25) | copy-start | bytes 9220
  17.7 15.2 %copy-start.1 = (bf16[384,768]{1,0:T(8,128)(2,1)S(1)}, bf16[384,768]{1,0:T(8,128)(2,1)}, u32[]{:S(2)}) copy-start(bf16[384,768]{1,0:T(8,128)(2,1)} %weight.2) | copy-start | bytes 1769476
  17.7 5.6 %collective-permute-start.5 = (bf16[136,384]{1,0:T(8,128)(2,1)S(1)}, bf16[136,384]{1,0:T(8,128)(2,1)S(1)}, u32[]{:S(2)}, u32[]{:S(2)}) collective-permute-start(bf16[136,384]{1,0:T(8,128)(2,1)S(1)} %merge_sides.2.refs_4_.refs_5_.mine), channel_id=1, source_target_pairs={{0,8},{1,17},{2,10},{3,19},{4,12},{5,21},{6,14},{7,23},{8,0},{9,25... | collective-permute-start | bytes 313352 | tf_op jit(solution)/shard_map/ppermute | solution.py:570
  20.1 6.0 %collective-permute-start.4 = (bf16[136,384]{1,0:T(8,128)(2,1)S(1)}, bf16[136,384]{1,0:T(8,128)(2,1)S(1)}, u32[]{:S(2)}, u32[]{:S(2)}) collective-permute-start(bf16[136,384]{1,0:T(8,128)(2,1)S(1)} %merge_sides.3.refs_6_.refs_0_), channel_id=1, source_target_pairs={{0,8},{1,17},{2,10},{3,19},{4,12},{5,21},{6,14},{7,23},{8,0},{9,25... | collective-permute-start | bytes 313352 | tf_op jit(solution)/shard_map/ppermute | solution.py:570
  23.5 5.9 %collective-permute-start.7 = (bf16[136,384]{1,0:T(8,128)(2,1)S(1)}, bf16[136,384]{1,0:T(8,128)(2,1)S(1)}, u32[]{:S(2)}, u32[]{:S(2)}) collective-permute-start(bf16[136,384]{1,0:T(8,128)(2,1)S(1)} %merge_even.4.refs_2_.refs_0_), channel_id=1, source_target_pairs={{0,16},{1,9},{2,18},{3,11},{4,20},{5,13},{6,22},{7,15},{8,24},{9,1... | collective-permute-start | bytes 313352 | tf_op jit(solution)/shard_map/ppermute | solution.py:570
  26.4 6.1 %collective-permute-start.6 = (bf16[136,384]{1,0:T(8,128)(2,1)S(1)}, bf16[136,384]{1,0:T(8,128)(2,1)S(1)}, u32[]{:S(2)}, u32[]{:S(2)}) collective-permute-start(bf16[136,384]{1,0:T(8,128)(2,1)S(1)} %merge_even.5.refs_0_), channel_id=1, source_target_pairs={{0,16},{1,9},{2,18},{3,11},{4,20},{5,13},{6,22},{7,15},{8,24},{9,1... | collective-permute-start | bytes 313352 | tf_op jit(solution)/shard_map/ppermute | solution.py:570
  29.7 3.1 %collective-permute-start.10 = (bf16[128,384]{1,0:T(8,128)(2,1)S(1)}, bf16[128,384]{1,0:T(8,128)(2,1)S(1)}, u32[]{:S(2)}, u32[]{:S(2)}) collective-permute-start(bf16[128,384]{1,0:T(8,128)(2,1)S(1)} %merge_even.6.refs_2_.refs_0_), channel_id=1, source_target_pairs={{0,1},{1,0},{2,3},{3,2},{4,5},{5,4},{6,7},{7,6},{8,9},{9,8},{10,11... | collective-permute-start | bytes 294920 | tf_op jit(solution)/shard_map/ppermute | solution.py:563
  32.7 1.4 %collective-permute-start.8 = (bf16[128,384]{1,0:T(8,128)(2,1)S(1)}, bf16[128,384]{1,0:T(8,128)(2,1)S(1)}, u32[]{:S(2)}, u32[]{:S(2)}) collective-permute-start(bf16[128,384]{1,0:T(8,128)(2,1)S(1)} %merge_even.7.refs_6_.attended), channel_id=1, source_target_pairs={{0,1},{1,0},{2,3},{3,2},{4,5},{5,4},{6,7},{7,6},{8,9},{9,8},{10,11... | collective-permute-start | bytes 294920 | tf_op jit(solution)/shard_map/ppermute | solution.py:563
  34.6 5.8 %collective-permute-start.11 = (bf16[128,768]{1,0:T(8,128)(2,1)S(1)}, bf16[128,768]{1,0:T(8,128)(2,1)S(1)}, u32[]{:S(2)}, u32[]{:S(2)}) collective-permute-start(bf16[128,768]{1,0:T(8,128)(2,1)S(1)} %get-tuple-element.75), channel_id=1, source_target_pairs={{0,2},{1,5},{2,0},{3,7},{4,6},{5,1},{6,4},{7,3},{8,10},{9,13},{10,... | collective-permute-start | bytes 589832 | tf_op jit(solution)/shard_map/ppermute | solution.py:570
  38.8 5.7 %collective-permute-start.14 = (bf16[128,768]{1,0:T(8,128)(2,1)S(1)}, bf16[128,768]{1,0:T(8,128)(2,1)S(1)}, u32[]{:S(2)}, u32[]{:S(2)}) collective-permute-start(bf16[128,768]{1,0:T(8,128)(2,1)S(1)} %get-tuple-element.75), channel_id=1, source_target_pairs={{0,4},{1,3},{2,6},{3,1},{4,0},{5,7},{6,2},{7,5},{8,12},{9,11},{10,... | collective-permute-start | bytes 589832 | tf_op jit(solution)/shard_map/ppermute | solution.py:570
  44.5 4.1 %collective-permute-start.15 = (bf16[128,768]{1,0:T(8,128)(2,1)S(1)}, bf16[128,768]{1,0:T(8,128)(2,1)S(1)}, u32[]{:S(2)}, u32[]{:S(2)}) collective-permute-start(bf16[128,768]{1,0:T(8,128)(2,1)S(1)} %collective-permute-done.14.far), channel_id=1, source_target_pairs={{0,1},{1,0},{2,3},{3,2},{4,5},{5,4},{6,7},{7,6},{8,9},{9,8},{10,11... | collective-permute-start | bytes 589832 | tf_op jit(solution)/shard_map/ppermute | solution.py:563
  44.5 4.1 %collective-permute-start.13 = (bf16[128,768]{1,0:T(8,128)(2,1)S(1)}, bf16[128,768]{1,0:T(8,128)(2,1)S(1)}, u32[]{:S(2)}, u32[]{:S(2)}) collective-permute-start(bf16[128,768]{1,0:T(8,128)(2,1)S(1)} %collective-permute-done.11.near), channel_id=1, source_target_pairs={{0,1},{1,0},{2,3},{3,2},{4,5},{5,4},{6,7},{7,6},{8,9},{9,8},{10,11... | collective-permute-start | bytes 589832 | tf_op jit(solution)/shard_map/ppermute | solution.py:563
  45.0 5.7 %collective-permute-start.12 = (bf16[128,768]{1,0:T(8,128)(2,1)S(1)}, bf16[128,768]{1,0:T(8,128)(2,1)S(1)}, u32[]{:S(2)}, u32[]{:S(2)}) collective-permute-start(bf16[128,768]{1,0:T(8,128)(2,1)S(1)} %collective-permute-done.11.near), channel_id=1, source_target_pairs={{0,4},{1,3},{2,6},{3,1},{4,0},{5,7},{6,2},{7,5},{8,12},{9,11},{10,... | collective-permute-start | bytes 589832 | tf_op jit(solution)/shard_map/ppermute | solution.py:570
  50.7 1.4 %collective-permute-start.16 = (bf16[128,768]{1,0:T(8,128)(2,1)S(1)}, bf16[128,768]{1,0:T(8,128)(2,1)S(1)}, u32[]{:S(2)}, u32[]{:S(2)}) collective-permute-start(bf16[128,768]{1,0:T(8,128)(2,1)S(1)} %collective-permute-done.12.mine), channel_id=1, source_target_pairs={{0,1},{1,0},{2,3},{3,2},{4,5},{5,4},{6,7},{7,6},{8,9},{9,8},{10,11... | collective-permute-start | bytes 589832 | tf_op jit(solution)/shard_map/ppermute | solution.py:563
  50.7 2.8 %copy-start.2 = (bf16[384,768]{1,0:T(8,128)(2,1)S(1)}, bf16[384,768]{1,0:T(8,128)(2,1)}, u32[]{:S(2)}) copy-start(bf16[384,768]{1,0:T(8,128)(2,1)} %weight.3) | copy-start | bytes 1769476
  53.4 1.5 %collective-permute-start.17 = (bf16[256,384]{1,0:T(8,128)(2,1)S(1)}, bf16[256,384]{1,0:T(8,128)(2,1)S(1)}, u32[]{:S(2)}, u32[]{:S(2)}) collective-permute-start(bf16[256,384]{1,0:T(8,128)(2,1)S(1)} %get-tuple-element.103), channel_id=1, source_target_pairs={{0,1},{1,0},{2,3},{3,2},{4,5},{5,4},{6,7},{7,6},{8,9},{9,8},{10,11... | collective-permute-start | bytes 589832 | tf_op jit(solution)/shard_map/ppermute | solution.py:563

commit v8 on v6

--- a/solution.py
+++ b/solution.py
@@ -700,7 +700,7 @@
     )
     (tokens_out,) = call(
         tokens_kernel, "vvvv", [((half_slots, model), F32)], count, base, swap(send), other_outputs,
-        far=(0,), scratch=scratch(half_slots, 3 if model % 384 == 0 else 1), name="tokens",
+        far=(0,), scratch=scratch(half_slots, 1), name="tokens",
     )
     return latent_out, tokens_out
 

time: 54.1 us -> 54.1 us (level)
  no operation moved by 1% of the time
where the time goes in v8:
time: 54.1 us; the launch traced here: 53.7 us
  Pallas kernels  22.4 us (41%)
  starting transfers between devices  18.9 us (35%)
  waiting for transfers between devices  10.7 us (20%)
  between operations  1.71 us (3%)
    pallas_call x21, Pallas kernels, call(): pl.pallas_call(kernel, out_shape=shapes, in_specs=[SPACES[kind] for kind...  22.4 us
    ppermute x11, starting transfers between devices, trade(): return lax.ppermute(array, ('cell', 'qgrp'), pairs)  17.9 us
    ppermute x11, waiting for transfers between devices, trade(): return lax.ppermute(array, ('cell', 'qgrp'), pairs)  9.38 us
    ppermute x7, waiting for transfers between devices, swap(): return lax.ppermute(array, 'qgrp', [(0, 1), (1, 0)])  1.3 us
  transfers between devices with their start and end apart: 18, of which 12 were waited for; matrix products, arithmetic and copies ran while one was open for 0% of the time, Pallas kernels for 28%

profile of v8, /device:TPU:0, one launch (start us, length us, event | category | flops | bytes accessed | tf_op | source)
XLA Modules:
  0.0 53.7 jit_solution(12870855651491534297)
XLA Ops:
  1.3 4.2 %encode_corner.1 = (bf16[272,384]{1,0:T(8,128)(2,1)S(1)}, bf16[512,384]{1,0:T(8,128)(2,1)S(1)}, bf16[512,384]{1,0:T(8,128)(2,1)S(1)}, f32[2,8,384]{2,1,0:T(8,128...) custom-call(s32[1]{0:T(128)S(6)} %copy.21.tally, ...), custom_call_target="tpu_custom_call" | custom-call | flops 805306368 | bytes 9674852 | tf_op jit(solution)/shard_map/encode_corner/pallas_call | solution.py:541
  5.5 0.5 collective-permute-start.9
  6.0 2.6 %collective-permute-start = (bf16[272,384]{1,0:T(8,128)(2,1)S(1)}, bf16[272,384]{1,0:T(8,128)(2,1)S(1)}, u32[]{:S(2)}, u32[]{:S(2)}) collective-permute-start(bf16[272,384]{1,0:T(8,128)(2,1)S(1)} %get-tuple-element.59), channel_id=1, source_target_pairs={{0,2},{1,5},{2,0},{3,7},{4,6},{5,1},{6,4},{7,3},{8,10},{9,13},{10,... | collective-permute-start | bytes 626696 | tf_op jit(solution)/shard_map/ppermute | solution.py:570
  8.5 1.5 %encode_side.1.refs_6_ = bf16[272,384]{1,0:T(8,128)(2,1)S(1)} custom-call(s32[8,128]{1,0:T(8,128)S(1)} %get-tuple-element.52.count.refs_0_, f32[2,8,384]{2,1,0:T(8,128)S(1)} %get-tuple-element.51.scales.refs_1_.refs_0_, bf16[1024,768]{1,0:T(8,128)(2,1)S(1)} %get-tuple-element.53.latents.refs_2_.refs_4_, bf16[768,384]{1,0:T(8,128)(2,1)S(1)} %get-tuple-element.54.wq.refs_3_, ...), custom_call_target="tpu_custom_call" | custom-call | flops 805306368 | bytes 3186688 | tf_op jit(solution)/shard_map/encode_side/pallas_call | solution.py:541
  10.1 0.1 collective-permute-start.1
  10.2 1.5 %encode_pass.1 = (f32[256,384]{1,0:T(8,128)S(1)}, f32[8,256]{1,0:T(8,128)S(1)}) custom-call(s32[8,128]{1,0:T(8,128)S(1)} %get-tuple-element.52.count.refs_0_, f32[2,8,384]{2,1,0:T(8,128)S(1)} %get-tuple-element.51.scales.refs_1_.refs_0_, bf16[1024,768]{1,0:T(8,128)(2,1)S(1)} %get-tuple-element.53.latents.refs_2_.refs_4_, ...), custom_call_target="tpu_custom_call" | custom-call | flops 805306368 | bytes 3379200 | tf_op jit(solution)/shard_map/encode_pass/pallas_call | solution.py:541
  11.7 0.0 copy-start.3
  11.7 0.0 copy-start.4
  11.7 0.0 copy-start.5
  11.8 0.6 %collective-permute-done.came = bf16[272,384]{1,0:T(8,128)(2,1)S(1)} collective-permute-done((bf16[272,384]{1,0:T(8,128)(2,1)S(1)}, bf16[272,384]{1,0:T(8,128)(2,1)S(1)}, u32[]{:S(2)}, u32[]{:S(2)}) %collective-permute-start) | collective-permute-done | bytes 208928 | tf_op jit(solution)/shard_map/ppermute | solution.py:570
  12.3 0.3 merge_pass.1
  12.6 2.1 %collective-permute-start.2 = (bf16[136,384]{1,0:T(8,128)(2,1)S(1)}, bf16[136,384]{1,0:T(8,128)(2,1)S(1)}, u32[]{:S(2)}, u32[]{:S(2)}) collective-permute-start(bf16[136,384]{1,0:T(8,128)(2,1)S(1)} %get-tuple-element.60.refs_6_), channel_id=1, source_target_pairs={{0,4},{1,3},{2,6},{3,1},{4,0},{5,7},{6,2},{7,5},{8,12},{9,11},{10,... | collective-permute-start | bytes 313352 | tf_op jit(solution)/shard_map/ppermute | solution.py:570
  14.7 0.1 collective-permute-start.3
  14.8 1.5 %encode_own.1 = (f32[256,384]{1,0:T(8,128)S(1)}, f32[8,256]{1,0:T(8,128)S(1)}) custom-call(s32[8,128]{1,0:T(8,128)S(1)} %get-tuple-element.52.count.refs_0_, f32[2,8,384]{2,1,0:T(8,128)S(1)} %get-tuple-element.51.scales.refs_1_.refs_0_, bf16[1024,768]{1,0:T(8,128)(2,1)S(1)} %get-tuple-element.53.latents.refs_2_.refs_4_, ...), custom_call_target="tpu_custom_call" | custom-call | flops 805306368 | bytes 3379200 | tf_op jit(solution)/shard_map/encode_own/pallas_call | solution.py:541
  16.4 0.4 collective-permute-done.1.first.refs_2_
  16.7 0.7 %collective-permute-done.2.second = bf16[136,384]{1,0:T(8,128)(2,1)S(1)} collective-permute-done((bf16[136,384]{1,0:T(8,128)(2,1)S(1)}, bf16[136,384]{1,0:T(8,128)(2,1)S(1)}, u32[]{:S(2)}, u32[]{:S(2)}) %collective-permute-start.2) | collective-permute-done | bytes 104480 | tf_op jit(solution)/shard_map/ppermute | solution.py:570
  17.4 0.3 merge_sides.2.refs_4_.refs_5_.mine
  17.7 0.0 copy-start.6
  17.7 0.0 copy-start.1
  17.7 2.1 %collective-permute-start.5 = (bf16[136,384]{1,0:T(8,128)(2,1)S(1)}, bf16[136,384]{1,0:T(8,128)(2,1)S(1)}, u32[]{:S(2)}, u32[]{:S(2)}) collective-permute-start(bf16[136,384]{1,0:T(8,128)(2,1)S(1)} %merge_sides.2.refs_4_.refs_5_.mine), channel_id=1, source_target_pairs={{0,8},{1,17},{2,10},{3,19},{4,12},{5,21},{6,14},{7,23},{8,0},{9,25... | collective-permute-start | bytes 313352 | tf_op jit(solution)/shard_map/ppermute | solution.py:570
  19.8 0.0 collective-permute-done.3.refs_3_
  19.9 0.3 merge_sides.3.refs_6_.refs_0_
  20.1 1.2 %collective-permute-start.4 = (bf16[136,384]{1,0:T(8,128)(2,1)S(1)}, bf16[136,384]{1,0:T(8,128)(2,1)S(1)}, u32[]{:S(2)}, u32[]{:S(2)}) collective-permute-start(bf16[136,384]{1,0:T(8,128)(2,1)S(1)} %merge_sides.3.refs_6_.refs_0_), channel_id=1, source_target_pairs={{0,8},{1,17},{2,10},{3,19},{4,12},{5,21},{6,14},{7,23},{8,0},{9,25... | collective-permute-start | bytes 313352 | tf_op jit(solution)/shard_map/ppermute | solution.py:570
  21.3 2.0 %collective-permute-done.5.came = bf16[136,384]{1,0:T(8,128)(2,1)S(1)} collective-permute-done((bf16[136,384]{1,0:T(8,128)(2,1)S(1)}, bf16[136,384]{1,0:T(8,128)(2,1)S(1)}, u32[]{:S(2)}, u32[]{:S(2)}) %collective-permute-start.5) | collective-permute-done | bytes 104480 | tf_op jit(solution)/shard_map/ppermute | solution.py:570
  23.3 0.2 merge_even.4.refs_2_.refs_0_
  23.5 2.6 %collective-permute-start.7 = (bf16[136,384]{1,0:T(8,128)(2,1)S(1)}, bf16[136,384]{1,0:T(8,128)(2,1)S(1)}, u32[]{:S(2)}, u32[]{:S(2)}) collective-permute-start(bf16[136,384]{1,0:T(8,128)(2,1)S(1)} %merge_even.4.refs_2_.refs_0_), channel_id=1, source_target_pairs={{0,16},{1,9},{2,18},{3,11},{4,20},{5,13},{6,22},{7,15},{8,24},{9,1... | collective-permute-start | bytes 313352 | tf_op jit(solution)/shard_map/ppermute | solution.py:570
  26.1 0.0 collective-permute-done.4.refs_1_
  26.1 0.2 merge_even.5.refs_0_
  26.4 1.8 %collective-permute-start.6 = (bf16[136,384]{1,0:T(8,128)(2,1)S(1)}, bf16[136,384]{1,0:T(8,128)(2,1)S(1)}, u32[]{:S(2)}, u32[]{:S(2)}) collective-permute-start(bf16[136,384]{1,0:T(8,128)(2,1)S(1)} %merge_even.5.refs_0_), channel_id=1, source_target_pairs={{0,16},{1,9},{2,18},{3,11},{4,20},{5,13},{6,22},{7,15},{8,24},{9,1... | collective-permute-start | bytes 313352 | tf_op jit(solution)/shard_map/ppermute | solution.py:570
  28.2 0.0 copy-done
  28.2 0.0 copy-done.3
  28.2 0.7 %decode_prepare.1 = (bf16[3,512,256]{2,1,0:T(8,128)(2,1)S(1)}, bf16[768,512]{1,0:T(8,128)(2,1)S(1)}, bf16[768,256]{1,0:T(8,128)(2,1)S(1)}) custom-call(f32[2,8,384]{2,1,0:T(8,128)S(1)} %get-tuple-element.51.scales.refs_1_.refs_0_, bf16[512,768]{1,0:T(8,128)(2,1)S(1)} %copy-done, bf16[768,384]{1,0:T(8,128)(2,1)S(1)} %copy-done.3, ...), custom_call_target="tpu_custom_call" | custom-call | bytes 4546560 | tf_op jit(solution)/shard_map/decode_prepare/pallas_call | solution.py:541
  28.9 0.5 collective-permute-done.7.refs_1_
  29.4 0.2 merge_even.6.refs_2_.refs_0_
  29.7 0.1 collective-permute-start.10
  29.8 2.7 %collective-permute-done.6.refs_1_ = bf16[136,384]{1,0:T(8,128)(2,1)S(1)} collective-permute-done((bf16[136,384]{1,0:T(8,128)(2,1)S(1)}, bf16[136,384]{1,0:T(8,128)(2,1)S(1)}, u32[]{:S(2)}, u32[]{:S(2)}) %collective-permute-start.6) | collective-permute-done | bytes 104480 | tf_op jit(solution)/shard_map/ppermute | solution.py:570
  32.5 0.2 merge_even.7.refs_6_.attended
  32.7 0.1 collective-permute-start.8
  32.8 0.0 collective-permute-done.10.refs_1_
  32.8 0.0 collective-permute-done.9.refs_3_.other_weight.weight
  32.9 0.5 latent_low.1.refs_0_
  33.4 0.7 %collective-permute-done.8.other = bf16[128,384]{1,0:T(8,128)(2,1)S(1)} collective-permute-done((bf16[128,384]{1,0:T(8,128)(2,1)S(1)}, bf16[128,384]{1,0:T(8,128)(2,1)S(1)}, u32[]{:S(2)}, u32[]{:S(2)}) %collective-permute-start.8) | collective-permute-done | bytes 98336 | tf_op jit(solution)/shard_map/ppermute | solution.py:563
  34.1 0.5 latent.1
  34.6 2.1 %collective-permute-start.11 = (bf16[128,768]{1,0:T(8,128)(2,1)S(1)}, bf16[128,768]{1,0:T(8,128)(2,1)S(1)}, u32[]{:S(2)}, u32[]{:S(2)}) collective-permute-start(bf16[128,768]{1,0:T(8,128)(2,1)S(1)} %get-tuple-element.68), channel_id=1, source_target_pairs={{0,2},{1,5},{2,0},{3,7},{4,6},{5,1},{6,4},{7,3},{8,10},{9,13},{10,... | collective-permute-start | bytes 589832 | tf_op jit(solution)/shard_map/ppermute | solution.py:570
  36.7 1.5 %collective-permute-start.14 = (bf16[128,768]{1,0:T(8,128)(2,1)S(1)}, bf16[128,768]{1,0:T(8,128)(2,1)S(1)}, u32[]{:S(2)}, u32[]{:S(2)}) collective-permute-start(bf16[128,768]{1,0:T(8,128)(2,1)S(1)} %get-tuple-element.68), channel_id=1, source_target_pairs={{0,4},{1,3},{2,6},{3,1},{4,0},{5,7},{6,2},{7,5},{8,12},{9,11},{10,... | collective-permute-start | bytes 589832 | tf_op jit(solution)/shard_map/ppermute | solution.py:570
  38.2 2.1 %decode_own.1 = (f32[1024,768]{1,0:T(8,128)}, f32[512,256]{1,0:T(8,128)S(1)}, f32[512,256]{1,0:T(8,128)S(1)}, f32[512,256]{1,0:T(8,128)S(1)}, f32[512,128]{1,0:T...) custom-call(bf16[3,512,256]{2,1,0:T(8,128)(2,1)S(1)} %get-tuple-element.64.refs_2_.refs_3_.queries.refs_0_, ...), custom_call_target="tpu_custom_call" | custom-call | flops 805306368 | bytes 7864320 | tf_op jit(solution)/shard_map/decode_own/pallas_call | solution.py:541
  40.4 1.4 %collective-permute-done.11.near = bf16[128,768]{1,0:T(8,128)(2,1)S(1)} collective-permute-done((bf16[128,768]{1,0:T(8,128)(2,1)S(1)}, bf16[128,768]{1,0:T(8,128)(2,1)S(1)}, u32[]{:S(2)}, u32[]{:S(2)}) %collective-permute-start.11) | collective-permute-done | bytes 196640 | tf_op jit(solution)/shard_map/ppermute | solution.py:570
  41.8 0.0 collective-permute-start.13
  41.8 0.6 %collective-permute-done.14.far = bf16[128,768]{1,0:T(8,128)(2,1)S(1)} collective-permute-done((bf16[128,768]{1,0:T(8,128)(2,1)S(1)}, bf16[128,768]{1,0:T(8,128)(2,1)S(1)}, u32[]{:S(2)}, u32[]{:S(2)}) %collective-permute-start.14) | collective-permute-done | bytes 196640 | tf_op jit(solution)/shard_map/ppermute | solution.py:570
  42.3 0.1 collective-permute-start.15
  42.5 1.7 %collective-permute-start.12 = (bf16[128,768]{1,0:T(8,128)(2,1)S(1)}, bf16[128,768]{1,0:T(8,128)(2,1)S(1)}, u32[]{:S(2)}, u32[]{:S(2)}) collective-permute-start(bf16[128,768]{1,0:T(8,128)(2,1)S(1)} %collective-permute-done.11.near), channel_id=1, source_target_pairs={{0,4},{1,3},{2,6},{3,1},{4,0},{5,7},{6,2},{7,5},{8,12},{9,11},{10,... | collective-permute-start | bytes 589832 | tf_op jit(solution)/shard_map/ppermute | solution.py:570
  44.2 2.0 %decode_sides.2 = (f32[1024,768]{1,0:T(8,128)}, f32[512,256]{1,0:T(8,128)S(1)}, f32[512,256]{1,0:T(8,128)S(1)}, f32[512,256]{1,0:T(8,128)S(1)}, f32[512,128]{1,0...) custom-call(bf16[3,512,256]{2,1,0:T(8,128)(2,1)S(1)} %get-tuple-element.64.refs_2_., ...), custom_call_target="tpu_custom_call", output_to_operand_aliasing={{0}: (5, {})} | custom-call | flops 805306368 | bytes 13369344 | tf_op jit(solution)/shard_map/decode_sides/pallas_call | solution.py:541
  46.2 0.0 collective-permute-done.13.near.refs_2_
  46.2 0.0 collective-permute-done.15.far.refs_3_
  46.2 1.3 %decode_sides.3 = (f32[1024,768]{1,0:T(8,128)}, f32[512,256]{1,0:T(8,128)S(1)}, f32[512,256]{1,0:T(8,128)S(1)}, f32[512,256]{1,0:T(8,128)S(1)}) custom-call(bf16[3,512,256]{2,1,0:T(8,128)(2,1)S(1)} %get-tuple-element.64.refs_2_.refs_3_.queries.refs_0_, bf16[768,512]{1,0:T(8,128)(2,1)S(1)} %get-tuple-element.65.weights, ...), custom_call_target="tpu_custom_call", output_to_operand_aliasing={{0}: (5, {})} | custom-call | flops 805306368 | bytes 11796480 | tf_op jit(solution)/shard_map/decode_sides/pallas_call | solution.py:541
  47.5 0.6 %collective-permute-done.12.mine = bf16[128,768]{1,0:T(8,128)(2,1)S(1)} collective-permute-done((bf16[128,768]{1,0:T(8,128)(2,1)S(1)}, bf16[128,768]{1,0:T(8,128)(2,1)S(1)}, u32[]{:S(2)}, u32[]{:S(2)}) %collective-permute-start.12) | collective-permute-done | bytes 196640 | tf_op jit(solution)/shard_map/ppermute | solution.py:570
  48.1 0.0 collective-permute-start.16
  48.1 0.9 %decode_rest.1 = (f32[512,128]{1,0:T(8,128)S(1)}, f32[512,128]{1,0:T(8,128)S(1)}, f32[512,128]{1,0:T(8,128)S(1)}) custom-call(bf16[3,512,256]{2,1,0:T(8,128)(2,1)S(1)} %get-tuple-element.64.refs_2_.refs_3_.queries.refs_0_, bf16[768,256]{1,0:T(8,128)(2,1)S(1)} %get-tuple-element.66.more_weights.refs_1_, ...), custom_call_target="tpu_custom_call" | custom-call | flops 805306368 | bytes 3145728 | tf_op jit(solution)/shard_map/decode_rest/pallas_call | solution.py:541
  49.1 0.5 collective-permute-done.16.came
  49.6 1.2 %decode_send.1 = (bf16[256,384]{1,0:T(8,128)(2,1)S(1)}, bf16[256,512]{1,0:T(8,128)(2,1)S(1)}, bf16[256,256]{1,0:T(8,128)(2,1)S(1)}) custom-call(bf16[3,512,256]{2,1,0:T(8,128)(2,1)S(1)} %get-tuple-element.64.refs_2_.refs_3_.queries.refs_0_, bf16[768,512]{1,0:T(8,128)(2,1)S(1)} %get-tuple-element.65.weights, ...), custom_call_target="tpu_custom_call" | custom-call | flops 402653184 | bytes 5308416 | tf_op jit(solution)/shard_map/decode_send/pallas_call | solution.py:541
  50.8 0.2 collective-permute-start.17
  51.0 1.2 %decode_keep.1 = (f32[1024,768]{1,0:T(8,128)}, f32[256,768]{1,0:T(8,128)S(1)}) custom-call(bf16[3,512,256]{2,1,0:T(8,128)(2,1)S(1)} %get-tuple-element.64.refs_2_.refs_3_.queries.refs_0_, bf16[256,512]{1,0:T(8,128)(2,1)S(1)} %get-tuple-element.94.both, bf16[256,256]{1,0:T(8,128)(2,1)S(1)} %get-tuple-element.95.more_both, ...), custom_call_target="tpu_custom_call", output_to_operand_aliasing={{0}: (7, {})} | custom-call | flops 402653184 | bytes 12386304 | tf_op jit(solution)/shard_map/decode_keep/pallas_call | solution.py:541
  52.2 0.1 collective-permute-done.17.other
  52.3 1.3 %tokens.3 = f32[256,768]{1,0:T(8,128)} custom-call(s32[8,128]{1,0:T(8,128)S(1)} %get-tuple-element.52.count.refs_0_, f32[256,768]{1,0:T(8,128)S(1)} %get-tuple-element.98.base, bf16[256,384]{1,0:T(8,128)(2,1)S(1)} %collective-permute-done.17.other, bf16[384,1536]{1,0:T(8,128)(2,1)S(1)} %collective-permute-done.9.refs_3_.other_weight.weight), custom_call_target="tpu_custom_call" | custom-call | bytes 2953216 | tf_op jit(solution)/shard_map/tokens/pallas_call | solution.py:541
  (8 shorter events, 0.0 us)
Async XLA Ops:
  5.5 27.4 %collective-permute-start.9 = (bf16[384,1536]{1,0:T(8,128)(2,1)S(1)}, bf16[384,1536]{1,0:T(8,128)(2,1)S(1)}, u32[]{:S(2)}, u32[]{:S(2)}) collective-permute-start(bf16[384,1536]{1,0:T(8,128)(2,1)S(1)} %get-tuple-element.67), channel_id=1, source_target_pairs={{0,1},{1,0},{2,3},{3,2},{4,5},{5,4},{6,7},{7,6},{8,9},{9,8},{10,11... | collective-permute-start | bytes 3538952 | tf_op jit(solution)/shard_map/ppermute | solution.py:563
  6.0 6.3 %collective-permute-start = (bf16[272,384]{1,0:T(8,128)(2,1)S(1)}, bf16[272,384]{1,0:T(8,128)(2,1)S(1)}, u32[]{:S(2)}, u32[]{:S(2)}) collective-permute-start(bf16[272,384]{1,0:T(8,128)(2,1)S(1)} %get-tuple-element.59), channel_id=1, source_target_pairs={{0,2},{1,5},{2,0},{3,7},{4,6},{5,1},{6,4},{7,3},{8,10},{9,13},{10,... | collective-permute-start | bytes 626696 | tf_op jit(solution)/shard_map/ppermute | solution.py:570
  10.1 6.6 %collective-permute-start.1 = (bf16[272,384]{1,0:T(8,128)(2,1)S(1)}, bf16[272,384]{1,0:T(8,128)(2,1)S(1)}, u32[]{:S(2)}, u32[]{:S(2)}) collective-permute-start(bf16[272,384]{1,0:T(8,128)(2,1)S(1)} %encode_side.1.refs_6_), channel_id=1, source_target_pairs={{0,2},{1,5},{2,0},{3,7},{4,6},{5,1},{6,4},{7,3},{8,10},{9,13},{10,... | collective-permute-start | bytes 626696 | tf_op jit(solution)/shard_map/ppermute | solution.py:570
  11.7 16.5 %copy-start = (bf16[512,768]{1,0:T(8,128)(2,1)S(1)}, bf16[512,768]{1,0:T(8,128)(2,1)}, u32[]{:S(2)}) copy-start(bf16[512,768]{1,0:T(8,128)(2,1)} %tokens.2) | copy-start | bytes 2359300
  11.7 16.5 %copy-start.3 = (bf16[768,384]{1,0:T(8,128)(2,1)S(1)}, bf16[768,384]{1,0:T(8,128)(2,1)}, u32[]{:S(2)}) copy-start(bf16[768,384]{1,0:T(8,128)(2,1)} %refs_2_.2) | copy-start | bytes 1769476
  11.7 16.4 %copy-start.4 = (bf16[768,384]{1,0:T(8,128)(2,1)S(1)}, bf16[768,384]{1,0:T(8,128)(2,1)}, u32[]{:S(2)}) copy-start(bf16[768,384]{1,0:T(8,128)(2,1)} %refs_3_.1) | copy-start | bytes 1769476
  11.7 16.4 %copy-start.5 = (bf16[768,384]{1,0:T(8,128)(2,1)S(1)}, bf16[768,384]{1,0:T(8,128)(2,1)}, u32[]{:S(2)}) copy-start(bf16[768,384]{1,0:T(8,128)(2,1)} %refs_4_.1) | copy-start | bytes 1769476
  12.6 4.8 %collective-permute-start.2 = (bf16[136,384]{1,0:T(8,128)(2,1)S(1)}, bf16[136,384]{1,0:T(8,128)(2,1)S(1)}, u32[]{:S(2)}, u32[]{:S(2)}) collective-permute-start(bf16[136,384]{1,0:T(8,128)(2,1)S(1)} %get-tuple-element.60.refs_6_), channel_id=1, source_target_pairs={{0,4},{1,3},{2,6},{3,1},{4,0},{5,7},{6,2},{7,5},{8,12},{9,11},{10,... | collective-permute-start | bytes 313352 | tf_op jit(solution)/shard_map/ppermute | solution.py:570
  14.7 5.1 %collective-permute-start.3 = (bf16[136,384]{1,0:T(8,128)(2,1)S(1)}, bf16[136,384]{1,0:T(8,128)(2,1)S(1)}, u32[]{:S(2)}, u32[]{:S(2)}) collective-permute-start(bf16[136,384]{1,0:T(8,128)(2,1)S(1)} %get-tuple-element.61.refs_7_), channel_id=1, source_target_pairs={{0,4},{1,3},{2,6},{3,1},{4,0},{5,7},{6,2},{7,5},{8,12},{9,11},{10,... | collective-permute-start | bytes 313352 | tf_op jit(solution)/shard_map/ppermute | solution.py:570
  17.7 15.1 %copy-start.6 = (f32[768]{0:T(1024)S(1)}, f32[768]{0:T(1024)}, u32[]{:S(2)}) copy-start(f32[768]{0:T(1024)} %param.25) | copy-start | bytes 9220
  17.7 15.2 %copy-start.1 = (bf16[384,768]{1,0:T(8,128)(2,1)S(1)}, bf16[384,768]{1,0:T(8,128)(2,1)}, u32[]{:S(2)}) copy-start(bf16[384,768]{1,0:T(8,128)(2,1)} %weight.2) | copy-start | bytes 1769476
  17.7 5.6 %collective-permute-start.5 = (bf16[136,384]{1,0:T(8,128)(2,1)S(1)}, bf16[136,384]{1,0:T(8,128)(2,1)S(1)}, u32[]{:S(2)}, u32[]{:S(2)}) collective-permute-start(bf16[136,384]{1,0:T(8,128)(2,1)S(1)} %merge_sides.2.refs_4_.refs_5_.mine), channel_id=1, source_target_pairs={{0,8},{1,17},{2,10},{3,19},{4,12},{5,21},{6,14},{7,23},{8,0},{9,25... | collective-permute-start | bytes 313352 | tf_op jit(solution)/shard_map/ppermute | solution.py:570
  20.1 6.0 %collective-permute-start.4 = (bf16[136,384]{1,0:T(8,128)(2,1)S(1)}, bf16[136,384]{1,0:T(8,128)(2,1)S(1)}, u32[]{:S(2)}, u32[]{:S(2)}) collective-permute-start(bf16[136,384]{1,0:T(8,128)(2,1)S(1)} %merge_sides.3.refs_6_.refs_0_), channel_id=1, source_target_pairs={{0,8},{1,17},{2,10},{3,19},{4,12},{5,21},{6,14},{7,23},{8,0},{9,25... | collective-permute-start | bytes 313352 | tf_op jit(solution)/shard_map/ppermute | solution.py:570
  23.5 5.9 %collective-permute-start.7 = (bf16[136,384]{1,0:T(8,128)(2,1)S(1)}, bf16[136,384]{1,0:T(8,128)(2,1)S(1)}, u32[]{:S(2)}, u32[]{:S(2)}) collective-permute-start(bf16[136,384]{1,0:T(8,128)(2,1)S(1)} %merge_even.4.refs_2_.refs_0_), channel_id=1, source_target_pairs={{0,16},{1,9},{2,18},{3,11},{4,20},{5,13},{6,22},{7,15},{8,24},{9,1... | collective-permute-start | bytes 313352 | tf_op jit(solution)/shard_map/ppermute | solution.py:570
  26.4 6.1 %collective-permute-start.6 = (bf16[136,384]{1,0:T(8,128)(2,1)S(1)}, bf16[136,384]{1,0:T(8,128)(2,1)S(1)}, u32[]{:S(2)}, u32[]{:S(2)}) collective-permute-start(bf16[136,384]{1,0:T(8,128)(2,1)S(1)} %merge_even.5.refs_0_), channel_id=1, source_target_pairs={{0,16},{1,9},{2,18},{3,11},{4,20},{5,13},{6,22},{7,15},{8,24},{9,1... | collective-permute-start | bytes 313352 | tf_op jit(solution)/shard_map/ppermute | solution.py:570
  29.7 3.1 %collective-permute-start.10 = (bf16[128,384]{1,0:T(8,128)(2,1)S(1)}, bf16[128,384]{1,0:T(8,128)(2,1)S(1)}, u32[]{:S(2)}, u32[]{:S(2)}) collective-permute-start(bf16[128,384]{1,0:T(8,128)(2,1)S(1)} %merge_even.6.refs_2_.refs_0_), channel_id=1, source_target_pairs={{0,1},{1,0},{2,3},{3,2},{4,5},{5,4},{6,7},{7,6},{8,9},{9,8},{10,11... | collective-permute-start | bytes 294920 | tf_op jit(solution)/shard_map/ppermute | solution.py:563
  32.7 1.4 %collective-permute-start.8 = (bf16[128,384]{1,0:T(8,128)(2,1)S(1)}, bf16[128,384]{1,0:T(8,128)(2,1)S(1)}, u32[]{:S(2)}, u32[]{:S(2)}) collective-permute-start(bf16[128,384]{1,0:T(8,128)(2,1)S(1)} %merge_even.7.refs_6_.attended), channel_id=1, source_target_pairs={{0,1},{1,0},{2,3},{3,2},{4,5},{5,4},{6,7},{7,6},{8,9},{9,8},{10,11... | collective-permute-start | bytes 294920 | tf_op jit(solution)/shard_map/ppermute | solution.py:563
  34.6 7.2 %collective-permute-start.11 = (bf16[128,768]{1,0:T(8,128)(2,1)S(1)}, bf16[128,768]{1,0:T(8,128)(2,1)S(1)}, u32[]{:S(2)}, u32[]{:S(2)}) collective-permute-start(bf16[128,768]{1,0:T(8,128)(2,1)S(1)} %get-tuple-element.68), channel_id=1, source_target_pairs={{0,2},{1,5},{2,0},{3,7},{4,6},{5,1},{6,4},{7,3},{8,10},{9,13},{10,... | collective-permute-start | bytes 589832 | tf_op jit(solution)/shard_map/ppermute | solution.py:570
  36.7 5.7 %collective-permute-start.14 = (bf16[128,768]{1,0:T(8,128)(2,1)S(1)}, bf16[128,768]{1,0:T(8,128)(2,1)S(1)}, u32[]{:S(2)}, u32[]{:S(2)}) collective-permute-start(bf16[128,768]{1,0:T(8,128)(2,1)S(1)} %get-tuple-element.68), channel_id=1, source_target_pairs={{0,4},{1,3},{2,6},{3,1},{4,0},{5,7},{6,2},{7,5},{8,12},{9,11},{10,... | collective-permute-start | bytes 589832 | tf_op jit(solution)/shard_map/ppermute | solution.py:570
  41.8 4.4 %collective-permute-start.13 = (bf16[128,768]{1,0:T(8,128)(2,1)S(1)}, bf16[128,768]{1,0:T(8,128)(2,1)S(1)}, u32[]{:S(2)}, u32[]{:S(2)}) collective-permute-start(bf16[128,768]{1,0:T(8,128)(2,1)S(1)} %collective-permute-done.11.near), channel_id=1, source_target_pairs={{0,1},{1,0},{2,3},{3,2},{4,5},{5,4},{6,7},{7,6},{8,9},{9,8},{10,11... | collective-permute-start | bytes 589832 | tf_op jit(solution)/shard_map/ppermute | solution.py:563
  42.3 3.9 %collective-permute-start.15 = (bf16[128,768]{1,0:T(8,128)(2,1)S(1)}, bf16[128,768]{1,0:T(8,128)(2,1)S(1)}, u32[]{:S(2)}, u32[]{:S(2)}) collective-permute-start(bf16[128,768]{1,0:T(8,128)(2,1)S(1)} %collective-permute-done.14.far), channel_id=1, source_target_pairs={{0,1},{1,0},{2,3},{3,2},{4,5},{5,4},{6,7},{7,6},{8,9},{9,8},{10,11... | collective-permute-start | bytes 589832 | tf_op jit(solution)/shard_map/ppermute | solution.py:563
  42.5 5.7 %collective-permute-start.12 = (bf16[128,768]{1,0:T(8,128)(2,1)S(1)}, bf16[128,768]{1,0:T(8,128)(2,1)S(1)}, u32[]{:S(2)}, u32[]{:S(2)}) collective-permute-start(bf16[128,768]{1,0:T(8,128)(2,1)S(1)} %collective-permute-done.11.near), channel_id=1, source_target_pairs={{0,4},{1,3},{2,6},{3,1},{4,0},{5,7},{6,2},{7,5},{8,12},{9,11},{10,... | collective-permute-start | bytes 589832 | tf_op jit(solution)/shard_map/ppermute | solution.py:570
  48.1 1.4 %collective-permute-start.16 = (bf16[128,768]{1,0:T(8,128)(2,1)S(1)}, bf16[128,768]{1,0:T(8,128)(2,1)S(1)}, u32[]{:S(2)}, u32[]{:S(2)}) collective-permute-start(bf16[128,768]{1,0:T(8,128)(2,1)S(1)} %collective-permute-done.12.mine), channel_id=1, source_target_pairs={{0,1},{1,0},{2,3},{3,2},{4,5},{5,4},{6,7},{7,6},{8,9},{9,8},{10,11... | collective-permute-start | bytes 589832 | tf_op jit(solution)/shard_map/ppermute | solution.py:563
  48.1 2.8 %copy-start.2 = (bf16[384,768]{1,0:T(8,128)(2,1)S(1)}, bf16[384,768]{1,0:T(8,128)(2,1)}, u32[]{:S(2)}) copy-start(bf16[384,768]{1,0:T(8,128)(2,1)} %weight.3) | copy-start | bytes 1769476
  50.8 1.5 %collective-permute-start.17 = (bf16[256,384]{1,0:T(8,128)(2,1)S(1)}, bf16[256,384]{1,0:T(8,128)(2,1)S(1)}, u32[]{:S(2)}, u32[]{:S(2)}) collective-permute-start(bf16[256,384]{1,0:T(8,128)(2,1)S(1)} %get-tuple-element.99), channel_id=1, source_target_pairs={{0,1},{1,0},{2,3},{3,2},{4,5},{5,4},{6,7},{7,6},{8,9},{9,8},{10,11... | collective-permute-start | bytes 589832 | tf_op jit(solution)/shard_map/ppermute | solution.py:563
